TPU v7x, 32 devices: a whole 2x2x4 slice. The times are simulated.
32 devices in a mesh: seq: 4 (over z), dp: 8 (over y, x, core).
Axes of the slice: x: 2, y: 2, z: 4, core: 2. Of those that a mesh axis runs over, the one named last changes fastest.
Arguments:
- tokens: bfloat16 [8, 1024, 2048], P('dp', 'seq'), may hold values from -6 to 6
- norm_gain: float32 [2048], replicated, may hold values from 0.5 to 1.5
- key_value_weight: bfloat16 [2048, 4096], P('seq'), may hold values from -0.125 to 0.125
- router_weight: bfloat16 [2048, 8], replicated, may hold values from -0.09375 to 0.09375
- query_weight: bfloat16 [8, 2048, 2048], P('dp', 'seq'), may hold values from -0.25 to 0.25
- output_weight: bfloat16 [8, 2048, 2048], P('dp', 'seq'), may hold values from -0.375 to 0.375
- mlp_gain: float32 [2048], replicated, may hold values from 0.5 to 1.5
- mlp_router_weight: bfloat16 [2048, 8], replicated, may hold values from -0.09375 to 0.09375
- mlp_in_weight: bfloat16 [8, 2048, 11264], P('dp', 'seq'), may hold values from -0.125 to 0.125
- mlp_out_weight: bfloat16 [8, 5632, 2048], P('dp', 'seq'), may hold values from -0.21875 to 0.21875
- key_value_down: bfloat16 [8, 2048, 16], replicated, may hold values from -0.125 to 0.125
- key_value_up: bfloat16 [8, 16, 4096], replicated, may hold values from -0.47851562 to 0.47851562
- query_down: bfloat16 [8, 2048, 16], replicated, may hold values from -0.125 to 0.125
- query_up: bfloat16 [8, 16, 2048], replicated, may hold values from -0.8984375 to 0.8984375
- output_down: bfloat16 [8, 2048, 16], replicated, may hold values from -0.375 to 0.375
- output_up: bfloat16 [8, 16, 2048], replicated, may hold values from -0.71875 to 0.71875
- mlp_in_down: bfloat16 [8, 2048, 16], replicated, may hold values from -0.125 to 0.125
- mlp_in_up: bfloat16 [8, 16, 11264], replicated, may hold values from -0.8984375 to 0.8984375
- mlp_out_down: bfloat16 [8, 5632, 16], replicated, may hold values from -0.21875 to 0.21875
- mlp_out_up: bfloat16 [8, 16, 2048], replicated, may hold values from -0.71875 to 0.71875
- routes: int32 [8, 1024, 2], P('dp', 'seq'), may hold values from 0 to 7, all different within a row; in each aligned block of 256 rows (0 to 255, 256 to 511, ..., all dimensions but the last counted through in order) at most 96 rows name the same one
- mlp_routes: int32 [8, 1024, 2], P('dp', 'seq'), may hold values from 0 to 7, all different within a row; in each aligned block of 256 rows (0 to 255, 256 to 511, ..., all dimensions but the last counted through in order) at most 96 rows name the same one
- adapter_index: int32 [8], P('dp'), may hold values from 0 to 7
- prefix_length: int32 [8], P('dp'), may hold values from 1 to 512
- out_grad: bfloat16 [8, 1024, 2048], P('dp', 'seq'), may hold values from -6 to 6
Outputs:
- out_tokens: bfloat16 [8, 1024, 2048], P('dp', 'seq')
- input_grad: float32 [8, 1024, 2048], P('dp', 'seq')
- key_value_down_grad: float32 [8, 2048, 16], replicated
- key_value_up_grad: float32 [8, 16, 4096], replicated
- query_down_grad: float32 [8, 2048, 16], replicated
- query_up_grad: float32 [8, 16, 2048], replicated
- output_down_grad: float32 [8, 2048, 16], replicated
- output_up_grad: float32 [8, 16, 2048], replicated
- mlp_in_down_grad: float32 [8, 2048, 16], replicated
- mlp_in_up_grad: float32 [8, 16, 11264], replicated
- mlp_out_down_grad: float32 [8, 5632, 16], replicated
- mlp_out_up_grad: float32 [8, 16, 2048], replicated
Inputs may be any that keep to these rules, and one draw needn't show every extreme that they name: `routes`: in each aligned block of 256 rows (one sequence's tokens on one device) no expert is named by more than 96 rows; a token's two experts differ. `mlp_routes`: in each aligned block of 256 rows (one sequence's tokens on one device) no expert is named by more than 96 rows; a token's two experts differ.
All inputs are finite; a program needn't handle non-finite values.
Results may differ from a plain program's by a relative error of at most 0.02.
Values may be sent and summed in bfloat16 or wider, within the bound.
No kernel may reach another device: no remote copies, remote signals or barrier semaphores. Data moves between devices by JAX's collectives and lax.ppermute only.
A program may use at most 448 MiB of HBM per device.

v0:
```python
import math

import jax
import jax.numpy as jnp
from jax import lax
from jax.sharding import PartitionSpec as P

KV_HEADS = 16
HD = 128


norm_eps = 1e-05
rope_base = 10000.0
masked_score = -1e30
largest_entry = lax.Precision.HIGHEST


def rms_norm(values, gain_vector):
    mean_square = jnp.mean(values * values, axis=-1, keepdims=True)
    return values * lax.rsqrt(mean_square + norm_eps) * gain_vector


def rope_tables(positions, head_dim):
    half_width = head_dim // 2
    step_ids = jnp.arange(half_width).astype(jnp.float32)
    frequency = jnp.power(rope_base, -step_ids / half_width)
    angles = positions[:, None] * frequency[None, :]
    return (jnp.cos(angles), jnp.sin(angles))


def rotate(values, cosine_table, sine_table):
    half_width = values.shape[-1] // 2
    first_half = values[..., :half_width]
    second_half = values[..., half_width:]
    return jnp.concatenate(
        [
            first_half * cosine_table - second_half * sine_table,
            second_half * cosine_table + first_half * sine_table,
        ],
        axis=-1,
    )


def gate_softmax(logits, route_ids):
    chosen = jnp.take_along_axis(logits, route_ids, axis=-1)
    highest_score = jnp.max(chosen, axis=-1, keepdims=True)
    weights = jnp.exp(chosen - highest_score)
    return weights / jnp.sum(weights, axis=-1, keepdims=True)


def allowed_keys(query_pos, length, prefix):
    key_pos = jnp.arange(length)
    return (key_pos[None, :] <= query_pos[:, None]) | (key_pos[None, :] < prefix)


def pick_rows(lookup, row_index):
    return jax.vmap(lambda lookup_one, index_one: lookup_one[index_one])(lookup, row_index)


def to_holders_full(buffer, copies):
    experts_here, seqs_here, slots_here, columns = buffer.shape
    widened = jnp.broadcast_to(
        buffer[:, None], (experts_here, copies, seqs_here, slots_here, columns)
    )
    return widened.reshape(experts_here * copies, seqs_here, slots_here, columns)


def to_holders_cut(buffer, copies):
    experts_here, seqs_here, slots_here, columns = buffer.shape
    pieces = buffer.reshape(experts_here, seqs_here, slots_here, copies, columns // copies)
    return pieces.transpose(0, 3, 1, 2, 4).reshape(
        experts_here * copies, seqs_here, slots_here, columns // copies
    )


def from_holders_join(home, copies):
    holders_here, seqs_here, slots_here, columns = home.shape
    experts_here = holders_here // copies
    joined = home.reshape(experts_here, copies, seqs_here, slots_here, columns).transpose(
        2, 0, 3, 1, 4
    )
    return joined.reshape(seqs_here, experts_here * slots_here, copies * columns)


def from_holders_add(home, copies):
    holders_here, seqs_here, slots_here, columns = home.shape
    experts_here = holders_here // copies
    added = jnp.sum(home.reshape(experts_here, copies, seqs_here, slots_here, columns), axis=1)
    return added.transpose(1, 0, 2, 3).reshape(seqs_here, experts_here * slots_here, columns)


def slot_layout(route_ids, expert_count, capacity):
    seq_count, row_count, top_count = route_ids.shape
    expert_hits = route_ids[..., None] == jnp.arange(expert_count)
    hits_flat = expert_hits.astype(jnp.int32).reshape(
        seq_count, row_count * top_count, expert_count
    )
    slot_ranks = jnp.sum((jnp.cumsum(hits_flat, axis=1) - 1) * hits_flat, axis=2)
    slot_ranks = slot_ranks.reshape(seq_count, row_count, top_count)
    placement = expert_hits[..., None] & (slot_ranks[..., None, None] == jnp.arange(capacity))
    slot_index = (route_ids * capacity + slot_ranks).reshape(seq_count, row_count * top_count)
    return (placement.astype(jnp.bfloat16), slot_index)


def gather_weights(key_value_weight, query_weight, output_weight, mlp_in_weight, mlp_out_weight):
    gathered = (
        lax.all_gather(key_value_weight, "seq", axis=0, tiled=True),
        lax.all_gather(query_weight, "seq", axis=1, tiled=True),
        lax.all_gather(output_weight, "seq", axis=1, tiled=True),
        lax.all_gather(mlp_in_weight, "seq", axis=1, tiled=True),
        lax.all_gather(mlp_out_weight, "seq", axis=1, tiled=True),
    )
    return (gathered[0], gathered[1][0], gathered[2][0], gathered[3][0], gathered[4][0])


def gather_keys(keys_local, values_local):
    return (
        lax.all_gather(keys_local, "seq", axis=1, tiled=True),
        lax.all_gather(values_local, "seq", axis=1, tiled=True),
    )


def send_home(first_part, second_part):
    return (
        lax.all_to_all(first_part, "dp", split_axis=0, concat_axis=0, tiled=True),
        lax.all_to_all(second_part, "dp", split_axis=0, concat_axis=0, tiled=True),
    )


def body(
    tokens,
    norm_gain,
    key_value_weight,
    router_weight,
    query_weight,
    output_weight,
    mlp_gain,
    mlp_router_weight,
    mlp_in_weight,
    mlp_out_weight,
    key_value_down,
    key_value_up,
    query_down,
    query_up,
    output_down,
    output_up,
    mlp_in_down,
    mlp_in_up,
    mlp_out_down,
    mlp_out_up,
    routes,
    mlp_routes,
    adapter_index,
    prefix_length,
    out_grad,
):
    seq_count, row_count, model_width = tokens.shape
    expert_count = router_weight.shape[1]
    top_count = routes.shape[2]
    copies = lax.axis_size("dp") // expert_count
    holder_part = lax.axis_index("dp") % copies
    length = row_count * lax.axis_size("seq")
    head_dim = HD
    kv_heads = KV_HEADS
    kv_width = kv_heads * head_dim
    capacity = 3 * row_count // 8
    score_scale = 1.0 / math.sqrt(head_dim)
    adapter_count, rank_count = (key_value_down.shape[0], key_value_down.shape[2])
    code_width = adapter_count * rank_count
    hidden_part = mlp_in_weight.shape[2] // 2
    inputs_float = tokens.astype(jnp.float32)
    normed_float, norm_back = jax.vjp(lambda values: rms_norm(values, norm_gain), inputs_float)
    normalized_input = normed_float.astype(jnp.bfloat16)
    normed_wide = normalized_input.astype(jnp.float32)
    pair_full, query_full, output_full, inner_full, outer_full = gather_weights(
        key_value_weight, query_weight, output_weight, mlp_in_weight, mlp_out_weight
    )
    adapter_hot = adapter_index[:, None] == jnp.arange(adapter_count)[None, :]
    hot_low = adapter_hot.astype(jnp.bfloat16)
    hot_float = adapter_hot.astype(jnp.float32)

    def choose_entries(lookup):
        return jnp.einsum(
            "sa,a...->s...", hot_low, lookup, preferred_element_type=jnp.float32
        ).astype(jnp.bfloat16)

    pair_down, adapter_pair_upper = (choose_entries(key_value_down), choose_entries(key_value_up))
    query_lower, query_upper = (choose_entries(query_down), choose_entries(query_up))
    output_lower, output_upper = (choose_entries(output_down), choose_entries(output_up))
    inner_lower, outer_upper = (choose_entries(mlp_in_down), choose_entries(mlp_out_up))
    adapter_pair_lower = jnp.einsum(
        "std,sdr->str", normalized_input, pair_down, preferred_element_type=jnp.float32
    ).astype(jnp.bfloat16)
    adapter_pair_values = jnp.einsum(
        "std,dc->stc", normalized_input, pair_full, preferred_element_type=jnp.float32
    )
    adapter_pair_values = adapter_pair_values + jnp.einsum(
        "str,src->stc", adapter_pair_lower, adapter_pair_upper, preferred_element_type=jnp.float32
    )
    query_pos = lax.axis_index("seq") * row_count + jnp.arange(row_count)
    cosine_table, sine_table = rope_tables(query_pos.astype(jnp.float32), head_dim)
    keys_local = rotate(
        adapter_pair_values[..., :kv_width].reshape(seq_count, row_count, kv_heads, head_dim),
        cosine_table[:, None, :],
        sine_table[:, None, :],
    ).astype(jnp.bfloat16)
    values_local = (
        adapter_pair_values[..., kv_width:]
        .reshape(seq_count, row_count, kv_heads, head_dim)
        .astype(jnp.bfloat16)
    )
    keys_all, values_all = gather_keys(keys_local, values_local)
    logits = jnp.einsum(
        "std,de->ste", normalized_input, router_weight, preferred_element_type=jnp.float32
    )
    gate_values, gate_back = jax.vjp(lambda values: gate_softmax(values, routes), logits)
    place_low, slot_index = slot_layout(routes, expert_count, capacity)
    query_send = jnp.einsum(
        "strem,std->esmd", place_low, normalized_input, preferred_element_type=jnp.float32
    )
    query_send = to_holders_full(query_send.astype(jnp.bfloat16), copies)
    query_parts = jnp.einsum(
        "nskd,dq->nskq",
        lax.all_to_all(query_send, "dp", split_axis=0, concat_axis=0, tiled=True),
        query_full,
        preferred_element_type=jnp.float32,
    )
    query_home = lax.all_to_all(query_parts, "dp", split_axis=0, concat_axis=0, tiled=True)
    query_base = pick_rows(from_holders_join(query_home, copies), slot_index)
    query_base = query_base.reshape(seq_count, row_count, top_count, query_base.shape[-1])
    query_low = jnp.einsum(
        "std,sdr->str", normalized_input, query_lower, preferred_element_type=jnp.float32
    ).astype(jnp.bfloat16)
    query_extra = jnp.einsum(
        "str,srq->stq", query_low, query_upper, preferred_element_type=jnp.float32
    )
    query_pre = query_base + query_extra[:, :, None, :]
    query_heads = query_pre.shape[-1] // head_dim
    query_rot = rotate(
        query_pre.reshape(seq_count, row_count, top_count, query_heads, head_dim),
        cosine_table[:, None, None, :],
        sine_table[:, None, None, :],
    ).astype(jnp.bfloat16)

    def attend(operands):
        query_seq, key_seq, value_seq, prefix = operands
        scores = (
            jnp.einsum("trhd,jhd->rhtj", query_seq, key_seq, preferred_element_type=jnp.float32)
            * score_scale
        )
        scores = jnp.where(allowed_keys(query_pos, length, prefix), scores, masked_score)
        highest_score = jnp.max(scores, axis=-1, keepdims=True)
        weights = jnp.exp(scores - highest_score)
        totals = jnp.sum(weights, axis=-1, keepdims=True)
        attended_seq = jnp.einsum(
            "rhtj,jhd->trhd",
            (weights / totals).astype(jnp.bfloat16),
            value_seq,
            preferred_element_type=jnp.float32,
        )
        return (attended_seq, highest_score + jnp.log(totals))

    attended, log_totals = lax.map(attend, (query_rot, keys_all, values_all, prefix_length))
    attended_low = attended.reshape(seq_count, row_count, top_count, query_heads * head_dim).astype(
        jnp.bfloat16
    )
    output_send = jnp.einsum(
        "strem,strq->esmq", place_low, attended_low, preferred_element_type=jnp.float32
    )
    output_send = to_holders_cut(output_send.astype(jnp.bfloat16), copies)
    output_parts = jnp.einsum(
        "nskq,qd->nskd",
        lax.all_to_all(output_send, "dp", split_axis=0, concat_axis=0, tiled=True),
        output_full,
        preferred_element_type=jnp.float32,
    )
    output_home = lax.all_to_all(output_parts, "dp", split_axis=0, concat_axis=0, tiled=True)
    branch_base = pick_rows(from_holders_add(output_home, copies), slot_index)
    branch_base = branch_base.reshape(seq_count, row_count, top_count, model_width)
    output_low = jnp.einsum(
        "strq,sqk->strk", attended_low, output_lower, preferred_element_type=jnp.float32
    ).astype(jnp.bfloat16)
    branch = branch_base + jnp.einsum(
        "strk,skd->strd", output_low, output_upper, preferred_element_type=jnp.float32
    )
    middle = inputs_float + jnp.sum(gate_values[..., None] * branch, axis=2)
    normed_mlp_float, mlp_norm_back = jax.vjp(lambda values: rms_norm(values, mlp_gain), middle)
    normed_mlp = normed_mlp_float.astype(jnp.bfloat16)
    normed_mlp_wide = normed_mlp.astype(jnp.float32)
    mlp_logits = jnp.einsum(
        "std,de->ste", normed_mlp, mlp_router_weight, preferred_element_type=jnp.float32
    )
    mlp_gates, mlp_gate_back = jax.vjp(lambda values: gate_softmax(values, mlp_routes), mlp_logits)
    mlp_place, mlp_slots = slot_layout(mlp_routes, expert_count, capacity)
    grad_float = out_grad.astype(jnp.float32)
    inner_low = jnp.einsum(
        "std,sdr->str", normed_mlp, inner_lower, preferred_element_type=jnp.float32
    ).astype(jnp.bfloat16)
    inner_code = jnp.einsum("sa,str->star", hot_low, inner_low, preferred_element_type=jnp.float32)
    inner_code = inner_code.reshape(seq_count, row_count, code_width).astype(jnp.bfloat16)
    mlp_branch_grad = (mlp_gates[..., None] * grad_float[:, :, None, :]).astype(jnp.bfloat16)
    outer_low_grad = jnp.einsum(
        "strd,skd->strk", mlp_branch_grad, outer_upper, preferred_element_type=jnp.float32
    ).astype(jnp.bfloat16)
    outer_code = jnp.einsum(
        "sa,strk->strak", hot_low, outer_low_grad, preferred_element_type=jnp.float32
    )
    outer_code = outer_code.reshape(seq_count, row_count, top_count, code_width).astype(
        jnp.bfloat16
    )
    row_send = jnp.einsum(
        "strem,std->esmd", mlp_place, normed_mlp, preferred_element_type=jnp.float32
    )
    code_send = jnp.einsum(
        "strem,stc->esmc", mlp_place, inner_code, preferred_element_type=jnp.float32
    )
    grad_send = jnp.einsum(
        "strem,strd->esmd", mlp_place, mlp_branch_grad, preferred_element_type=jnp.float32
    )
    back_send = jnp.einsum(
        "strem,strc->esmc", mlp_place, outer_code, preferred_element_type=jnp.float32
    )
    row_send = to_holders_full(row_send.astype(jnp.bfloat16), copies)
    code_send = to_holders_full(code_send.astype(jnp.bfloat16), copies)
    grad_send = to_holders_full(grad_send.astype(jnp.bfloat16), copies)
    back_send = to_holders_full(back_send.astype(jnp.bfloat16), copies)
    inner_slice = lax.dynamic_slice_in_dim(
        mlp_in_up.reshape(adapter_count, rank_count, 2, copies, hidden_part), holder_part, 1, 3
    )
    inner_slice = inner_slice.reshape(code_width, 2 * hidden_part)
    outer_slice = lax.dynamic_slice_in_dim(
        mlp_out_down.reshape(adapter_count, copies, hidden_part, rank_count), holder_part, 1, 1
    )
    outer_slice = outer_slice.reshape(adapter_count, hidden_part, rank_count).transpose(1, 0, 2)
    outer_slice = outer_slice.reshape(hidden_part, code_width)
    rows_in = lax.all_to_all(row_send, "dp", split_axis=0, concat_axis=0, tiled=True)
    code_in = lax.all_to_all(code_send, "dp", split_axis=0, concat_axis=0, tiled=True)
    grad_in = lax.all_to_all(grad_send, "dp", split_axis=0, concat_axis=0, tiled=True)
    back_in = lax.all_to_all(back_send, "dp", split_axis=0, concat_axis=0, tiled=True)
    inner_pre = jnp.einsum("nskd,df->nskf", rows_in, inner_full, preferred_element_type=jnp.float32)
    inner_pre = inner_pre + jnp.einsum(
        "nskc,cf->nskf", code_in, inner_slice, preferred_element_type=jnp.float32
    )
    activated = (jax.nn.silu(inner_pre[..., :hidden_part]) * inner_pre[..., hidden_part:]).astype(
        jnp.bfloat16
    )
    down_parts = jnp.einsum(
        "nskf,fd->nskd", activated, outer_full, preferred_element_type=jnp.float32
    )
    low_parts = jnp.einsum(
        "nskf,fc->nskc", activated, outer_slice, preferred_element_type=jnp.float32
    )
    expert_kept = (down_parts, low_parts, inner_pre, activated, code_in, grad_in, back_in)
    down_parts, low_parts, inner_kept, activated_kept, code_kept, grad_kept, back_kept = expert_kept
    down_home, low_home = send_home(down_parts, low_parts)
    mlp_base = pick_rows(from_holders_add(down_home, copies), mlp_slots)
    mlp_base = mlp_base.reshape(seq_count, row_count, top_count, model_width)
    low_sums = pick_rows(from_holders_add(low_home, copies), mlp_slots)
    low_sums = low_sums.reshape(seq_count, row_count, top_count, adapter_count, rank_count)
    outer_low = jnp.einsum("sa,strak->strk", hot_float, low_sums, precision=largest_entry).astype(
        jnp.bfloat16
    )
    mlp_branch = mlp_base + jnp.einsum(
        "strk,skd->strd", outer_low, outer_upper, preferred_element_type=jnp.float32
    )
    result = (middle + jnp.sum(mlp_gates[..., None] * mlp_branch, axis=2)).astype(jnp.bfloat16)
    pair_back, query_back, output_back, inner_back, outer_back = gather_weights(
        key_value_weight, query_weight, output_weight, mlp_in_weight, mlp_out_weight
    )
    keys_back, values_back = gather_keys(keys_local, values_local)
    mlp_gate_grad = jnp.sum(grad_float[:, :, None, :] * mlp_branch, axis=-1)
    mlp_logit_grad = mlp_gate_back(mlp_gate_grad)[0]
    outer_upper_grad = jnp.einsum(
        "strk,strd->skd", outer_low, mlp_branch_grad, preferred_element_type=jnp.float32
    )
    activated_grad = jnp.einsum(
        "nskd,fd->nskf", grad_kept, outer_back, preferred_element_type=jnp.float32
    )
    activated_grad = activated_grad + jnp.einsum(
        "nskc,fc->nskf", back_kept, outer_slice, preferred_element_type=jnp.float32
    )
    gate_part = inner_kept[..., :hidden_part]
    up_part = inner_kept[..., hidden_part:]
    sigmoid_gate = jax.nn.sigmoid(gate_part)
    gate_part_grad = (
        activated_grad * up_part * sigmoid_gate * (1.0 + gate_part * (1.0 - sigmoid_gate))
    )
    up_part_grad = activated_grad * gate_part * sigmoid_gate
    inner_pre_grad = jnp.concatenate([gate_part_grad, up_part_grad], axis=-1).astype(jnp.bfloat16)
    row_grad_parts = jnp.einsum(
        "nskf,df->nskd", inner_pre_grad, inner_back, preferred_element_type=jnp.float32
    )
    code_grad_parts = jnp.einsum(
        "nskf,cf->nskc", inner_pre_grad, inner_slice, preferred_element_type=jnp.float32
    )
    inner_slice_grad = jnp.einsum(
        "nskc,nskf->cf", code_kept, inner_pre_grad, preferred_element_type=jnp.float32
    )
    outer_slice_grad = jnp.einsum(
        "nskf,nskc->fc", activated_kept, back_kept, preferred_element_type=jnp.float32
    )
    row_home, code_home = send_home(row_grad_parts, code_grad_parts)
    mlp_row_grad = pick_rows(from_holders_add(row_home, copies), mlp_slots)
    mlp_row_grad = jnp.sum(
        mlp_row_grad.reshape(seq_count, row_count, top_count, model_width), axis=2
    )
    code_sums = pick_rows(from_holders_add(code_home, copies), mlp_slots)
    code_sums = code_sums.reshape(seq_count, row_count, top_count, adapter_count, rank_count)
    inner_low_grad = jnp.einsum("sa,strak->stk", hot_float, code_sums, precision=largest_entry)
    inner_lower_grad = jnp.einsum(
        "std,str->sdr", normed_mlp_wide, inner_low_grad, precision=largest_entry
    )
    normed_mlp_grad = mlp_row_grad + jnp.einsum(
        "str,sdr->std", inner_low_grad, inner_lower.astype(jnp.float32), precision=largest_entry
    )
    normed_mlp_grad = normed_mlp_grad + jnp.einsum(
        "ste,de->std",
        mlp_logit_grad,
        mlp_router_weight.astype(jnp.float32),
        precision=largest_entry,
    )
    middle_grad = mlp_norm_back(normed_mlp_grad)[0] + grad_float
    inner_up_full = jnp.zeros((adapter_count, rank_count, 2, copies, hidden_part), jnp.float32)
    inner_up_full = lax.dynamic_update_slice_in_dim(
        inner_up_full,
        inner_slice_grad.reshape(adapter_count, rank_count, 2, 1, hidden_part),
        holder_part,
        3,
    )
    inner_up_full = inner_up_full.reshape(adapter_count, rank_count, 2 * copies * hidden_part)
    outer_down_full = jnp.zeros((adapter_count, copies, hidden_part, rank_count), jnp.float32)
    outer_piece = outer_slice_grad.reshape(hidden_part, adapter_count, rank_count).transpose(
        1, 0, 2
    )
    outer_down_full = lax.dynamic_update_slice_in_dim(
        outer_down_full,
        outer_piece.reshape(adapter_count, 1, hidden_part, rank_count),
        holder_part,
        1,
    )
    outer_down_full = outer_down_full.reshape(adapter_count, copies * hidden_part, rank_count)
    gate_grad = jnp.sum(middle_grad[:, :, None, :] * branch, axis=-1)
    branch_grad = (gate_values[..., None] * middle_grad[:, :, None, :]).astype(jnp.bfloat16)
    logit_grad = gate_back(gate_grad)[0]
    output_upper_grad = jnp.einsum(
        "strk,strd->skd", output_low, branch_grad, preferred_element_type=jnp.float32
    )
    output_low_grad = jnp.einsum(
        "strd,skd->strk", branch_grad, output_upper, preferred_element_type=jnp.float32
    )
    output_lower_grad = jnp.einsum(
        "strq,strk->sqk", attended_low.astype(jnp.float32), output_low_grad, precision=largest_entry
    )
    attended_extra = jnp.einsum(
        "strk,sqk->strq", output_low_grad, output_lower.astype(jnp.float32), precision=largest_entry
    )
    branch_send = jnp.einsum(
        "strem,strd->esmd", place_low, branch_grad, preferred_element_type=jnp.float32
    )
    branch_send = to_holders_full(branch_send.astype(jnp.bfloat16), copies)
    head_parts = jnp.einsum(
        "nskd,qd->nskq",
        lax.all_to_all(branch_send, "dp", split_axis=0, concat_axis=0, tiled=True),
        output_back,
        preferred_element_type=jnp.float32,
    )
    head_home = lax.all_to_all(head_parts, "dp", split_axis=0, concat_axis=0, tiled=True)
    attended_grad = pick_rows(from_holders_join(head_home, copies), slot_index)
    attended_grad = (
        attended_grad.reshape(seq_count, row_count, top_count, query_heads * head_dim)
        + attended_extra
    )
    attended_grad = attended_grad.astype(jnp.bfloat16).reshape(
        seq_count, row_count, top_count, query_heads, head_dim
    )

    def attend_back(operands):
        query_seq, key_seq, value_seq, prefix, log_total, grad_seq = operands
        scores = (
            jnp.einsum("trhd,jhd->rhtj", query_seq, key_seq, preferred_element_type=jnp.float32)
            * score_scale
        )
        scores = jnp.where(allowed_keys(query_pos, length, prefix), scores, masked_score)
        probabilities = jnp.exp(scores - log_total)
        prob_grad = jnp.einsum(
            "trhd,jhd->rhtj", grad_seq, value_seq, preferred_element_type=jnp.float32
        )
        weighted_grad = jnp.sum(probabilities * prob_grad, axis=-1, keepdims=True)
        score_grad = (probabilities * (prob_grad - weighted_grad)).astype(jnp.bfloat16)
        query_grad = (
            jnp.einsum("rhtj,jhd->trhd", score_grad, key_seq, preferred_element_type=jnp.float32)
            * score_scale
        )
        key_grad = (
            jnp.einsum("rhtj,trhd->jhd", score_grad, query_seq, preferred_element_type=jnp.float32)
            * score_scale
        )
        value_grad = jnp.einsum(
            "rhtj,trhd->jhd",
            probabilities.astype(jnp.bfloat16),
            grad_seq,
            preferred_element_type=jnp.float32,
        )
        return (query_grad, key_grad, value_grad)

    rot_grad, key_grads, value_grads = lax.map(
        attend_back, (query_rot, keys_back, values_back, prefix_length, log_totals, attended_grad)
    )
    key_home, value_home = (
        lax.psum_scatter(key_grads, "seq", scatter_dimension=1, tiled=True),
        lax.psum_scatter(value_grads, "seq", scatter_dimension=1, tiled=True),
    )
    key_pre_grad = rotate(key_home, cosine_table[:, None, :], -sine_table[:, None, :])
    pair_grad = jnp.concatenate(
        [
            key_pre_grad.reshape(seq_count, row_count, kv_width),
            value_home.reshape(seq_count, row_count, kv_width),
        ],
        axis=-1,
    ).astype(jnp.bfloat16)
    query_pre_grad = rotate(rot_grad, cosine_table[:, None, None, :], -sine_table[:, None, None, :])
    query_pre_grad = query_pre_grad.reshape(
        seq_count, row_count, top_count, query_heads * head_dim
    ).astype(jnp.bfloat16)
    query_send_back = jnp.einsum(
        "strem,strq->esmq", place_low, query_pre_grad, preferred_element_type=jnp.float32
    )
    query_send_back = to_holders_cut(query_send_back.astype(jnp.bfloat16), copies)
    input_parts = jnp.einsum(
        "nskq,dq->nskd",
        lax.all_to_all(query_send_back, "dp", split_axis=0, concat_axis=0, tiled=True),
        query_back,
        preferred_element_type=jnp.float32,
    )
    input_home = lax.all_to_all(
        input_parts.astype(jnp.bfloat16), "dp", split_axis=0, concat_axis=0, tiled=True
    ).astype(input_parts.dtype)
    normed_grad = pick_rows(from_holders_add(input_home, copies), slot_index)
    normed_grad = jnp.sum(normed_grad.reshape(seq_count, row_count, top_count, model_width), axis=2)
    query_upper_grad = jnp.einsum(
        "stk,strq->skq", query_low, query_pre_grad, preferred_element_type=jnp.float32
    )
    query_low_grad = jnp.einsum(
        "strq,skq->stk", query_pre_grad, query_upper, preferred_element_type=jnp.float32
    )
    query_lower_grad = jnp.einsum(
        "std,str->sdr", normed_wide, query_low_grad, precision=largest_entry
    )
    pair_upper_grad = jnp.einsum(
        "str,stc->src", adapter_pair_lower, pair_grad, preferred_element_type=jnp.float32
    )
    pair_low_grad = jnp.einsum(
        "stc,src->str", pair_grad, adapter_pair_upper, preferred_element_type=jnp.float32
    )
    pair_lower_grad = jnp.einsum(
        "std,str->sdr", normed_wide, pair_low_grad, precision=largest_entry
    )
    normed_grad = normed_grad + jnp.einsum(
        "str,sdr->std", query_low_grad, query_lower.astype(jnp.float32), precision=largest_entry
    )
    normed_grad = normed_grad + jnp.einsum(
        "stc,dc->std", pair_grad, pair_back, preferred_element_type=jnp.float32
    )
    normed_grad = normed_grad + jnp.einsum(
        "str,sdr->std", pair_low_grad, pair_down.astype(jnp.float32), precision=largest_entry
    )
    normed_grad = normed_grad + jnp.einsum(
        "ste,de->std", logit_grad, router_weight.astype(jnp.float32), precision=largest_entry
    )
    input_grad = norm_back(normed_grad)[0] + middle_grad

    def per_adapter(per_sequence):
        return jnp.einsum("sa,s...->a...", hot_float, per_sequence, precision=largest_entry)

    adapter_totals = lax.psum(
        (
            per_adapter(pair_lower_grad),
            per_adapter(pair_upper_grad),
            per_adapter(query_lower_grad),
            per_adapter(query_upper_grad),
            per_adapter(output_lower_grad),
            per_adapter(output_upper_grad),
            per_adapter(inner_lower_grad),
            inner_up_full,
            outer_down_full,
            per_adapter(outer_upper_grad),
        ),
        ("seq", "dp"),
    )
    return (
        result,
        input_grad,
        adapter_totals[0],
        adapter_totals[1],
        adapter_totals[2],
        adapter_totals[3],
        adapter_totals[4],
        adapter_totals[5],
        adapter_totals[6],
        adapter_totals[7],
        adapter_totals[8],
        adapter_totals[9],
    )


def solution(mesh):
    placed = (
        P("dp", "seq", None),
        P(),
        P("seq", None),
        P(),
        P("dp", "seq", None),
        P("dp", "seq", None),
        P(),
        P(),
        P("dp", "seq", None),
        P("dp", "seq", None),
        P(),
        P(),
        P(),
        P(),
        P(),
        P(),
        P(),
        P(),
        P(),
        P(),
        P("dp", "seq", None),
        P("dp", "seq", None),
        P("dp"),
        P("dp"),
        P("dp", "seq", None),
    )
    return jax.shard_map(
        body,
        mesh=mesh,
        in_specs=placed,
        out_specs=(
            P("dp", "seq", None),
            P("dp", "seq", None),
            P(),
            P(),
            P(),
            P(),
            P(),
            P(),
            P(),
            P(),
            P(),
            P(),
        ),
        check_vma=False,
    )
```

profile of v0, /device:TPU:0, one launch (start us, length us, event | category | flops | bytes accessed | tf_op | source)
XLA Modules:
  0.0 3143.9 jit_solution(7900302807374109782)
XLA Ops:
  19.8 279.3 %all-gather.8.cloned.1.call-done = bf16[2048,4096]{1,0:T(8,128)(2,1)} async-done(((bf16[512,4096]{1,0:T(8,128)(2,1)}), bf16[2048,4096]{1,0:T(8,128)(2,1)}) %all-gather.8.cloned.1.call-update) | async-done | bytes 16777232 | tf_op jit(solution)/shard_map/all_gather | solution.py:107
  299.1 8.5 fusion.274
  326.6 41.4 %all_to_all.80 = bf16[8,1,96,2048]{3,2,1,0:T(8,128)(2,1)} all-to-all(bf16[8,1,96,2048]{3,2,1,0:T(8,128)(2,1)S(1)} %convert_bitcast_fusion.1), channel_id=1, replica_groups=mesh['seq'=4,'dp'=8] {'dp'}, dimensions={0} | all-to-all | bytes 6291456 | tf_op jit(solution)/shard_map/all_to_all | solution.py:224
  368.0 80.5 %all-gather.14.cloned.1.call-done = bf16[1,2048,2048]{2,1,0:T(8,128)(2,1)} async-done(((bf16[1,512,2048]{2,1,0:T(8,128)(2,1)}), bf16[1,2048,2048]{2,1,0:T(8,128)(2,1)}) %all-gather.14.cloned.1.call-update) | async-done | bytes 8388624 | tf_op jit(solution)/shard_map/all_gather | solution.py:108
  448.6 11.7 fusion.57
  476.5 60.2 %all-to-all-done.1 = f32[8,1,96,2048]{3,2,1,0:T(8,128)} async-done(((f32[8,1,96,2048]{3,2,1,0:T(8,128)}), f32[8,1,96,2048]{3,2,1,0:T(8,128)}, u32[]{:S(2)}, u32[]{:S(2)}) %all-to-all-start.1) | async-done | bytes 6291488 | tf_op jit(solution)/shard_map/all_to_all | solution.py:228
  536.7 13.1 gather_fusion
  559.1 16.7 fusion.27
  575.9 14.9 fusion.7
  590.7 20.1 all-gather.10.cloned.1.call-done
  610.9 19.5 convert_bitcast_fusion.3
  641.6 118.5 %all-gather.16.cloned.1.call-done = bf16[1,2048,2048]{2,1,0:T(8,128)(2,1)} async-done(((bf16[1,512,2048]{2,1,0:T(8,128)(2,1)}), bf16[1,2048,2048]{2,1,0:T(8,128)(2,1)}) %all-gather.16.cloned.1.call-update) | async-done | bytes 8388624 | tf_op jit(solution)/shard_map/all_gather | solution.py:109
  760.1 11.9 fusion.60
  777.2 5.5 fusion.179
  782.7 7.1 copy.413
  808.9 39.9 %all-to-all-done.3 = f32[8,1,96,2048]{3,2,1,0:T(8,128)} async-done(((f32[8,1,96,2048]{3,2,1,0:T(8,128)}), f32[8,1,96,2048]{3,2,1,0:T(8,128)}, u32[]{:S(2)}, u32[]{:S(2)}) %all-to-all-start.3) | async-done | bytes 6291488 | tf_op jit(solution)/shard_map/all_to_all | solution.py:277
  848.8 12.8 gather_fusion.1
  861.6 5.9 reshape.1536
  867.6 7.4 multiply_reduce_fusion.3
  903.5 26.3 all-to-all-done.8
  934.3 216.6 %all-gather.20.cloned.1.call-done = bf16[1,5632,2048]{2,1,0:T(8,128)(2,1)} async-done(((bf16[1,1408,2048]{2,1,0:T(8,128)(2,1)}), bf16[1,5632,2048]{2,1,0:T(8,128)(2,1)}) %all-gather.20.cloned.1.call-update) | async-done | bytes 23068688 | tf_op jit(solution)/shard_map/all_gather | solution.py:111
  1150.9 27.0 fusion.9
  1181.8 736.8 %all-gather.18.cloned.1.call-done = bf16[1,2048,11264]{2,1,0:T(8,128)(2,1)} async-done(((bf16[1,512,11264]{2,1,0:T(8,128)(2,1)}), bf16[1,2048,11264]{2,1,0:T(8,128)(2,1)}) %all-gather.18.cloned.1.call-update) | async-done | bytes 46137360 | tf_op jit(solution)/shard_map/all_gather | solution.py:110
  1918.6 45.3 %fusion.2 = f32[8,96,11264]{2,1,0:T(8,128)} fusion(bf16[1,2048,11264]{2,1,0:T(8,128)(2,1)} %all-gather.18.cloned.1.call-done, bf16[8,1,96,2048]{3,2,1,0:T(8,128)(2,1)} %all-to-all-done.4), kind=kOutput, calls=%fused_computation.14 | convolution fusion | flops 35433480192 | bytes 83886080 | tf_op jit(solution)/shard_map/nskd,df->nskf/dot_general | solution.py:340
  1967.5 25.2 add_bitcast_fusion
  1992.8 26.5 fusion.34
  2019.3 7.0 fusion.139
  2030.7 9.1 fusion.145
  2044.0 24.9 fusion.66
  2073.6 45.2 %fusion.71 = f32[8,1,96,2048]{3,2,1,0:T(8,128)} fusion(bf16[1,2048,11264]{2,1,0:T(8,128)(2,1)} %all-gather.18.cloned.1.call-done, bf16[8,96,5632]{2,1,0:T(8,128)(2,1)} %get-tuple-element.104, bf16[8,96,5632]{2,1,0:T(8,128)(2,1)} %get-tuple-element.103), kind=kOutput, calls=%fused_computation.109 | convolution fusion | flops 35468083200 | bytes 69730304 | tf_op jit(solution)/shard_map/nskf,df->nskd/dot_general | solution.py:390
  2118.8 26.5 all-to-all-done.6
  2162.5 12.8 gather_fusion.2
  2175.3 6.0 reshape.1549
  2181.3 6.9 multiply_reduce_fusion.1
  2188.6 33.5 %all-to-all-done.10 = f32[8,1,96,2048]{3,2,1,0:T(8,128)} async-done(((f32[8,1,96,2048]{3,2,1,0:T(8,128)}), f32[8,1,96,2048]{3,2,1,0:T(8,128)}, u32[]{:S(2)}, u32[]{:S(2)}) %all-to-all-start.10) | async-done | bytes 6291488 | tf_op jit(solution)/shard_map/all_to_all | solution.py:125
  2222.0 12.8 gather_fusion.4
  2234.8 6.0 reshape.1554
  2240.9 7.2 reduce_sum.269
  2250.4 24.4 scatter_fusion
  2281.7 40.8 %all_to_all.81 = bf16[8,1,96,2048]{3,2,1,0:T(8,128)(2,1)S(1)} all-to-all(bf16[8,1,96,2048]{3,2,1,0:T(8,128)(2,1)S(1)} %fusion.94), channel_id=1, replica_groups=mesh['seq'=4,'dp'=8] {'dp'}, dimensions={0} | all-to-all | bytes 6291456 | tf_op jit(solution)/shard_map/all_to_all | solution.py:463
  2322.6 8.6 fusion.63
  2336.9 70.8 %all-to-all-done.13 = f32[8,1,96,2048]{3,2,1,0:T(8,128)} async-done(((f32[8,1,96,2048]{3,2,1,0:T(8,128)}), f32[8,1,96,2048]{3,2,1,0:T(8,128)}, u32[]{:S(2)}, u32[]{:S(2)}) %all-to-all-start.13) | async-done | bytes 6291488 | tf_op jit(solution)/shard_map/all_to_all | solution.py:467
  2407.7 12.8 gather_fusion.6
  2420.5 5.9 reshape.1558
  2426.4 6.2 fusion.56
  2438.8 25.6 fusion.4
  2464.4 28.2 fusion.6
  2492.6 14.9 fusion.35
  2507.6 18.5 fusion.83
  2527.4 6.4 fusion.44
  2533.9 11.2 fusion.24
  2548.7 11.3 multiply_bitcast_fusion
  2574.3 5.2 fusion.95
  2587.2 61.4 %reduce-scatter.3.cloned.1.call-done = f32[1,256,16,128]{3,1,2,0:T(8,128)} async-done(((f32[1,1024,16,128]{3,1,2,0:T(8,128)}), f32[1,256,16,128]{3,1,2,0:T(8,128)}) %reduce-scatter.3.cloned.1.call-update) | async-done | bytes 2097168 | tf_op jit(solution)/shard_map/reduce_scatter | solution.py:510
  2655.8 140.4 %reduce-scatter.5.cloned.1.call-done = f32[1,256,16,128]{1,3,2,0:T(8,128)} async-done(((f32[1,1024,16,128]{1,3,2,0:T(8,128)}), f32[1,256,16,128]{1,3,2,0:T(8,128)}) %reduce-scatter.5.cloned.1.call-update) | async-done | bytes 2097168 | tf_op jit(solution)/shard_map/reduce_scatter | solution.py:511
  2805.2 12.0 fusion.96
  2825.5 24.4 scatter_fusion.1
  2849.8 26.7 all-to-all-done.15
  2876.6 5.4 convert.84
  2882.0 13.1 gather_fusion.7
  2895.0 6.1 reshape.1560
  2901.2 7.5 reduce_sum.322
  2908.7 13.3 fusion.172
  2931.1 188.3 %all-reduce.3.cloned.1.call-done = (f32[8,2048,16]{1,2,0:T(8,128)}, f32[8,16,4096]{2,1,0:T(8,128)}, f32[8,2048,16]{1,2,0:T(8,128)}, f32[8,16,2048]{2,1,0:T(8,128...) async-done(((f32[8,2048,16]{1,2,0:T(8,128)}, ...) | async-done | bytes 18087952 | tf_op jit(solution)/shard_map/psum | solution.py:575
  (528 shorter events, 260.1 us)
Async XLA Ops:
  7.2 1960.4 %copy-start = (bf16[8,16,11264]{2,1,0:T(8,128)(2,1)S(1)}, bf16[8,16,11264]{2,1,0:T(8,128)(2,1)}, u32[]{:S(2)}) copy-start(bf16[8,16,11264]{2,1,0:T(8,128)(2,1)} %param.44) | copy-start | bytes 8650756
  7.2 291.9 %all-gather.8.cloned.1.call-start = ((), (), s32[]{:S(2)}) async-start(), calls=%async_computation.18 | async-start | bytes 20971520 | tf_op jit(solution)/shard_map/all_gather | solution.py:107
  8.0 440.6 %all-gather.14.cloned.1.call-start = ((), (), s32[]{:S(2)}) async-start(), calls=%async_computation.21 | async-start | bytes 10485760 | tf_op jit(solution)/shard_map/all_gather | solution.py:108
  8.7 550.4 %all-gather.12.cloned.1.call-start = ((), (), s32[]{:S(2)}) async-start(), calls=%async_computation.20 | async-start | bytes 5242880 | tf_op jit(solution)/shard_map/all_gather | solution.py:118
  10.2 297.5 %copy-start.34 = (bf16[1,2048,16]{2,1,0:T(8,128)(2,1)}, bf16[1,2048,16]{2,1,0:T(8,128)(2,1)S(1)}, u32[]{:S(2)}) copy-start(bf16[1,2048,16]{2,1,0:T(8,128)(2,1)S(1)} %copy.400) | copy-start | bytes 196612
  13.7 541.9 %copy-start.41 = (f32[256,64]{1,0:T(8,128)}, f32[256,64]{1,0:T(8,128)S(1)}, u32[]{:S(2)}) copy-start(f32[256,64]{1,0:T(8,128)S(1)} %get-tuple-element.124) | copy-start | bytes 196612
  19.8 287.8 %copy-start.106 = (bf16[256,16]{0,1:T(8,128)(2,1)}, bf16[256,16]{0,1:T(8,128)(2,1)S(1)}, u32[]{:S(2)}) copy-start(bf16[256,16]{0,1:T(8,128)(2,1)S(1)} %convolution_convert_fusion.3) | copy-start | bytes 24580
  314.2 296.6 %all-gather.10.cloned.1.call-start = ((), (), s32[]{:S(2)}) async-start(), calls=%async_computation.19 | async-start | bytes 5242880 | tf_op jit(solution)/shard_map/all_gather | solution.py:119
  319.3 440.8 %all-gather.16.cloned.1.call-start = ((), (), s32[]{:S(2)}) async-start(), calls=%async_computation.22 | async-start | bytes 10485760 | tf_op jit(solution)/shard_map/all_gather | solution.py:109
  319.9 831.0 %all-gather.20.cloned.1.call-start = ((), (), s32[]{:S(2)}) async-start(), calls=%async_computation.24 | async-start | bytes 28835840 | tf_op jit(solution)/shard_map/all_gather | solution.py:111
  320.5 1598.1 %all-gather.18.cloned.1.call-start = ((), (), s32[]{:S(2)}) async-start(), calls=%async_computation.23 | async-start | bytes 57671680 | tf_op jit(solution)/shard_map/all_gather | solution.py:110
  460.3 76.5 %all-to-all-start.1 = ((f32[8,1,96,2048]{3,2,1,0:T(8,128)}), f32[8,1,96,2048]{3,2,1,0:T(8,128)}, u32[]{:S(2)}, u32[]{:S(2)}) async-start(f32[8,1,96,2048]{3,2,1,0:T(8,128)} %fusion.57), calls=%async_computation.1 | async-start | bytes 12582912 | tf_op jit(solution)/shard_map/all_to_all | solution.py:228
  466.0 166.2 %copy-start.137 = (pred[256,2,8]{0,1,2:T(4,128)(4,1)}, pred[256,2,8]{0,1,2:T(4,128)(4,1)S(1)}, u32[]{:S(2)}) copy-start(pred[256,2,8]{0,1,2:T(4,128)(4,1)S(1)} %copy.345) | copy-start | bytes 12292
  476.3 73.6 %copy-start.2 = (s32[512,1]{0,1:T(1,128)}, s32[512,1]{0,1:T(1,128)S(1)}, u32[]{:S(2)}) copy-start(s32[512,1]{0,1:T(1,128)S(1)} %fusion.212) | copy-start | bytes 6148
  476.5 134.3 %copy-start.27 = (pred[256,1024]{0,1:T(8,128)(4,1)}, pred[256,1024]{0,1:T(8,128)(4,1)S(1)}, u32[]{:S(2)}) copy-start(pred[256,1024]{0,1:T(8,128)(4,1)S(1)} %fusion.159) | copy-start | bytes 786436
  575.9 35.0 %copy-start.74 = (f32[2,16,256]{2,0,1:T(2,128)}, f32[2,16,256]{2,0,1:T(2,128)S(1)}, u32[]{:S(2)}) copy-start(f32[2,16,256]{2,0,1:T(2,128)S(1)} %get-tuple-element.132) | copy-start | bytes 98308
  590.7 39.7 %copy-start.89 = (f32[2,16,256]{2,0,1:T(2,128)}, f32[2,16,256]{2,0,1:T(2,128)S(1)}, u32[]{:S(2)}) copy-start(f32[2,16,256]{2,0,1:T(2,128)S(1)} %fusion.7) | copy-start | bytes 98308
  637.1 123.1 %all-to-all-start.2 = ((bf16[8,1,96,2048]{3,2,1,0:T(8,128)(2,1)}), bf16[8,1,96,2048]{3,2,1,0:T(8,128)(2,1)}, u32[]{:S(2)}, u32[]{:S(2)}) async-start(bf16[8,1,96,2048]{3,2,1,0:T(8,128)(2,1)} %fusion.92), calls=%async_computation.2 | async-start | bytes 6291456 | tf_op jit(solution)/shard_map/all_to_all | solution.py:273
  772.0 76.7 %all-to-all-start.3 = ((f32[8,1,96,2048]{3,2,1,0:T(8,128)}), f32[8,1,96,2048]{3,2,1,0:T(8,128)}, u32[]{:S(2)}, u32[]{:S(2)}) async-start(f32[8,1,96,2048]{3,2,1,0:T(8,128)} %fusion.60), calls=%async_computation.3 | async-start | bytes 12582912 | tf_op jit(solution)/shard_map/all_to_all | solution.py:277
  789.8 18.7 copy-start.61
  797.1 51.7 %copy-start.3 = (s32[512,1]{0,1:T(1,128)S(1)}, s32[512,1]{0,1:T(1,128)}, u32[]{:S(2)}) copy-start(s32[512,1]{0,1:T(1,128)} %copy-done.2) | copy-start | bytes 6148
  799.4 62.2 %copy-start.93 = (f32[1,256,2]{1,2,0:T(2,128)}, f32[1,256,2]{1,2,0:T(2,128)S(1)}, u32[]{:S(2)}) copy-start(f32[1,256,2]{1,2,0:T(2,128)S(1)} %get-tuple-element.102) | copy-start | bytes 6148
  799.5 82.8 %copy-start.80 = (pred[256,2,96]{0,2,1:T(8,128)(4,1)}, pred[256,2,96]{0,2,1:T(8,128)(4,1)S(1)}, u32[]{:S(2)}) copy-start(pred[256,2,96]{0,2,1:T(8,128)(4,1)S(1)} %iota_compare_fusion.1) | copy-start | bytes 147460
  800.5 67.1 %copy-start.110 = (f32[256,2]{0,1:T(2,128)}, f32[256,2]{0,1:T(2,128)S(1)}, u32[]{:S(2)}) copy-start(f32[256,2]{0,1:T(2,128)S(1)} %divide_bitcast_fusion.1) | copy-start | bytes 6148
  802.0 65.6 %copy-start.65 = (bf16[1,16,2048]{2,0,1:T(2,128)(2,1)}, bf16[1,16,2048]{2,0,1:T(2,128)(2,1)S(1)}, u32[]{:S(2)}) copy-start(bf16[1,16,2048]{2,0,1:T(2,128)(2,1)S(1)} %fusion.177) | copy-start | bytes 196612
  803.5 89.6 %copy-start.67 = (bf16[1,16,2048]{2,0,1:T(2,128)(2,1)}, bf16[1,16,2048]{2,0,1:T(2,128)(2,1)S(1)}, u32[]{:S(2)}) copy-start(bf16[1,16,2048]{2,0,1:T(2,128)(2,1)S(1)} %fusion.173) | copy-start | bytes 196612
  808.9 58.6 %copy-start.81 = (bf16[256,2,16]{0,2,1:T(8,128)(2,1)}, bf16[256,2,16]{0,2,1:T(8,128)(2,1)S(1)}, u32[]{:S(2)}) copy-start(bf16[256,2,16]{0,2,1:T(8,128)(2,1)S(1)} %convolution_convert_fusion) | copy-start | bytes 49156
  887.4 42.4 %all-to-all-start.8 = ((bf16[8,1,96,2048]{3,2,1,0:T(8,128)(2,1)}), bf16[8,1,96,2048]{3,2,1,0:T(8,128)(2,1)}, u32[]{:S(2)}, u32[]{:S(2)}) async-start(bf16[8,1,96,2048]{3,2,1,0:T(8,128)(2,1)} %fusion.93), calls=%async_computation.8 | async-start | bytes 6291456 | tf_op jit(solution)/shard_map/all_to_all | solution.py:338
  929.8 248.1 %all-to-all-start.4 = ((bf16[8,1,96,2048]{3,2,1,0:T(8,128)(2,1)}), bf16[8,1,96,2048]{3,2,1,0:T(8,128)(2,1)}, u32[]{:S(2)}, u32[]{:S(2)}) async-start(bf16[8,1,96,2048]{3,2,1,0:T(8,128)(2,1)} %convert_bitcast_fusion), calls=%async_computation.4 | async-start | bytes 6291456 | tf_op jit(solution)/shard_map/all_to_all | solution.py:336
  1177.9 786.0 %all-to-all-start.5 = ((bf16[8,1,96,128]{3,2,1,0:T(8,128)(2,1)}), bf16[8,1,96,128]{3,2,1,0:T(8,128)(2,1)S(1)}, u32[]{:S(2)}, u32[]{:S(2)}) async-start(bf16[8,1,96,128]{3,2,1,0:T(8,128)(2,1)} %convert_bitcast_fusion.4), calls=%async_computation.5 | async-start | bytes 393216 | tf_op jit(solution)/shard_map/all_to_all | solution.py:337
  1963.9 28.9 copy-start.44
  1963.9 28.9 all-to-all-start.9
  1992.8 26.5 copy-start.59
  2026.3 13.5 all-to-all-start.7
  2039.8 29.1 all-to-all-start.11
  2068.9 76.4 %all-to-all-start.6 = ((f32[8,1,96,2048]{3,2,1,0:T(8,128)}), f32[8,1,96,2048]{3,2,1,0:T(8,128)}, u32[]{:S(2)}, u32[]{:S(2)}) async-start(f32[8,1,96,2048]{3,2,1,0:T(8,128)} %fusion.66), calls=%async_computation.6 | async-start | bytes 12582912 | tf_op jit(solution)/shard_map/all_to_all | solution.py:125
  2118.8 31.6 %copy-start.116 = (s32[512]{0:T(512)S(1)}, s32[512]{0:T(512)}, u32[]{:S(2)}) copy-start(s32[512]{0:T(512)} %copy-done.115) | copy-start | bytes 6148
  2118.8 31.9 %copy-start.99 = (s32[1,256,2]{1,2,0:T(2,128)S(1)}, s32[1,256,2]{1,2,0:T(2,128)}, u32[]{:S(2)}) copy-start(s32[1,256,2]{1,2,0:T(2,128)} %param.48) | copy-start | bytes 6148
  2118.8 32.2 %copy-start.136 = (s32[256,2,1]{0,1,2:T(2,128)S(1)}, s32[256,2,1]{0,1,2:T(2,128)}, u32[]{:S(2)}) copy-start(s32[256,2,1]{0,1,2:T(2,128)} %get-tuple-element.120) | copy-start | bytes 6148
  2118.8 32.5 %copy-start.126 = (f32[256]{0:T(256)S(1)}, f32[256]{0:T(256)}, u32[]{:S(2)}) copy-start(f32[256]{0:T(256)} %copy-done.125) | copy-start | bytes 3076
  2145.3 76.8 %all-to-all-start.10 = ((f32[8,1,96,2048]{3,2,1,0:T(8,128)}), f32[8,1,96,2048]{3,2,1,0:T(8,128)}, u32[]{:S(2)}, u32[]{:S(2)}) async-start(f32[8,1,96,2048]{3,2,1,0:T(8,128)} %fusion.71), calls=%async_computation.10 | async-start | bytes 12582912 | tf_op jit(solution)/shard_map/all_to_all | solution.py:125
  2162.2 85.9 %copy-start.49 = (f32[256,16]{1,0:T(8,128)}, f32[256,16]{1,0:T(8,128)S(1)}, u32[]{:S(2)}) copy-start(f32[256,16]{1,0:T(8,128)S(1)} %multiply_reduce_fusion.5) | copy-start | bytes 49156
  2162.4 18.8 copy-start.87
  2250.4 24.4 copy-start.7
  2250.4 24.4 copy-start.84
  2250.4 24.4 copy-start.109
  2278.6 44.0 %slice-start.2 = ((s8[8388608]{0:T(1024)(128)(4,1)}), s8[4194304]{0:T(1024)(128)(4,1)S(1)}, s32[]{:S(2)}) async-start(s8[8388608]{0:T(1024)(128)(4,1)} %bitcast.756), calls=%async_computation.30 | async-start | bytes 8388608
  2279.8 42.8 %slice-start.3 = ((s8[8388608]{0:T(1024)(128)(4,1)}), s8[4194304]{0:T(1024)(128)(4,1)S(1)}, s32[]{:S(2)}) async-start(s8[8388608]{0:T(1024)(128)(4,1)} %bitcast.756), calls=%async_computation.31 | async-start | bytes 8388608
  2331.2 76.5 %copy-start.4 = (s32[512,1]{0,1:T(1,128)S(1)}, s32[512,1]{0,1:T(1,128)}, u32[]{:S(2)}) copy-start(s32[512,1]{0,1:T(1,128)} %copy-done.2) | copy-start | bytes 6148
  2331.2 76.5 %all-to-all-start.13 = ((f32[8,1,96,2048]{3,2,1,0:T(8,128)}), f32[8,1,96,2048]{3,2,1,0:T(8,128)}, u32[]{:S(2)}, u32[]{:S(2)}) async-start(f32[8,1,96,2048]{3,2,1,0:T(8,128)} %fusion.63), calls=%async_computation.13 | async-start | bytes 12582912 | tf_op jit(solution)/shard_map/all_to_all | solution.py:467
  2336.1 312.5 %reduce-scatter.3.cloned.1.call-start = ((), (), s32[]{:S(2)}) async-start(), calls=%async_computation.25 | async-start | bytes 10485760 | tf_op jit(solution)/shard_map/reduce_scatter | solution.py:510
  2507.6 288.6 %reduce-scatter.5.cloned.1.call-start = ((), (), s32[]{:S(2)}) async-start(), calls=%async_computation.26 | async-start | bytes 10485760 | tf_op jit(solution)/shard_map/reduce_scatter | solution.py:511
  2533.8 11.3 copy-start.114
  2533.9 11.9 copy-start.21
  2533.9 11.9 copy-start.50
  2533.9 12.5 copy-start.82
  2548.7 11.3 copy-start.42
  2548.7 11.3 copy-start.46
  2579.5 225.6 %all-to-all-start.14 = ((bf16[8,1,96,2048]{3,2,1,0:T(8,128)(2,1)}), bf16[8,1,96,2048]{3,2,1,0:T(8,128)(2,1)}, u32[]{:S(2)}, u32[]{:S(2)}) async-start(bf16[8,1,96,2048]{3,2,1,0:T(8,128)(2,1)} %fusion.95), calls=%async_computation.14 | async-start | bytes 6291456 | tf_op jit(solution)/shard_map/all_to_all | solution.py:531
  2584.1 535.3 %all-reduce.3.cloned.1.call-start = ((), (), s32[]{:S(2)}) async-start(), calls=%async_computation.27 | async-start | bytes 36175872 | tf_op jit(solution)/shard_map/psum | solution.py:575
  2651.6 146.5 %copy-start.107 = (bf16[256,16]{0,1:T(8,128)(2,1)S(1)}, bf16[256,16]{0,1:T(8,128)(2,1)}, u32[]{:S(2)}) copy-start(bf16[256,16]{0,1:T(8,128)(2,1)} %copy-done.106) | copy-start | bytes 24580
  2653.1 147.1 %copy-start.64 = (bf16[1,16,4096]{2,0,1:T(2,128)(2,1)S(1)}, bf16[1,16,4096]{2,0,1:T(2,128)(2,1)}, u32[]{:S(2)}) copy-start(bf16[1,16,4096]{2,0,1:T(2,128)(2,1)} %fusion.157) | copy-start | bytes 393220
  2817.2 59.4 %all-to-all-start.15 = ((bf16[8,1,96,2048]{3,2,1,0:T(8,128)(2,1)}), bf16[8,1,96,2048]{3,2,1,0:T(8,128)(2,1)}, u32[]{:S(2)}, u32[]{:S(2)}) async-start(bf16[8,1,96,2048]{3,2,1,0:T(8,128)(2,1)} %fusion.96), calls=%async_computation.15 | async-start | bytes 6291456 | tf_op jit(solution)/shard_map/all_to_all | solution.py:535
  2908.7 13.3 copy-start.39
  (104 other events, 478.5 us)
Sparse Core Ops, SparseCore 0:
  9.6 289.4 all-gather.7
  300.7 147.8 all-gather.13
  450.7 78.9 all-gather.11
  531.7 79.0 all-gather.9
  612.3 147.8 all-gather.15
  761.6 389.3 all-gather.19
  1152.5 766.0 all-gather.17
  2507.7 140.8 reduce-scatter.2
  2651.0 145.1 reduce-scatter.4
  2805.3 314.0 all-reduce.2
where the time goes:
time: 3160 us; the launch traced here: 3140 us
  waiting for transfers between devices  2130 us (67%)
  matrix products  489 us (15%)
  local copies, waits for them, and re-layouts  193 us (6%)
  other arithmetic  168 us (5%)
  blocking collectives  82.2 us (3%)
  starting transfers between devices  64.4 us (2%)
    all_gather x1, waiting for transfers between devices, gather_weights(): lax.all_gather(mlp_in_weight, 'seq', axis=1, tiled=True)  737 us
    all_gather x1, waiting for transfers between devices, gather_weights(): lax.all_gather(key_value_weight, 'seq', axis=0, tiled=True)  279 us
    all_gather x1, waiting for transfers between devices, gather_weights(): lax.all_gather(mlp_out_weight, 'seq', axis=1, tiled=True)  217 us
    psum x1, waiting for transfers between devices, body(): lax.psum((per_adapter(pair_lower_grad), per_adapter(pair_upper_grad), per...  188 us
    reduce_scatter x1, waiting for transfers between devices, body(): lax.psum_scatter(value_grads, 'seq', scatter_dimension=1, tiled=True)  140 us
    all_gather x1, waiting for transfers between devices, gather_weights(): lax.all_gather(output_weight, 'seq', axis=1, tiled=True)  119 us
    gather x10, local copies, waits for them, and re-layouts, pick_rows(): lookup_one[index_one]  82.9 us
    all_gather x1, waiting for transfers between devices, gather_weights(): lax.all_gather(query_weight, 'seq', axis=1, tiled=True)  80.5 us
  transfers between devices with their start and end apart: 24, of which 16 were waited for; matrix products, arithmetic and copies ran while one was open for 20% of the time, Pallas kernels for 0%

commit v1 on v0

v1 whole, which is shorter than its diff:
```python
import functools
import math

import jax
import jax.numpy as jnp
from jax import lax
from jax.experimental import pallas as pl
from jax.experimental.pallas import tpu as pltpu
from jax.sharding import PartitionSpec as P

KV_HEADS = 16
HD = 128

norm_eps = 1e-05
rope_base = 10000.0
masked_score = -1e30
vmem_bytes = 48 * 2**20

bf16 = jnp.bfloat16
f32 = jnp.float32


def product(left, right, left_dim, right_dim):
    return lax.dot_general(
        left, right, (((left_dim,), (right_dim,)), ((), ())), preferred_element_type=f32
    )


def nn(left, right):
    return product(left, right, 1, 0)


def nt(left, right):
    return product(left, right, 1, 1)


def tn(left, right):
    return product(left, right, 0, 0)


def pair_kernel(key_blocks, n_ref, w_ref, low_ref, up_ref, cos_ref, sin_ref, out_ref):
    made = nn(n_ref[...], w_ref[...]) + nn(low_ref[...], up_ref[...])

    @pl.when(pl.program_id(0) < key_blocks)
    def _():
        for start in range(0, made.shape[1], HD):
            head = made[:, start : start + HD]
            turned = head * cos_ref[...] + pltpu.roll(head, HD // 2, 1) * sin_ref[...]
            out_ref[:, start : start + HD] = turned.astype(bf16)

    @pl.when(pl.program_id(0) >= key_blocks)
    def _():
        out_ref[...] = made.astype(bf16)


def project_pairs(normed, weight, low, upper, cosine, sine):
    rows, width = normed.shape
    columns = weight.shape[1]
    block = 512
    return pl.pallas_call(
        functools.partial(pair_kernel, columns // 2 // block),
        grid=(columns // block,),
        in_specs=[
            pl.BlockSpec((rows, width), lambda i: (0, 0)),
            pl.BlockSpec((width, block), lambda i: (0, i)),
            pl.BlockSpec(low.shape, lambda i: (0, 0)),
            pl.BlockSpec((upper.shape[0], block), lambda i: (0, i)),
            pl.BlockSpec((rows, HD), lambda i: (0, 0)),
            pl.BlockSpec((rows, HD), lambda i: (0, 0)),
        ],
        out_specs=pl.BlockSpec((rows, block), lambda i: (0, i)),
        out_shape=jax.ShapeDtypeStruct((rows, columns), bf16),
        compiler_params=pltpu.CompilerParams(vmem_limit_bytes=vmem_bytes),
        name="pairs",
    )(normed, weight, low, upper, cosine, sine)


def attend_kernel(
    scale,
    home_ref,
    place_ref,
    low_ref,
    up_ref,
    cos_ref,
    sin_ref,
    key_ref,
    value_ref,
    bias_ref,
    attended_ref,
    slots_ref,
    query_ref,
    total_ref,
):
    rows = cos_ref.shape[0]
    base = nn(place_ref[...], home_ref[...])
    extra = nn(low_ref[...], up_ref[...])
    keys, values = key_ref[...], value_ref[...]
    for route in range(2):
        part = pl.ds(route * rows, rows)
        query = base[route * rows : (route + 1) * rows] + extra
        query = query * cos_ref[...] + pltpu.roll(query, HD // 2, 1) * sin_ref[...]
        query = query.astype(bf16)
        query_ref[part, :] = query
        scores = nt(query, keys) * scale + bias_ref[...]
        highest = jnp.max(scores, axis=1, keepdims=True)
        weights = jnp.exp(scores - highest)
        total = jnp.sum(weights, axis=1, keepdims=True)
        attended = nn(weights.astype(bf16), values) / total
        attended_ref[part, :] = attended.astype(bf16)
        total_ref[0, part, :] = highest + jnp.log(total)
    slots_ref[...] = tn(place_ref[...], attended_ref[...]).astype(bf16)


def attend(home, place, low, upper, cosine, sine, pairs, bias):
    rows2, slots = place.shape
    rows, length = bias.shape
    heads = home.shape[1] // HD
    kv_heads = pairs.shape[1] // (2 * HD)
    whole = lambda array: pl.BlockSpec(array.shape, lambda h: (0, 0))
    return pl.pallas_call(
        functools.partial(attend_kernel, 1.0 / math.sqrt(HD)),
        grid=(heads,),
        in_specs=[
            pl.BlockSpec((slots, HD), lambda h: (0, h)),
            whole(place),
            whole(low),
            pl.BlockSpec((upper.shape[0], HD), lambda h: (0, h)),
            whole(cosine),
            whole(sine),
            pl.BlockSpec((length, HD), lambda h: (0, h)),
            pl.BlockSpec((length, HD), lambda h: (0, kv_heads + h)),
            whole(bias),
        ],
        out_specs=[
            pl.BlockSpec((rows2, HD), lambda h: (0, h)),
            pl.BlockSpec((slots, HD), lambda h: (0, h)),
            pl.BlockSpec((rows2, HD), lambda h: (0, h)),
            pl.BlockSpec((1, rows2, 1), lambda h: (h, 0, 0)),
        ],
        out_shape=[
            jax.ShapeDtypeStruct((rows2, heads * HD), bf16),
            jax.ShapeDtypeStruct((slots, heads * HD), bf16),
            jax.ShapeDtypeStruct((rows2, heads * HD), bf16),
            jax.ShapeDtypeStruct((heads, rows2, 1), f32),
        ],
        compiler_params=pltpu.CompilerParams(vmem_limit_bytes=vmem_bytes),
        cost_estimate=pl.CostEstimate(
            flops=4 * heads * rows2 * length * HD,
            bytes_accessed=4 * length * heads * HD,
            transcendentals=heads * rows2 * length,
        ),
        name="attend",
    )(home, place, low, upper, cosine, sine, pairs, pairs, bias)


def attend_back_kernel(
    scale,
    query_ref,
    key_ref,
    value_ref,
    bias_ref,
    total_ref,
    home_ref,
    place_ref,
    gate_ref,
    low_ref,
    down_ref,
    cos_ref,
    sin_ref,
    cos_all_ref,
    sin_all_ref,
    pair_ref,
    slots_ref,
    sum_ref,
    turned_ref,
):
    rows = cos_ref.shape[0]
    base = nn(place_ref[...], home_ref[...])
    extra = nn(low_ref[...], down_ref[...])
    keys, values = key_ref[...], value_ref[...]
    key_grad = value_grad = None
    for route in range(2):
        part = pl.ds(route * rows, rows)
        query = query_ref[part, :]
        grad = (base[route * rows : (route + 1) * rows] + extra) * gate_ref[part, :]
        grad = grad.astype(bf16)
        scores = nt(query, keys) * scale + bias_ref[...]
        weights = jnp.exp(scores - total_ref[0, part, :])
        weight_grad = nt(grad, values)
        mean_grad = jnp.sum(weights * weight_grad, axis=1, keepdims=True)
        score_grad = (weights * (weight_grad - mean_grad)).astype(bf16)
        query_grad = nn(score_grad, keys) * scale
        query_grad = query_grad * cos_ref[...] - pltpu.roll(query_grad, HD // 2, 1) * sin_ref[...]
        turned_ref[part, :] = query_grad.astype(bf16)
        key_part = tn(score_grad, query)
        value_part = tn(weights.astype(bf16), grad)
        key_grad = key_part if route == 0 else key_grad + key_part
        value_grad = value_part if route == 0 else value_grad + value_part
    key_grad = key_grad * scale
    key_grad = key_grad * cos_all_ref[...] - pltpu.roll(key_grad, HD // 2, 1) * sin_all_ref[...]
    pair_ref[0, :, :] = key_grad.astype(bf16)
    pair_ref[1, :, :] = value_grad.astype(bf16)
    slots_ref[...] = tn(place_ref[...], turned_ref[...]).astype(bf16)
    first = turned_ref[pl.ds(0, rows), :].astype(f32)
    sum_ref[...] = (first + turned_ref[pl.ds(rows, rows), :].astype(f32)).astype(bf16)


def attend_back(query, pairs, bias, totals, home, place, gates, low, down, cosine, sine, cosine_all, sine_all):
    rows2, slots = place.shape
    rows, length = bias.shape
    heads = home.shape[1] // HD
    kv_heads = pairs.shape[1] // (2 * HD)
    whole = lambda array: pl.BlockSpec(array.shape, lambda h: (0, 0))
    return pl.pallas_call(
        functools.partial(attend_back_kernel, 1.0 / math.sqrt(HD)),
        grid=(heads,),
        in_specs=[
            pl.BlockSpec((rows2, HD), lambda h: (0, h)),
            pl.BlockSpec((length, HD), lambda h: (0, h)),
            pl.BlockSpec((length, HD), lambda h: (0, kv_heads + h)),
            whole(bias),
            pl.BlockSpec((1, rows2, 1), lambda h: (h, 0, 0)),
            pl.BlockSpec((slots, HD), lambda h: (0, h)),
            whole(place),
            whole(gates),
            whole(low),
            pl.BlockSpec((down.shape[0], HD), lambda h: (0, h)),
            whole(cosine),
            whole(sine),
            whole(cosine_all),
            whole(sine_all),
        ],
        out_specs=[
            pl.BlockSpec((2, length, HD), lambda h: (0, 0, h)),
            pl.BlockSpec((slots, HD), lambda h: (0, h)),
            pl.BlockSpec((rows, HD), lambda h: (0, h)),
        ],
        out_shape=[
            jax.ShapeDtypeStruct((2, length, heads * HD), bf16),
            jax.ShapeDtypeStruct((slots, heads * HD), bf16),
            jax.ShapeDtypeStruct((rows, heads * HD), bf16),
        ],
        scratch_shapes=[pltpu.VMEM((rows2, HD), bf16)],
        compiler_params=pltpu.CompilerParams(vmem_limit_bytes=vmem_bytes),
        cost_estimate=pl.CostEstimate(
            flops=10 * heads * rows2 * length * HD,
            bytes_accessed=8 * length * heads * HD,
            transcendentals=heads * rows2 * length,
        ),
        name="attend_back",
    )(query, pairs, pairs, bias, totals, home, place, gates, low, down, cosine, sine, cosine_all, sine_all)


def exchange(buffer):
    return lax.all_to_all(buffer, "dp", split_axis=0, concat_axis=0, tiled=True)


def shifted(array, shift, size):
    if shift == 0:
        return array
    return lax.ppermute(array, "seq", [(k, (k - shift) % size) for k in range(size)])


def send_full(slots, experts, copies):
    buffer = slots.reshape(experts, slots.shape[0] // experts, slots.shape[1])
    if copies > 1:
        buffer = jnp.repeat(buffer, copies, axis=0)
    return exchange(buffer)


def send_cut(slots, experts, copies):
    buffer = slots.reshape(experts, slots.shape[0] // experts, slots.shape[1])
    if copies > 1:
        _, rows, columns = buffer.shape
        buffer = buffer.reshape(experts, rows, copies, columns // copies).transpose(0, 2, 1, 3)
        buffer = buffer.reshape(experts * copies, rows, columns // copies)
    return exchange(buffer)


def home_join(parts, experts, copies):
    home = exchange(parts)
    _, rows, columns = home.shape
    if copies > 1:
        home = home.reshape(experts, copies, rows, columns).transpose(0, 2, 1, 3)
    return home.reshape(experts * rows, copies * columns)


def home_add(parts, experts, copies):
    home = exchange(parts)
    _, rows, columns = home.shape
    if copies > 1:
        home = home.reshape(experts, copies, rows, columns).astype(f32)
        home = jnp.sum(home, axis=1).astype(parts.dtype)
    return home.reshape(experts * rows, columns)


def slot_layout(route_ids, experts, capacity):
    flat = route_ids.T.reshape(-1)
    count = flat.shape[0]
    hits = flat[:, None] == jnp.arange(experts)[None, :]
    earlier = jnp.arange(count)[:, None] > jnp.arange(count)[None, :]
    before = nn(earlier.astype(bf16), hits.astype(bf16))
    rank = jnp.sum(jnp.where(hits, before, 0.0), axis=1).astype(jnp.int32)
    slot = flat * capacity + rank
    return (slot[:, None] == jnp.arange(experts * capacity)[None, :]).astype(bf16)


def either(place):
    rows = place.shape[0] // 2
    return place[:rows] + place[rows:]


def norm_back(values, scale, gain, grad):
    weighted = grad * gain
    mean = jnp.mean(weighted * values, axis=-1, keepdims=True)
    return weighted * scale - values * (scale * scale * scale * mean)


def norm_scale(values):
    return lax.rsqrt(jnp.mean(values * values, axis=-1, keepdims=True) + norm_eps)


def gate_pair(logits, route_ids):
    hits = (route_ids[:, :, None] == jnp.arange(logits.shape[1])).astype(f32)
    chosen = jnp.sum(hits * logits[:, None, :], axis=2)
    weights = jnp.exp(chosen - jnp.max(chosen, axis=1, keepdims=True))
    return weights / jnp.sum(weights, axis=1, keepdims=True), hits


def gate_back(gates, hits, grad):
    mean = jnp.sum(gates * grad, axis=1, keepdims=True)
    return jnp.sum((gates * (grad - mean))[:, :, None] * hits, axis=1)


def rope_full(positions):
    half = HD // 2
    frequency = jnp.power(rope_base, -jnp.arange(half).astype(f32) / half)
    angles = positions.astype(f32)[:, None] * frequency[None, :]
    cosine, sine = jnp.cos(angles), jnp.sin(angles)
    return jnp.concatenate([cosine, cosine], 1), jnp.concatenate([-sine, sine], 1)


def picked(lookup, index):
    return lax.dynamic_index_in_dim(lookup, index, 0, keepdims=False)


def body(
    tokens,
    norm_gain,
    key_value_weight,
    router_weight,
    query_weight,
    output_weight,
    mlp_gain,
    mlp_router_weight,
    mlp_in_weight,
    mlp_out_weight,
    key_value_down,
    key_value_up,
    query_down,
    query_up,
    output_down,
    output_up,
    mlp_in_down,
    mlp_in_up,
    mlp_out_down,
    mlp_out_up,
    routes,
    mlp_routes,
    adapter_index,
    prefix_length,
    out_grad,
):
    seqs, rows, width = tokens.shape
    assert seqs == 1
    size, spot = lax.axis_size("seq"), lax.axis_index("seq")
    holders, holder = lax.axis_size("dp"), lax.axis_index("dp")
    experts = router_weight.shape[1]
    copies = holders // experts
    part = holder % copies
    capacity = 3 * rows // 8
    length = rows * size
    adapters, _, rank = key_value_down.shape
    codes = adapters * rank
    hidden = mlp_in_weight.shape[2] // 2
    share = hidden // size

    def flat_down(lookup):
        return lookup.transpose(0, 2, 1)

    adapter = adapter_index[0]
    adapter_all = lax.all_gather(adapter_index, "dp", axis=0, tiled=True)

    piece = key_value_weight.shape[0] // holders
    pair_weight = lax.all_gather(
        lax.dynamic_slice_in_dim(key_value_weight, holder * piece, piece, 0),
        ("seq", "dp"),
        axis=0,
        tiled=True,
    )
    query_full = lax.all_gather(query_weight[0], "seq", axis=0, tiled=True)
    output_full = lax.all_gather(output_weight[0], "seq", axis=0, tiled=True)
    inner_cut = mlp_in_weight[0].reshape(-1, 2, size, share)
    inner_full = jnp.zeros((size, inner_cut.shape[0], 2 * share), bf16)
    for shift in range(size):
        target = (spot - shift) % size
        sent = lax.dynamic_index_in_dim(inner_cut, target, 2, keepdims=False)
        got = shifted(sent.reshape(-1, 2 * share), shift, size)
        inner_full = lax.dynamic_update_index_in_dim(inner_full, got, (spot + shift) % size, 0)
    inner_full = inner_full.reshape(-1, 2 * share)
    outer_full = mlp_out_weight[0]

    inputs = tokens[0].astype(f32)
    input_scale = norm_scale(inputs)
    normed = (inputs * input_scale * norm_gain).astype(bf16)
    pair_down, pair_up = picked(flat_down(key_value_down), adapter), picked(key_value_up, adapter)
    query_lower, query_upper = picked(flat_down(query_down), adapter), picked(query_up, adapter)
    output_lower, output_upper = picked(flat_down(output_down), adapter), picked(output_up, adapter)
    pair_low = nt(normed, pair_down).astype(bf16)
    query_low = nt(normed, query_lower).astype(bf16)
    cosine_all, sine_all = rope_full(jnp.arange(length))
    positions = spot * rows + jnp.arange(rows)
    cosine = lax.dynamic_slice_in_dim(cosine_all, spot * rows, rows, 0)
    sine = lax.dynamic_slice_in_dim(sine_all, spot * rows, rows, 0)
    key_pos = jnp.arange(length)
    allowed = (key_pos[None, :] <= positions[:, None]) | (key_pos[None, :] < prefix_length[0])
    bias = jnp.where(allowed, 0.0, masked_score).astype(f32)
    pairs_local = project_pairs(normed, pair_weight, pair_low, pair_up, cosine, sine)
    pairs = lax.all_gather(pairs_local, "seq", axis=0, tiled=True)

    gates, hits = gate_pair(nn(normed, router_weight), routes[0])
    place = slot_layout(routes[0], experts, capacity)
    place_any = either(place)

    query_rows = send_full(tn(place_any, normed).astype(bf16), experts, copies)
    query_parts = nn(query_rows.reshape(-1, width), query_full).astype(bf16)
    query_home = home_join(query_parts.reshape(holders, capacity, -1), experts, copies)
    attended, output_slots, query_rot, totals = attend(
        query_home, place, query_low, query_upper, cosine, sine, pairs, bias
    )

    output_rows = send_cut(output_slots, experts, copies)
    output_parts = nn(output_rows.reshape(holders * capacity, -1), output_full).astype(bf16)
    output_home = home_add(output_parts.reshape(holders, capacity, width), experts, copies)
    output_low = nt(attended, output_lower).astype(bf16)
    branch = nn(place, output_home) + nn(output_low, output_upper)
    branch = branch.reshape(2, rows, width)
    middle = inputs + gates[:, :1] * branch[0] + gates[:, 1:] * branch[1]
    middle_scale = norm_scale(middle)
    normed_mlp = (middle * middle_scale * mlp_gain).astype(bf16)
    mlp_gates, mlp_hits = gate_pair(nn(normed_mlp, mlp_router_weight), mlp_routes[0])

    mask = (jnp.arange(codes)[None, None, :] // rank == adapter_all[:, None, None]).astype(bf16)
    mask = jnp.broadcast_to(mask, (holders, capacity, codes)).reshape(-1, codes)
    inner_down = flat_down(mlp_in_down).reshape(codes, width)
    outer_up = mlp_out_up.reshape(codes, width)
    inner_up = mlp_in_up.reshape(codes, 2, copies, size, share)
    inner_up = lax.dynamic_index_in_dim(inner_up, part, 2, keepdims=False)
    inner_up = lax.dynamic_index_in_dim(inner_up, spot, 2, keepdims=False).reshape(codes, 2 * share)
    outer_down = flat_down(mlp_out_down).reshape(codes, copies, size, share)
    outer_down = lax.dynamic_index_in_dim(outer_down, part, 1, keepdims=False)
    outer_down = lax.dynamic_index_in_dim(outer_down, spot, 1, keepdims=False)

    places = [slot_layout(shifted(mlp_routes[0], d, size), experts, capacity) for d in range(size)]
    grad_rows, hidden_grads, outer_codes = [], [], []
    for d in range(size):
        rows_there = shifted(out_grad[0], d, size)
        got = send_full(tn(either(places[d]), rows_there).astype(bf16), experts, copies)
        got = got.reshape(-1, width)
        code = nt(got, outer_up).astype(bf16) * mask
        grad_rows.append(got)
        outer_codes.append(code)
        hidden_grads.append((nt(got, outer_full) + nn(code, outer_down)).astype(bf16))

    order = list(range(size))
    gates_there = [shifted(mlp_gates, d, size) for d in order]
    gate_slots = jnp.stack(
        [
            jnp.sum(places[d].astype(f32) * gates_there[d].T.reshape(-1)[:, None], axis=0)
            for d in order
        ]
    )
    gate_slots = gate_slots.reshape(size, experts, capacity).transpose(1, 0, 2)
    gate_slots = exchange(jnp.repeat(gate_slots, copies, axis=0))

    row_total, down_total = None, None
    gate_sums, sums = [], None
    for d in order:
        rows_there = shifted(normed_mlp, d, size)
        got = send_full(tn(either(places[d]), rows_there).astype(bf16), experts, copies)
        got = got.reshape(-1, width)
        code = nt(got, inner_down).astype(bf16) * mask
        pre = nn(got, inner_full) + nn(code, inner_up)
        gate_part, up_part = pre[:, :share], pre[:, share:]
        sigmoid = 1.0 / (1.0 + jnp.exp(-gate_part))
        active = gate_part * sigmoid
        activated = (active * up_part).astype(bf16)
        hidden_grad = hidden_grads[d].astype(f32)
        gate_sums.append(jnp.sum(activated.astype(f32) * hidden_grad, axis=1))
        pre_grad = jnp.concatenate(
            [
                (hidden_grad * up_part * sigmoid * (1.0 + gate_part * (1.0 - sigmoid))).astype(bf16),
                (hidden_grad * active).astype(bf16),
            ],
            axis=1,
        )
        code_grad = nt(pre_grad, inner_up).astype(bf16) * mask
        row_grad = (nt(pre_grad, inner_full) + nn(code_grad, inner_down)).astype(bf16)
        outer_low = nt(activated, outer_down).astype(bf16) * mask
        down = (nn(activated, outer_full) + nn(outer_low, outer_up)).astype(bf16)
        weight = gates_there[d].T.reshape(-1)[:, None]
        combine = either((places[d].astype(f32) * weight).astype(bf16))
        row_home = home_add(row_grad.reshape(holders, capacity, width), experts, copies)
        row_back = shifted(nn(combine, row_home).astype(bf16), -d % size, size).astype(f32)
        row_total = row_back if row_total is None else row_total + row_back
        down_home = home_add(down.reshape(holders, capacity, width), experts, copies)
        down_back = shifted(nn(combine, down_home).astype(bf16), -d % size, size).astype(f32)
        down_total = down_back if down_total is None else down_total + down_back
        scale = gate_slots[:, d, :].reshape(-1, 1)

        def scaled(array):
            return (array.astype(f32) * scale).astype(bf16)

        new = (
            tn(scaled(code), pre_grad),
            tn(scaled(outer_codes[d]), activated),
            tn(scaled(code_grad), got),
            tn(scaled(outer_low), grad_rows[d]),
        )
        sums = new if sums is None else tuple(a + b for a, b in zip(sums, new))

    gate_sums = jnp.stack(gate_sums, 0).reshape(size, holders, capacity).transpose(1, 0, 2)
    gate_sums = exchange(gate_sums).reshape(experts, copies, size, capacity)
    gate_sums = jnp.sum(gate_sums, axis=1).transpose(1, 0, 2).reshape(size, -1)
    gate_parts = [
        jnp.sum(places[d].astype(f32) * gate_sums[d][None, :], axis=1).reshape(2, rows)
        for d in range(size)
    ]
    mlp_gate_grad = gate_parts[0]
    for d in range(1, size):
        mlp_gate_grad = mlp_gate_grad + shifted(gate_parts[d], -d % size, size)
    mlp_logit_grad = gate_back(mlp_gates, mlp_hits, mlp_gate_grad.T)
    result = (middle + down_total).astype(bf16)

    inner_up_sum, outer_down_sum, inner_down_sum, outer_up_sum = sums

    def widened(array):
        if copies == 1:
            return array
        whole = jnp.zeros((codes, copies, array.shape[1]), f32)
        whole = lax.dynamic_update_index_in_dim(whole, array, part, 1)
        return whole.reshape(codes, -1)

    wide = [widened(inner_up_sum), widened(outer_down_sum), inner_down_sum, outer_up_sum]
    ends = [sum(a.shape[1] for a in wide[: k + 1]) for k in range(3)]
    mlp_sums = lax.psum_scatter(
        jnp.concatenate(wide, axis=1), "dp", scatter_dimension=0, tiled=True
    ).astype(bf16)
    mlp_sums = lax.all_gather(mlp_sums, ("seq", "dp"), axis=0, tiled=True)
    mlp_sums = mlp_sums.astype(f32).reshape(size, codes, -1)
    inner_up_grad, outer_down_grad, inner_down_grad, outer_up_grad = jnp.split(mlp_sums, ends, axis=2)
    inner_up_grad = inner_up_grad.reshape(size, codes, copies, 2, share).transpose(1, 3, 2, 0, 4)
    inner_up_grad = inner_up_grad.reshape(adapters, rank, -1)
    outer_down_grad = outer_down_grad.reshape(size, codes, copies, share).transpose(1, 2, 0, 3)
    outer_down_grad = outer_down_grad.reshape(adapters, rank, -1).transpose(0, 2, 1)
    inner_down_grad = jnp.sum(inner_down_grad, 0).reshape(adapters, rank, width).transpose(0, 2, 1)
    outer_up_grad = jnp.sum(outer_up_grad, 0).reshape(adapters, rank, width)

    normed_mlp_grad = row_total + nt(mlp_logit_grad.astype(bf16), mlp_router_weight)
    middle_grad = norm_back(middle, middle_scale, mlp_gain, normed_mlp_grad)
    middle_grad = middle_grad + out_grad[0].astype(f32)
    middle_low = middle_grad.astype(bf16)
    branch_rows = send_full(tn(place_any, middle_low).astype(bf16), experts, copies)
    head_parts = nt(branch_rows.reshape(-1, width), output_full).astype(bf16)
    head_home = home_join(head_parts.reshape(holders, capacity, -1), experts, copies)
    gate_grad = jnp.sum(middle_grad[None] * branch, axis=2).T
    logit_grad = gate_back(gates, hits, gate_grad)
    gate_column = gates.T.reshape(-1, 1)
    output_low_grad = nt(middle_low, output_upper)
    output_low_back = output_low_grad.astype(bf16)
    output_low_scaled = (jnp.tile(output_low_grad, (2, 1)) * gate_column).astype(bf16)
    output_lower_grad = tn(output_low_scaled, attended)
    output_low_sum = (output_low.astype(f32) * gate_column).reshape(2, rows, rank).sum(0)
    output_upper_grad = tn(output_low_sum.astype(bf16), middle_low)

    pair_parts, query_slots, query_sum = attend_back(
        query_rot,
        pairs,
        bias,
        totals,
        head_home,
        place,
        gate_column,
        output_low_back,
        output_lower,
        cosine,
        sine,
        cosine_all,
        sine_all,
    )
    query_back = send_cut(query_slots, experts, copies)
    pair_grad = lax.psum_scatter(pair_parts, "seq", scatter_dimension=1, tiled=True)
    input_parts = nt(query_back.reshape(holders * capacity, -1), query_full).astype(bf16)
    input_home = home_add(input_parts.reshape(holders, capacity, width), experts, copies)
    query_low_grad = nt(query_sum, query_upper).astype(bf16)
    query_upper_grad = tn(query_low, query_sum)
    query_lower_grad = tn(query_low_grad, normed)
    normed_grad = nn(place_any, input_home) + nn(query_low_grad, query_lower)
    normed_grad = normed_grad + nt(logit_grad.astype(bf16), router_weight)
    key_grad, value_grad = pair_grad[0], pair_grad[1]
    half = key_grad.shape[1]
    pair_low_grad = nt(key_grad, pair_up[:, :half]) + nt(value_grad, pair_up[:, half:])
    pair_low_grad = pair_low_grad.astype(bf16)
    pair_upper_grad = jnp.concatenate([tn(pair_low, key_grad), tn(pair_low, value_grad)], axis=1)
    pair_lower_grad = tn(pair_low_grad, normed)
    normed_grad = normed_grad + nt(key_grad, pair_weight[:, :half])
    normed_grad = normed_grad + nt(value_grad, pair_weight[:, half:])
    normed_grad = normed_grad + nn(pair_low_grad, pair_down)
    input_grad = norm_back(inputs, input_scale, norm_gain, normed_grad) + middle_grad

    def over_sequences(arrays):
        ends = [sum(a.shape[1] for a in arrays[: k + 1]) for k in range(len(arrays) - 1)]
        joined = jnp.concatenate(arrays, axis=1)
        joined = joined.reshape(rank, size, -1).transpose(1, 0, 2)
        mine = lax.psum_scatter(joined, "seq", scatter_dimension=0, tiled=True)
        every = lax.all_gather(mine[0].astype(bf16), ("seq", "dp"), axis=0, tiled=False)
        every = every.reshape(size, holders, rank, -1).astype(f32)
        chosen = (adapter_all[:, None] == jnp.arange(adapters)[None, :]).astype(f32)
        total = sum(
            every[:, k, None] * chosen[k][None, :, None, None] for k in range(holders)
        )
        total = total.transpose(1, 2, 0, 3).reshape(adapters, rank, -1)
        return jnp.split(total, ends, axis=2)

    late = over_sequences(
        [
            pair_lower_grad,
            pair_upper_grad,
            query_lower_grad,
            query_upper_grad,
            output_lower_grad,
            output_upper_grad,
        ]
    )
    return (
        result[None],
        input_grad[None],
        late[0].transpose(0, 2, 1),
        late[1],
        late[2].transpose(0, 2, 1),
        late[3],
        late[4].transpose(0, 2, 1),
        late[5],
        inner_down_grad,
        inner_up_grad,
        outer_down_grad,
        outer_up_grad,
    )


def solution(mesh):
    split = P("dp", "seq", None)
    placed = (
        (split, P(), P("seq", None), P(), split, split, P(), P(), split, split)
        + (P(),) * 10
        + (split, split, P("dp"), P("dp"), split)
    )
    return jax.shard_map(
        body,
        mesh=mesh,
        in_specs=placed,
        out_specs=(split, split) + (P(),) * 10,
        check_vma=False,
    )
```

time: 3160 us -> 2330 us (0.74)
  waiting for transfers between devices: 2130 us -> 1170 us
  starting transfers between devices: 64.4 us -> 189 us
  other arithmetic: 168 us -> 47.2 us
  Pallas kernels: 0 us -> 89.9 us
  blocking collectives: 82.2 us -> 144 us
    all_gather x7 -> x6, waiting for transfers between devices: 1450 us -> 317 us  [the longest x1 113 us: body(): pairs = lax.all_gather(pairs_local, 'seq', axis=0, tiled=True)]
    ppermute x0 -> x24, waiting for transfers between devices: none -> 399 us  [shifted(): lax.ppermute(array, 'seq', [(k, (k - shift) % size) for k in range(size)])]
    psum x1 -> x0, waiting for transfers between devices: 188 us -> none  [body(): lax.psum((per_adapter(pair_lower_grad), per_adapter(pair_upper_grad), per...]
    gather x20 -> x0, local copies, waits for them, and re-layouts: 91.2 us -> none  [the longest x10 82.9 us: pick_rows(): lookup_one[index_one]]
    pallas_call x0 -> x3, Pallas kernels: none -> 89.9 us  [the longest x1 44.4 us: attend_back(): pl.pallas_call(functools.partial(attend_back_kernel, 1.0 / math.sqrt(HD))...]
    ppermute x0 -> x24, starting transfers between devices: none -> 81.4 us  [shifted(): lax.ppermute(array, 'seq', [(k, (k - shift) % size) for k in range(size)])]
    scatter-add x4 -> x0, other arithmetic: 49.9 us -> none  [gate_softmax(): chosen = jnp.take_along_axis(logits, route_ids, axis=-1)]
    all_to_all x14 -> x24, starting transfers between devices: 63.6 us -> 107 us  [exchange(): return lax.all_to_all(buffer, 'dp', split_axis=0, concat_axis=0, tiled=True)]
  transfers between devices with their start and end apart: 24 -> 57, of which waited for: 16 -> 27; matrix products, arithmetic and copies ran while one was open for 20% -> 26% of each run, Pallas kernels for 0% -> 2%
where the time goes in v1:
time: 2330 us; the launch traced here: 2300 us
  waiting for transfers between devices  1170 us (50%)
  matrix products  462 us (20%)
  starting transfers between devices  189 us (8%)
  local copies, waits for them, and re-layouts  172 us (7%)
  blocking collectives  144 us (6%)
  Pallas kernels  89.9 us (4%)
  other arithmetic  47.2 us (2%)
    dot_general x116, matrix products, product(): lax.dot_general(left, right, (((left_dim,), (right_dim,)), ((), ())), pre...  462 us
    ppermute x24, waiting for transfers between devices, shifted(): lax.ppermute(array, 'seq', [(k, (k - shift) % size) for k in range(size)])  399 us
    all_to_all x24, waiting for transfers between devices, exchange(): return lax.all_to_all(buffer, 'dp', split_axis=0, concat_axis=0, tiled=True)  288 us
    all_gather x1, waiting for transfers between devices, body(): pairs = lax.all_gather(pairs_local, 'seq', axis=0, tiled=True)  113 us
    all_gather x1, waiting for transfers between devices, body(): lax.all_gather(lax.dynamic_slice_in_dim(key_value_weight, holder * piece,...  113 us
    reduce_scatter x1, waiting for transfers between devices, body(): lax.psum_scatter(pair_parts, 'seq', scatter_dimension=1, tiled=True)  110 us
    all_to_all x24, starting transfers between devices, exchange(): return lax.all_to_all(buffer, 'dp', split_axis=0, concat_axis=0, tiled=True)  107 us
    all_to_all x2, blocking collectives, exchange(): return lax.all_to_all(buffer, 'dp', split_axis=0, concat_axis=0, tiled=True)  104 us
  transfers between devices with their start and end apart: 57, of which 27 were waited for; matrix products, arithmetic and copies ran while one was open for 26% of the time, Pallas kernels for 2%

profile of v1, /device:TPU:0, one launch (start us, length us, event | category | flops | bytes accessed | tf_op | source)
XLA Modules:
  0.0 2296.6 jit_solution(16228592499942330566)
XLA Ops:
  15.7 113.4 %all-gather.9.cloned.1.call-done.w_ref = bf16[2048,4096]{1,0:T(8,128)(2,1)} async-done(((bf16[64,4096]{1,0:T(8,128)(2,1)}), bf16[2048,4096]{1,0:T(8,128)(2,1)}) %all-gather.9.cloned.1.call-update) | async-done | bytes 16777232 | tf_op jit(solution)/shard_map/all_gather | solution.py:395
  129.1 11.9 pairs.1
  154.9 33.1 %all-to-all-done = bf16[8,96,2048]{2,1,0:T(8,128)(2,1)} async-done(((bf16[8,96,2048]{2,1,0:T(8,128)(2,1)}), bf16[8,96,2048]{2,1,0:T(8,128)(2,1)}, u32[]{:S(2)}, u32[]{:S(2)}) %all-to-all-start) | async-done | bytes 3145760 | tf_op jit(solution)/shard_map/all_to_all | solution.py:255
  193.0 85.5 %all-gather.17.cloned.1.call-done = bf16[1,2048,2048]{2,1,0:T(8,128)(2,1)} async-done(((bf16[1,512,2048]{2,1,0:T(8,128)(2,1)}), bf16[1,2048,2048]{2,1,0:T(8,128)(2,1)}) %all-gather.17.cloned.1.call-update) | async-done | bytes 8388624 | tf_op jit(solution)/shard_map/all_gather | solution.py:401
  278.5 11.9 fusion.53
  300.1 15.8 copy.146
  316.0 9.1 constant_dynamic-slice_fusion.2
  330.4 33.4 %collective-permute-done.15 = bf16[256,2048]{1,0:T(8,128)(2,1)S(1)} collective-permute-done((bf16[256,2048]{1,0:T(8,128)(2,1)}, bf16[256,2048]{1,0:T(8,128)(2,1)S(1)}, u32[]{:S(2)}, u32[]{:S(2)}) %collective-permute-start.15) | collective-permute-done | bytes 1048608 | tf_op jit(solution)/shard_map/ppermute | solution.py:261
  371.1 40.0 %all-reduce = s32[8]{0:T(128)S(1)} all-reduce(s32[8]{0:T(128)S(1)} %dynamic-update-slice), channel_id=1, replica_groups=mesh['seq'=4,'dp'=8] {'dp'}, use_global_device_ids=true, to_apply=%add | all-reduce | flops 8 | bytes 64
  416.3 6.4 squeeze.89
  434.6 113.4 %all-gather.11.cloned.1.call-done.key_ref.value_ref = bf16[1024,4096]{1,0:T(8,128)(2,1)} async-done(((bf16[256,4096]{1,0:T(8,128)(2,1)}), bf16[1024,4096]{1,0:T(8,128)(2,1)}) %all-gather.11.cloned.1.call-update) | async-done | bytes 8388624 | tf_op jit(solution)/shard_map/all_gather | solution.py:429
  549.2 33.7 %attend.1 = (bf16[512,2048]{1,0:T(8,128)(2,1)S(1)}, bf16[768,2048]{1,0:T(8,128)(2,1)}, bf16[512,2048]{1,0:T(8,128)(2,1)}, f32[16,512,1]{2,1,0:T(8,128)}) custom-call(bf16[768,2048]{1,0:T(8,128)(2,1)} %bitcast.8.home_ref, bf16[512,768]{1,0:T(8,128)(2,1)S(1)} %fusion.98.place_ref, bf16[256,16]{1,0:T(8,128)(2,1)S(1)} %convolution_convert_fusion.31.low_ref, ...), custom_call_target="tpu_custom_call" | custom-call | flops 4294967296 | bytes 8388608 | tf_op jit(solution)/shard_map/attend/pallas_call | solution.py:120
  605.8 8.7 collective-permute-start.1
  614.8 23.9 %collective-permute-start.2 = (bf16[512,2816]{0,1:T(8,128)(2,1)}, bf16[512,2816]{0,1:T(8,128)(2,1)}, u32[]{:S(2)}, u32[]{:S(2)}) collective-permute-start(bf16[512,2816]{0,1:T(8,128)(2,1)} %bitcast.602), channel_id=1, source_target_pairs={{0,8},{8,16},{16,24},{24,0},{1,9},{9,17},{17,25},{25,1},{2,10},{10... | collective-permute-start | bytes 8650760 | tf_op jit(solution)/shard_map/ppermute | solution.py:261
  652.2 9.8 fusion.18
  670.1 243.8 %collective-permute-done.1 = bf16[512,2816]{0,1:T(8,128)(2,1)} collective-permute-done((bf16[512,2816]{0,1:T(8,128)(2,1)}, bf16[512,2816]{0,1:T(8,128)(2,1)}, u32[]{:S(2)}, u32[]{:S(2)}) %collective-permute-start.1) | collective-permute-done | bytes 2883616 | tf_op jit(solution)/shard_map/ppermute | solution.py:261
  922.0 11.9 fusion.59
  950.8 9.9 fusion.16
  960.7 8.1 fusion.14
  968.8 7.8 all-to-all-done.3
  996.5 22.5 all-to-all-done.18
  1024.0 9.8 fusion.12
  1044.0 15.7 collective-permute-done.4
  1059.7 23.1 %collective-permute-start.12 = (f32[256,2]{0,1:T(2,128)S(1)}, f32[256,2]{0,1:T(2,128)S(1)}, u32[]{:S(2)}, u32[]{:S(2)}) collective-permute-start(f32[256,2]{0,1:T(2,128)S(1)} %fusion.194), channel_id=1, source_target_pairs={{0,8},{8,16},{16,24},{24,0},{1,9},{9,17},{17,25},{25,1},{2,10},{10... | collective-permute-start | bytes 6152 | tf_op jit(solution)/shard_map/ppermute | solution.py:261
  1106.1 13.8 convolution_add_fusion.3
  1120.0 6.6 fusion.30
  1148.6 13.8 convolution_add_fusion.2
  1162.4 6.6 fusion.35
  1169.1 13.2 all-to-all-done.8
  1191.3 13.8 convolution_add_fusion.1
  1205.2 6.5 fusion.40
  1211.7 13.3 all-to-all-done.10
  1229.2 14.0 convolution_add_fusion
  1243.2 6.5 fusion.45
  1258.3 14.5 add_convert_fusion.2
  1289.4 15.4 add_convert_fusion.1
  1304.8 22.5 all-to-all-done.15
  1332.2 15.3 add_convert_fusion
  1347.5 22.6 all-to-all-done.17
  1374.5 15.4 add_convert_fusion.3
  1390.3 22.1 all-to-all-done.19
  1445.1 9.8 all-to-all-done.13
  1456.8 43.7 %collective-permute-done.18 = bf16[256,2048]{1,0:T(8,128)(2,1)} collective-permute-done((bf16[256,2048]{1,0:T(8,128)(2,1)}, bf16[256,2048]{1,0:T(8,128)(2,1)}, u32[]{:S(2)}, u32[]{:S(2)}) %collective-permute-start.18) | collective-permute-done | bytes 1048608 | tf_op jit(solution)/shard_map/ppermute | solution.py:261
  1510.0 41.6 %all_to_all.130 = bf16[8,96,2048]{2,1,0:T(8,128)(2,1)S(1)} all-to-all(bf16[8,96,2048]{2,1,0:T(8,128)(2,1)S(1)} %bitcast.558), channel_id=1, replica_groups=mesh['seq'=4,'dp'=8] {'dp'}, dimensions={0} | all-to-all | bytes 6291456 | tf_op jit(solution)/shard_map/all_to_all | solution.py:255
  1551.6 8.1 fusion.62
  1569.9 32.3 %all-to-all-done.22 = bf16[8,96,2048]{2,1,0:T(8,128)(2,1)} async-done(((bf16[8,96,2048]{2,1,0:T(8,128)(2,1)}), bf16[8,96,2048]{2,1,0:T(8,128)(2,1)}, u32[]{:S(2)}, u32[]{:S(2)}) %all-to-all-start.22) | async-done | bytes 3145760 | tf_op jit(solution)/shard_map/all_to_all | solution.py:255
  1604.3 44.4 %attend_back.1 = (bf16[2,1024,2048]{2,1,0:T(8,128)(2,1)}, bf16[768,2048]{1,0:T(8,128)(2,1)}, bf16[256,2048]{1,0:T(8,128)(2,1)S(1)}) custom-call(bf16[512,2048]{1,0:T(8,128)(2,1)} %get-tuple-element.21.query_ref, bf16[1024,4096]{1,0:T(8,128)(2,1)} %all-gather.11.cloned.1.call-done.key_ref.value_ref, ...), custom_call_target="tpu_custom_call" | custom-call | flops 10737418240 | bytes 16777216 | tf_op jit(solution)/shard_map/attend_back/pallas_call | solution.py:214
  1701.9 110.2 %reduce-scatter.4.cloned.1.call-done = bf16[2,256,2048]{2,1,0:T(8,128)(2,1)} async-done(((bf16[2,1024,2048]{2,1,0:T(8,128)(2,1)}), bf16[2,256,2048]{2,1,0:T(8,128)(2,1)}) %reduce-scatter.4.cloned.1.call-update) | async-done | bytes 2097168 | tf_op jit(solution)/shard_map/reduce_scatter | solution.py:602
  1819.4 7.8 fusion.26
  1834.4 58.6 %reduce-scatter.8.cloned.1.call-done = f32[16,8320]{1,0:T(8,128)} async-done(((f32[128,8320]{1,0:T(8,128)}), f32[16,8320]{1,0:T(8,128)}) %reduce-scatter.8.cloned.1.call-update) | async-done | bytes 532496 | tf_op jit(solution)/shard_map/reduce_scatter | solution.py:556
  1894.8 7.8 fusion.24
  1909.7 7.8 fusion.22
  1920.1 29.4 %all-to-all-done.7 = bf16[8,96,2048]{2,1,0:T(8,128)(2,1)} async-done(((bf16[8,96,2048]{2,1,0:T(8,128)(2,1)}), bf16[8,96,2048]{2,1,0:T(8,128)(2,1)}, u32[]{:S(2)}, u32[]{:S(2)}) %all-to-all-start.7) | async-done | bytes 3145760 | tf_op jit(solution)/shard_map/all_to_all | solution.py:255
  1949.5 62.1 %all_to_all.131 = bf16[8,96,2048]{2,1,0:T(8,128)(2,1)} all-to-all(bf16[8,96,2048]{2,1,0:T(8,128)(2,1)} %bitcast.563), channel_id=1, replica_groups=mesh['seq'=4,'dp'=8] {'dp'}, dimensions={0} | all-to-all | bytes 6291456 | tf_op jit(solution)/shard_map/all_to_all | solution.py:255
  2016.3 7.7 fusion.20
  2026.6 27.5 %all-to-all-done.23 = bf16[8,96,2048]{2,1,0:T(8,128)(2,1)} async-done(((bf16[8,96,2048]{2,1,0:T(8,128)(2,1)}), bf16[8,96,2048]{2,1,0:T(8,128)(2,1)}, u32[]{:S(2)}, u32[]{:S(2)}) %all-to-all-start.23) | async-done | bytes 3145760 | tf_op jit(solution)/shard_map/all_to_all | solution.py:255
  2058.7 12.0 fusion.56
  2070.6 25.9 %all-to-all-done.11 = bf16[8,96,2048]{2,1,0:T(8,128)(2,1)} async-done(((bf16[8,96,2048]{2,1,0:T(8,128)(2,1)}), bf16[8,96,2048]{2,1,0:T(8,128)(2,1)}, u32[]{:S(2)}, u32[]{:S(2)}) %all-to-all-start.11) | async-done | bytes 3145760 | tf_op jit(solution)/shard_map/all_to_all | solution.py:255
  2117.6 15.9 collective-permute-done.6
  2133.5 44.3 %collective-permute-done.10 = bf16[256,2048]{1,0:T(8,128)(2,1)} collective-permute-done((bf16[256,2048]{1,0:T(8,128)(2,1)}, bf16[256,2048]{1,0:T(8,128)(2,1)}, u32[]{:S(2)}, u32[]{:S(2)}) %collective-permute-start.10) | collective-permute-done | bytes 1048608 | tf_op jit(solution)/shard_map/ppermute | solution.py:261
  2192.9 10.6 bitcast_convert_fusion
  2209.2 7.8 reshape.626
  2217.0 8.9 copy.200
  2225.9 7.9 reshape.627
  (673 shorter events, 507.9 us)
Async XLA Ops:
  7.2 121.9 %all-gather.9.cloned.1.call-start = ((), (), s32[]{:S(2)}) async-start(), calls=%async_computation.29 | async-start | bytes 17301504 | tf_op jit(solution)/shard_map/all_gather | solution.py:395
  9.2 269.3 %all-gather.17.cloned.1.call-start = ((), (), s32[]{:S(2)}) async-start(), calls=%async_computation.36 | async-start | bytes 10485760 | tf_op jit(solution)/shard_map/all_gather | solution.py:401
  10.0 538.0 %all-gather.11.cloned.1.call-start = ((), (), s32[]{:S(2)}) async-start(), calls=%async_computation.30 | async-start | bytes 10485760 | tf_op jit(solution)/shard_map/all_gather | solution.py:429
  13.9 419.3 %copy-start.149 = (f32[256]{0:T(256)}, f32[256]{0:T(256)S(1)}, u32[]{:S(2)}) copy-start(f32[256]{0:T(256)S(1)} %add_rsqrt_fusion.1) | copy-start | bytes 3076
  15.7 309.4 %copy-start.2 = (bf16[256,2048]{1,0:T(8,128)(2,1)}, bf16[256,2048]{1,0:T(8,128)(2,1)S(1)}, u32[]{:S(2)}) copy-start(bf16[256,2048]{1,0:T(8,128)(2,1)S(1)} %fusion.77.n_ref) | copy-start | bytes 3145732
  145.5 42.5 %all-to-all-start = ((bf16[8,96,2048]{2,1,0:T(8,128)(2,1)}), bf16[8,96,2048]{2,1,0:T(8,128)(2,1)}, u32[]{:S(2)}, u32[]{:S(2)}) async-start(bf16[8,96,2048]{2,1,0:T(8,128)(2,1)} %bitcast.557), calls=%async_computation | async-start | bytes 6291456 | tf_op jit(solution)/shard_map/all_to_all | solution.py:255
  188.0 102.4 %all-to-all-start.12 = ((bf16[8,96,2048]{2,1,0:T(8,128)(2,1)}), bf16[8,96,2048]{2,1,0:T(8,128)(2,1)}, u32[]{:S(2)}, u32[]{:S(2)}) async-start(bf16[8,96,2048]{2,1,0:T(8,128)(2,1)} %bitcast.556), calls=%async_computation.12 | async-start | bytes 6291456 | tf_op jit(solution)/shard_map/all_to_all | solution.py:255
  192.4 729.6 %all-gather.19.cloned.1.call-start = ((), (), s32[]{:S(2)}) async-start(), calls=%async_computation.37 | async-start | bytes 10485760 | tf_op jit(solution)/shard_map/all_gather | solution.py:402
  290.4 76.2 %all-to-all-start.1 = ((bf16[8,96,2048]{2,1,0:T(8,128)(2,1)}), bf16[8,96,2048]{2,1,0:T(8,128)(2,1)}, u32[]{:S(2)}, u32[]{:S(2)}) async-start(bf16[8,96,2048]{2,1,0:T(8,128)(2,1)} %bitcast.591), calls=%async_computation.1 | async-start | bytes 6291456 | tf_op jit(solution)/shard_map/all_to_all | solution.py:255
  294.9 31.9 %collective-permute-start.3 = (s32[256,2]{0,1:T(2,128)S(1)}, s32[256,2]{0,1:T(2,128)S(1)}, u32[]{:S(2)}, u32[]{:S(2)}) collective-permute-start(s32[256,2]{0,1:T(2,128)S(1)} %bitcast.616), channel_id=1, source_target_pairs={{0,24},{8,0},{16,8},{24,16},{1,25},{9,1},{17,9},{25,17},{2,26},{10... | collective-permute-start | bytes 6152 | tf_op jit(solution)/shard_map/ppermute | solution.py:261
  295.2 310.6 %collective-permute-start.7 = (s32[256,2]{0,1:T(2,128)S(1)}, s32[256,2]{0,1:T(2,128)S(1)}, u32[]{:S(2)}, u32[]{:S(2)}) collective-permute-start(s32[256,2]{0,1:T(2,128)S(1)} %bitcast.617), channel_id=1, source_target_pairs={{0,16},{8,24},{16,0},{24,8},{1,17},{9,25},{17,1},{25,9},{2,18},{10... | collective-permute-start | bytes 6152 | tf_op jit(solution)/shard_map/ppermute | solution.py:261
  295.7 68.2 %collective-permute-start.15 = (bf16[256,2048]{1,0:T(8,128)(2,1)}, bf16[256,2048]{1,0:T(8,128)(2,1)S(1)}, u32[]{:S(2)}, u32[]{:S(2)}) collective-permute-start(bf16[256,2048]{1,0:T(8,128)(2,1)} %bitcast.71), channel_id=1, source_target_pairs={{0,24},{8,0},{16,8},{24,16},{1,25},{9,1},{17,9},{25,17},{2,26},{10... | collective-permute-start | bytes 3145736 | tf_op jit(solution)/shard_map/ppermute | solution.py:261
  299.3 340.1 %collective-permute-start.17 = (bf16[256,2048]{1,0:T(8,128)(2,1)}, bf16[256,2048]{1,0:T(8,128)(2,1)}, u32[]{:S(2)}, u32[]{:S(2)}) collective-permute-start(bf16[256,2048]{1,0:T(8,128)(2,1)} %bitcast.71), channel_id=1, source_target_pairs={{0,16},{8,24},{16,0},{24,8},{1,17},{9,25},{17,1},{25,9},{2,18},{10... | collective-permute-start | bytes 3145736 | tf_op jit(solution)/shard_map/ppermute | solution.py:261
  299.3 315.5 %collective-permute-start.11 = (s32[256,2]{0,1:T(2,128)S(1)}, s32[256,2]{0,1:T(2,128)S(1)}, u32[]{:S(2)}, u32[]{:S(2)}) collective-permute-start(s32[256,2]{0,1:T(2,128)S(1)} %bitcast.618), channel_id=1, source_target_pairs={{0,8},{8,16},{16,24},{24,0},{1,9},{9,17},{17,25},{25,1},{2,10},{10... | collective-permute-start | bytes 6152 | tf_op jit(solution)/shard_map/ppermute | solution.py:261
  326.8 317.0 %collective-permute-start.19 = (bf16[256,2048]{1,0:T(8,128)(2,1)}, bf16[256,2048]{1,0:T(8,128)(2,1)}, u32[]{:S(2)}, u32[]{:S(2)}) collective-permute-start(bf16[256,2048]{1,0:T(8,128)(2,1)} %bitcast.71), channel_id=1, source_target_pairs={{0,8},{8,16},{16,24},{24,0},{1,9},{9,17},{17,25},{25,1},{2,10},{10... | collective-permute-start | bytes 3145736 | tf_op jit(solution)/shard_map/ppermute | solution.py:261
  363.9 301.7 %collective-permute-start = (bf16[512,2816]{0,1:T(8,128)(2,1)}, bf16[512,2816]{0,1:T(8,128)(2,1)}, u32[]{:S(2)}, u32[]{:S(2)}) collective-permute-start(bf16[512,2816]{0,1:T(8,128)(2,1)} %bitcast.604), channel_id=1, source_target_pairs={{0,24},{8,0},{16,8},{24,16},{1,25},{9,1},{17,9},{25,17},{2,26},{10... | collective-permute-start | bytes 8650760 | tf_op jit(solution)/shard_map/ppermute | solution.py:261
  366.6 216.3 %all-to-all-start.14 = ((bf16[8,96,2048]{2,1,0:T(8,128)(2,1)}), bf16[8,96,2048]{2,1,0:T(8,128)(2,1)}, u32[]{:S(2)}, u32[]{:S(2)}) async-start(bf16[8,96,2048]{2,1,0:T(8,128)(2,1)} %bitcast.552), calls=%async_computation.14 | async-start | bytes 6291456 | tf_op jit(solution)/shard_map/all_to_all | solution.py:255
  411.1 176.4 %copy-start.161 = (s32[8]{0:T(128)}, s32[8]{0:T(128)S(1)}, u32[]{:S(2)}) copy-start(s32[8]{0:T(128)S(1)} %all-reduce) | copy-start | bytes 100
  429.0 552.0 %copy-start.19 = (bf16[16,2048]{1,0:T(8,128)(2,1)}, bf16[16,2048]{1,0:T(8,128)(2,1)S(1)}, u32[]{:S(2)}) copy-start(bf16[16,2048]{1,0:T(8,128)(2,1)S(1)} %dynamic-slice_bitcast_fusion.1.down_ref) | copy-start | bytes 196612
  582.9 398.2 %copy-start.4 = (bf16[512,2048]{1,0:T(8,128)(2,1)}, bf16[512,2048]{1,0:T(8,128)(2,1)S(1)}, u32[]{:S(2)}) copy-start(bf16[512,2048]{1,0:T(8,128)(2,1)S(1)} %get-tuple-element.20) | copy-start | bytes 6291460
  582.9 64.8 %all-to-all-start.2 = ((bf16[8,96,2048]{2,1,0:T(8,128)(2,1)}), bf16[8,96,2048]{2,1,0:T(8,128)(2,1)}, u32[]{:S(2)}, u32[]{:S(2)}) async-start(bf16[8,96,2048]{2,1,0:T(8,128)(2,1)} %bitcast.592), calls=%async_computation.2 | async-start | bytes 6291456 | tf_op jit(solution)/shard_map/all_to_all | solution.py:255
  599.2 381.9 %copy-start.141 = (f32[1,2,2,128]{3,1,2,0:T(2,128)}, f32[1,2,2,128]{3,1,2,0:T(2,128)S(1)}, u32[]{:S(2)}) copy-start(f32[1,2,2,128]{3,1,2,0:T(2,128)S(1)} %copy.189) | copy-start | bytes 6148
  605.8 308.2 %collective-permute-start.1 = (bf16[512,2816]{0,1:T(8,128)(2,1)}, bf16[512,2816]{0,1:T(8,128)(2,1)}, u32[]{:S(2)}, u32[]{:S(2)}) collective-permute-start(bf16[512,2816]{0,1:T(8,128)(2,1)} %bitcast.603), channel_id=1, source_target_pairs={{0,16},{8,24},{16,0},{24,8},{1,17},{9,25},{17,1},{25,9},{2,18},{10... | collective-permute-start | bytes 8650760 | tf_op jit(solution)/shard_map/ppermute | solution.py:261
  614.8 327.6 %collective-permute-start.2 = (bf16[512,2816]{0,1:T(8,128)(2,1)}, bf16[512,2816]{0,1:T(8,128)(2,1)}, u32[]{:S(2)}, u32[]{:S(2)}) collective-permute-start(bf16[512,2816]{0,1:T(8,128)(2,1)} %bitcast.602), channel_id=1, source_target_pairs={{0,8},{8,16},{16,24},{24,0},{1,9},{9,17},{17,25},{25,1},{2,10},{10... | collective-permute-start | bytes 8650760 | tf_op jit(solution)/shard_map/ppermute | solution.py:261
  647.7 286.3 %all-to-all-start.16 = ((bf16[8,96,2048]{2,1,0:T(8,128)(2,1)}), bf16[8,96,2048]{2,1,0:T(8,128)(2,1)}, u32[]{:S(2)}, u32[]{:S(2)}) async-start(bf16[8,96,2048]{2,1,0:T(8,128)(2,1)} %bitcast.555), calls=%async_computation.16 | async-start | bytes 6291456 | tf_op jit(solution)/shard_map/all_to_all | solution.py:255
  934.0 42.6 %all-to-all-start.3 = ((bf16[8,96,2048]{2,1,0:T(8,128)(2,1)}), bf16[8,96,2048]{2,1,0:T(8,128)(2,1)}, u32[]{:S(2)}, u32[]{:S(2)}) async-start(bf16[8,96,2048]{2,1,0:T(8,128)(2,1)} %bitcast.597), calls=%async_computation.3 | async-start | bytes 6291456 | tf_op jit(solution)/shard_map/all_to_all | solution.py:255
  976.6 42.4 %all-to-all-start.18 = ((bf16[8,96,2048]{2,1,0:T(8,128)(2,1)}), bf16[8,96,2048]{2,1,0:T(8,128)(2,1)}, u32[]{:S(2)}, u32[]{:S(2)}) async-start(bf16[8,96,2048]{2,1,0:T(8,128)(2,1)} %bitcast.549), calls=%async_computation.18 | async-start | bytes 6291456 | tf_op jit(solution)/shard_map/all_to_all | solution.py:255
  991.3 93.8 %collective-permute-start.5 = (bf16[256,2048]{1,0:T(8,128)(2,1)S(1)}, bf16[256,2048]{1,0:T(8,128)(2,1)}, u32[]{:S(2)}, u32[]{:S(2)}) collective-permute-start(bf16[256,2048]{1,0:T(8,128)(2,1)S(1)} %multiply_convert_fusion.4), channel_id=1, source_target_pairs={{0,24},{8,0},{16,8},{24,16},{1,25},{9,1},{17,9},{25,17},{2,26},{10... | collective-permute-start | bytes 3145736 | tf_op jit(solution)/shard_map/ppermute | solution.py:261
  991.4 97.8 %collective-permute-start.9 = (bf16[256,2048]{1,0:T(8,128)(2,1)S(1)}, bf16[256,2048]{1,0:T(8,128)(2,1)}, u32[]{:S(2)}, u32[]{:S(2)}) collective-permute-start(bf16[256,2048]{1,0:T(8,128)(2,1)S(1)} %multiply_convert_fusion.4), channel_id=1, source_target_pairs={{0,16},{8,24},{16,0},{24,8},{1,17},{9,25},{17,1},{25,9},{2,18},{10... | collective-permute-start | bytes 3145736 | tf_op jit(solution)/shard_map/ppermute | solution.py:261
  991.5 101.7 %collective-permute-start.13 = (bf16[256,2048]{1,0:T(8,128)(2,1)S(1)}, bf16[256,2048]{1,0:T(8,128)(2,1)}, u32[]{:S(2)}, u32[]{:S(2)}) collective-permute-start(bf16[256,2048]{1,0:T(8,128)(2,1)S(1)} %multiply_convert_fusion.4), channel_id=1, source_target_pairs={{0,8},{8,16},{16,24},{24,0},{1,9},{9,17},{17,25},{25,1},{2,10},{10... | collective-permute-start | bytes 3145736 | tf_op jit(solution)/shard_map/ppermute | solution.py:261
  1019.0 78.1 %all-to-all-start.4 = ((bf16[8,96,2048]{2,1,0:T(8,128)(2,1)}), bf16[8,96,2048]{2,1,0:T(8,128)(2,1)}, u32[]{:S(2)}, u32[]{:S(2)}) async-start(bf16[8,96,2048]{2,1,0:T(8,128)(2,1)} %bitcast.551), calls=%async_computation.4 | async-start | bytes 6291456 | tf_op jit(solution)/shard_map/all_to_all | solution.py:255
  1023.6 36.1 %collective-permute-start.4 = (f32[256,2]{0,1:T(2,128)S(1)}, f32[256,2]{0,1:T(2,128)S(1)}, u32[]{:S(2)}, u32[]{:S(2)}) collective-permute-start(f32[256,2]{0,1:T(2,128)S(1)} %fusion.194), channel_id=1, source_target_pairs={{0,24},{8,0},{16,8},{24,16},{1,25},{9,1},{17,9},{25,17},{2,26},{10... | collective-permute-start | bytes 6152 | tf_op jit(solution)/shard_map/ppermute | solution.py:261
  1043.9 199.3 %copy-start.93 = (bf16[768,128]{1,0:T(8,128)(2,1)}, bf16[768,128]{1,0:T(8,128)(2,1)S(1)}, u32[]{:S(2)}) copy-start(bf16[768,128]{1,0:T(8,128)(2,1)S(1)} %bitcast_multiply_fusion.2) | copy-start | bytes 589828
  1043.9 40.1 %collective-permute-start.8 = (f32[256,2]{0,1:T(2,128)S(1)}, f32[256,2]{0,1:T(2,128)S(1)}, u32[]{:S(2)}, u32[]{:S(2)}) collective-permute-start(f32[256,2]{0,1:T(2,128)S(1)} %fusion.194), channel_id=1, source_target_pairs={{0,16},{8,24},{16,0},{24,8},{1,17},{9,25},{17,1},{25,9},{2,18},{10... | collective-permute-start | bytes 6152 | tf_op jit(solution)/shard_map/ppermute | solution.py:261
  1059.7 24.9 %collective-permute-start.12 = (f32[256,2]{0,1:T(2,128)S(1)}, f32[256,2]{0,1:T(2,128)S(1)}, u32[]{:S(2)}, u32[]{:S(2)}) collective-permute-start(f32[256,2]{0,1:T(2,128)S(1)} %fusion.194), channel_id=1, source_target_pairs={{0,8},{8,16},{16,24},{24,0},{1,9},{9,17},{17,25},{25,1},{2,10},{10... | collective-permute-start | bytes 6152 | tf_op jit(solution)/shard_map/ppermute | solution.py:261
  1097.1 42.6 %all-to-all-start.6 = ((bf16[8,96,2048]{2,1,0:T(8,128)(2,1)}), bf16[8,96,2048]{2,1,0:T(8,128)(2,1)}, u32[]{:S(2)}, u32[]{:S(2)}) async-start(bf16[8,96,2048]{2,1,0:T(8,128)(2,1)} %bitcast.554), calls=%async_computation.6 | async-start | bytes 6291456 | tf_op jit(solution)/shard_map/all_to_all | solution.py:255
  1139.7 42.6 %all-to-all-start.8 = ((bf16[8,96,2048]{2,1,0:T(8,128)(2,1)}), bf16[8,96,2048]{2,1,0:T(8,128)(2,1)}, u32[]{:S(2)}, u32[]{:S(2)}) async-start(bf16[8,96,2048]{2,1,0:T(8,128)(2,1)} %bitcast.553), calls=%async_computation.8 | async-start | bytes 6291456 | tf_op jit(solution)/shard_map/all_to_all | solution.py:255
  1182.3 42.8 %all-to-all-start.10 = ((bf16[8,96,2048]{2,1,0:T(8,128)(2,1)}), bf16[8,96,2048]{2,1,0:T(8,128)(2,1)}, u32[]{:S(2)}, u32[]{:S(2)}) async-start(bf16[8,96,2048]{2,1,0:T(8,128)(2,1)} %bitcast.550), calls=%async_computation.10 | async-start | bytes 6291456 | tf_op jit(solution)/shard_map/all_to_all | solution.py:255
  1250.4 34.6 %all-to-all-start.20 = ((f32[8,4,96]{2,1,0:T(4,128)}), f32[8,4,96]{2,1,0:T(4,128)S(1)}, u32[]{:S(2)}, u32[]{:S(2)}) async-start(f32[8,4,96]{2,1,0:T(4,128)} %maximum_bitcast_fusion), calls=%async_computation.20 | async-start | bytes 32768 | tf_op jit(solution)/shard_map/all_to_all | solution.py:255
  1285.0 42.3 %all-to-all-start.15 = ((bf16[8,96,2048]{2,1,0:T(8,128)(2,1)}), bf16[8,96,2048]{2,1,0:T(8,128)(2,1)}, u32[]{:S(2)}, u32[]{:S(2)}) async-start(bf16[8,96,2048]{2,1,0:T(8,128)(2,1)} %bitcast.599), calls=%async_computation.15 | async-start | bytes 6291456 | tf_op jit(solution)/shard_map/all_to_all | solution.py:255
  1327.3 42.8 %all-to-all-start.17 = ((bf16[8,96,2048]{2,1,0:T(8,128)(2,1)}), bf16[8,96,2048]{2,1,0:T(8,128)(2,1)}, u32[]{:S(2)}, u32[]{:S(2)}) async-start(bf16[8,96,2048]{2,1,0:T(8,128)(2,1)} %bitcast.600), calls=%async_computation.17 | async-start | bytes 6291456 | tf_op jit(solution)/shard_map/all_to_all | solution.py:255
  1370.1 42.3 %all-to-all-start.19 = ((bf16[8,96,2048]{2,1,0:T(8,128)(2,1)}), bf16[8,96,2048]{2,1,0:T(8,128)(2,1)}, u32[]{:S(2)}, u32[]{:S(2)}) async-start(bf16[8,96,2048]{2,1,0:T(8,128)(2,1)} %bitcast.596), calls=%async_computation.19 | async-start | bytes 6291456 | tf_op jit(solution)/shard_map/all_to_all | solution.py:255
  1412.5 42.5 %all-to-all-start.13 = ((bf16[8,96,2048]{2,1,0:T(8,128)(2,1)}), bf16[8,96,2048]{2,1,0:T(8,128)(2,1)}, u32[]{:S(2)}, u32[]{:S(2)}) async-start(bf16[8,96,2048]{2,1,0:T(8,128)(2,1)} %bitcast.593), calls=%async_computation.13 | async-start | bytes 6291456 | tf_op jit(solution)/shard_map/all_to_all | solution.py:255
  1417.7 21.4 collective-permute-start.21
  1420.2 23.0 %collective-permute-start.22 = (f32[2,256]{1,0:T(2,128)S(1)}, f32[2,256]{1,0:T(2,128)S(1)}, u32[]{:S(2)}, u32[]{:S(2)}) collective-permute-start(f32[2,256]{1,0:T(2,128)S(1)} %reshape.610), channel_id=1, source_target_pairs={{0,16},{8,24},{16,0},{24,8},{1,17},{9,25},{17,1},{25,9},{2,18},{10... | collective-permute-start | bytes 6152 | tf_op jit(solution)/shard_map/ppermute | solution.py:261
  1423.5 19.8 collective-permute-start.23
  1428.5 28.3 %collective-permute-start.16 = (bf16[256,2048]{1,0:T(8,128)(2,1)}, bf16[256,2048]{1,0:T(8,128)(2,1)}, u32[]{:S(2)}, u32[]{:S(2)}) collective-permute-start(bf16[256,2048]{1,0:T(8,128)(2,1)} %convolution_convert_fusion.12), channel_id=1, source_target_pairs={{0,8},{8,16},{16,24},{24,0},{1,9},{9,17},{17,25},{25,1},{2,10},{10... | collective-permute-start | bytes 3145736 | tf_op jit(solution)/shard_map/ppermute | solution.py:261
  1433.2 67.3 %collective-permute-start.18 = (bf16[256,2048]{1,0:T(8,128)(2,1)}, bf16[256,2048]{1,0:T(8,128)(2,1)}, u32[]{:S(2)}, u32[]{:S(2)}) collective-permute-start(bf16[256,2048]{1,0:T(8,128)(2,1)} %convolution_convert_fusion.11), channel_id=1, source_target_pairs={{0,16},{8,24},{16,0},{24,8},{1,17},{9,25},{17,1},{25,9},{2,18},{10... | collective-permute-start | bytes 3145736 | tf_op jit(solution)/shard_map/ppermute | solution.py:261
  1439.1 61.5 %collective-permute-start.20 = (bf16[256,2048]{1,0:T(8,128)(2,1)}, bf16[256,2048]{1,0:T(8,128)(2,1)}, u32[]{:S(2)}, u32[]{:S(2)}) collective-permute-start(bf16[256,2048]{1,0:T(8,128)(2,1)} %convolution_convert_fusion.10), channel_id=1, source_target_pairs={{0,24},{8,0},{16,8},{24,16},{1,25},{9,1},{17,9},{25,17},{2,26},{10... | collective-permute-start | bytes 3145736 | tf_op jit(solution)/shard_map/ppermute | solution.py:261
  1559.7 42.5 %all-to-all-start.22 = ((bf16[8,96,2048]{2,1,0:T(8,128)(2,1)}), bf16[8,96,2048]{2,1,0:T(8,128)(2,1)}, u32[]{:S(2)}, u32[]{:S(2)}) async-start(bf16[8,96,2048]{2,1,0:T(8,128)(2,1)} %bitcast.598), calls=%async_computation.22 | async-start | bytes 6291456 | tf_op jit(solution)/shard_map/all_to_all | solution.py:255
  1564.3 247.7 %reduce-scatter.4.cloned.1.call-start = ((), (), s32[]{:S(2)}) async-start(), calls=%async_computation.31 | async-start | bytes 10485760 | tf_op jit(solution)/shard_map/reduce_scatter | solution.py:602
  1650.3 8.6 all-to-all-start.25
  1653.7 239.4 %reduce-scatter.8.cloned.1.call-start = ((), (), s32[]{:S(2)}) async-start(), calls=%async_computation.34 | async-start | bytes 4792320 | tf_op jit(solution)/shard_map/reduce_scatter | solution.py:556
  1697.2 490.7 %reduce-scatter.6.cloned.1.call-start = ((), (), s32[]{:S(2)}) async-start(), calls=%async_computation.32 | async-start | bytes 1146880 | tf_op jit(solution)/shard_map/reduce_scatter | solution.py:625
  1829.9 75.4 %all-to-all-start.5 = ((bf16[8,96,2048]{2,1,0:T(8,128)(2,1)}), bf16[8,96,2048]{2,1,0:T(8,128)(2,1)}, u32[]{:S(2)}, u32[]{:S(2)}) async-start(bf16[8,96,2048]{2,1,0:T(8,128)(2,1)} %bitcast.560), calls=%async_computation.5 | async-start | bytes 6291456 | tf_op jit(solution)/shard_map/all_to_all | solution.py:255
  1834.3 358.5 %all-gather.15.cloned.1.call-start = ((), (), s32[]{:S(2)}) async-start(), calls=%async_computation.35 | async-start | bytes 8785920 | tf_op jit(solution)/shard_map/all_gather | solution.py:559
  1905.3 44.2 %all-to-all-start.7 = ((bf16[8,96,2048]{2,1,0:T(8,128)(2,1)}), bf16[8,96,2048]{2,1,0:T(8,128)(2,1)}, u32[]{:S(2)}, u32[]{:S(2)}) async-start(bf16[8,96,2048]{2,1,0:T(8,128)(2,1)} %bitcast.561), calls=%async_computation.7 | async-start | bytes 6291456 | tf_op jit(solution)/shard_map/all_to_all | solution.py:255
  2011.6 42.5 %all-to-all-start.23 = ((bf16[8,96,2048]{2,1,0:T(8,128)(2,1)}), bf16[8,96,2048]{2,1,0:T(8,128)(2,1)}, u32[]{:S(2)}, u32[]{:S(2)}) async-start(bf16[8,96,2048]{2,1,0:T(8,128)(2,1)} %bitcast.590), calls=%async_computation.23 | async-start | bytes 6291456 | tf_op jit(solution)/shard_map/all_to_all | solution.py:255
  2054.2 42.4 %all-to-all-start.11 = ((bf16[8,96,2048]{2,1,0:T(8,128)(2,1)}), bf16[8,96,2048]{2,1,0:T(8,128)(2,1)}, u32[]{:S(2)}, u32[]{:S(2)}) async-start(bf16[8,96,2048]{2,1,0:T(8,128)(2,1)} %bitcast.562), calls=%async_computation.11 | async-start | bytes 6291456 | tf_op jit(solution)/shard_map/all_to_all | solution.py:255
  2096.6 87.1 %all-to-all-start.24 = ((bf16[8,96,2048]{2,1,0:T(8,128)(2,1)}), bf16[8,96,2048]{2,1,0:T(8,128)(2,1)}, u32[]{:S(2)}, u32[]{:S(2)}) async-start(bf16[8,96,2048]{2,1,0:T(8,128)(2,1)} %bitcast.594), calls=%async_computation.24 | async-start | bytes 6291456 | tf_op jit(solution)/shard_map/all_to_all | solution.py:255
  2101.2 170.5 %all-gather.13.cloned.1.call-start = ((), (), s32[]{:S(2)}) async-start(), calls=%async_computation.33 | async-start | bytes 3784704 | tf_op jit(solution)/shard_map/all_gather | solution.py:626
  2105.2 28.2 %collective-permute-start.6 = (bf16[256,2048]{1,0:T(8,128)(2,1)}, bf16[256,2048]{1,0:T(8,128)(2,1)}, u32[]{:S(2)}, u32[]{:S(2)}) collective-permute-start(bf16[256,2048]{1,0:T(8,128)(2,1)} %convolution_convert_fusion.16), channel_id=1, source_target_pairs={{0,8},{8,16},{16,24},{24,0},{1,9},{9,17},{17,25},{25,1},{2,10},{10... | collective-permute-start | bytes 3145736 | tf_op jit(solution)/shard_map/ppermute | solution.py:261
  2108.7 69.1 %collective-permute-start.10 = (bf16[256,2048]{1,0:T(8,128)(2,1)}, bf16[256,2048]{1,0:T(8,128)(2,1)}, u32[]{:S(2)}, u32[]{:S(2)}) collective-permute-start(bf16[256,2048]{1,0:T(8,128)(2,1)} %convolution_convert_fusion.15), channel_id=1, source_target_pairs={{0,16},{8,24},{16,0},{24,8},{1,17},{9,25},{17,1},{25,9},{2,18},{10... | collective-permute-start | bytes 3145736 | tf_op jit(solution)/shard_map/ppermute | solution.py:261
  2115.0 62.8 %collective-permute-start.14 = (bf16[256,2048]{1,0:T(8,128)(2,1)}, bf16[256,2048]{1,0:T(8,128)(2,1)}, u32[]{:S(2)}, u32[]{:S(2)}) collective-permute-start(bf16[256,2048]{1,0:T(8,128)(2,1)} %convolution_convert_fusion.14), channel_id=1, source_target_pairs={{0,24},{8,0},{16,8},{24,16},{1,25},{9,1},{17,9},{25,17},{2,26},{10... | collective-permute-start | bytes 3145736 | tf_op jit(solution)/shard_map/ppermute | solution.py:261
  (161 other events, 2243.8 us)
Sparse Core Ops, SparseCore 0:
  11.5 117.5 all-gather.8
  130.6 147.8 all-gather.16
  280.7 267.2 all-gather.10
  549.4 359.2 all-gather.18
  1648.8 163.1 reduce-scatter.3
  1815.9 77.0 reduce-scatter.7
  1896.0 25.0 reduce-scatter.5
  1924.9 101.8 all-gather.14
  2189.6 82.0 all-gather.12

commit v2 on v1

--- a/solution.py
+++ b/solution.py
@@ -3,6 +3,7 @@
 
 import jax
 import jax.numpy as jnp
+import numpy as np
 from jax import lax
 from jax.experimental import pallas as pl
 from jax.experimental.pallas import tpu as pltpu
@@ -38,41 +39,66 @@
     return product(left, right, 0, 0)
 
 
-def pair_kernel(key_blocks, n_ref, w_ref, low_ref, up_ref, cos_ref, sin_ref, out_ref):
-    made = nn(n_ref[...], w_ref[...]) + nn(low_ref[...], up_ref[...])
-
-    @pl.when(pl.program_id(0) < key_blocks)
+def pair_kernel(count, key_blocks, *refs):
+    normed_refs = refs[:count]
+    w_ref, down_ref, up_ref, cos_ref, sin_ref, out_ref, low_ref = refs[count:]
+    rows = normed_refs[0].shape[0]
+    step = pl.program_id(0)
+
+    @pl.when(step == 0)
     def _():
-        for start in range(0, made.shape[1], HD):
-            head = made[:, start : start + HD]
-            turned = head * cos_ref[...] + pltpu.roll(head, HD // 2, 1) * sin_ref[...]
-            out_ref[:, start : start + HD] = turned.astype(bf16)
-
-    @pl.when(pl.program_id(0) >= key_blocks)
-    def _():
-        out_ref[...] = made.astype(bf16)
-
-
-def project_pairs(normed, weight, low, upper, cosine, sine):
-    rows, width = normed.shape
+        for k in range(count):
+            low_ref[pl.ds(k * rows, rows), :] = nt(normed_refs[k][...], down_ref[...]).astype(bf16)
+
+    for k in range(count):
+        part = pl.ds(k * rows, rows)
+        made = nn(normed_refs[k][...], w_ref[...]) + nn(low_ref[part, :], up_ref[...])
+
+        @pl.when(step < key_blocks)
+        def _():
+            for start in range(0, made.shape[1], HD):
+                head = made[:, start : start + HD]
+                turned = head * cos_ref[part, :] + pltpu.roll(head, HD // 2, 1) * sin_ref[part, :]
+                out_ref[part, start : start + HD] = turned.astype(bf16)
+
+        @pl.when(step >= key_blocks)
+        def _():
+            out_ref[part, :] = made.astype(bf16)
+
+
+def project_pairs(normed_parts, weight, down, upper, cosine, sine):
+    count = len(normed_parts)
+    rows, width = normed_parts[0].shape
     columns = weight.shape[1]
     block = 512
+    whole = lambda array: pl.BlockSpec(array.shape, lambda i: (0, 0))
     return pl.pallas_call(
-        functools.partial(pair_kernel, columns // 2 // block),
+        functools.partial(pair_kernel, count, columns // 2 // block),
         grid=(columns // block,),
-        in_specs=[
-            pl.BlockSpec((rows, width), lambda i: (0, 0)),
+        in_specs=[whole(n) for n in normed_parts]
+        + [
             pl.BlockSpec((width, block), lambda i: (0, i)),
-            pl.BlockSpec(low.shape, lambda i: (0, 0)),
+            whole(down),
             pl.BlockSpec((upper.shape[0], block), lambda i: (0, i)),
-            pl.BlockSpec((rows, HD), lambda i: (0, 0)),
-            pl.BlockSpec((rows, HD), lambda i: (0, 0)),
+            whole(cosine),
+            whole(sine),
         ],
-        out_specs=pl.BlockSpec((rows, block), lambda i: (0, i)),
-        out_shape=jax.ShapeDtypeStruct((rows, columns), bf16),
+        out_specs=[
+            pl.BlockSpec((count * rows, block), lambda i: (0, i)),
+            pl.BlockSpec((count * rows, down.shape[0]), lambda i: (0, 0)),
+        ],
+        out_shape=[
+            jax.ShapeDtypeStruct((count * rows, columns), bf16),
+            jax.ShapeDtypeStruct((count * rows, down.shape[0]), bf16),
+        ],
         compiler_params=pltpu.CompilerParams(vmem_limit_bytes=vmem_bytes),
+        cost_estimate=pl.CostEstimate(
+            flops=2 * count * rows * width * columns,
+            bytes_accessed=2 * width * columns,
+            transcendentals=0,
+        ),
         name="pairs",
-    )(normed, weight, low, upper, cosine, sine)
+    )(*normed_parts, weight, down, upper, cosine, sine)
 
 
 def attend_kernel(
@@ -169,7 +195,8 @@
     sin_ref,
     cos_all_ref,
     sin_all_ref,
-    pair_ref,
+    key_grad_ref,
+    value_grad_ref,
     slots_ref,
     sum_ref,
     turned_ref,
@@ -198,8 +225,8 @@
         value_grad = value_part if route == 0 else value_grad + value_part
     key_grad = key_grad * scale
     key_grad = key_grad * cos_all_ref[...] - pltpu.roll(key_grad, HD // 2, 1) * sin_all_ref[...]
-    pair_ref[0, :, :] = key_grad.astype(bf16)
-    pair_ref[1, :, :] = value_grad.astype(bf16)
+    key_grad_ref[...] = key_grad.astype(bf16)
+    value_grad_ref[...] = value_grad.astype(bf16)
     slots_ref[...] = tn(place_ref[...], turned_ref[...]).astype(bf16)
     first = turned_ref[pl.ds(0, rows), :].astype(f32)
     sum_ref[...] = (first + turned_ref[pl.ds(rows, rows), :].astype(f32)).astype(bf16)
@@ -231,12 +258,14 @@
             whole(sine_all),
         ],
         out_specs=[
-            pl.BlockSpec((2, length, HD), lambda h: (0, 0, h)),
+            pl.BlockSpec((length, HD), lambda h: (0, h)),
+            pl.BlockSpec((length, HD), lambda h: (0, h)),
             pl.BlockSpec((slots, HD), lambda h: (0, h)),
             pl.BlockSpec((rows, HD), lambda h: (0, h)),
         ],
         out_shape=[
-            jax.ShapeDtypeStruct((2, length, heads * HD), bf16),
+            jax.ShapeDtypeStruct((length, heads * HD), bf16),
+            jax.ShapeDtypeStruct((length, heads * HD), bf16),
             jax.ShapeDtypeStruct((slots, heads * HD), bf16),
             jax.ShapeDtypeStruct((rows, heads * HD), bf16),
         ],
@@ -332,12 +361,178 @@
     return jnp.sum((gates * (grad - mean))[:, :, None] * hits, axis=1)
 
 
-def rope_full(positions):
+def rope_full(length, start):
     half = HD // 2
-    frequency = jnp.power(rope_base, -jnp.arange(half).astype(f32) / half)
-    angles = positions.astype(f32)[:, None] * frequency[None, :]
-    cosine, sine = jnp.cos(angles), jnp.sin(angles)
-    return jnp.concatenate([cosine, cosine], 1), jnp.concatenate([-sine, sine], 1)
+    frequency = rope_base ** (-np.arange(half) / half)
+    angles = np.arange(length)[:, None] * frequency[None, :]
+    cosine, sine = np.cos(angles), np.sin(angles)
+    tables = np.concatenate([cosine, cosine, -sine, sine], 1).astype(np.float32)
+    tables = jnp.asarray(np.concatenate([tables, tables], 0))
+    tables = lax.dynamic_slice_in_dim(tables, start, length, 0)
+    return tables[:, :HD], tables[:, HD:]
+
+
+def after(array, *earlier):
+    return lax.optimization_barrier((array,) + earlier)[0]
+
+
+def cut_kernel(target_ref, in_ref, out_ref):
+    out_ref[...] = in_ref[...]
+
+
+def cut_share(weight, target, size):
+    rows, columns = weight.shape
+    share = columns // 2 // size
+    if share % 128:
+        cut = weight.reshape(rows, 2, size, share)
+        return lax.dynamic_index_in_dim(cut, target, 2, keepdims=False).reshape(rows, 2 * share)
+    return pl.pallas_call(
+        cut_kernel,
+        grid_spec=pltpu.PrefetchScalarGridSpec(
+            num_scalar_prefetch=1,
+            grid=(2,),
+            in_specs=[pl.BlockSpec((rows, share), lambda i, t: (0, i * size + t[0]))],
+            out_specs=pl.BlockSpec((rows, share), lambda i, t: (0, i)),
+        ),
+        out_shape=jax.ShapeDtypeStruct((rows, 2 * share), bf16),
+        compiler_params=pltpu.CompilerParams(vmem_limit_bytes=vmem_bytes),
+        name="cut",
+    )(target.reshape(1).astype(jnp.int32), weight)
+
+
+def unpack_kernel(size, share, in_ref, inner_up_ref, outer_down_ref, inner_down_ref, outer_up_ref):
+    spot = pl.program_id(1)
+    got = in_ref[0, 0].astype(f32)
+    hidden = size * share
+    width = inner_down_ref.shape[2]
+    start = pl.multiple_of(spot * share, 128)
+    inner_up_ref[0, :, pl.ds(start, share)] = got[:, :share]
+    inner_up_ref[0, :, pl.ds(pl.multiple_of(hidden + start, 128), share)] = got[:, share : 2 * share]
+    outer_down_ref[0, :, pl.ds(start, share)] = got[:, 2 * share : 3 * share]
+    inner_down = got[:, 3 * share : 3 * share + width]
+    outer_up = got[:, 3 * share + width :]
+
+    @pl.when(spot == 0)
+    def _():
+        inner_down_ref[0] = inner_down
+        outer_up_ref[0] = outer_up
+
+    @pl.when(spot > 0)
+    def _():
+        inner_down_ref[0] += inner_down
+        outer_up_ref[0] += outer_up
+
+
+def unpack_sums(sums, share, width):
+    size, adapters, rank, columns = sums.shape
+    hidden = size * share
+    shapes = [2 * hidden, hidden, width, width]
+    return pl.pallas_call(
+        functools.partial(unpack_kernel, size, share),
+        grid=(adapters, size),
+        in_specs=[pl.BlockSpec((1, 1, rank, columns), lambda a, k: (k, a, 0, 0))],
+        out_specs=[pl.BlockSpec((1, rank, n), lambda a, k: (a, 0, 0)) for n in shapes],
+        out_shape=[jax.ShapeDtypeStruct((adapters, rank, n), f32) for n in shapes],
+        compiler_params=pltpu.CompilerParams(vmem_limit_bytes=vmem_bytes),
+        name="unpack",
+    )(sums)
+
+
+def silu_parts(gate_part, up_part, hidden_grad):
+    sigmoid = 1.0 / (1.0 + jnp.exp(-gate_part))
+    active = gate_part * sigmoid
+    activated = (active * up_part).astype(bf16)
+    gate_grad = hidden_grad * up_part * sigmoid * (1.0 + gate_part * (1.0 - sigmoid))
+    return activated, gate_grad.astype(bf16), (hidden_grad * active).astype(bf16)
+
+
+def halves(value):
+    high = value.astype(bf16)
+    return high, (value - high.astype(f32)).astype(bf16)
+
+
+def expert_kernel(size, share, spot_ref, x_ref, hidden_ref, mask_ref, up_ref, down_ref, *refs):
+    w_refs = refs[:size]
+    row_ref, active_ref, pre_ref, code_ref, back_ref = refs[size:]
+    depth = w_refs[0].shape[0]
+    width = size * depth
+    columns = [pl.ds(pl.multiple_of((spot_ref[0] + k) % size * depth, 128), depth) for k in range(size)]
+    code = nt(x_ref[...], down_ref[...]).astype(bf16) * mask_ref[...]
+    code_ref[...] = code
+    sums = None
+    for start in range(0, share, 256):
+        end = min(start + 256, share)
+
+        def hidden(first, last):
+            made = nn(code, up_ref[:, first:last])
+            for k in range(size):
+                made = made + nn(x_ref[:, columns[k]], w_refs[k][:, first:last])
+            return made
+
+        gate_part, up_part = hidden(start, end), hidden(share + start, share + end)
+        hidden_grad = hidden_ref[:, start:end].astype(f32)
+        activated, gate_grad, up_grad = silu_parts(gate_part, up_part, hidden_grad)
+        active_ref[:, start:end] = activated
+        pre_ref[:, start:end] = gate_grad
+        pre_ref[:, share + start : share + end] = up_grad
+        part = jnp.sum(activated.astype(f32) * hidden_grad, axis=1, keepdims=True)
+        sums = part if sums is None else sums + part
+    back = nt(pre_ref[...], up_ref[...]).astype(bf16) * mask_ref[...]
+    back_ref[...] = back
+    for k in range(size):
+        base = (spot_ref[0] + k) % size * depth
+        for start in range(0, depth, 256):
+            end = min(start + 256, depth)
+            here = pl.ds(pl.multiple_of(base + start, 128), end - start)
+            made = nt(pre_ref[...], w_refs[k][start:end, :]) + nn(back, down_ref[:, here])
+            row_ref[:, here] = made.astype(bf16)
+    high, low = halves(sums)
+    lane = lax.broadcasted_iota(jnp.int32, (sums.shape[0], 128), 1)
+    packed = jnp.where(lane == 0, high.astype(f32), jnp.where(lane == 1, low.astype(f32), 0.0))
+    row_ref[:, width:] = packed.astype(bf16)
+
+
+def expert_block(got, hidden_grad, mask, inner_up, inner_down, inner_parts, spot):
+    size = len(inner_parts)
+    rows, width = got.shape
+    share = hidden_grad.shape[1]
+    codes = mask.shape[1]
+    if share % 128 or width // size % 256:
+        code = nt(got, inner_down).astype(bf16) * mask
+        twice = jnp.concatenate(inner_parts + inner_parts, axis=0)
+        first = (size - spot) % size * (width // size)
+        inner_full = lax.dynamic_slice_in_dim(twice, first, width, 0)
+        pre = nn(got, inner_full) + nn(code, inner_up)
+        hidden_float = hidden_grad.astype(f32)
+        activated, gate_grad, up_grad = silu_parts(pre[:, :share], pre[:, share:], hidden_float)
+        pre_grad = jnp.concatenate([gate_grad, up_grad], axis=1)
+        back = nt(pre_grad, inner_up).astype(bf16) * mask
+        row_grad = (nt(pre_grad, inner_full) + nn(back, inner_down)).astype(bf16)
+        sums = jnp.stack(halves(jnp.sum(activated.astype(f32) * hidden_float, axis=1)), axis=1)
+        row_grad = jnp.concatenate([row_grad, jnp.pad(sums, ((0, 0), (0, 126)))], axis=1)
+        return row_grad, activated, pre_grad, code, back
+    block = rows // 2
+    ahead = lambda n: pl.BlockSpec((block, n), lambda i, s: (i, 0))
+    whole = lambda array: pl.BlockSpec(array.shape, lambda i, s: (0, 0), pipeline_mode=pl.Buffered(1))
+    shapes = [width + 128, share, 2 * share, codes, codes]
+    return pl.pallas_call(
+        functools.partial(expert_kernel, size, share),
+        grid_spec=pltpu.PrefetchScalarGridSpec(
+            num_scalar_prefetch=1,
+            grid=(2,),
+            in_specs=[ahead(width), ahead(share), ahead(codes), whole(inner_up), whole(inner_down)]
+            + [whole(part) for part in inner_parts],
+            out_specs=[ahead(n) for n in shapes],
+        ),
+        out_shape=[jax.ShapeDtypeStruct((rows, n), bf16) for n in shapes],
+        compiler_params=pltpu.CompilerParams(vmem_limit_bytes=vmem_bytes),
+        cost_estimate=pl.CostEstimate(
+            flops=8 * rows * width * share,
+            bytes_accessed=4 * width * share + 10 * rows * width,
+            transcendentals=rows * share,
+        ),
+        name="experts",
+    )(spot.reshape(1).astype(jnp.int32), got, hidden_grad, mask, inner_up, inner_down, *inner_parts)
 
 
 def picked(lookup, index):
@@ -389,7 +584,10 @@
         return lookup.transpose(0, 2, 1)
 
     adapter = adapter_index[0]
-    adapter_all = lax.all_gather(adapter_index, "dp", axis=0, tiled=True)
+    adapter_all = exchange(jnp.broadcast_to(adapter_index[None], (holders, 128)))[:, 0]
+    inputs = tokens[0].astype(f32)
+    input_scale = norm_scale(inputs)
+    normed = (inputs * input_scale * norm_gain).astype(bf16)
 
     piece = key_value_weight.shape[0] // holders
     pair_weight = lax.all_gather(
@@ -398,57 +596,31 @@
         axis=0,
         tiled=True,
     )
-    query_full = lax.all_gather(query_weight[0], "seq", axis=0, tiled=True)
-    output_full = lax.all_gather(output_weight[0], "seq", axis=0, tiled=True)
-    inner_cut = mlp_in_weight[0].reshape(-1, 2, size, share)
-    inner_full = jnp.zeros((size, inner_cut.shape[0], 2 * share), bf16)
-    for shift in range(size):
-        target = (spot - shift) % size
-        sent = lax.dynamic_index_in_dim(inner_cut, target, 2, keepdims=False)
-        got = shifted(sent.reshape(-1, 2 * share), shift, size)
-        inner_full = lax.dynamic_update_index_in_dim(inner_full, got, (spot + shift) % size, 0)
-    inner_full = inner_full.reshape(-1, 2 * share)
+    lanes = jnp.pad(mlp_routes[0].astype(bf16), ((0, 0), (0, 126)))
+    packet = jnp.concatenate([normed, out_grad[0], lanes], axis=1)
+    early = [packet] + [shifted(packet, d, size) for d in range(1, size)]
+    normed_parts = [normed] + [p[:, :width] for p in early[1:]]
+    grad_parts = [out_grad[0]] + [p[:, width : 2 * width] for p in early[1:]]
+    routes_there = [p[:, 2 * width : 2 * width + 2].astype(jnp.int32) for p in early]
+    gates, hits = gate_pair(nn(normed, router_weight), routes[0])
+    place = slot_layout(routes[0], experts, capacity)
+    place_any = either(place)
+    query_rows = send_full(tn(place_any, normed).astype(bf16), experts, copies)
+    query_own = after(query_weight[0], pair_weight, query_rows, *early[1:])
+    query_full = lax.all_gather(query_own, "seq", axis=0, tiled=True)
+    output_full = lax.all_gather(after(output_weight[0], query_full), "seq", axis=0, tiled=True)
     outer_full = mlp_out_weight[0]
 
-    inputs = tokens[0].astype(f32)
-    input_scale = norm_scale(inputs)
-    normed = (inputs * input_scale * norm_gain).astype(bf16)
     pair_down, pair_up = picked(flat_down(key_value_down), adapter), picked(key_value_up, adapter)
     query_lower, query_upper = picked(flat_down(query_down), adapter), picked(query_up, adapter)
     output_lower, output_upper = picked(flat_down(output_down), adapter), picked(output_up, adapter)
-    pair_low = nt(normed, pair_down).astype(bf16)
     query_low = nt(normed, query_lower).astype(bf16)
-    cosine_all, sine_all = rope_full(jnp.arange(length))
     positions = spot * rows + jnp.arange(rows)
-    cosine = lax.dynamic_slice_in_dim(cosine_all, spot * rows, rows, 0)
-    sine = lax.dynamic_slice_in_dim(sine_all, spot * rows, rows, 0)
-    key_pos = jnp.arange(length)
+    key_pos = (spot * rows + jnp.arange(length)) % length
+    cosine_all, sine_all = rope_full(length, spot * rows)
+    cosine, sine = cosine_all[:rows], sine_all[:rows]
     allowed = (key_pos[None, :] <= positions[:, None]) | (key_pos[None, :] < prefix_length[0])
     bias = jnp.where(allowed, 0.0, masked_score).astype(f32)
-    pairs_local = project_pairs(normed, pair_weight, pair_low, pair_up, cosine, sine)
-    pairs = lax.all_gather(pairs_local, "seq", axis=0, tiled=True)
-
-    gates, hits = gate_pair(nn(normed, router_weight), routes[0])
-    place = slot_layout(routes[0], experts, capacity)
-    place_any = either(place)
-
-    query_rows = send_full(tn(place_any, normed).astype(bf16), experts, copies)
-    query_parts = nn(query_rows.reshape(-1, width), query_full).astype(bf16)
-    query_home = home_join(query_parts.reshape(holders, capacity, -1), experts, copies)
-    attended, output_slots, query_rot, totals = attend(
-        query_home, place, query_low, query_upper, cosine, sine, pairs, bias
-    )
-
-    output_rows = send_cut(output_slots, experts, copies)
-    output_parts = nn(output_rows.reshape(holders * capacity, -1), output_full).astype(bf16)
-    output_home = home_add(output_parts.reshape(holders, capacity, width), experts, copies)
-    output_low = nt(attended, output_lower).astype(bf16)
-    branch = nn(place, output_home) + nn(output_low, output_upper)
-    branch = branch.reshape(2, rows, width)
-    middle = inputs + gates[:, :1] * branch[0] + gates[:, 1:] * branch[1]
-    middle_scale = norm_scale(middle)
-    normed_mlp = (middle * middle_scale * mlp_gain).astype(bf16)
-    mlp_gates, mlp_hits = gate_pair(nn(normed_mlp, mlp_router_weight), mlp_routes[0])
 
     mask = (jnp.arange(codes)[None, None, :] // rank == adapter_all[:, None, None]).astype(bf16)
     mask = jnp.broadcast_to(mask, (holders, capacity, codes)).reshape(-1, codes)
@@ -461,61 +633,114 @@
     outer_down = lax.dynamic_index_in_dim(outer_down, part, 1, keepdims=False)
     outer_down = lax.dynamic_index_in_dim(outer_down, spot, 1, keepdims=False)
 
-    places = [slot_layout(shifted(mlp_routes[0], d, size), experts, capacity) for d in range(size)]
+    places = [slot_layout(routes_there[d], experts, capacity) for d in range(size)]
     grad_rows, hidden_grads, outer_codes = [], [], []
     for d in range(size):
-        rows_there = shifted(out_grad[0], d, size)
-        got = send_full(tn(either(places[d]), rows_there).astype(bf16), experts, copies)
+        got = send_full(tn(either(places[d]), grad_parts[d]).astype(bf16), experts, copies)
         got = got.reshape(-1, width)
         code = nt(got, outer_up).astype(bf16) * mask
         grad_rows.append(got)
         outer_codes.append(code)
         hidden_grads.append((nt(got, outer_full) + nn(code, outer_down)).astype(bf16))
 
-    order = list(range(size))
-    gates_there = [shifted(mlp_gates, d, size) for d in order]
+    query_parts = nn(query_rows.reshape(-1, width), query_full).astype(bf16)
+    query_home = home_join(query_parts.reshape(holders, capacity, -1), experts, copies)
+    pairs, pair_low = project_pairs(
+        normed_parts, pair_weight, pair_down, pair_up, cosine_all, sine_all
+    )
+    far = size // 2
+    inner_sent = [cut_share(mlp_in_weight[0], (spot - d) % size, size) for d in range(size)]
+    inner_parts = list(inner_sent)
+    inner_parts[far] = shifted(after(inner_sent[far], query_full), far, size)
+    query_home = after(query_home, *grad_rows[:2])
+    attended, output_slots, query_rot, totals = attend(
+        query_home, place, query_low, query_upper, cosine, sine, pairs, bias
+    )
+
+    output_rows = send_cut(output_slots, experts, copies)
+    output_rows = after(output_rows, inner_parts[far], *grad_rows[2:])
+    output_parts = nn(output_rows.reshape(holders * capacity, -1), output_full).astype(bf16)
+    distances = [d for d in range(1, size) if d != far]
+    for d in distances[:-1]:
+        inner_parts[d] = shifted(after(inner_sent[d], output_full), d, size)
+    output_home = home_add(output_parts.reshape(holders, capacity, width), experts, copies)
+    output_low = nt(attended, output_lower).astype(bf16)
+    branch = nn(place, output_home) + nn(output_low, output_upper)
+    branch = branch.reshape(2, rows, width)
+    middle = inputs + gates[:, :1] * branch[0] + gates[:, 1:] * branch[1]
+    middle_scale = norm_scale(middle)
+    normed_mlp = (middle * middle_scale * mlp_gain).astype(bf16)
+    mlp_gates, mlp_hits = gate_pair(nn(normed_mlp, mlp_router_weight), mlp_routes[0])
+
+    lanes = jnp.pad(jnp.concatenate(halves(mlp_gates), axis=1), ((0, 0), (0, 124)))
+    packet = jnp.concatenate([normed_mlp, lanes], axis=1)
+    packet = after(packet, *(inner_parts[d] for d in distances[:-1]))
+    packet_all = lax.all_gather(packet, "seq", axis=0, tiled=True)
+    for d in distances[-1:]:
+        inner_parts[d] = shifted(after(inner_sent[d], inner_parts[distances[0]]), d, size)
+    packet_all = after(packet_all, *(inner_parts[d] for d in distances[-1:]))
+    packets = [packet] + [
+        lax.dynamic_slice_in_dim(packet_all, (spot + d) % size * rows, rows, 0)
+        for d in range(1, size)
+    ]
+    gates_there = [
+        (p[:, width : width + 2].astype(f32) + p[:, width + 2 : width + 4].astype(f32)).T.reshape(-1, 1)
+        for p in packets
+    ]
+    combines = [either((places[d].astype(f32) * gates_there[d]).astype(bf16)) for d in range(size)]
+    got_rows = [
+        send_full(tn(either(places[d]), packets[d][:, :width]).astype(bf16), experts, copies)
+        for d in range(size)
+    ]
     gate_slots = jnp.stack(
-        [
-            jnp.sum(places[d].astype(f32) * gates_there[d].T.reshape(-1)[:, None], axis=0)
-            for d in order
-        ]
+        [jnp.sum(places[d].astype(f32) * gates_there[d], axis=0) for d in range(size)]
     )
     gate_slots = gate_slots.reshape(size, experts, capacity).transpose(1, 0, 2)
     gate_slots = exchange(jnp.repeat(gate_slots, copies, axis=0))
 
-    row_total, down_total = None, None
-    gate_sums, sums = [], None
+    order = [d for d in range(1, size) if d != far] + ([far] if size > 1 else []) + [0]
+    kept, row_total, backs = {}, None, []
+    for turn, d in enumerate(order):
+        if turn:
+            got_rows[d] = after(got_rows[d], kept[order[turn - 1]][0])
+        kept[d] = expert_block(
+            got_rows[d].reshape(-1, width),
+            hidden_grads[d],
+            mask,
+            inner_up,
+            inner_down,
+            inner_parts,
+            spot,
+        )
+        row_grad = after(kept[d][0], backs[0]) if turn > 2 else kept[d][0]
+        row_home = home_add(row_grad.reshape(holders, capacity, -1), experts, copies)
+        row_sum = nn(combines[d], row_home[:, :width])
+        gate_sum = nn(places[d], row_home[:, width:])
+        lanes = gate_sum[:rows] + jnp.roll(gate_sum[rows:], 2, axis=1)
+        row_back = jnp.concatenate([row_sum, lanes], axis=1)
+        if d:
+            row_back = shifted(row_back.astype(bf16), -d % size, size)
+        backs.append(row_back)
+        row_back = row_back.astype(f32)
+        row_total = row_back if row_total is None else row_total + row_back
+    gate_sum = row_total[:, width : width + 4]
+    row_total = row_total[:, :width]
+    mlp_gate_grad = gate_sum.reshape(rows, 2, 2).sum(2)
+    mlp_logit_grad = gate_back(mlp_gates, mlp_hits, mlp_gate_grad)
+
+    down_near, down_parts, down_sent, sums = [], [], [], None
     for d in order:
-        rows_there = shifted(normed_mlp, d, size)
-        got = send_full(tn(either(places[d]), rows_there).astype(bf16), experts, copies)
-        got = got.reshape(-1, width)
-        code = nt(got, inner_down).astype(bf16) * mask
-        pre = nn(got, inner_full) + nn(code, inner_up)
-        gate_part, up_part = pre[:, :share], pre[:, share:]
-        sigmoid = 1.0 / (1.0 + jnp.exp(-gate_part))
-        active = gate_part * sigmoid
-        activated = (active * up_part).astype(bf16)
-        hidden_grad = hidden_grads[d].astype(f32)
-        gate_sums.append(jnp.sum(activated.astype(f32) * hidden_grad, axis=1))
-        pre_grad = jnp.concatenate(
-            [
-                (hidden_grad * up_part * sigmoid * (1.0 + gate_part * (1.0 - sigmoid))).astype(bf16),
-                (hidden_grad * active).astype(bf16),
-            ],
-            axis=1,
-        )
-        code_grad = nt(pre_grad, inner_up).astype(bf16) * mask
-        row_grad = (nt(pre_grad, inner_full) + nn(code_grad, inner_down)).astype(bf16)
+        _, activated, pre_grad, code, back = kept[d]
         outer_low = nt(activated, outer_down).astype(bf16) * mask
         down = (nn(activated, outer_full) + nn(outer_low, outer_up)).astype(bf16)
-        weight = gates_there[d].T.reshape(-1)[:, None]
-        combine = either((places[d].astype(f32) * weight).astype(bf16))
-        row_home = home_add(row_grad.reshape(holders, capacity, width), experts, copies)
-        row_back = shifted(nn(combine, row_home).astype(bf16), -d % size, size).astype(f32)
-        row_total = row_back if row_total is None else row_total + row_back
-        down_home = home_add(down.reshape(holders, capacity, width), experts, copies)
-        down_back = shifted(nn(combine, down_home).astype(bf16), -d % size, size).astype(f32)
-        down_total = down_back if down_total is None else down_total + down_back
+        if d in (0, 1, size - 1):
+            if d:
+                down_sent.append(down)
+                down = shifted(after(down, row_home), -d % size, size)
+            down_near.append(down)
+        else:
+            down_sent.append(down)
+            down_parts.append((d, down))
         scale = gate_slots[:, d, :].reshape(-1, 1)
 
         def scaled(array):
@@ -524,23 +749,10 @@
         new = (
             tn(scaled(code), pre_grad),
             tn(scaled(outer_codes[d]), activated),
-            tn(scaled(code_grad), got),
+            tn(scaled(back), got_rows[d].reshape(-1, width)),
             tn(scaled(outer_low), grad_rows[d]),
         )
         sums = new if sums is None else tuple(a + b for a, b in zip(sums, new))
-
-    gate_sums = jnp.stack(gate_sums, 0).reshape(size, holders, capacity).transpose(1, 0, 2)
-    gate_sums = exchange(gate_sums).reshape(experts, copies, size, capacity)
-    gate_sums = jnp.sum(gate_sums, axis=1).transpose(1, 0, 2).reshape(size, -1)
-    gate_parts = [
-        jnp.sum(places[d].astype(f32) * gate_sums[d][None, :], axis=1).reshape(2, rows)
-        for d in range(size)
-    ]
-    mlp_gate_grad = gate_parts[0]
-    for d in range(1, size):
-        mlp_gate_grad = mlp_gate_grad + shifted(gate_parts[d], -d % size, size)
-    mlp_logit_grad = gate_back(mlp_gates, mlp_hits, mlp_gate_grad.T)
-    result = (middle + down_total).astype(bf16)
 
     inner_up_sum, outer_down_sum, inner_down_sum, outer_up_sum = sums
 
@@ -553,18 +765,22 @@
 
     wide = [widened(inner_up_sum), widened(outer_down_sum), inner_down_sum, outer_up_sum]
     ends = [sum(a.shape[1] for a in wide[: k + 1]) for k in range(3)]
-    mlp_sums = lax.psum_scatter(
-        jnp.concatenate(wide, axis=1), "dp", scatter_dimension=0, tiled=True
-    ).astype(bf16)
+    mlp_own = jnp.concatenate(wide, axis=1).astype(bf16)
+    mlp_sums = lax.psum_scatter(mlp_own, "dp", scatter_dimension=0, tiled=True)
     mlp_sums = lax.all_gather(mlp_sums, ("seq", "dp"), axis=0, tiled=True)
-    mlp_sums = mlp_sums.astype(f32).reshape(size, codes, -1)
-    inner_up_grad, outer_down_grad, inner_down_grad, outer_up_grad = jnp.split(mlp_sums, ends, axis=2)
-    inner_up_grad = inner_up_grad.reshape(size, codes, copies, 2, share).transpose(1, 3, 2, 0, 4)
-    inner_up_grad = inner_up_grad.reshape(adapters, rank, -1)
-    outer_down_grad = outer_down_grad.reshape(size, codes, copies, share).transpose(1, 2, 0, 3)
-    outer_down_grad = outer_down_grad.reshape(adapters, rank, -1).transpose(0, 2, 1)
-    inner_down_grad = jnp.sum(inner_down_grad, 0).reshape(adapters, rank, width).transpose(0, 2, 1)
-    outer_up_grad = jnp.sum(outer_up_grad, 0).reshape(adapters, rank, width)
+    if copies == 1 and share % 128 == 0:
+        inner_up_grad, outer_down_grad, inner_down_grad, outer_up_grad = unpack_sums(
+            mlp_sums.reshape(size, adapters, rank, -1), share, width
+        )
+    else:
+        mlp_sums = mlp_sums.astype(f32).reshape(size, codes, -1)
+        inner_up_grad, outer_down_grad, inner_down_grad, outer_up_grad = jnp.split(mlp_sums, ends, axis=2)
+        inner_up_grad = inner_up_grad.reshape(size, codes, copies, 2, share).transpose(1, 3, 2, 0, 4)
+        inner_up_grad = inner_up_grad.reshape(adapters, rank, -1)
+        outer_down_grad = outer_down_grad.reshape(size, codes, copies, share).transpose(1, 2, 0, 3)
+        outer_down_grad = outer_down_grad.reshape(adapters, rank, -1)
+        inner_down_grad = jnp.sum(inner_down_grad, 0).reshape(adapters, rank, width)
+        outer_up_grad = jnp.sum(outer_up_grad, 0).reshape(adapters, rank, width)
 
     normed_mlp_grad = row_total + nt(mlp_logit_grad.astype(bf16), mlp_router_weight)
     middle_grad = norm_back(middle, middle_scale, mlp_gain, normed_mlp_grad)
@@ -573,6 +789,7 @@
     branch_rows = send_full(tn(place_any, middle_low).astype(bf16), experts, copies)
     head_parts = nt(branch_rows.reshape(-1, width), output_full).astype(bf16)
     head_home = home_join(head_parts.reshape(holders, capacity, -1), experts, copies)
+    head_home = after(head_home, mlp_own, *down_sent)
     gate_grad = jnp.sum(middle_grad[None] * branch, axis=2).T
     logit_grad = gate_back(gates, hits, gate_grad)
     gate_column = gates.T.reshape(-1, 1)
@@ -583,7 +800,27 @@
     output_low_sum = (output_low.astype(f32) * gate_column).reshape(2, rows, rank).sum(0)
     output_upper_grad = tn(output_low_sum.astype(bf16), middle_low)
 
-    pair_parts, query_slots, query_sum = attend_back(
+    def over_sequences(arrays):
+        joined = [a.reshape(rank, size, -1) for a in arrays]
+        ends = [sum(a.shape[2] for a in joined[: k + 1]) for k in range(len(arrays) - 1)]
+        joined = jnp.concatenate(joined, axis=2).transpose(1, 0, 2)
+        mine = picked(joined, spot)
+        for d in range(1, size):
+            theirs = picked(joined, (spot + d) % size).astype(bf16)
+            mine = mine + shifted(theirs, -d % size, size).astype(f32)
+        every = lax.all_gather(mine.astype(bf16), ("seq", "dp"), axis=0, tiled=False)
+        every = every.reshape(size, holders, rank, -1).astype(f32)
+        chosen = (adapter_all[:, None] == jnp.arange(adapters)[None, :]).astype(f32)
+        made = []
+        for part in jnp.split(every, ends, axis=3):
+            part = part.transpose(1, 2, 0, 3)
+            total = sum(
+                part[k][None] * chosen[k][:, None, None, None] for k in range(holders)
+            )
+            made.append(total.reshape(adapters, rank, -1))
+        return made
+
+    key_grad, value_grad, query_slots, query_sum = attend_back(
         query_rot,
         pairs,
         bias,
@@ -599,42 +836,27 @@
         sine_all,
     )
     query_back = send_cut(query_slots, experts, copies)
-    pair_grad = lax.psum_scatter(pair_parts, "seq", scatter_dimension=1, tiled=True)
-    input_parts = nt(query_back.reshape(holders * capacity, -1), query_full).astype(bf16)
-    input_home = home_add(input_parts.reshape(holders, capacity, width), experts, copies)
+    half = key_grad.shape[1]
+    pair_low_grad = nt(key_grad, pair_up[:, :half]) + nt(value_grad, pair_up[:, half:])
+    pair_low_grad = pair_low_grad.astype(bf16)
+    normed_grad = None
+    for d in range(size - 1, -1, -1):
+        block = slice(d * rows, (d + 1) * rows)
+        back = nt(key_grad[block], pair_weight[:, :half]) + nt(value_grad[block], pair_weight[:, half:])
+        back = back + nn(pair_low_grad[block], pair_down)
+        if d:
+            back = shifted(back.astype(bf16), -d % size, size).astype(f32)
+        normed_grad = back if normed_grad is None else normed_grad + back
+    pair_upper_grad = jnp.concatenate([tn(pair_low, key_grad), tn(pair_low, value_grad)], axis=1)
+    pair_lower_grad = sum(
+        tn(pair_low_grad[d * rows : (d + 1) * rows], normed_parts[d]) for d in range(size)
+    )
     query_low_grad = nt(query_sum, query_upper).astype(bf16)
     query_upper_grad = tn(query_low, query_sum)
     query_lower_grad = tn(query_low_grad, normed)
-    normed_grad = nn(place_any, input_home) + nn(query_low_grad, query_lower)
-    normed_grad = normed_grad + nt(logit_grad.astype(bf16), router_weight)
-    key_grad, value_grad = pair_grad[0], pair_grad[1]
-    half = key_grad.shape[1]
-    pair_low_grad = nt(key_grad, pair_up[:, :half]) + nt(value_grad, pair_up[:, half:])
-    pair_low_grad = pair_low_grad.astype(bf16)
-    pair_upper_grad = jnp.concatenate([tn(pair_low, key_grad), tn(pair_low, value_grad)], axis=1)
-    pair_lower_grad = tn(pair_low_grad, normed)
-    normed_grad = normed_grad + nt(key_grad, pair_weight[:, :half])
-    normed_grad = normed_grad + nt(value_grad, pair_weight[:, half:])
-    normed_grad = normed_grad + nn(pair_low_grad, pair_down)
-    input_grad = norm_back(inputs, input_scale, norm_gain, normed_grad) + middle_grad
-
-    def over_sequences(arrays):
-        ends = [sum(a.shape[1] for a in arrays[: k + 1]) for k in range(len(arrays) - 1)]
-        joined = jnp.concatenate(arrays, axis=1)
-        joined = joined.reshape(rank, size, -1).transpose(1, 0, 2)
-        mine = lax.psum_scatter(joined, "seq", scatter_dimension=0, tiled=True)
-        every = lax.all_gather(mine[0].astype(bf16), ("seq", "dp"), axis=0, tiled=False)
-        every = every.reshape(size, holders, rank, -1).astype(f32)
-        chosen = (adapter_all[:, None] == jnp.arange(adapters)[None, :]).astype(f32)
-        total = sum(
-            every[:, k, None] * chosen[k][None, :, None, None] for k in range(holders)
-        )
-        total = total.transpose(1, 2, 0, 3).reshape(adapters, rank, -1)
-        return jnp.split(total, ends, axis=2)
-
     late = over_sequences(
         [
-            pair_lower_grad,
+            after(pair_lower_grad, mlp_sums),
             pair_upper_grad,
             query_lower_grad,
             query_upper_grad,
@@ -642,18 +864,33 @@
             output_upper_grad,
         ]
     )
+    input_parts = nt(query_back.reshape(holders * capacity, -1), query_full).astype(bf16)
+    input_home = home_add(input_parts.reshape(holders, capacity, width), experts, copies)
+    normed_grad = normed_grad + nn(place_any, input_home) + nn(query_low_grad, query_lower)
+    normed_grad = normed_grad + nt(logit_grad.astype(bf16), router_weight)
+    input_grad = norm_back(inputs, input_scale, norm_gain, normed_grad) + middle_grad
+
+    down_near = sum(after(down, input_home).astype(f32) for down in down_near)
+    down_near = down_near.astype(bf16).reshape(holders, capacity, width)
+    down_total = nn(combines[0], home_add(down_near, experts, copies))
+    for d, down in down_parts:
+        down = after(down, query_back).reshape(holders, capacity, width)
+        home = home_add(down, experts, copies)
+        down_total = down_total + shifted(nn(combines[d], home).astype(bf16), -d % size, size).astype(f32)
+    result = (middle + down_total).astype(bf16)
+
     return (
         result[None],
         input_grad[None],
-        late[0].transpose(0, 2, 1),
+        flat_down(late[0]),
         late[1],
-        late[2].transpose(0, 2, 1),
+        flat_down(late[2]),
         late[3],
-        late[4].transpose(0, 2, 1),
+        flat_down(late[4]),
         late[5],
-        inner_down_grad,
+        flat_down(inner_down_grad),
         inner_up_grad,
-        outer_down_grad,
+        flat_down(outer_down_grad),
         outer_up_grad,
     )
 

time: 2330 us -> 1870 us (0.80)
  waiting for transfers between devices: 1170 us -> 945 us
  Pallas kernels: 89.9 us -> 265 us
  blocking collectives: 144 us -> 0 us
  matrix products: 462 us -> 349 us
  local copies, waits for them, and re-layouts: 172 us -> 91.9 us
  starting transfers between devices: 189 us -> 130 us
    pallas_call x1 -> x10, Pallas kernels: 11.9 us -> 188 us  [the longest x4 125 us: expert_block(): pl.pallas_call(functools.partial(expert_kernel, size, share), grid_spec=p...]
    reduce_scatter x3 -> x1, waiting for transfers between devices: 169 us -> 0.01 us  [body(): mlp_sums = lax.psum_scatter(mlp_own, 'dp', scatter_dimension=0, tiled=True)]
    dot_general x116 -> x105, matrix products: 462 us -> 349 us  [product(): lax.dot_general(left, right, (((left_dim,), (right_dim,)), ((), ())), pre...]
    all_gather x4, waiting for transfers between devices: 204 us -> 99.7 us  [the longest x1 99.3 us: body(): query_full = lax.all_gather(query_own, 'seq', axis=0, tiled=True)]
    all_to_all x2 -> x0, blocking collectives: 104 us -> none  [exchange(): return lax.all_to_all(buffer, 'dp', split_axis=0, concat_axis=0, tiled=True)]
    ppermute x24 -> x18, waiting for transfers between devices: 399 us -> 498 us  [shifted(): lax.ppermute(array, 'seq', [(k, (k - shift) % size) for k in range(size)])]
    ppermute x24 -> x18, starting transfers between devices: 81.4 us -> 19.7 us  [shifted(): lax.ppermute(array, 'seq', [(k, (k - shift) % size) for k in range(size)])]
    unnamed x1 -> x0, blocking collectives: 40 us -> none
  transfers between devices with their start and end apart: 57 -> 49, of which waited for: 27 -> 28; matrix products, arithmetic and copies ran while one was open for 26% -> 23% of each run, Pallas kernels for 2% -> 14%
where the time goes in v2:
time: 1870 us; the launch traced here: 1860 us
  waiting for transfers between devices  945 us (51%)
  matrix products  349 us (19%)
  Pallas kernels  265 us (14%)
  starting transfers between devices  130 us (7%)
  local copies, waits for them, and re-layouts  91.9 us (5%)
  other arithmetic  56.8 us (3%)
  between operations  19.1 us (1%)
    ppermute x18, waiting for transfers between devices, shifted(): lax.ppermute(array, 'seq', [(k, (k - shift) % size) for k in range(size)])  498 us
    dot_general x105, matrix products, product(): lax.dot_general(left, right, (((left_dim,), (right_dim,)), ((), ())), pre...  349 us
    all_to_all x24, waiting for transfers between devices, exchange(): return lax.all_to_all(buffer, 'dp', split_axis=0, concat_axis=0, tiled=True)  256 us
    pallas_call x4, Pallas kernels, expert_block(): pl.pallas_call(functools.partial(expert_kernel, size, share), grid_spec=p...  125 us
    all_to_all x24, starting transfers between devices, exchange(): return lax.all_to_all(buffer, 'dp', split_axis=0, concat_axis=0, tiled=True)  109 us
    all_gather x1, waiting for transfers between devices, body(): query_full = lax.all_gather(query_own, 'seq', axis=0, tiled=True)  99.3 us
    all_gather x1, waiting for transfers between devices, body(): lax.all_gather(lax.dynamic_slice_in_dim(key_value_weight, holder * piece,...  91.2 us
    pallas_call x1, Pallas kernels, attend_back(): pl.pallas_call(functools.partial(attend_back_kernel, 1.0 / math.sqrt(HD))...  44 us
  transfers between devices with their start and end apart: 49, of which 28 were waited for; matrix products, arithmetic and copies ran while one was open for 23% of the time, Pallas kernels for 14%

profile of v2, /device:TPU:0, one launch (start us, length us, event | category | flops | bytes accessed | tf_op | source)
XLA Modules:
  0.0 1856.3 jit_solution(9961781715745280900)
XLA Ops:
  17.3 5.3 all-to-all-start
  30.7 54.8 %collective-permute-done.2 = bf16[256,4224]{1,0:T(8,128)(2,1)} collective-permute-done((bf16[256,4224]{1,0:T(8,128)(2,1)S(1)}, bf16[256,4224]{1,0:T(8,128)(2,1)}, u32[]{:S(2)}, u32[]{:S(2)}) %collective-permute-start.2) | collective-permute-done | bytes 2162720 | tf_op jit(solution)/shard_map/ppermute | solution.py:290
  85.5 112.5 %collective-permute-done.1 = bf16[256,4224]{1,0:T(8,128)(2,1)} collective-permute-done((bf16[256,4224]{1,0:T(8,128)(2,1)S(1)}, bf16[256,4224]{1,0:T(8,128)(2,1)}, u32[]{:S(2)}, u32[]{:S(2)}) %collective-permute-start.1) | collective-permute-done | bytes 2162720 | tf_op jit(solution)/shard_map/ppermute | solution.py:290
  198.0 91.2 %all-gather.8.cloned.1.call-done.refs_4_ = bf16[2048,4096]{1,0:T(8,128)(2,1)} async-done(((bf16[64,4096]{1,0:T(8,128)(2,1)}), bf16[2048,4096]{1,0:T(8,128)(2,1)}) %all-gather.8.cloned.1.call-update) | async-done | bytes 16777232 | tf_op jit(solution)/shard_map/all_gather | solution.py:593
  304.9 31.6 %all-to-all-done.2 = bf16[8,96,2048]{2,1,0:T(8,128)(2,1)} async-done(((bf16[8,96,2048]{2,1,0:T(8,128)(2,1)}), bf16[8,96,2048]{2,1,0:T(8,128)(2,1)}, u32[]{:S(2)}, u32[]{:S(2)}) %all-to-all-start.2) | async-done | bytes 3145760 | tf_op jit(solution)/shard_map/all_to_all | solution.py:284
  341.0 99.3 %all-gather.10.cloned.1.call-done = bf16[2048,2048]{1,0:T(8,128)(2,1)} async-done(((bf16[512,2048]{1,0:T(8,128)(2,1)}), bf16[2048,2048]{1,0:T(8,128)(2,1)}) %all-gather.10.cloned.1.call-update) | async-done | bytes 8388624 | tf_op jit(solution)/shard_map/all_gather | solution.py:610
  451.1 12.4 convolution_convert_fusion.3
  463.5 25.5 %all-to-all-done.5 = bf16[8,96,2048]{2,1,0:T(8,128)(2,1)} async-done(((bf16[8,96,2048]{2,1,0:T(8,128)(2,1)}), bf16[8,96,2048]{2,1,0:T(8,128)(2,1)}, u32[]{:S(2)}, u32[]{:S(2)}) %all-to-all-start.5) | async-done | bytes 3145760 | tf_op jit(solution)/shard_map/all_to_all | solution.py:284
  506.3 25.0 %all-to-all-done.1 = bf16[8,96,2048]{2,1,0:T(8,128)(2,1)} async-done(((bf16[8,96,2048]{2,1,0:T(8,128)(2,1)}), bf16[8,96,2048]{2,1,0:T(8,128)(2,1)}, u32[]{:S(2)}, u32[]{:S(2)}) %all-to-all-start.1) | async-done | bytes 3145760 | tf_op jit(solution)/shard_map/all_to_all | solution.py:284
  531.3 4.8 all-to-all-start.6
  545.9 31.7 %pairs.1 = (bf16[1024,4096]{1,0:T(8,128)(2,1)}, bf16[1024,16]{1,0:T(8,128)(2,1)S(1)}) custom-call(bf16[256,2048]{1,0:T(8,128)(2,1)S(1)} %fusion.92.refs_0_, bf16[256,2048]{1,0:T(8,128)(2,1)S(1)} %slice.670.refs_1_, bf16[256,2048]{1,0:T(8,128)(2,1)S(1)} %slice.671.refs_2_, bf16[256,2048]{1,0:T(8,128)(2,1)S(1)} %slice.672.refs_3_, ...), custom_call_target="tpu_custom_call" | custom-call | flops 17179869184 | bytes 16777216 | tf_op jit(solution)/shard_map/pairs/pallas_call | solution.py:75
  578.2 33.7 %attend.1 = (bf16[512,2048]{1,0:T(8,128)(2,1)S(1)}, bf16[768,2048]{1,0:T(8,128)(2,1)}, bf16[512,2048]{1,0:T(8,128)(2,1)}, f32[16,512,1]{2,1,0:T(8,128)}) custom-call(bf16[768,2048]{1,0:T(8,128)(2,1)} %bitcast.10.home_ref, bf16[512,768]{1,0:T(8,128)(2,1)S(1)} %fusion.118.place_ref, bf16[256,16]{1,0:T(8,128)(2,1)S(1)} %convolution_convert_fusion.23.low_ref, ...), custom_call_target="tpu_custom_call" | custom-call | flops 4294967296 | bytes 8388608 | tf_op jit(solution)/shard_map/attend/pallas_call | solution.py:146
  617.7 95.5 %collective-permute-done.3.refs_2_ = bf16[512,2816]{1,0:T(8,128)(2,1)} collective-permute-done((bf16[512,2816]{1,0:T(8,128)(2,1)}, bf16[512,2816]{1,0:T(8,128)(2,1)}, u32[]{:S(2)}, u32[]{:S(2)}) %collective-permute-start.3) | collective-permute-done | bytes 2883616 | tf_op jit(solution)/shard_map/ppermute | solution.py:290
  713.2 11.9 convolution_convert_fusion.2
  736.5 31.0 %all-to-all-done.7 = bf16[8,96,2048]{2,1,0:T(8,128)(2,1)} async-done(((bf16[8,96,2048]{2,1,0:T(8,128)(2,1)}), bf16[8,96,2048]{2,1,0:T(8,128)(2,1)}, u32[]{:S(2)}, u32[]{:S(2)}) %all-to-all-start.7) | async-done | bytes 3145760 | tf_op jit(solution)/shard_map/all_to_all | solution.py:284
  784.6 16.6 collective-permute-done.4.refs_1_
  818.4 6.4 squeeze.90
  824.8 7.6 dynamic-slice_reduce_fusion
  843.7 9.8 fusion.6
  855.9 91.5 %collective-permute-done.5.refs_3_ = bf16[512,2816]{1,0:T(8,128)(2,1)} collective-permute-done((bf16[512,2816]{1,0:T(8,128)(2,1)}, bf16[512,2816]{1,0:T(8,128)(2,1)}, u32[]{:S(2)}, u32[]{:S(2)}) %collective-permute-start.5) | collective-permute-done | bytes 2883616 | tf_op jit(solution)/shard_map/ppermute | solution.py:290
  979.6 7.0 fusion.10
  992.6 13.7 all-to-all-done.8
  1010.7 8.6 fusion.8
  1021.4 9.8 fusion.14
  1035.1 13.6 all-to-all-done.12
  1048.6 4.6 all-to-all-start.11
  1070.1 31.1 %experts.4 = (bf16[768,2176]{1,0:T(8,128)(2,1)}, bf16[768,1408]{1,0:T(8,128)(2,1)S(1)}, bf16[768,2816]{1,0:T(8,128)(2,1)}, bf16[768,128]{1,0:T(8,128)(2,1)S(1)}, bf16[768,128]{1,0:T(8,128)(2,1)S(1)}) custom-call(s32[1]{0:T(128)} %bitcast.45.spot_ref, bf16[768,2048]{1,0:T(8,128)(2,1)} %bitcast.48.x_ref, bf16[768,1408]{1,0:T(8,128)(2,1)S(1)} %copy-done.21, ...), custom_call_target="tpu_custom_call" | custom-call | flops 17716740096 | bytes 27262976 | tf_op jit(solution)/shard_map/experts/pallas_call | solution.py:518
  1103.2 4.7 all-to-all-start.10
  1110.5 31.1 %experts.5 = (bf16[768,2176]{1,0:T(8,128)(2,1)}, bf16[768,1408]{1,0:T(8,128)(2,1)S(1)}, bf16[768,2816]{1,0:T(8,128)(2,1)}, bf16[768,128]{1,0:T(8,128)(2,1)S(1)}, bf16[768,128]{1,0:T(8,128)(2,1)S(1)}) custom-call(s32[1]{0:T(128)} %bitcast.45.spot_ref, bf16[768,2048]{1,0:T(8,128)(2,1)} %bitcast.60.x_ref, bf16[768,1408]{1,0:T(8,128)(2,1)S(1)} %copy-done.19, ...), custom_call_target="tpu_custom_call" | custom-call | flops 17716740096 | bytes 27262976 | tf_op jit(solution)/shard_map/experts/pallas_call | solution.py:518
  1144.5 31.4 %experts.6 = (bf16[768,2176]{1,0:T(8,128)(2,1)}, bf16[768,1408]{1,0:T(8,128)(2,1)S(1)}, bf16[768,2816]{1,0:T(8,128)(2,1)}, bf16[768,128]{1,0:T(8,128)(2,1)S(1)}, bf16[768,128]{1,0:T(8,128)(2,1)S(1)}) custom-call(s32[1]{0:T(128)} %bitcast.45.spot_ref, bf16[768,2048]{1,0:T(8,128)(2,1)} %bitcast.62.x_ref, bf16[768,1408]{1,0:T(8,128)(2,1)S(1)} %copy-done.20, ...), custom_call_target="tpu_custom_call" | custom-call | flops 17716740096 | bytes 27262976 | tf_op jit(solution)/shard_map/experts/pallas_call | solution.py:518
  1177.9 4.6 all-to-all-start.13
  1185.2 31.2 %experts.7 = (bf16[768,2176]{1,0:T(8,128)(2,1)}, bf16[768,1408]{1,0:T(8,128)(2,1)S(1)}, bf16[768,2816]{1,0:T(8,128)(2,1)}, bf16[768,128]{1,0:T(8,128)(2,1)S(1)}, bf16[768,128]{1,0:T(8,128)(2,1)S(1)}) custom-call(s32[1]{0:T(128)} %bitcast.45.spot_ref, bf16[768,2048]{1,0:T(8,128)(2,1)} %bitcast.63.x_ref, bf16[768,1408]{1,0:T(8,128)(2,1)S(1)} %copy-done.18, ...), custom_call_target="tpu_custom_call" | custom-call | flops 17716740096 | bytes 27262976 | tf_op jit(solution)/shard_map/experts/pallas_call | solution.py:518
  1258.8 23.9 %all-to-all-done.15 = bf16[8,96,2176]{2,1,0:T(8,128)(2,1)} async-done(((bf16[8,96,2176]{2,1,0:T(8,128)(2,1)}), bf16[8,96,2176]{2,1,0:T(8,128)(2,1)}, u32[]{:S(2)}, u32[]{:S(2)}) %all-to-all-start.15) | async-done | bytes 3342368 | tf_op jit(solution)/shard_map/all_to_all | solution.py:284
  1282.6 5.1 all-to-all-start.16
  1297.0 9.3 add_convert_fusion.4
  1306.3 19.4 %collective-permute-done.6 = bf16[256,2176]{1,0:T(8,128)(2,1)S(1)} collective-permute-done((bf16[256,2176]{1,0:T(8,128)(2,1)S(1)}, bf16[256,2176]{1,0:T(8,128)(2,1)S(1)}, u32[]{:S(2)}, u32[]{:S(2)}) %collective-permute-start.6) | collective-permute-done | bytes 1114144 | tf_op jit(solution)/shard_map/ppermute | solution.py:290
  1327.7 4.6 all-to-all-start.14
  1351.5 26.5 %all-to-all-done.14 = bf16[8,96,2176]{2,1,0:T(8,128)(2,1)} async-done(((bf16[8,96,2176]{2,1,0:T(8,128)(2,1)}), bf16[8,96,2176]{2,1,0:T(8,128)(2,1)}, u32[]{:S(2)}, u32[]{:S(2)}) %all-to-all-start.14) | async-done | bytes 3342368 | tf_op jit(solution)/shard_map/all_to_all | solution.py:284
  1382.7 34.0 %collective-permute-done.9 = bf16[256,2176]{1,0:T(8,128)(2,1)} collective-permute-done((bf16[256,2176]{1,0:T(8,128)(2,1)}, bf16[256,2176]{1,0:T(8,128)(2,1)}, u32[]{:S(2)}, u32[]{:S(2)}) %collective-permute-start.9) | collective-permute-done | bytes 1114144 | tf_op jit(solution)/shard_map/ppermute | solution.py:290
  1432.2 9.9 add_convert_fusion.3
  1446.7 6.4 add_convert_fusion.1
  1453.1 18.6 %all-to-all-done.17 = bf16[8,96,2048]{2,1,0:T(8,128)(2,1)} async-done(((bf16[8,96,2048]{2,1,0:T(8,128)(2,1)}), bf16[8,96,2048]{2,1,0:T(8,128)(2,1)}, u32[]{:S(2)}, u32[]{:S(2)}) %all-to-all-start.17) | async-done | bytes 3145760 | tf_op jit(solution)/shard_map/all_to_all | solution.py:284
  1471.8 11.9 convolution_convert_fusion.1
  1488.2 10.0 add_convert_fusion.2
  1509.0 32.3 %all-to-all-done.18 = bf16[8,96,2048]{2,1,0:T(8,128)(2,1)} async-done(((bf16[8,96,2048]{2,1,0:T(8,128)(2,1)}), bf16[8,96,2048]{2,1,0:T(8,128)(2,1)}, u32[]{:S(2)}, u32[]{:S(2)}) %all-to-all-start.18) | async-done | bytes 3145760 | tf_op jit(solution)/shard_map/all_to_all | solution.py:284
  1546.0 44.0 %attend_back.1 = (bf16[1024,2048]{1,0:T(8,128)(2,1)}, bf16[1024,2048]{1,0:T(8,128)(2,1)}, bf16[768,2048]{1,0:T(8,128)(2,1)}, bf16[256,2048]{1,0:T(8,128)(2,1)S(1)}) custom-call(bf16[512,2048]{1,0:T(8,128)(2,1)} %get-tuple-element.89.query_ref, bf16[1024,4096]{1,0:T(8,128)(2,1)} %get-tuple-element.69.key_ref.value_ref, ...), custom_call_target="tpu_custom_call" | custom-call | flops 10737418240 | bytes 16777216 | tf_op jit(solution)/shard_map/attend_back/pallas_call | solution.py:241
  1590.0 5.0 all-to-all-start.20
  1605.0 5.9 fusion.18
  1610.9 5.7 fusion.59
  1619.8 5.7 fusion.22
  1625.6 7.3 fusion.53
  1632.8 11.9 convolution_convert_fusion
  1657.7 5.0 collective-permute-done.15
  1666.6 25.0 %collective-permute-done.16 = bf16[16,3584]{1,0:T(8,128)(2,1)S(1)} collective-permute-done((bf16[16,3584]{1,0:T(8,128)(2,1)S(1)}, bf16[16,3584]{1,0:T(8,128)(2,1)S(1)}, u32[]{:S(2)}, u32[]{:S(2)}) %collective-permute-start.16) | collective-permute-done | bytes 114720 | tf_op jit(solution)/shard_map/ppermute | solution.py:290
  1696.8 6.3 fusion.20
  1703.2 6.2 fusion.56
  1710.9 5.1 fusion.16
  1716.0 6.7 add_convert_fusion
  1722.6 12.9 all-to-all-done.23
  1740.0 6.7 fusion.62
  1754.0 37.4 %collective-permute-done.13 = bf16[256,2048]{1,0:T(8,128)(2,1)} collective-permute-done((bf16[256,2048]{1,0:T(8,128)(2,1)}, bf16[256,2048]{1,0:T(8,128)(2,1)}, u32[]{:S(2)}, u32[]{:S(2)}) %collective-permute-start.13) | collective-permute-done | bytes 1048608 | tf_op jit(solution)/shard_map/ppermute | solution.py:290
  1796.3 19.5 %unpack.1 = (f32[8,16,11264]{2,1,0:T(8,128)}, f32[8,16,5632]{2,1,0:T(8,128)}, f32[8,16,2048]{2,1,0:T(8,128)}, f32[8,16,2048]{2,1,0:T(8,128)}) custom-call(bf16[4,8,16,8320]{3,2,1,0:T(8,128)(2,1)} %bitcast.646), custom_call_target="tpu_custom_call" | custom-call | tf_op jit(solution)/shard_map/unpack/pallas_call | solution.py:430
  1815.9 5.4 collective-permute-done.11
  1821.3 4.8 fusion.134
  (737 shorter events, 409.2 us)
Async XLA Ops:
  7.2 534.5 %copy-start = (bf16[8,16,4096]{2,1,0:T(8,128)(2,1)S(1)}, bf16[8,16,4096]{2,1,0:T(8,128)(2,1)}, u32[]{:S(2)}) copy-start(bf16[8,16,4096]{2,1,0:T(8,128)(2,1)} %param.37) | copy-start | bytes 3145732
  7.2 282.0 %all-gather.8.cloned.1.call-start = ((), (), s32[]{:S(2)}) async-start(), calls=%async_computation.25 | async-start | bytes 17301504 | tf_op jit(solution)/shard_map/all_gather | solution.py:593
  12.3 528.0 %copy-start.149 = (f32[256]{0:T(256)}, f32[256]{0:T(256)S(1)}, u32[]{:S(2)}) copy-start(f32[256]{0:T(256)S(1)} %add_rsqrt_fusion.1) | copy-start | bytes 3076
  14.6 715.8 %copy-start.2 = (bf16[256,2048]{1,0:T(8,128)(2,1)}, bf16[256,2048]{1,0:T(8,128)(2,1)S(1)}, u32[]{:S(2)}) copy-start(bf16[256,2048]{1,0:T(8,128)(2,1)S(1)} %fusion.92.refs_0_) | copy-start | bytes 3145732
  17.3 180.7 %all-to-all-start = ((bf16[8,96,2048]{2,1,0:T(8,128)(2,1)}), bf16[8,96,2048]{2,1,0:T(8,128)(2,1)}, u32[]{:S(2)}, u32[]{:S(2)}) async-start(bf16[8,96,2048]{2,1,0:T(8,128)(2,1)} %bitcast.635), calls=%async_computation | async-start | bytes 6291456 | tf_op jit(solution)/shard_map/all_to_all | solution.py:284
  22.6 417.7 %all-gather.10.cloned.1.call-start = ((), (), s32[]{:S(2)}) async-start(), calls=%async_computation.26 | async-start | bytes 10485760 | tf_op jit(solution)/shard_map/all_gather | solution.py:610
  22.8 266.5 %copy-start.90 = (s32[1,256,2]{2,1,0:T(8,128)}, s32[1,256,2]{2,1,0:T(8,128)S(1)}, u32[]{:S(2)}) copy-start(s32[1,256,2]{2,1,0:T(8,128)S(1)} %copy.318) | copy-start | bytes 6148
  24.3 61.2 %collective-permute-start.2 = (bf16[256,4224]{1,0:T(8,128)(2,1)S(1)}, bf16[256,4224]{1,0:T(8,128)(2,1)}, u32[]{:S(2)}, u32[]{:S(2)}) collective-permute-start(bf16[256,4224]{1,0:T(8,128)(2,1)S(1)} %fusion.89), channel_id=1, source_target_pairs={{0,8},{8,16},{16,24},{24,0},{1,9},{9,17},{17,25},{25,1},{2,10},{10... | collective-permute-start | bytes 6488072 | tf_op jit(solution)/shard_map/ppermute | solution.py:290
  26.8 171.3 %collective-permute-start.1 = (bf16[256,4224]{1,0:T(8,128)(2,1)S(1)}, bf16[256,4224]{1,0:T(8,128)(2,1)}, u32[]{:S(2)}, u32[]{:S(2)}) collective-permute-start(bf16[256,4224]{1,0:T(8,128)(2,1)S(1)} %fusion.89), channel_id=1, source_target_pairs={{0,16},{8,24},{16,0},{24,8},{1,17},{9,25},{17,1},{25,9},{2,18},{10... | collective-permute-start | bytes 6488072 | tf_op jit(solution)/shard_map/ppermute | solution.py:290
  29.3 168.7 %collective-permute-start = (bf16[256,4224]{1,0:T(8,128)(2,1)S(1)}, bf16[256,4224]{1,0:T(8,128)(2,1)}, u32[]{:S(2)}, u32[]{:S(2)}) collective-permute-start(bf16[256,4224]{1,0:T(8,128)(2,1)S(1)} %fusion.89), channel_id=1, source_target_pairs={{0,24},{8,0},{16,8},{24,16},{1,25},{9,1},{17,9},{25,17},{2,26},{10... | collective-permute-start | bytes 6488072 | tf_op jit(solution)/shard_map/ppermute | solution.py:290
  294.1 42.4 %all-to-all-start.2 = ((bf16[8,96,2048]{2,1,0:T(8,128)(2,1)}), bf16[8,96,2048]{2,1,0:T(8,128)(2,1)}, u32[]{:S(2)}, u32[]{:S(2)}) async-start(bf16[8,96,2048]{2,1,0:T(8,128)(2,1)} %bitcast.639), calls=%async_computation.2 | async-start | bytes 6291456 | tf_op jit(solution)/shard_map/all_to_all | solution.py:284
  336.5 110.1 %all-to-all-start.3 = ((bf16[8,96,2048]{2,1,0:T(8,128)(2,1)}), bf16[8,96,2048]{2,1,0:T(8,128)(2,1)}, u32[]{:S(2)}, u32[]{:S(2)}) async-start(bf16[8,96,2048]{2,1,0:T(8,128)(2,1)} %bitcast.636), calls=%async_computation.3 | async-start | bytes 6291456 | tf_op jit(solution)/shard_map/all_to_all | solution.py:284
  340.9 372.2 %all-gather.12.cloned.1.call-start = ((), (), s32[]{:S(2)}) async-start(), calls=%async_computation.27 | async-start | bytes 10485760 | tf_op jit(solution)/shard_map/all_gather | solution.py:611
  446.6 42.4 %all-to-all-start.5 = ((bf16[8,96,2048]{2,1,0:T(8,128)(2,1)}), bf16[8,96,2048]{2,1,0:T(8,128)(2,1)}, u32[]{:S(2)}, u32[]{:S(2)}) async-start(bf16[8,96,2048]{2,1,0:T(8,128)(2,1)} %bitcast.640), calls=%async_computation.5 | async-start | bytes 6291456 | tf_op jit(solution)/shard_map/all_to_all | solution.py:284
  489.0 42.3 %all-to-all-start.1 = ((bf16[8,96,2048]{2,1,0:T(8,128)(2,1)}), bf16[8,96,2048]{2,1,0:T(8,128)(2,1)}, u32[]{:S(2)}, u32[]{:S(2)}) async-start(bf16[8,96,2048]{2,1,0:T(8,128)(2,1)} %bitcast.673), calls=%async_computation.1 | async-start | bytes 6291456 | tf_op jit(solution)/shard_map/all_to_all | solution.py:284
  531.3 81.9 %all-to-all-start.6 = ((bf16[8,96,2048]{2,1,0:T(8,128)(2,1)}), bf16[8,96,2048]{2,1,0:T(8,128)(2,1)}, u32[]{:S(2)}, u32[]{:S(2)}) async-start(bf16[8,96,2048]{2,1,0:T(8,128)(2,1)} %bitcast.632), calls=%async_computation.6 | async-start | bytes 6291456 | tf_op jit(solution)/shard_map/all_to_all | solution.py:284
  577.5 135.6 %collective-permute-start.3 = (bf16[512,2816]{1,0:T(8,128)(2,1)}, bf16[512,2816]{1,0:T(8,128)(2,1)}, u32[]{:S(2)}, u32[]{:S(2)}) collective-permute-start(bf16[512,2816]{1,0:T(8,128)(2,1)} %cut.4), channel_id=1, source_target_pairs={{0,16},{8,24},{16,0},{24,8},{1,17},{9,25},{17,1},{25,9},{2,18},{10... | collective-permute-start | bytes 8650760 | tf_op jit(solution)/shard_map/ppermute | solution.py:290
  613.2 99.9 %all-to-all-start.4 = ((bf16[8,96,2048]{2,1,0:T(8,128)(2,1)}), bf16[8,96,2048]{2,1,0:T(8,128)(2,1)}, u32[]{:S(2)}, u32[]{:S(2)}) async-start(bf16[8,96,2048]{2,1,0:T(8,128)(2,1)} %bitcast.677), calls=%async_computation.4 | async-start | bytes 6291456 | tf_op jit(solution)/shard_map/all_to_all | solution.py:284
  725.0 42.5 %all-to-all-start.7 = ((bf16[8,96,2048]{2,1,0:T(8,128)(2,1)}), bf16[8,96,2048]{2,1,0:T(8,128)(2,1)}, u32[]{:S(2)}, u32[]{:S(2)}) async-start(bf16[8,96,2048]{2,1,0:T(8,128)(2,1)} %bitcast.674), calls=%async_computation.7 | async-start | bytes 6291456 | tf_op jit(solution)/shard_map/all_to_all | solution.py:284
  729.6 218.2 %all-gather.14.cloned.1.call-start = ((), (), s32[]{:S(2)}) async-start(), calls=%async_computation.28 | async-start | bytes 5570560 | tf_op jit(solution)/shard_map/all_gather | solution.py:678
  730.8 82.8 %copy-start.107 = (f32[256,2]{0,1:T(2,128)}, f32[256,2]{0,1:T(2,128)S(1)}, u32[]{:S(2)}) copy-start(f32[256,2]{0,1:T(2,128)S(1)} %select_reduce_fusion.3) | copy-start | bytes 6148
  730.8 82.8 %copy-start.118 = (f32[256]{0:T(256)}, f32[256]{0:T(256)S(1)}, u32[]{:S(2)}) copy-start(f32[256]{0:T(256)S(1)} %reduce_max.18) | copy-start | bytes 3076
  736.3 65.0 %collective-permute-start.4 = (bf16[512,2816]{1,0:T(8,128)(2,1)}, bf16[512,2816]{1,0:T(8,128)(2,1)}, u32[]{:S(2)}, u32[]{:S(2)}) collective-permute-start(bf16[512,2816]{1,0:T(8,128)(2,1)} %cut.5), channel_id=1, source_target_pairs={{0,24},{8,0},{16,8},{24,16},{1,25},{9,1},{17,9},{25,17},{2,26},{10... | collective-permute-start | bytes 8650760 | tf_op jit(solution)/shard_map/ppermute | solution.py:290
  801.9 36.6 %all-to-all-start.9 = ((s32[8,1,128]{2,1,0:T(1,128)}), s32[8,1,128]{2,1,0:T(1,128)}, u32[]{:S(2)}, u32[]{:S(2)}) async-start(s32[8,1,128]{2,1,0:T(1,128)} %broadcast_in_dim.27), calls=%async_computation.9 | async-start | bytes 8192 | tf_op jit(solution)/shard_map/all_to_all | solution.py:284
  818.1 129.3 %collective-permute-start.5 = (bf16[512,2816]{1,0:T(8,128)(2,1)}, bf16[512,2816]{1,0:T(8,128)(2,1)}, u32[]{:S(2)}, u32[]{:S(2)}) collective-permute-start(bf16[512,2816]{1,0:T(8,128)(2,1)} %cut.6), channel_id=1, source_target_pairs={{0,8},{8,16},{16,24},{24,0},{1,9},{9,17},{17,25},{25,1},{2,10},{10... | collective-permute-start | bytes 8650760 | tf_op jit(solution)/shard_map/ppermute | solution.py:290
  834.6 221.7 %copy-start.55 = (bf16[128,1,1408]{2,0,1:T(8,128)(2,1)}, bf16[128,1,1408]{2,0,1:T(8,128)(2,1)S(1)}, u32[]{:S(2)}) copy-start(bf16[128,1,1408]{2,0,1:T(8,128)(2,1)S(1)} %copy.365) | copy-start | bytes 1081348
  843.7 107.0 %copy-start.139 = (s32[512]{0:T(512)S(1)}, s32[512]{0:T(512)}, u32[]{:S(2)}) copy-start(s32[512]{0:T(512)} %copy-done.138) | copy-start | bytes 6148
  853.5 98.5 %copy-start.136 = (s32[512]{0:T(512)S(1)}, s32[512]{0:T(512)}, u32[]{:S(2)}) copy-start(s32[512]{0:T(512)} %copy-done.135) | copy-start | bytes 6148
  853.5 99.8 %copy-start.142 = (s32[512]{0:T(512)S(1)}, s32[512]{0:T(512)}, u32[]{:S(2)}) copy-start(s32[512]{0:T(512)} %copy-done.141) | copy-start | bytes 6148
  955.1 8.8 all-to-all-start.19
  963.9 42.4 %all-to-all-start.8 = ((bf16[8,96,2048]{2,1,0:T(8,128)(2,1)}), bf16[8,96,2048]{2,1,0:T(8,128)(2,1)}, u32[]{:S(2)}, u32[]{:S(2)}) async-start(bf16[8,96,2048]{2,1,0:T(8,128)(2,1)} %bitcast.637), calls=%async_computation.8 | async-start | bytes 6291456 | tf_op jit(solution)/shard_map/all_to_all | solution.py:284
  1006.3 42.3 %all-to-all-start.12 = ((bf16[8,96,2048]{2,1,0:T(8,128)(2,1)}), bf16[8,96,2048]{2,1,0:T(8,128)(2,1)}, u32[]{:S(2)}, u32[]{:S(2)}) async-start(bf16[8,96,2048]{2,1,0:T(8,128)(2,1)} %bitcast.638), calls=%async_computation.12 | async-start | bytes 6291456 | tf_op jit(solution)/shard_map/all_to_all | solution.py:284
  1048.6 53.9 %all-to-all-start.11 = ((bf16[8,96,2048]{2,1,0:T(8,128)(2,1)}), bf16[8,96,2048]{2,1,0:T(8,128)(2,1)}, u32[]{:S(2)}, u32[]{:S(2)}) async-start(bf16[8,96,2048]{2,1,0:T(8,128)(2,1)} %bitcast.634), calls=%async_computation.11 | async-start | bytes 6291456 | tf_op jit(solution)/shard_map/all_to_all | solution.py:284
  1103.2 74.0 %all-to-all-start.10 = ((bf16[8,96,2048]{2,1,0:T(8,128)(2,1)}), bf16[8,96,2048]{2,1,0:T(8,128)(2,1)}, u32[]{:S(2)}, u32[]{:S(2)}) async-start(bf16[8,96,2048]{2,1,0:T(8,128)(2,1)} %bitcast.633), calls=%async_computation.10 | async-start | bytes 6291456 | tf_op jit(solution)/shard_map/all_to_all | solution.py:284
  1177.9 60.1 %all-to-all-start.13 = ((bf16[8,96,2176]{2,1,0:T(8,128)(2,1)}), bf16[8,96,2176]{2,1,0:T(8,128)(2,1)}, u32[]{:S(2)}, u32[]{:S(2)}) async-start(bf16[8,96,2176]{2,1,0:T(8,128)(2,1)} %bitcast.670), calls=%async_computation.13 | async-start | bytes 6684672 | tf_op jit(solution)/shard_map/all_to_all | solution.py:284
  1238.0 44.6 %all-to-all-start.15 = ((bf16[8,96,2176]{2,1,0:T(8,128)(2,1)}), bf16[8,96,2176]{2,1,0:T(8,128)(2,1)}, u32[]{:S(2)}, u32[]{:S(2)}) async-start(bf16[8,96,2176]{2,1,0:T(8,128)(2,1)} %bitcast.669), calls=%async_computation.15 | async-start | bytes 6684672 | tf_op jit(solution)/shard_map/all_to_all | solution.py:284
  1282.6 45.1 %all-to-all-start.16 = ((bf16[8,96,2176]{2,1,0:T(8,128)(2,1)}), bf16[8,96,2176]{2,1,0:T(8,128)(2,1)}, u32[]{:S(2)}, u32[]{:S(2)}) async-start(bf16[8,96,2176]{2,1,0:T(8,128)(2,1)} %bitcast.668), calls=%async_computation.16 | async-start | bytes 6684672 | tf_op jit(solution)/shard_map/all_to_all | solution.py:284
  1296.9 28.8 %collective-permute-start.6 = (bf16[256,2176]{1,0:T(8,128)(2,1)S(1)}, bf16[256,2176]{1,0:T(8,128)(2,1)S(1)}, u32[]{:S(2)}, u32[]{:S(2)}) collective-permute-start(bf16[256,2176]{1,0:T(8,128)(2,1)S(1)} %pad_maximum_fusion.1), channel_id=1, source_target_pairs={{0,8},{8,16},{16,24},{24,0},{1,9},{9,17},{17,25},{25,1},{2,10},{10... | collective-permute-start | bytes 3342344 | tf_op jit(solution)/shard_map/ppermute | solution.py:290
  1327.7 50.3 %all-to-all-start.14 = ((bf16[8,96,2176]{2,1,0:T(8,128)(2,1)}), bf16[8,96,2176]{2,1,0:T(8,128)(2,1)}, u32[]{:S(2)}, u32[]{:S(2)}) async-start(bf16[8,96,2176]{2,1,0:T(8,128)(2,1)} %bitcast.667), calls=%async_computation.14 | async-start | bytes 6684672 | tf_op jit(solution)/shard_map/all_to_all | solution.py:284
  1332.4 109.7 %reduce-scatter.2.cloned.1.call-start = ((), (), s32[]{:S(2)}) async-start(), calls=%async_computation.29 | async-start | bytes 2396160 | tf_op jit(solution)/shard_map/reduce_scatter | solution.py:769
  1342.6 40.1 %collective-permute-start.8 = (bf16[256,2176]{1,0:T(8,128)(2,1)}, bf16[256,2176]{1,0:T(8,128)(2,1)}, u32[]{:S(2)}, u32[]{:S(2)}) collective-permute-start(bf16[256,2176]{1,0:T(8,128)(2,1)} %pad_maximum_fusion.2), channel_id=1, source_target_pairs={{0,24},{8,0},{16,8},{24,16},{1,25},{9,1},{17,9},{25,17},{2,26},{10... | collective-permute-start | bytes 3342344 | tf_op jit(solution)/shard_map/ppermute | solution.py:290
  1347.6 69.1 %collective-permute-start.9 = (bf16[256,2176]{1,0:T(8,128)(2,1)}, bf16[256,2176]{1,0:T(8,128)(2,1)}, u32[]{:S(2)}, u32[]{:S(2)}) collective-permute-start(bf16[256,2176]{1,0:T(8,128)(2,1)} %pad_maximum_fusion.3), channel_id=1, source_target_pairs={{0,16},{8,24},{16,0},{24,8},{1,17},{9,25},{17,1},{25,9},{2,18},{10... | collective-permute-start | bytes 3342344 | tf_op jit(solution)/shard_map/ppermute | solution.py:290
  1427.5 44.2 %all-to-all-start.17 = ((bf16[8,96,2048]{2,1,0:T(8,128)(2,1)}), bf16[8,96,2048]{2,1,0:T(8,128)(2,1)}, u32[]{:S(2)}, u32[]{:S(2)}) async-start(bf16[8,96,2048]{2,1,0:T(8,128)(2,1)} %bitcast.641), calls=%async_computation.17 | async-start | bytes 6291456 | tf_op jit(solution)/shard_map/all_to_all | solution.py:284
  1432.0 217.5 %all-gather.16.cloned.1.call-start = ((), (), s32[]{:S(2)}) async-start(), calls=%async_computation.30 | async-start | bytes 8785920 | tf_op jit(solution)/shard_map/all_gather | solution.py:770
  1483.7 57.6 %all-to-all-start.18 = ((bf16[8,96,2048]{2,1,0:T(8,128)(2,1)}), bf16[8,96,2048]{2,1,0:T(8,128)(2,1)}, u32[]{:S(2)}, u32[]{:S(2)}) async-start(bf16[8,96,2048]{2,1,0:T(8,128)(2,1)} %bitcast.676), calls=%async_computation.18 | async-start | bytes 6291456 | tf_op jit(solution)/shard_map/all_to_all | solution.py:284
  1498.9 42.4 %copy-start.16 = (f32[256,1024]{1,0:T(8,128)S(1)}, f32[256,1024]{1,0:T(8,128)}, u32[]{:S(2)}) copy-start(f32[256,1024]{1,0:T(8,128)} %or_select_fusion.bias_ref) | copy-start | bytes 3145732
  1502.3 213.6 %collective-permute-start.7 = (bf16[768,2048]{1,0:T(8,128)(2,1)}, bf16[768,2048]{1,0:T(8,128)(2,1)}, u32[]{:S(2)}, u32[]{:S(2)}) collective-permute-start(bf16[768,2048]{1,0:T(8,128)(2,1)} %add_convert_fusion.4), channel_id=1, source_target_pairs={{0,8},{8,16},{16,24},{24,0},{1,9},{9,17},{17,25},{25,1},{2,10},{10... | collective-permute-start | bytes 9437192 | tf_op jit(solution)/shard_map/ppermute | solution.py:290
  1503.3 212.6 %collective-permute-start.10 = (bf16[768,2048]{1,0:T(8,128)(2,1)}, bf16[768,2048]{1,0:T(8,128)(2,1)}, u32[]{:S(2)}, u32[]{:S(2)}) collective-permute-start(bf16[768,2048]{1,0:T(8,128)(2,1)} %add_convert_fusion.3), channel_id=1, source_target_pairs={{0,24},{8,0},{16,8},{24,16},{1,25},{9,1},{17,9},{25,17},{2,26},{10... | collective-permute-start | bytes 9437192 | tf_op jit(solution)/shard_map/ppermute | solution.py:290
  1590.0 42.8 %all-to-all-start.20 = ((bf16[8,96,2048]{2,1,0:T(8,128)(2,1)}), bf16[8,96,2048]{2,1,0:T(8,128)(2,1)}, u32[]{:S(2)}, u32[]{:S(2)}) async-start(bf16[8,96,2048]{2,1,0:T(8,128)(2,1)} %bitcast.675), calls=%async_computation.20 | async-start | bytes 6291456 | tf_op jit(solution)/shard_map/all_to_all | solution.py:284
  1644.8 47.6 %all-to-all-start.21 = ((bf16[8,96,2048]{2,1,0:T(8,128)(2,1)}), bf16[8,96,2048]{2,1,0:T(8,128)(2,1)}, u32[]{:S(2)}, u32[]{:S(2)}) async-start(bf16[8,96,2048]{2,1,0:T(8,128)(2,1)} %bitcast.672), calls=%async_computation.21 | async-start | bytes 6291456 | tf_op jit(solution)/shard_map/all_to_all | solution.py:284
  1649.4 176.7 %all-gather.18.cloned.1.call-start = ((), (), s32[]{:S(2)}) async-start(), calls=%async_computation.31 | async-start | bytes 3784704 | tf_op jit(solution)/shard_map/all_gather | solution.py:811
  1652.4 10.3 collective-permute-start.15
  1652.7 10.4 collective-permute-start.17
  1656.3 35.3 %collective-permute-start.16 = (bf16[16,3584]{1,0:T(8,128)(2,1)S(1)}, bf16[16,3584]{1,0:T(8,128)(2,1)S(1)}, u32[]{:S(2)}, u32[]{:S(2)}) collective-permute-start(bf16[16,3584]{1,0:T(8,128)(2,1)S(1)} %get-tuple-element.195), channel_id=1, source_target_pairs={{0,16},{8,24},{16,0},{24,8},{1,17},{9,25},{17,1},{25,9},{2,18},{10... | collective-permute-start | bytes 344072 | tf_op jit(solution)/shard_map/ppermute | solution.py:290
  1662.7 91.2 %collective-permute-start.14 = (bf16[256,2048]{1,0:T(8,128)(2,1)S(1)}, bf16[256,2048]{1,0:T(8,128)(2,1)}, u32[]{:S(2)}, u32[]{:S(2)}) collective-permute-start(bf16[256,2048]{1,0:T(8,128)(2,1)S(1)} %copy-done.94), channel_id=1, source_target_pairs={{0,8},{8,16},{16,24},{24,0},{1,9},{9,17},{17,25},{25,1},{2,10},{10... | collective-permute-start | bytes 3145736 | tf_op jit(solution)/shard_map/ppermute | solution.py:290
  1663.1 90.9 %collective-permute-start.12 = (bf16[256,2048]{1,0:T(8,128)(2,1)}, bf16[256,2048]{1,0:T(8,128)(2,1)}, u32[]{:S(2)}, u32[]{:S(2)}) collective-permute-start(bf16[256,2048]{1,0:T(8,128)(2,1)} %fusion.70), channel_id=1, source_target_pairs={{0,24},{8,0},{16,8},{24,16},{1,25},{9,1},{17,9},{25,17},{2,26},{10... | collective-permute-start | bytes 3145736 | tf_op jit(solution)/shard_map/ppermute | solution.py:290
  1692.3 43.2 %all-to-all-start.23 = ((bf16[8,96,2048]{2,1,0:T(8,128)(2,1)}), bf16[8,96,2048]{2,1,0:T(8,128)(2,1)}, u32[]{:S(2)}, u32[]{:S(2)}) async-start(bf16[8,96,2048]{2,1,0:T(8,128)(2,1)} %bitcast.671), calls=%async_computation.23 | async-start | bytes 6291456 | tf_op jit(solution)/shard_map/all_to_all | solution.py:284
  1710.9 80.5 %collective-permute-start.13 = (bf16[256,2048]{1,0:T(8,128)(2,1)}, bf16[256,2048]{1,0:T(8,128)(2,1)}, u32[]{:S(2)}, u32[]{:S(2)}) collective-permute-start(bf16[256,2048]{1,0:T(8,128)(2,1)} %fusion.71), channel_id=1, source_target_pairs={{0,16},{8,24},{16,0},{24,8},{1,17},{9,25},{17,1},{25,9},{2,18},{10... | collective-permute-start | bytes 3145736 | tf_op jit(solution)/shard_map/ppermute | solution.py:290
  1735.5 85.8 %all-to-all-start.22 = ((bf16[8,96,2048]{2,1,0:T(8,128)(2,1)}), bf16[8,96,2048]{2,1,0:T(8,128)(2,1)}, u32[]{:S(2)}, u32[]{:S(2)}) async-start(bf16[8,96,2048]{2,1,0:T(8,128)(2,1)} %bitcast.644), calls=%async_computation.22 | async-start | bytes 6291456 | tf_op jit(solution)/shard_map/all_to_all | solution.py:284
  1750.8 40.6 %copy-start.54 = (bf16[1,256,2048]{2,1,0:T(8,128)(2,1)S(1)}, bf16[1,256,2048]{2,1,0:T(8,128)(2,1)}, u32[]{:S(2)}) copy-start(bf16[1,256,2048]{2,1,0:T(8,128)(2,1)} %param.26) | copy-start | bytes 3145732
  1750.8 70.5 %collective-permute-start.11 = (bf16[256,2048]{1,0:T(8,128)(2,1)S(1)}, bf16[256,2048]{1,0:T(8,128)(2,1)}, u32[]{:S(2)}, u32[]{:S(2)}) collective-permute-start(bf16[256,2048]{1,0:T(8,128)(2,1)S(1)} %convolution_convert_fusion.14), channel_id=1, source_target_pairs={{0,16},{8,24},{16,0},{24,8},{1,17},{9,25},{17,1},{25,9},{2,18},{10... | collective-permute-start | bytes 3145736 | tf_op jit(solution)/shard_map/ppermute | solution.py:290
  1753.9 40.6 %copy-start.154 = (f32[256]{0:T(256)S(1)}, f32[256]{0:T(256)}, u32[]{:S(2)}) copy-start(f32[256]{0:T(256)} %copy-done.153) | copy-start | bytes 3076
  1753.9 40.6 %copy-start.47 = (f32[256,2048]{1,0:T(8,128)S(1)}, f32[256,2048]{1,0:T(8,128)}, u32[]{:S(2)}) copy-start(f32[256,2048]{1,0:T(8,128)} %copy-done.44) | copy-start | bytes 6291460
  1753.9 40.6 %copy-start.150 = (f32[256]{0:T(256)S(1)}, f32[256]{0:T(256)}, u32[]{:S(2)}) copy-start(f32[256]{0:T(256)} %copy-done.149) | copy-start | bytes 3076
  (163 other events, 1147.6 us)
Sparse Core Ops, SparseCore 0:
  11.5 277.7 all-gather.7
  290.8 149.4 all-gather.9
  441.9 215.1 all-gather.11
  801.4 146.3 all-gather.13
  1336.3 48.1 reduce-scatter.1
  1442.2 159.9 all-gather.15
  1692.5 112.2 all-gather.17

commit v3 on v2

--- a/solution.py
+++ b/solution.py
@@ -434,8 +434,44 @@
         out_specs=[pl.BlockSpec((1, rank, n), lambda a, k: (a, 0, 0)) for n in shapes],
         out_shape=[jax.ShapeDtypeStruct((adapters, rank, n), f32) for n in shapes],
         compiler_params=pltpu.CompilerParams(vmem_limit_bytes=vmem_bytes),
+        cost_estimate=pl.CostEstimate(
+            flops=0, bytes_accessed=12 * adapters * rank * (3 * hidden + 2 * width), transcendentals=0
+        ),
         name="unpack",
     )(sums)
+
+
+def gather_adapters_kernel(adapters, ids_ref, in_ref, *out_refs):
+    holders = in_ref.shape[1]
+    start = 0
+    for out_ref in out_refs:
+        columns = out_ref.shape[2]
+        parts = [in_ref[0, k, :, start : start + columns].astype(f32) for k in range(holders)]
+        for a in range(adapters):
+            total = None
+            for k in range(holders):
+                one = jnp.where(ids_ref[k] == a, parts[k], 0.0)
+                total = one if total is None else total + one
+            out_ref[a] = total
+        start += columns
+
+
+def gather_adapters(every, adapter_all, adapters, widths):
+    size, holders, rank, columns = every.shape
+    return pl.pallas_call(
+        functools.partial(gather_adapters_kernel, adapters),
+        grid_spec=pltpu.PrefetchScalarGridSpec(
+            num_scalar_prefetch=1,
+            grid=(size,),
+            in_specs=[pl.BlockSpec((1, holders, rank, columns), lambda k, s: (k, 0, 0, 0))],
+            out_specs=[
+                pl.BlockSpec((adapters, rank, n // size), lambda k, s: (0, 0, k)) for n in widths
+            ],
+        ),
+        out_shape=[jax.ShapeDtypeStruct((adapters, rank, n), f32) for n in widths],
+        compiler_params=pltpu.CompilerParams(vmem_limit_bytes=vmem_bytes),
+        name="gather_adapters",
+    )(adapter_all, every)
 
 
 def silu_parts(gate_part, up_part, hidden_grad):
@@ -589,26 +625,28 @@
     input_scale = norm_scale(inputs)
     normed = (inputs * input_scale * norm_gain).astype(bf16)
 
-    piece = key_value_weight.shape[0] // holders
-    pair_weight = lax.all_gather(
-        lax.dynamic_slice_in_dim(key_value_weight, holder * piece, piece, 0),
-        ("seq", "dp"),
-        axis=0,
-        tiled=True,
-    )
-    lanes = jnp.pad(mlp_routes[0].astype(bf16), ((0, 0), (0, 126)))
-    packet = jnp.concatenate([normed, out_grad[0], lanes], axis=1)
-    early = [packet] + [shifted(packet, d, size) for d in range(1, size)]
-    normed_parts = [normed] + [p[:, :width] for p in early[1:]]
-    grad_parts = [out_grad[0]] + [p[:, width : 2 * width] for p in early[1:]]
-    routes_there = [p[:, 2 * width : 2 * width + 2].astype(jnp.int32) for p in early]
     gates, hits = gate_pair(nn(normed, router_weight), routes[0])
     place = slot_layout(routes[0], experts, capacity)
     place_any = either(place)
     query_rows = send_full(tn(place_any, normed).astype(bf16), experts, copies)
-    query_own = after(query_weight[0], pair_weight, query_rows, *early[1:])
-    query_full = lax.all_gather(query_own, "seq", axis=0, tiled=True)
-    output_full = lax.all_gather(after(output_weight[0], query_full), "seq", axis=0, tiled=True)
+    query_full = lax.all_gather(query_weight[0], "seq", axis=0, tiled=True)
+    normed_parts = [shifted(normed, d, size) for d in range(size)]
+    piece = key_value_weight.shape[0] // holders
+    pair_piece = lax.dynamic_slice_in_dim(key_value_weight, holder * piece, piece, 0)
+    place_mlp = slot_layout(mlp_routes[0], experts, capacity)
+    grad_own = send_full(tn(either(place_mlp), out_grad[0]).astype(bf16), experts, copies)
+    pair_piece = after(
+        pair_piece, query_full, query_rows, grad_own, adapter_all, *normed_parts[1:]
+    )
+    pair_weight = lax.all_gather(pair_piece, ("seq", "dp"), axis=0, tiled=True)
+    lanes = jnp.pad(mlp_routes[0].astype(bf16), ((0, 0), (0, 126)))
+    packet = jnp.concatenate([out_grad[0], lanes], axis=1)
+    packet_late = after(packet, query_full)
+    early = [packet] + [shifted(packet_late, d, size) for d in range(1, size)]
+    output_own = after(output_weight[0], pair_weight, *early[1:])
+    output_full = lax.all_gather(output_own, "seq", axis=0, tiled=True)
+    grad_parts = [out_grad[0]] + [p[:, :width] for p in early[1:]]
+    routes_there = [p[:, width : width + 2].astype(jnp.int32) for p in early]
     outer_full = mlp_out_weight[0]
 
     pair_down, pair_up = picked(flat_down(key_value_down), adapter), picked(key_value_up, adapter)
@@ -633,16 +671,20 @@
     outer_down = lax.dynamic_index_in_dim(outer_down, part, 1, keepdims=False)
     outer_down = lax.dynamic_index_in_dim(outer_down, spot, 1, keepdims=False)
 
-    places = [slot_layout(routes_there[d], experts, capacity) for d in range(size)]
+    places = [place_mlp] + [slot_layout(r, experts, capacity) for r in routes_there[1:]]
     grad_rows, hidden_grads, outer_codes = [], [], []
     for d in range(size):
-        got = send_full(tn(either(places[d]), grad_parts[d]).astype(bf16), experts, copies)
+        if d:
+            got = send_full(tn(either(places[d]), grad_parts[d]).astype(bf16), experts, copies)
+        else:
+            got = grad_own
         got = got.reshape(-1, width)
         code = nt(got, outer_up).astype(bf16) * mask
         grad_rows.append(got)
         outer_codes.append(code)
         hidden_grads.append((nt(got, outer_full) + nn(code, outer_down)).astype(bf16))
 
+    query_rows = after(query_rows, *normed_parts[1:])
     query_parts = nn(query_rows.reshape(-1, width), query_full).astype(bf16)
     query_home = home_join(query_parts.reshape(holders, capacity, -1), experts, copies)
     pairs, pair_low = project_pairs(
@@ -651,8 +693,8 @@
     far = size // 2
     inner_sent = [cut_share(mlp_in_weight[0], (spot - d) % size, size) for d in range(size)]
     inner_parts = list(inner_sent)
-    inner_parts[far] = shifted(after(inner_sent[far], query_full), far, size)
-    query_home = after(query_home, *grad_rows[:2])
+    inner_parts[far] = shifted(after(inner_sent[far], *early[1:]), far, size)
+    query_home = after(query_home, *early[1:], *grad_rows[:2])
     attended, output_slots, query_rot, totals = attend(
         query_home, place, query_low, query_upper, cosine, sine, pairs, bias
     )
@@ -661,7 +703,7 @@
     output_rows = after(output_rows, inner_parts[far], *grad_rows[2:])
     output_parts = nn(output_rows.reshape(holders * capacity, -1), output_full).astype(bf16)
     distances = [d for d in range(1, size) if d != far]
-    for d in distances[:-1]:
+    for d in distances:
         inner_parts[d] = shifted(after(inner_sent[d], output_full), d, size)
     output_home = home_add(output_parts.reshape(holders, capacity, width), experts, copies)
     output_low = nt(attended, output_lower).astype(bf16)
@@ -675,30 +717,28 @@
     lanes = jnp.pad(jnp.concatenate(halves(mlp_gates), axis=1), ((0, 0), (0, 124)))
     packet = jnp.concatenate([normed_mlp, lanes], axis=1)
     packet = after(packet, *(inner_parts[d] for d in distances[:-1]))
-    packet_all = lax.all_gather(packet, "seq", axis=0, tiled=True)
-    for d in distances[-1:]:
-        inner_parts[d] = shifted(after(inner_sent[d], inner_parts[distances[0]]), d, size)
-    packet_all = after(packet_all, *(inner_parts[d] for d in distances[-1:]))
-    packets = [packet] + [
-        lax.dynamic_slice_in_dim(packet_all, (spot + d) % size * rows, rows, 0)
-        for d in range(1, size)
-    ]
+    packets = [shifted(packet, d, size) for d in range(size)]
     gates_there = [
         (p[:, width : width + 2].astype(f32) + p[:, width + 2 : width + 4].astype(f32)).T.reshape(-1, 1)
         for p in packets
     ]
     combines = [either((places[d].astype(f32) * gates_there[d]).astype(bf16)) for d in range(size)]
-    got_rows = [
-        send_full(tn(either(places[d]), packets[d][:, :width]).astype(bf16), experts, copies)
-        for d in range(size)
-    ]
+    order = list(range(1, size)) + [0]
+    got_rows = {}
+    for d in order[-1:] + order[:-1]:
+        rows_there = packets[d][:, :width]
+        if d == order[0]:
+            rows_there = after(rows_there, got_rows[0], *(inner_parts[k] for k in distances[-1:]))
+        elif d:
+            rows_there = after(rows_there, got_rows[d - 1])
+        sent = tn(either(places[d]), rows_there).astype(bf16)
+        got_rows[d] = send_full(sent, experts, copies)
     gate_slots = jnp.stack(
         [jnp.sum(places[d].astype(f32) * gates_there[d], axis=0) for d in range(size)]
     )
     gate_slots = gate_slots.reshape(size, experts, capacity).transpose(1, 0, 2)
     gate_slots = exchange(jnp.repeat(gate_slots, copies, axis=0))
 
-    order = [d for d in range(1, size) if d != far] + ([far] if size > 1 else []) + [0]
     kept, row_total, backs = {}, None, []
     for turn, d in enumerate(order):
         if turn:
@@ -802,23 +842,14 @@
 
     def over_sequences(arrays):
         joined = [a.reshape(rank, size, -1) for a in arrays]
-        ends = [sum(a.shape[2] for a in joined[: k + 1]) for k in range(len(arrays) - 1)]
         joined = jnp.concatenate(joined, axis=2).transpose(1, 0, 2)
         mine = picked(joined, spot)
         for d in range(1, size):
             theirs = picked(joined, (spot + d) % size).astype(bf16)
             mine = mine + shifted(theirs, -d % size, size).astype(f32)
         every = lax.all_gather(mine.astype(bf16), ("seq", "dp"), axis=0, tiled=False)
-        every = every.reshape(size, holders, rank, -1).astype(f32)
-        chosen = (adapter_all[:, None] == jnp.arange(adapters)[None, :]).astype(f32)
-        made = []
-        for part in jnp.split(every, ends, axis=3):
-            part = part.transpose(1, 2, 0, 3)
-            total = sum(
-                part[k][None] * chosen[k][:, None, None, None] for k in range(holders)
-            )
-            made.append(total.reshape(adapters, rank, -1))
-        return made
+        every = every.reshape(size, holders, rank, -1)
+        return gather_adapters(every, adapter_all, adapters, [a.shape[1] for a in arrays])
 
     key_grad, value_grad, query_slots, query_sum = attend_back(
         query_rot,

time: 1870 us -> 1860 us (level)
  starting transfers between devices: 130 us -> 167 us
  waiting for transfers between devices: 945 us -> 919 us
    ppermute x18 -> x24, waiting for transfers between devices: 498 us -> 570 us  [shifted(): lax.ppermute(array, 'seq', [(k, (k - shift) % size) for k in range(size)])]
    all_gather x4 -> x3, waiting for transfers between devices: 191 us -> 122 us  [the longest x1 76.1 us: body(): pair_weight = lax.all_gather(pair_piece, ('seq', 'dp'), axis=0, tiled=True)]
    ppermute x18 -> x24, starting transfers between devices: 19.7 us -> 56 us  [shifted(): lax.ppermute(array, 'seq', [(k, (k - shift) % size) for k in range(size)])]
    all_to_all x24, waiting for transfers between devices: 256 us -> 226 us  [exchange(): return lax.all_to_all(buffer, 'dp', split_axis=0, concat_axis=0, tiled=True)]
    unnamed x424 -> x354, local copies, waits for them, and re-layouts: 40 us -> 31.6 us
  transfers between devices with their start and end apart: 49 -> 54, of which waited for: 28 -> 31; matrix products, arithmetic and copies ran while one was open for 23% -> 23% of each run, Pallas kernels for 14% -> 14%
where the time goes in v3:
time: 1860 us; the launch traced here: 1850 us
  waiting for transfers between devices  919 us (49%)
  matrix products  353 us (19%)
  Pallas kernels  272 us (15%)
  starting transfers between devices  167 us (9%)
  local copies, waits for them, and re-layouts  76.5 us (4%)
  other arithmetic  44.1 us (2%)
    ppermute x24, waiting for transfers between devices, shifted(): lax.ppermute(array, 'seq', [(k, (k - shift) % size) for k in range(size)])  570 us
    dot_general x105, matrix products, product(): lax.dot_general(left, right, (((left_dim,), (right_dim,)), ((), ())), pre...  353 us
    all_to_all x24, waiting for transfers between devices, exchange(): return lax.all_to_all(buffer, 'dp', split_axis=0, concat_axis=0, tiled=True)  226 us
    pallas_call x4, Pallas kernels, expert_block(): pl.pallas_call(functools.partial(expert_kernel, size, share), grid_spec=p...  125 us
    all_to_all x24, starting transfers between devices, exchange(): return lax.all_to_all(buffer, 'dp', split_axis=0, concat_axis=0, tiled=True)  111 us
    all_gather x1, waiting for transfers between devices, body(): pair_weight = lax.all_gather(pair_piece, ('seq', 'dp'), axis=0, tiled=True)  76.1 us
    ppermute x24, starting transfers between devices, shifted(): lax.ppermute(array, 'seq', [(k, (k - shift) % size) for k in range(size)])  56 us
    all_gather x1, waiting for transfers between devices, body(): query_full = lax.all_gather(query_weight[0], 'seq', axis=0, tiled=True)  45.8 us
  transfers between devices with their start and end apart: 54, of which 31 were waited for; matrix products, arithmetic and copies ran while one was open for 23% of the time, Pallas kernels for 14%

profile of v3, /device:TPU:0, one launch (start us, length us, event | category | flops | bytes accessed | tf_op | source)
XLA Modules:
  0.0 1849.9 jit_solution(5023063168512526313)
XLA Ops:
  9.2 5.2 all-to-all-start.4
  31.5 32.4 %all-to-all-done = bf16[8,96,2048]{2,1,0:T(8,128)(2,1)} async-done(((bf16[8,96,2048]{2,1,0:T(8,128)(2,1)}), bf16[8,96,2048]{2,1,0:T(8,128)(2,1)}, u32[]{:S(2)}, u32[]{:S(2)}) %all-to-all-start) | async-done | bytes 3145760 | tf_op jit(solution)/shard_map/all_to_all | solution.py:284
  75.9 42.9 %collective-permute-done.2.refs_3_ = bf16[256,2048]{1,0:T(8,128)(2,1)} collective-permute-done((bf16[256,2048]{1,0:T(8,128)(2,1)S(1)}, bf16[256,2048]{1,0:T(8,128)(2,1)}, u32[]{:S(2)}, u32[]{:S(2)}) %collective-permute-start.2) | collective-permute-done | bytes 1048608 | tf_op jit(solution)/shard_map/ppermute | solution.py:290
  118.8 76.5 %collective-permute-done.1.refs_2_ = bf16[256,2048]{1,0:T(8,128)(2,1)} collective-permute-done((bf16[256,2048]{1,0:T(8,128)(2,1)S(1)}, bf16[256,2048]{1,0:T(8,128)(2,1)}, u32[]{:S(2)}, u32[]{:S(2)}) %collective-permute-start.1) | collective-permute-done | bytes 1048608 | tf_op jit(solution)/shard_map/ppermute | solution.py:290
  195.3 10.4 collective-permute-done.refs_1_
  205.6 45.8 %all-gather.14.cloned.1.call-done = bf16[1,2048,2048]{2,1,0:T(8,128)(2,1)} async-done(((bf16[1,512,2048]{2,1,0:T(8,128)(2,1)}), bf16[1,2048,2048]{2,1,0:T(8,128)(2,1)}) %all-gather.14.cloned.1.call-update) | async-done | bytes 8388624 | tf_op jit(solution)/shard_map/all_gather | solution.py:632
  251.5 11.9 convolution_convert_fusion.3
  273.1 28.8 %collective-permute-done.5 = bf16[256,2176]{1,0:T(8,128)(2,1)S(1)} collective-permute-done((bf16[256,2176]{1,0:T(8,128)(2,1)S(1)}, bf16[256,2176]{1,0:T(8,128)(2,1)S(1)}, u32[]{:S(2)}, u32[]{:S(2)}) %collective-permute-start.5) | collective-permute-done | bytes 1114144 | tf_op jit(solution)/shard_map/ppermute | solution.py:290
  301.9 64.2 %collective-permute-done.4 = bf16[256,2176]{1,0:T(8,128)(2,1)S(1)} collective-permute-done((bf16[256,2176]{1,0:T(8,128)(2,1)S(1)}, bf16[256,2176]{1,0:T(8,128)(2,1)S(1)}, u32[]{:S(2)}, u32[]{:S(2)}) %collective-permute-start.4) | collective-permute-done | bytes 1114144 | tf_op jit(solution)/shard_map/ppermute | solution.py:290
  367.2 76.1 %all-gather.8.cloned.1.call-done.refs_4_ = bf16[2048,4096]{1,0:T(8,128)(2,1)} async-done(((bf16[64,4096]{1,0:T(8,128)(2,1)}), bf16[2048,4096]{1,0:T(8,128)(2,1)}) %all-gather.8.cloned.1.call-update) | async-done | bytes 16777232 | tf_op jit(solution)/shard_map/all_gather | solution.py:641
  460.9 31.1 %all-to-all-done.3 = bf16[8,96,2048]{2,1,0:T(8,128)(2,1)} async-done(((bf16[8,96,2048]{2,1,0:T(8,128)(2,1)}), bf16[8,96,2048]{2,1,0:T(8,128)(2,1)}, u32[]{:S(2)}, u32[]{:S(2)}) %all-to-all-start.3) | async-done | bytes 3145760 | tf_op jit(solution)/shard_map/all_to_all | solution.py:284
  492.1 5.0 all-to-all-start.6
  510.8 24.3 %all-to-all-done.6 = bf16[8,96,2048]{2,1,0:T(8,128)(2,1)} async-done(((bf16[8,96,2048]{2,1,0:T(8,128)(2,1)}), bf16[8,96,2048]{2,1,0:T(8,128)(2,1)}, u32[]{:S(2)}, u32[]{:S(2)}) %all-to-all-start.6) | async-done | bytes 3145760 | tf_op jit(solution)/shard_map/all_to_all | solution.py:284
  544.4 32.6 %pairs.1 = (bf16[1024,4096]{1,0:T(8,128)(2,1)}, bf16[1024,16]{1,0:T(8,128)(2,1)S(1)}) custom-call(bf16[256,2048]{1,0:T(8,128)(2,1)S(1)} %fusion.91.refs_0_, bf16[256,2048]{1,0:T(8,128)(2,1)} %collective-permute-done.refs_1_, bf16[256,2048]{1,0:T(8,128)(2,1)} %collective-permute-done.1.refs_2_, bf16[256,2048]{1,0:T(8,128)(2,1)} %collective-permute-done.2.refs_3_, ...), custom_call_target="tpu_custom_call" | custom-call | flops 17179869184 | bytes 16777216 | tf_op jit(solution)/shard_map/pairs/pallas_call | solution.py:75
  577.0 33.7 %attend.1 = (bf16[512,2048]{1,0:T(8,128)(2,1)S(1)}, bf16[768,2048]{1,0:T(8,128)(2,1)}, bf16[512,2048]{1,0:T(8,128)(2,1)}, f32[16,512,1]{2,1,0:T(8,128)}) custom-call(bf16[768,2048]{1,0:T(8,128)(2,1)} %bitcast.8.home_ref, bf16[512,768]{1,0:T(8,128)(2,1)S(1)} %fusion.117.place_ref, bf16[256,16]{1,0:T(8,128)(2,1)S(1)} %convolution_convert_fusion.23.low_ref, ...), custom_call_target="tpu_custom_call" | custom-call | flops 4294967296 | bytes 8388608 | tf_op jit(solution)/shard_map/attend/pallas_call | solution.py:146
  638.0 6.3 squeeze.95
  644.4 6.8 dynamic-slice_reduce_fusion
  655.9 60.7 %collective-permute-done.6.refs_2_ = bf16[512,2816]{1,0:T(8,128)(2,1)} collective-permute-done((bf16[512,2816]{1,0:T(8,128)(2,1)}, bf16[512,2816]{1,0:T(8,128)(2,1)}, u32[]{:S(2)}, u32[]{:S(2)}) %collective-permute-start.6) | collective-permute-done | bytes 2883616 | tf_op jit(solution)/shard_map/ppermute | solution.py:290
  716.6 12.1 convolution_convert_fusion.2
  733.1 8.6 fusion.6
  743.9 9.9 fusion.8
  756.9 14.1 all-to-all-done.8
  784.4 96.9 %collective-permute-done.7.refs_1_ = bf16[512,2816]{1,0:T(8,128)(2,1)} collective-permute-done((bf16[512,2816]{1,0:T(8,128)(2,1)}, bf16[512,2816]{1,0:T(8,128)(2,1)}, u32[]{:S(2)}, u32[]{:S(2)}) %collective-permute-start.7) | collective-permute-done | bytes 2883616 | tf_op jit(solution)/shard_map/ppermute | solution.py:290
  890.0 9.8 fusion.10
  912.5 16.9 collective-permute-done.10
  931.7 20.9 %collective-permute-done.8 = bf16[256,2176]{1,0:T(8,128)(2,1)} collective-permute-done((bf16[256,2176]{1,0:T(8,128)(2,1)}, bf16[256,2176]{1,0:T(8,128)(2,1)}, u32[]{:S(2)}, u32[]{:S(2)}) %collective-permute-start.8) | collective-permute-done | bytes 1114144 | tf_op jit(solution)/shard_map/ppermute | solution.py:290
  955.1 45.3 %collective-permute-done.11 = bf16[256,2176]{1,0:T(8,128)(2,1)} collective-permute-done((bf16[256,2176]{1,0:T(8,128)(2,1)}, bf16[256,2176]{1,0:T(8,128)(2,1)}, u32[]{:S(2)}, u32[]{:S(2)}) %collective-permute-start.11) | collective-permute-done | bytes 1114144 | tf_op jit(solution)/shard_map/ppermute | solution.py:290
  1030.8 7.0 fusion.14
  1049.4 7.4 all-to-all-done.10
  1068.3 31.0 %experts.4 = (bf16[768,2176]{1,0:T(8,128)(2,1)}, bf16[768,1408]{1,0:T(8,128)(2,1)S(1)}, bf16[768,2816]{1,0:T(8,128)(2,1)}, bf16[768,128]{1,0:T(8,128)(2,1)S(1)}, bf16[768,128]{1,0:T(8,128)(2,1)S(1)}) custom-call(s32[1]{0:T(128)} %bitcast.46.spot_ref, bf16[768,2048]{1,0:T(8,128)(2,1)} %bitcast.50.x_ref, bf16[768,1408]{1,0:T(8,128)(2,1)S(1)} %copy-done.19, ...), custom_call_target="tpu_custom_call" | custom-call | flops 17716740096 | bytes 27262976 | tf_op jit(solution)/shard_map/experts/pallas_call | solution.py:554
  1101.7 9.0 add_convert_fusion.4
  1123.1 31.0 %experts.5 = (bf16[768,2176]{1,0:T(8,128)(2,1)}, bf16[768,1408]{1,0:T(8,128)(2,1)S(1)}, bf16[768,2816]{1,0:T(8,128)(2,1)}, bf16[768,128]{1,0:T(8,128)(2,1)S(1)}, bf16[768,128]{1,0:T(8,128)(2,1)S(1)}) custom-call(s32[1]{0:T(128)} %bitcast.46.spot_ref, bf16[768,2048]{1,0:T(8,128)(2,1)} %bitcast.60.x_ref, bf16[768,1408]{1,0:T(8,128)(2,1)S(1)} %copy-done.18, ...), custom_call_target="tpu_custom_call" | custom-call | flops 17716740096 | bytes 27262976 | tf_op jit(solution)/shard_map/experts/pallas_call | solution.py:554
  1185.5 16.7 all-to-all-done.12
  1209.3 31.1 %experts.6 = (bf16[768,2176]{1,0:T(8,128)(2,1)}, bf16[768,1408]{1,0:T(8,128)(2,1)S(1)}, bf16[768,2816]{1,0:T(8,128)(2,1)}, bf16[768,128]{1,0:T(8,128)(2,1)S(1)}, bf16[768,128]{1,0:T(8,128)(2,1)S(1)}) custom-call(s32[1]{0:T(128)} %bitcast.46.spot_ref, bf16[768,2048]{1,0:T(8,128)(2,1)} %bitcast.62.x_ref, bf16[768,1408]{1,0:T(8,128)(2,1)S(1)} %copy-done.17, ...), custom_call_target="tpu_custom_call" | custom-call | flops 17716740096 | bytes 27262976 | tf_op jit(solution)/shard_map/experts/pallas_call | solution.py:554
  1240.5 31.9 %experts.7 = (bf16[768,2176]{1,0:T(8,128)(2,1)}, bf16[768,1408]{1,0:T(8,128)(2,1)S(1)}, bf16[768,2816]{1,0:T(8,128)(2,1)}, bf16[768,128]{1,0:T(8,128)(2,1)S(1)}, bf16[768,128]{1,0:T(8,128)(2,1)S(1)}) custom-call(s32[1]{0:T(128)} %bitcast.46.spot_ref, bf16[768,2048]{1,0:T(8,128)(2,1)} %bitcast.63.x_ref, bf16[768,1408]{1,0:T(8,128)(2,1)S(1)} %copy-done.16, ...), custom_call_target="tpu_custom_call" | custom-call | flops 17716740096 | bytes 27262976 | tf_op jit(solution)/shard_map/experts/pallas_call | solution.py:554
  1304.8 20.6 %all-to-all-done.16 = bf16[8,96,2176]{2,1,0:T(8,128)(2,1)} async-done(((bf16[8,96,2176]{2,1,0:T(8,128)(2,1)}), bf16[8,96,2176]{2,1,0:T(8,128)(2,1)}, u32[]{:S(2)}, u32[]{:S(2)}) %all-to-all-start.16) | async-done | bytes 3342368 | tf_op jit(solution)/shard_map/all_to_all | solution.py:284
  1340.2 33.7 %all-to-all-done.14 = bf16[8,96,2176]{2,1,0:T(8,128)(2,1)} async-done(((bf16[8,96,2176]{2,1,0:T(8,128)(2,1)}), bf16[8,96,2176]{2,1,0:T(8,128)(2,1)}, u32[]{:S(2)}, u32[]{:S(2)}) %all-to-all-start.14) | async-done | bytes 3342368 | tf_op jit(solution)/shard_map/all_to_all | solution.py:284
  1380.6 8.8 collective-permute-done.15
  1405.6 9.9 add_convert_fusion.3
  1420.2 6.4 add_convert_fusion.1
  1426.6 16.9 all-to-all-done.17
  1443.6 11.9 convolution_convert_fusion.1
  1460.0 10.0 add_convert_fusion.2
  1470.0 17.4 collective-permute-start.13
  1499.5 15.5 all-to-all-done.18
  1518.1 44.1 %attend_back.1 = (bf16[1024,2048]{1,0:T(8,128)(2,1)}, bf16[1024,2048]{1,0:T(8,128)(2,1)}, bf16[768,2048]{1,0:T(8,128)(2,1)}, bf16[256,2048]{1,0:T(8,128)(2,1)S(1)}) custom-call(bf16[512,2048]{1,0:T(8,128)(2,1)} %get-tuple-element.103.query_ref, bf16[1024,4096]{1,0:T(8,128)(2,1)} %get-tuple-element.81.key_ref.value_ref, ...), custom_call_target="tpu_custom_call" | custom-call | flops 10737418240 | bytes 16777216 | tf_op jit(solution)/shard_map/attend_back/pallas_call | solution.py:241
  1577.7 5.7 fusion.18
  1583.4 5.9 fusion.58
  1592.6 5.9 fusion.22
  1598.4 7.5 fusion.52
  1605.9 11.9 convolution_convert_fusion
  1625.5 15.3 collective-permute-start.21
  1644.7 6.7 collective-permute-done.21
  1655.7 25.3 %collective-permute-done.22 = bf16[16,3584]{1,0:T(8,128)(2,1)S(1)} collective-permute-done((bf16[16,3584]{1,0:T(8,128)(2,1)S(1)}, bf16[16,3584]{1,0:T(8,128)(2,1)S(1)}, u32[]{:S(2)}, u32[]{:S(2)}) %collective-permute-start.22) | collective-permute-done | bytes 114720 | tf_op jit(solution)/shard_map/ppermute | solution.py:290
  1686.2 6.3 fusion.20
  1692.6 6.2 fusion.55
  1700.3 5.1 fusion.16
  1705.3 6.6 add_convert_fusion
  1711.9 13.0 all-to-all-done.23
  1729.5 6.6 fusion.61
  1743.4 35.0 %collective-permute-done.19 = bf16[256,2048]{1,0:T(8,128)(2,1)} collective-permute-done((bf16[256,2048]{1,0:T(8,128)(2,1)}, bf16[256,2048]{1,0:T(8,128)(2,1)}, u32[]{:S(2)}, u32[]{:S(2)}) %collective-permute-start.19) | collective-permute-done | bytes 1048608 | tf_op jit(solution)/shard_map/ppermute | solution.py:290
  1783.3 27.4 %collective-permute-done.17 = bf16[256,2048]{1,0:T(8,128)(2,1)} collective-permute-done((bf16[256,2048]{1,0:T(8,128)(2,1)S(1)}, bf16[256,2048]{1,0:T(8,128)(2,1)}, u32[]{:S(2)}, u32[]{:S(2)}) %collective-permute-start.17) | collective-permute-done | bytes 1048608 | tf_op jit(solution)/shard_map/ppermute | solution.py:290
  1815.5 19.3 %unpack.1 = (f32[8,16,11264]{2,1,0:T(8,128)}, f32[8,16,5632]{2,1,0:T(8,128)}, f32[8,16,2048]{2,1,0:T(8,128)}, f32[8,16,2048]{2,1,0:T(8,128)}) custom-call(bf16[4,8,16,8320]{3,2,1,0:T(8,128)(2,1)} %bitcast.432), custom_call_target="tpu_custom_call" | custom-call | bytes 32243712 | tf_op jit(solution)/shard_map/unpack/pallas_call | solution.py:430
  1836.9 6.0 gather_adapters.1
  (661 shorter events, 426.6 us)
Async XLA Ops:
  7.2 537.0 %copy-start = (bf16[8,16,4096]{2,1,0:T(8,128)(2,1)S(1)}, bf16[8,16,4096]{2,1,0:T(8,128)(2,1)}, u32[]{:S(2)}) copy-start(bf16[8,16,4096]{2,1,0:T(8,128)(2,1)} %param.37) | copy-start | bytes 3145732
  7.2 244.3 %all-gather.14.cloned.1.call-start = ((), (), s32[]{:S(2)}) async-start(), calls=%async_computation.29 | async-start | bytes 10485760 | tf_op jit(solution)/shard_map/all_gather | solution.py:632
  9.2 12.1 all-to-all-start.4
  16.8 601.1 %copy-start.142 = (f32[256]{0:T(256)}, f32[256]{0:T(256)S(1)}, u32[]{:S(2)}) copy-start(f32[256]{0:T(256)S(1)} %add_rsqrt_fusion.1) | copy-start | bytes 3076
  21.3 42.6 %all-to-all-start = ((bf16[8,96,2048]{2,1,0:T(8,128)(2,1)}), bf16[8,96,2048]{2,1,0:T(8,128)(2,1)}, u32[]{:S(2)}, u32[]{:S(2)}) async-start(bf16[8,96,2048]{2,1,0:T(8,128)(2,1)} %bitcast.427), calls=%async_computation | async-start | bytes 6291456 | tf_op jit(solution)/shard_map/all_to_all | solution.py:284
  26.1 225.4 %copy-start.97 = (s32[1,256,2]{2,1,0:T(8,128)}, s32[1,256,2]{2,1,0:T(8,128)S(1)}, u32[]{:S(2)}) copy-start(s32[1,256,2]{2,1,0:T(8,128)S(1)} %copy.246) | copy-start | bytes 6148
  26.5 884.7 %copy-start.132 = (s32[512]{0:T(512)}, s32[512]{0:T(512)S(1)}, u32[]{:S(2)}) copy-start(s32[512]{0:T(512)S(1)} %convert_add_fusion.4) | copy-start | bytes 6148
  63.9 141.8 %all-to-all-start.2 = ((bf16[8,96,2048]{2,1,0:T(8,128)(2,1)}), bf16[8,96,2048]{2,1,0:T(8,128)(2,1)}, u32[]{:S(2)}, u32[]{:S(2)}) async-start(bf16[8,96,2048]{2,1,0:T(8,128)(2,1)} %bitcast.422), calls=%async_computation.2 | async-start | bytes 6291456 | tf_op jit(solution)/shard_map/all_to_all | solution.py:284
  68.3 374.9 %all-gather.8.cloned.1.call-start = ((), (), s32[]{:S(2)}) async-start(), calls=%async_computation.25 | async-start | bytes 17301504 | tf_op jit(solution)/shard_map/all_gather | solution.py:641
  68.4 50.4 %collective-permute-start.2 = (bf16[256,2048]{1,0:T(8,128)(2,1)S(1)}, bf16[256,2048]{1,0:T(8,128)(2,1)}, u32[]{:S(2)}, u32[]{:S(2)}) collective-permute-start(bf16[256,2048]{1,0:T(8,128)(2,1)S(1)} %fusion.91.refs_0_), channel_id=1, source_target_pairs={{0,8},{8,16},{16,24},{24,0},{1,9},{9,17},{17,25},{25,1},{2,10},{10... | collective-permute-start | bytes 3145736 | tf_op jit(solution)/shard_map/ppermute | solution.py:290
  70.0 125.3 %collective-permute-start.1 = (bf16[256,2048]{1,0:T(8,128)(2,1)S(1)}, bf16[256,2048]{1,0:T(8,128)(2,1)}, u32[]{:S(2)}, u32[]{:S(2)}) collective-permute-start(bf16[256,2048]{1,0:T(8,128)(2,1)S(1)} %fusion.91.refs_0_), channel_id=1, source_target_pairs={{0,16},{8,24},{16,0},{24,8},{1,17},{9,25},{17,1},{25,9},{2,18},{10... | collective-permute-start | bytes 3145736 | tf_op jit(solution)/shard_map/ppermute | solution.py:290
  72.6 133.0 %collective-permute-start = (bf16[256,2048]{1,0:T(8,128)(2,1)S(1)}, bf16[256,2048]{1,0:T(8,128)(2,1)}, u32[]{:S(2)}, u32[]{:S(2)}) collective-permute-start(bf16[256,2048]{1,0:T(8,128)(2,1)S(1)} %fusion.91.refs_0_), channel_id=1, source_target_pairs={{0,24},{8,0},{16,8},{24,16},{1,25},{9,1},{17,9},{25,17},{2,26},{10... | collective-permute-start | bytes 3145736 | tf_op jit(solution)/shard_map/ppermute | solution.py:290
  75.9 576.9 %copy-start.44 = (s32[8]{0:T(128)}, s32[8]{0:T(128)S(1)}, u32[]{:S(2)}) copy-start(s32[8]{0:T(128)S(1)} %slice_reduce_fusion.4.ids_ref) | copy-start | bytes 100
  263.4 186.1 %all-to-all-start.1 = ((bf16[8,96,2048]{2,1,0:T(8,128)(2,1)}), bf16[8,96,2048]{2,1,0:T(8,128)(2,1)}, u32[]{:S(2)}, u32[]{:S(2)}) async-start(bf16[8,96,2048]{2,1,0:T(8,128)(2,1)} %bitcast.458), calls=%async_computation.1 | async-start | bytes 6291456 | tf_op jit(solution)/shard_map/all_to_all | solution.py:284
  267.8 448.7 %all-gather.10.cloned.1.call-start = ((), (), s32[]{:S(2)}) async-start(), calls=%async_computation.26 | async-start | bytes 10485760 | tf_op jit(solution)/shard_map/all_gather | solution.py:647
  269.2 32.7 %collective-permute-start.5 = (bf16[256,2176]{1,0:T(8,128)(2,1)S(1)}, bf16[256,2176]{1,0:T(8,128)(2,1)S(1)}, u32[]{:S(2)}, u32[]{:S(2)}) collective-permute-start(bf16[256,2176]{1,0:T(8,128)(2,1)S(1)} %fusion.127), channel_id=1, source_target_pairs={{0,8},{8,16},{16,24},{24,0},{1,9},{9,17},{17,25},{25,1},{2,10},{10... | collective-permute-start | bytes 3342344 | tf_op jit(solution)/shard_map/ppermute | solution.py:290
  269.7 96.5 %collective-permute-start.4 = (bf16[256,2176]{1,0:T(8,128)(2,1)S(1)}, bf16[256,2176]{1,0:T(8,128)(2,1)S(1)}, u32[]{:S(2)}, u32[]{:S(2)}) collective-permute-start(bf16[256,2176]{1,0:T(8,128)(2,1)S(1)} %fusion.127), channel_id=1, source_target_pairs={{0,16},{8,24},{16,0},{24,8},{1,17},{9,25},{17,1},{25,9},{2,18},{10... | collective-permute-start | bytes 3342344 | tf_op jit(solution)/shard_map/ppermute | solution.py:290
  270.0 97.1 %collective-permute-start.3 = (bf16[256,2176]{1,0:T(8,128)(2,1)S(1)}, bf16[256,2176]{1,0:T(8,128)(2,1)}, u32[]{:S(2)}, u32[]{:S(2)}) collective-permute-start(bf16[256,2176]{1,0:T(8,128)(2,1)S(1)} %fusion.127), channel_id=1, source_target_pairs={{0,24},{8,0},{16,8},{24,16},{1,25},{9,1},{17,9},{25,17},{2,26},{10... | collective-permute-start | bytes 3342344 | tf_op jit(solution)/shard_map/ppermute | solution.py:290
  449.5 42.6 %all-to-all-start.3 = ((bf16[8,96,2048]{2,1,0:T(8,128)(2,1)}), bf16[8,96,2048]{2,1,0:T(8,128)(2,1)}, u32[]{:S(2)}, u32[]{:S(2)}) async-start(bf16[8,96,2048]{2,1,0:T(8,128)(2,1)} %bitcast.426), calls=%async_computation.3 | async-start | bytes 6291456 | tf_op jit(solution)/shard_map/all_to_all | solution.py:284
  455.9 545.5 %copy-start.134 = (s32[512]{0:T(512)}, s32[512]{0:T(512)S(1)}, u32[]{:S(2)}) copy-start(s32[512]{0:T(512)S(1)} %convert_add_fusion.2) | copy-start | bytes 6148
  492.1 43.0 %all-to-all-start.6 = ((bf16[8,96,2048]{2,1,0:T(8,128)(2,1)}), bf16[8,96,2048]{2,1,0:T(8,128)(2,1)}, u32[]{:S(2)}, u32[]{:S(2)}) async-start(bf16[8,96,2048]{2,1,0:T(8,128)(2,1)} %bitcast.423), calls=%async_computation.6 | async-start | bytes 6291456 | tf_op jit(solution)/shard_map/all_to_all | solution.py:284
  497.6 153.7 %copy-start.118 = (f32[256,2]{0,1:T(2,128)}, f32[256,2]{0,1:T(2,128)S(1)}, u32[]{:S(2)}) copy-start(f32[256,2]{0,1:T(2,128)S(1)} %select_reduce_fusion.3) | copy-start | bytes 6148
  497.6 153.7 %copy-start.128 = (f32[256]{0:T(256)}, f32[256]{0:T(256)S(1)}, u32[]{:S(2)}) copy-start(f32[256]{0:T(256)S(1)} %reduce_max.18) | copy-start | bytes 3076
  505.7 424.7 %copy-start.136 = (s32[512]{0:T(512)}, s32[512]{0:T(512)S(1)}, u32[]{:S(2)}) copy-start(s32[512]{0:T(512)S(1)} %convert_add_fusion.1) | copy-start | bytes 6148
  535.0 77.0 %all-to-all-start.7 = ((bf16[8,96,2048]{2,1,0:T(8,128)(2,1)}), bf16[8,96,2048]{2,1,0:T(8,128)(2,1)}, u32[]{:S(2)}, u32[]{:S(2)}) async-start(bf16[8,96,2048]{2,1,0:T(8,128)(2,1)} %bitcast.421), calls=%async_computation.7 | async-start | bytes 6291456 | tf_op jit(solution)/shard_map/all_to_all | solution.py:284
  544.2 172.3 %collective-permute-start.6 = (bf16[512,2816]{1,0:T(8,128)(2,1)}, bf16[512,2816]{1,0:T(8,128)(2,1)}, u32[]{:S(2)}, u32[]{:S(2)}) collective-permute-start(bf16[512,2816]{1,0:T(8,128)(2,1)} %cut.4), channel_id=1, source_target_pairs={{0,16},{8,24},{16,0},{24,8},{1,17},{9,25},{17,1},{25,9},{2,18},{10... | collective-permute-start | bytes 8650760 | tf_op jit(solution)/shard_map/ppermute | solution.py:290
  612.1 104.5 %all-to-all-start.5 = ((bf16[8,96,2048]{2,1,0:T(8,128)(2,1)}), bf16[8,96,2048]{2,1,0:T(8,128)(2,1)}, u32[]{:S(2)}, u32[]{:S(2)}) async-start(bf16[8,96,2048]{2,1,0:T(8,128)(2,1)} %bitcast.456), calls=%async_computation.5 | async-start | bytes 6291456 | tf_op jit(solution)/shard_map/all_to_all | solution.py:284
  617.0 164.3 %copy-start.138 = (s32[256,2]{0,1:T(2,128)}, s32[256,2]{0,1:T(2,128)S(1)}, u32[]{:S(2)}) copy-start(s32[256,2]{0,1:T(2,128)S(1)} %copy.252) | copy-start | bytes 6148
  728.6 42.4 %all-to-all-start.8 = ((bf16[8,96,2048]{2,1,0:T(8,128)(2,1)}), bf16[8,96,2048]{2,1,0:T(8,128)(2,1)}, u32[]{:S(2)}, u32[]{:S(2)}) async-start(bf16[8,96,2048]{2,1,0:T(8,128)(2,1)} %bitcast.461), calls=%async_computation.8 | async-start | bytes 6291456 | tf_op jit(solution)/shard_map/all_to_all | solution.py:284
  754.5 126.9 %collective-permute-start.7 = (bf16[512,2816]{1,0:T(8,128)(2,1)}, bf16[512,2816]{1,0:T(8,128)(2,1)}, u32[]{:S(2)}, u32[]{:S(2)}) collective-permute-start(bf16[512,2816]{1,0:T(8,128)(2,1)} %cut.5), channel_id=1, source_target_pairs={{0,24},{8,0},{16,8},{24,16},{1,25},{9,1},{17,9},{25,17},{2,26},{10... | collective-permute-start | bytes 8650760 | tf_op jit(solution)/shard_map/ppermute | solution.py:290
  754.7 254.8 %collective-permute-start.9 = (bf16[512,2816]{1,0:T(8,128)(2,1)}, bf16[512,2816]{1,0:T(8,128)(2,1)}, u32[]{:S(2)}, u32[]{:S(2)}) collective-permute-start(bf16[512,2816]{1,0:T(8,128)(2,1)} %cut.6), channel_id=1, source_target_pairs={{0,8},{8,16},{16,24},{24,0},{1,9},{9,17},{17,25},{25,1},{2,10},{10... | collective-permute-start | bytes 8650760 | tf_op jit(solution)/shard_map/ppermute | solution.py:290
  885.5 120.1 %all-to-all-start.9 = ((bf16[8,96,2048]{2,1,0:T(8,128)(2,1)}), bf16[8,96,2048]{2,1,0:T(8,128)(2,1)}, u32[]{:S(2)}, u32[]{:S(2)}) async-start(bf16[8,96,2048]{2,1,0:T(8,128)(2,1)} %bitcast.420), calls=%async_computation.9 | async-start | bytes 6291456 | tf_op jit(solution)/shard_map/all_to_all | solution.py:284
  899.8 29.6 %collective-permute-start.10 = (bf16[256,2176]{1,0:T(8,128)(2,1)}, bf16[256,2176]{1,0:T(8,128)(2,1)}, u32[]{:S(2)}, u32[]{:S(2)}) collective-permute-start(bf16[256,2176]{1,0:T(8,128)(2,1)} %fusion.128), channel_id=1, source_target_pairs={{0,8},{8,16},{16,24},{24,0},{1,9},{9,17},{17,25},{25,1},{2,10},{10... | collective-permute-start | bytes 3342344 | tf_op jit(solution)/shard_map/ppermute | solution.py:290
  902.7 50.0 %collective-permute-start.8 = (bf16[256,2176]{1,0:T(8,128)(2,1)}, bf16[256,2176]{1,0:T(8,128)(2,1)}, u32[]{:S(2)}, u32[]{:S(2)}) collective-permute-start(bf16[256,2176]{1,0:T(8,128)(2,1)} %fusion.128), channel_id=1, source_target_pairs={{0,24},{8,0},{16,8},{24,16},{1,25},{9,1},{17,9},{25,17},{2,26},{10... | collective-permute-start | bytes 3342344 | tf_op jit(solution)/shard_map/ppermute | solution.py:290
  910.1 90.2 %collective-permute-start.11 = (bf16[256,2176]{1,0:T(8,128)(2,1)}, bf16[256,2176]{1,0:T(8,128)(2,1)}, u32[]{:S(2)}, u32[]{:S(2)}) collective-permute-start(bf16[256,2176]{1,0:T(8,128)(2,1)} %fusion.128), channel_id=1, source_target_pairs={{0,16},{8,24},{16,0},{24,8},{1,17},{9,25},{17,1},{25,9},{2,18},{10... | collective-permute-start | bytes 3342344 | tf_op jit(solution)/shard_map/ppermute | solution.py:290
  1005.6 8.6 all-to-all-start.19
  1014.3 42.6 %all-to-all-start.10 = ((bf16[8,96,2048]{2,1,0:T(8,128)(2,1)}), bf16[8,96,2048]{2,1,0:T(8,128)(2,1)}, u32[]{:S(2)}, u32[]{:S(2)}) async-start(bf16[8,96,2048]{2,1,0:T(8,128)(2,1)} %bitcast.424), calls=%async_computation.10 | async-start | bytes 6291456 | tf_op jit(solution)/shard_map/all_to_all | solution.py:284
  1061.0 49.8 %all-to-all-start.11 = ((bf16[8,96,2048]{2,1,0:T(8,128)(2,1)}), bf16[8,96,2048]{2,1,0:T(8,128)(2,1)}, u32[]{:S(2)}, u32[]{:S(2)}) async-start(bf16[8,96,2048]{2,1,0:T(8,128)(2,1)} %bitcast.428), calls=%async_computation.11 | async-start | bytes 6291456 | tf_op jit(solution)/shard_map/all_to_all | solution.py:284
  1110.8 48.9 %all-to-all-start.13 = ((bf16[8,96,2176]{2,1,0:T(8,128)(2,1)}), bf16[8,96,2176]{2,1,0:T(8,128)(2,1)}, u32[]{:S(2)}, u32[]{:S(2)}) async-start(bf16[8,96,2176]{2,1,0:T(8,128)(2,1)} %bitcast.454), calls=%async_computation.13 | async-start | bytes 6684672 | tf_op jit(solution)/shard_map/all_to_all | solution.py:284
  1159.7 42.5 %all-to-all-start.12 = ((bf16[8,96,2048]{2,1,0:T(8,128)(2,1)}), bf16[8,96,2048]{2,1,0:T(8,128)(2,1)}, u32[]{:S(2)}, u32[]{:S(2)}) async-start(bf16[8,96,2048]{2,1,0:T(8,128)(2,1)} %bitcast.425), calls=%async_computation.12 | async-start | bytes 6291456 | tf_op jit(solution)/shard_map/all_to_all | solution.py:284
  1185.5 86.9 %collective-permute-start.12 = (bf16[256,2176]{1,0:T(8,128)(2,1)}, bf16[256,2176]{1,0:T(8,128)(2,1)}, u32[]{:S(2)}, u32[]{:S(2)}) collective-permute-start(bf16[256,2176]{1,0:T(8,128)(2,1)} %pad_maximum_fusion.1), channel_id=1, source_target_pairs={{0,8},{8,16},{16,24},{24,0},{1,9},{9,17},{17,25},{25,1},{2,10},{10... | collective-permute-start | bytes 3342344 | tf_op jit(solution)/shard_map/ppermute | solution.py:290
  1202.2 78.4 %all-to-all-start.15 = ((bf16[8,96,2176]{2,1,0:T(8,128)(2,1)}), bf16[8,96,2176]{2,1,0:T(8,128)(2,1)}, u32[]{:S(2)}, u32[]{:S(2)}) async-start(bf16[8,96,2176]{2,1,0:T(8,128)(2,1)} %bitcast.452), calls=%async_computation.15 | async-start | bytes 6684672 | tf_op jit(solution)/shard_map/all_to_all | solution.py:284
  1280.6 44.8 %all-to-all-start.16 = ((bf16[8,96,2176]{2,1,0:T(8,128)(2,1)}), bf16[8,96,2176]{2,1,0:T(8,128)(2,1)}, u32[]{:S(2)}, u32[]{:S(2)}) async-start(bf16[8,96,2176]{2,1,0:T(8,128)(2,1)} %bitcast.453), calls=%async_computation.16 | async-start | bytes 6684672 | tf_op jit(solution)/shard_map/all_to_all | solution.py:284
  1325.4 48.4 %all-to-all-start.14 = ((bf16[8,96,2176]{2,1,0:T(8,128)(2,1)}), bf16[8,96,2176]{2,1,0:T(8,128)(2,1)}, u32[]{:S(2)}, u32[]{:S(2)}) async-start(bf16[8,96,2176]{2,1,0:T(8,128)(2,1)} %bitcast.451), calls=%async_computation.14 | async-start | bytes 6684672 | tf_op jit(solution)/shard_map/all_to_all | solution.py:284
  1330.0 85.5 %reduce-scatter.2.cloned.1.call-start = ((), (), s32[]{:S(2)}) async-start(), calls=%async_computation.27 | async-start | bytes 2396160 | tf_op jit(solution)/shard_map/reduce_scatter | solution.py:809
  1332.8 47.8 %collective-permute-start.14 = (bf16[256,2176]{1,0:T(8,128)(2,1)}, bf16[256,2176]{1,0:T(8,128)(2,1)}, u32[]{:S(2)}, u32[]{:S(2)}) collective-permute-start(bf16[256,2176]{1,0:T(8,128)(2,1)} %pad_maximum_fusion.2), channel_id=1, source_target_pairs={{0,16},{8,24},{16,0},{24,8},{1,17},{9,25},{17,1},{25,9},{2,18},{10... | collective-permute-start | bytes 3342344 | tf_op jit(solution)/shard_map/ppermute | solution.py:290
  1338.6 50.9 %collective-permute-start.15 = (bf16[256,2176]{1,0:T(8,128)(2,1)}, bf16[256,2176]{1,0:T(8,128)(2,1)}, u32[]{:S(2)}, u32[]{:S(2)}) collective-permute-start(bf16[256,2176]{1,0:T(8,128)(2,1)} %pad_maximum_fusion.3), channel_id=1, source_target_pairs={{0,24},{8,0},{16,8},{24,16},{1,25},{9,1},{17,9},{25,17},{2,26},{10... | collective-permute-start | bytes 3342344 | tf_op jit(solution)/shard_map/ppermute | solution.py:290
  1400.7 42.9 %all-to-all-start.17 = ((bf16[8,96,2048]{2,1,0:T(8,128)(2,1)}), bf16[8,96,2048]{2,1,0:T(8,128)(2,1)}, u32[]{:S(2)}, u32[]{:S(2)}) async-start(bf16[8,96,2048]{2,1,0:T(8,128)(2,1)} %bitcast.429), calls=%async_computation.17 | async-start | bytes 6291456 | tf_op jit(solution)/shard_map/all_to_all | solution.py:284
  1405.6 216.9 %all-gather.12.cloned.1.call-start = ((), (), s32[]{:S(2)}) async-start(), calls=%async_computation.28 | async-start | bytes 8785920 | tf_op jit(solution)/shard_map/all_gather | solution.py:810
  1455.5 59.6 %all-to-all-start.18 = ((bf16[8,96,2048]{2,1,0:T(8,128)(2,1)}), bf16[8,96,2048]{2,1,0:T(8,128)(2,1)}, u32[]{:S(2)}, u32[]{:S(2)}) async-start(bf16[8,96,2048]{2,1,0:T(8,128)(2,1)} %bitcast.460), calls=%async_computation.18 | async-start | bytes 6291456 | tf_op jit(solution)/shard_map/all_to_all | solution.py:284
  1470.0 235.3 %collective-permute-start.13 = (bf16[768,2048]{1,0:T(8,128)(2,1)}, bf16[768,2048]{1,0:T(8,128)(2,1)}, u32[]{:S(2)}, u32[]{:S(2)}) collective-permute-start(bf16[768,2048]{1,0:T(8,128)(2,1)} %add_convert_fusion.4), channel_id=1, source_target_pairs={{0,8},{8,16},{16,24},{24,0},{1,9},{9,17},{17,25},{25,1},{2,10},{10... | collective-permute-start | bytes 9437192 | tf_op jit(solution)/shard_map/ppermute | solution.py:290
  1487.4 218.0 %collective-permute-start.16 = (bf16[768,2048]{1,0:T(8,128)(2,1)}, bf16[768,2048]{1,0:T(8,128)(2,1)}, u32[]{:S(2)}, u32[]{:S(2)}) collective-permute-start(bf16[768,2048]{1,0:T(8,128)(2,1)} %add_convert_fusion.2), channel_id=1, source_target_pairs={{0,24},{8,0},{16,8},{24,16},{1,25},{9,1},{17,9},{25,17},{2,26},{10... | collective-permute-start | bytes 9437192 | tf_op jit(solution)/shard_map/ppermute | solution.py:290
  1563.2 42.7 %all-to-all-start.20 = ((bf16[8,96,2048]{2,1,0:T(8,128)(2,1)}), bf16[8,96,2048]{2,1,0:T(8,128)(2,1)}, u32[]{:S(2)}, u32[]{:S(2)}) async-start(bf16[8,96,2048]{2,1,0:T(8,128)(2,1)} %bitcast.459), calls=%async_computation.20 | async-start | bytes 6291456 | tf_op jit(solution)/shard_map/all_to_all | solution.py:284
  1617.9 63.8 %all-to-all-start.21 = ((bf16[8,96,2048]{2,1,0:T(8,128)(2,1)}), bf16[8,96,2048]{2,1,0:T(8,128)(2,1)}, u32[]{:S(2)}, u32[]{:S(2)}) async-start(bf16[8,96,2048]{2,1,0:T(8,128)(2,1)} %bitcast.457), calls=%async_computation.21 | async-start | bytes 6291456 | tf_op jit(solution)/shard_map/all_to_all | solution.py:284
  1622.5 212.4 %all-gather.16.cloned.1.call-start = ((), (), s32[]{:S(2)}) async-start(), calls=%async_computation.30 | async-start | bytes 3784704 | tf_op jit(solution)/shard_map/all_gather | solution.py:850
  1625.5 25.9 %collective-permute-start.21 = (bf16[16,3584]{1,0:T(8,128)(2,1)S(1)}, bf16[16,3584]{1,0:T(8,128)(2,1)S(1)}, u32[]{:S(2)}, u32[]{:S(2)}) collective-permute-start(bf16[16,3584]{1,0:T(8,128)(2,1)S(1)} %get-tuple-element.155), channel_id=1, source_target_pairs={{0,8},{8,16},{16,24},{24,0},{1,9},{9,17},{17,25},{25,1},{2,10},{10... | collective-permute-start | bytes 344072 | tf_op jit(solution)/shard_map/ppermute | solution.py:290
  1640.8 12.2 collective-permute-start.23
  1642.8 38.2 %collective-permute-start.22 = (bf16[16,3584]{1,0:T(8,128)(2,1)S(1)}, bf16[16,3584]{1,0:T(8,128)(2,1)S(1)}, u32[]{:S(2)}, u32[]{:S(2)}) collective-permute-start(bf16[16,3584]{1,0:T(8,128)(2,1)S(1)} %get-tuple-element.157), channel_id=1, source_target_pairs={{0,16},{8,24},{16,0},{24,8},{1,17},{9,25},{17,1},{25,9},{2,18},{10... | collective-permute-start | bytes 344072 | tf_op jit(solution)/shard_map/ppermute | solution.py:290
  1651.3 92.0 %collective-permute-start.20 = (bf16[256,2048]{1,0:T(8,128)(2,1)}, bf16[256,2048]{1,0:T(8,128)(2,1)}, u32[]{:S(2)}, u32[]{:S(2)}) collective-permute-start(bf16[256,2048]{1,0:T(8,128)(2,1)} %fusion.71), channel_id=1, source_target_pairs={{0,8},{8,16},{16,24},{24,0},{1,9},{9,17},{17,25},{25,1},{2,10},{10... | collective-permute-start | bytes 3145736 | tf_op jit(solution)/shard_map/ppermute | solution.py:290
  1653.0 90.3 %collective-permute-start.18 = (bf16[256,2048]{1,0:T(8,128)(2,1)}, bf16[256,2048]{1,0:T(8,128)(2,1)}, u32[]{:S(2)}, u32[]{:S(2)}) collective-permute-start(bf16[256,2048]{1,0:T(8,128)(2,1)} %fusion.69), channel_id=1, source_target_pairs={{0,24},{8,0},{16,8},{24,16},{1,25},{9,1},{17,9},{25,17},{2,26},{10... | collective-permute-start | bytes 3145736 | tf_op jit(solution)/shard_map/ppermute | solution.py:290
  1681.7 43.2 %all-to-all-start.23 = ((bf16[8,96,2048]{2,1,0:T(8,128)(2,1)}), bf16[8,96,2048]{2,1,0:T(8,128)(2,1)}, u32[]{:S(2)}, u32[]{:S(2)}) async-start(bf16[8,96,2048]{2,1,0:T(8,128)(2,1)} %bitcast.455), calls=%async_computation.23 | async-start | bytes 6291456 | tf_op jit(solution)/shard_map/all_to_all | solution.py:284
  1700.2 78.1 %collective-permute-start.19 = (bf16[256,2048]{1,0:T(8,128)(2,1)}, bf16[256,2048]{1,0:T(8,128)(2,1)}, u32[]{:S(2)}, u32[]{:S(2)}) collective-permute-start(bf16[256,2048]{1,0:T(8,128)(2,1)} %fusion.70), channel_id=1, source_target_pairs={{0,16},{8,24},{16,0},{24,8},{1,17},{9,25},{17,1},{25,9},{2,18},{10... | collective-permute-start | bytes 3145736 | tf_op jit(solution)/shard_map/ppermute | solution.py:290
  1724.9 85.8 %all-to-all-start.22 = ((bf16[8,96,2048]{2,1,0:T(8,128)(2,1)}), bf16[8,96,2048]{2,1,0:T(8,128)(2,1)}, u32[]{:S(2)}, u32[]{:S(2)}) async-start(bf16[8,96,2048]{2,1,0:T(8,128)(2,1)} %bitcast.430), calls=%async_computation.22 | async-start | bytes 6291456 | tf_op jit(solution)/shard_map/all_to_all | solution.py:284
  1740.2 70.5 %collective-permute-start.17 = (bf16[256,2048]{1,0:T(8,128)(2,1)S(1)}, bf16[256,2048]{1,0:T(8,128)(2,1)}, u32[]{:S(2)}, u32[]{:S(2)}) collective-permute-start(bf16[256,2048]{1,0:T(8,128)(2,1)S(1)} %convolution_convert_fusion.14), channel_id=1, source_target_pairs={{0,16},{8,24},{16,0},{24,8},{1,17},{9,25},{17,1},{25,9},{2,18},{10... | collective-permute-start | bytes 3145736 | tf_op jit(solution)/shard_map/ppermute | solution.py:290
  (158 other events, 2043.5 us)
Sparse Core Ops, SparseCore 0:
  9.6 241.8 all-gather.13
  254.9 188.3 all-gather.7
  444.8 232.8 all-gather.9
  1340.3 44.6 reduce-scatter.1
  1415.7 179.1 all-gather.11
  1681.8 113.2 all-gather.15

commit v4 on v3

--- a/solution.py
+++ b/solution.py
@@ -52,7 +52,7 @@
 
     for k in range(count):
         part = pl.ds(k * rows, rows)
-        made = nn(normed_refs[k][...], w_ref[...]) + nn(low_ref[part, :], up_ref[...])
+        made = nn(normed_refs[k][...], w_ref[0]) + nn(low_ref[part, :], up_ref[...])
 
         @pl.when(step < key_blocks)
         def _():
@@ -69,15 +69,15 @@
 def project_pairs(normed_parts, weight, down, upper, cosine, sine):
     count = len(normed_parts)
     rows, width = normed_parts[0].shape
-    columns = weight.shape[1]
-    block = 512
+    blocks, _, block = weight.shape
+    columns = blocks * block
     whole = lambda array: pl.BlockSpec(array.shape, lambda i: (0, 0))
     return pl.pallas_call(
-        functools.partial(pair_kernel, count, columns // 2 // block),
-        grid=(columns // block,),
+        functools.partial(pair_kernel, count, blocks // 2),
+        grid=(blocks,),
         in_specs=[whole(n) for n in normed_parts]
         + [
-            pl.BlockSpec((width, block), lambda i: (0, i)),
+            pl.BlockSpec((1, width, block), lambda i: (i, 0, 0)),
             whole(down),
             pl.BlockSpec((upper.shape[0], block), lambda i: (0, i)),
             whole(cosine),
@@ -99,6 +99,54 @@
         ),
         name="pairs",
     )(*normed_parts, weight, down, upper, cosine, sine)
+
+
+def pair_back_kernel(key_blocks, key_ref, value_ref, w_ref, low_ref, down_ref, out_ref, sum_ref):
+    step = pl.program_id(0)
+
+    @pl.when(step == 0)
+    def _():
+        sum_ref[...] = nn(low_ref[...], down_ref[...])
+
+    @pl.when(step < key_blocks)
+    def _():
+        sum_ref[...] += nt(key_ref[...], w_ref[0])
+
+    @pl.when(step >= key_blocks)
+    def _():
+        sum_ref[...] += nt(value_ref[...], w_ref[0])
+
+    @pl.when(step == pl.num_programs(0) - 1)
+    def _():
+        out_ref[...] = sum_ref[...].astype(bf16)
+
+
+def pair_back(key_grad, value_grad, weight, low_grad, down):
+    blocks, width, block = weight.shape
+    rows = key_grad.shape[0]
+    half = blocks // 2
+    whole = lambda array: pl.BlockSpec(array.shape, lambda i: (0, 0))
+    return pl.pallas_call(
+        functools.partial(pair_back_kernel, half),
+        grid=(blocks,),
+        in_specs=[
+            pl.BlockSpec((rows, block), lambda i: (0, jnp.minimum(i, half - 1))),
+            pl.BlockSpec((rows, block), lambda i: (0, jnp.maximum(i - half, 0))),
+            pl.BlockSpec((1, width, block), lambda i: (i, 0, 0)),
+            whole(low_grad),
+            whole(down),
+        ],
+        out_specs=pl.BlockSpec((rows, width), lambda i: (0, 0)),
+        out_shape=jax.ShapeDtypeStruct((rows, width), bf16),
+        scratch_shapes=[pltpu.VMEM((rows, width), f32)],
+        compiler_params=pltpu.CompilerParams(vmem_limit_bytes=vmem_bytes),
+        cost_estimate=pl.CostEstimate(
+            flops=2 * rows * width * blocks * block,
+            bytes_accessed=2 * width * blocks * block,
+            transcendentals=0,
+        ),
+        name="pair_back",
+    )(key_grad, value_grad, weight, low_grad, down)
 
 
 def attend_kernel(
@@ -284,6 +332,13 @@
     return lax.all_to_all(buffer, "dp", split_axis=0, concat_axis=0, tiled=True)
 
 
+def in_order(parts, spot):
+    count = len(parts)
+    twice = jnp.concatenate(parts + parts, axis=0)
+    rows = parts[0].shape[0]
+    return lax.dynamic_slice_in_dim(twice, (count - spot) % count * rows, count * rows, 0)
+
+
 def shifted(array, shift, size):
     if shift == 0:
         return array
@@ -535,9 +590,7 @@
     codes = mask.shape[1]
     if share % 128 or width // size % 256:
         code = nt(got, inner_down).astype(bf16) * mask
-        twice = jnp.concatenate(inner_parts + inner_parts, axis=0)
-        first = (size - spot) % size * (width // size)
-        inner_full = lax.dynamic_slice_in_dim(twice, first, width, 0)
+        inner_full = in_order(inner_parts, spot)
         pre = nn(got, inner_full) + nn(code, inner_up)
         hidden_float = hidden_grad.astype(f32)
         activated, gate_grad, up_grad = silu_parts(pre[:, :share], pre[:, share:], hidden_float)
@@ -630,21 +683,21 @@
     place_any = either(place)
     query_rows = send_full(tn(place_any, normed).astype(bf16), experts, copies)
     query_full = lax.all_gather(query_weight[0], "seq", axis=0, tiled=True)
-    normed_parts = [shifted(normed, d, size) for d in range(size)]
-    piece = key_value_weight.shape[0] // holders
-    pair_piece = lax.dynamic_slice_in_dim(key_value_weight, holder * piece, piece, 0)
+    block = key_value_weight.shape[1] // holders
+    pair_piece = lax.dynamic_slice_in_dim(key_value_weight, holder * block, block, 1)
+    packet = jnp.concatenate([normed, pair_piece.reshape(-1, width)], axis=0)
+    packets = [packet] + [shifted(packet, d, size) for d in range(1, size)]
+    normed_parts = [normed] + [p[:rows] for p in packets[1:]]
+    pieces = [pair_piece] + [p[rows:].reshape(-1, block) for p in packets[1:]]
     place_mlp = slot_layout(mlp_routes[0], experts, capacity)
     grad_own = send_full(tn(either(place_mlp), out_grad[0]).astype(bf16), experts, copies)
-    pair_piece = after(
-        pair_piece, query_full, query_rows, grad_own, adapter_all, *normed_parts[1:]
-    )
-    pair_weight = lax.all_gather(pair_piece, ("seq", "dp"), axis=0, tiled=True)
+    pair_own = in_order(pieces, spot)
+    pair_own = after(pair_own, query_full, query_rows, grad_own, adapter_all)
+    pair_weight = lax.all_gather(pair_own, "dp", axis=0, tiled=False)
     lanes = jnp.pad(mlp_routes[0].astype(bf16), ((0, 0), (0, 126)))
     packet = jnp.concatenate([out_grad[0], lanes], axis=1)
     packet_late = after(packet, query_full)
     early = [packet] + [shifted(packet_late, d, size) for d in range(1, size)]
-    output_own = after(output_weight[0], pair_weight, *early[1:])
-    output_full = lax.all_gather(output_own, "seq", axis=0, tiled=True)
     grad_parts = [out_grad[0]] + [p[:, :width] for p in early[1:]]
     routes_there = [p[:, width : width + 2].astype(jnp.int32) for p in early]
     outer_full = mlp_out_weight[0]
@@ -672,18 +725,6 @@
     outer_down = lax.dynamic_index_in_dim(outer_down, spot, 1, keepdims=False)
 
     places = [place_mlp] + [slot_layout(r, experts, capacity) for r in routes_there[1:]]
-    grad_rows, hidden_grads, outer_codes = [], [], []
-    for d in range(size):
-        if d:
-            got = send_full(tn(either(places[d]), grad_parts[d]).astype(bf16), experts, copies)
-        else:
-            got = grad_own
-        got = got.reshape(-1, width)
-        code = nt(got, outer_up).astype(bf16) * mask
-        grad_rows.append(got)
-        outer_codes.append(code)
-        hidden_grads.append((nt(got, outer_full) + nn(code, outer_down)).astype(bf16))
-
     query_rows = after(query_rows, *normed_parts[1:])
     query_parts = nn(query_rows.reshape(-1, width), query_full).astype(bf16)
     query_home = home_join(query_parts.reshape(holders, capacity, -1), experts, copies)
@@ -694,17 +735,19 @@
     inner_sent = [cut_share(mlp_in_weight[0], (spot - d) % size, size) for d in range(size)]
     inner_parts = list(inner_sent)
     inner_parts[far] = shifted(after(inner_sent[far], *early[1:]), far, size)
-    query_home = after(query_home, *early[1:], *grad_rows[:2])
+    output_own = after(output_weight[0], pair_weight, query_home, *early[1:])
+    output_full = lax.all_gather(output_own, "seq", axis=0, tiled=True)
     attended, output_slots, query_rot, totals = attend(
         query_home, place, query_low, query_upper, cosine, sine, pairs, bias
     )
 
     output_rows = send_cut(output_slots, experts, copies)
-    output_rows = after(output_rows, inner_parts[far], *grad_rows[2:])
+    output_rows = after(output_rows, inner_parts[far])
     output_parts = nn(output_rows.reshape(holders * capacity, -1), output_full).astype(bf16)
     distances = [d for d in range(1, size) if d != far]
+    before = output_full
     for d in distances:
-        inner_parts[d] = shifted(after(inner_sent[d], output_full), d, size)
+        before = inner_parts[d] = shifted(after(inner_sent[d], before), d, size)
     output_home = home_add(output_parts.reshape(holders, capacity, width), experts, copies)
     output_low = nt(attended, output_lower).astype(bf16)
     branch = nn(place, output_home) + nn(output_low, output_upper)
@@ -716,53 +759,59 @@
 
     lanes = jnp.pad(jnp.concatenate(halves(mlp_gates), axis=1), ((0, 0), (0, 124)))
     packet = jnp.concatenate([normed_mlp, lanes], axis=1)
-    packet = after(packet, *(inner_parts[d] for d in distances[:-1]))
+    packet = after(packet, *(inner_parts[d] for d in distances[:1]))
     packets = [shifted(packet, d, size) for d in range(size)]
     gates_there = [
         (p[:, width : width + 2].astype(f32) + p[:, width + 2 : width + 4].astype(f32)).T.reshape(-1, 1)
         for p in packets
     ]
     combines = [either((places[d].astype(f32) * gates_there[d]).astype(bf16)) for d in range(size)]
-    order = list(range(1, size)) + [0]
-    got_rows = {}
-    for d in order[-1:] + order[:-1]:
-        rows_there = packets[d][:, :width]
-        if d == order[0]:
-            rows_there = after(rows_there, got_rows[0], *(inner_parts[k] for k in distances[-1:]))
-        elif d:
-            rows_there = after(rows_there, got_rows[d - 1])
-        sent = tn(either(places[d]), rows_there).astype(bf16)
-        got_rows[d] = send_full(sent, experts, copies)
+    order = list(range(size))
+    grad_rows = [grad_own.reshape(-1, width)]
+    for d in order[1:]:
+        sent = tn(either(places[d]), after(grad_parts[d], output_home)).astype(bf16)
+        grad_rows.append(send_full(sent, experts, copies).reshape(-1, width))
+    outer_codes = [nt(got, outer_up).astype(bf16) * mask for got in grad_rows]
+    hidden_grads = [
+        (nt(got, outer_full) + nn(code, outer_down)).astype(bf16)
+        for got, code in zip(grad_rows, outer_codes)
+    ]
     gate_slots = jnp.stack(
         [jnp.sum(places[d].astype(f32) * gates_there[d], axis=0) for d in range(size)]
     )
     gate_slots = gate_slots.reshape(size, experts, capacity).transpose(1, 0, 2)
     gate_slots = exchange(jnp.repeat(gate_slots, copies, axis=0))
 
-    kept, row_total, backs = {}, None, []
-    for turn, d in enumerate(order):
-        if turn:
-            got_rows[d] = after(got_rows[d], kept[order[turn - 1]][0])
-        kept[d] = expert_block(
-            got_rows[d].reshape(-1, width),
-            hidden_grads[d],
-            mask,
-            inner_up,
-            inner_down,
-            inner_parts,
-            spot,
-        )
-        row_grad = after(kept[d][0], backs[0]) if turn > 2 else kept[d][0]
-        row_home = home_add(row_grad.reshape(holders, capacity, -1), experts, copies)
-        row_sum = nn(combines[d], row_home[:, :width])
-        gate_sum = nn(places[d], row_home[:, width:])
+    def send_rows(d, *earlier):
+        sent = tn(either(places[d]), after(packets[d][:, :width], *earlier)).astype(bf16)
+        return send_full(sent, experts, copies).reshape(-1, width)
+
+    def work(d, got):
+        return expert_block(got, hidden_grads[d], mask, inner_up, inner_down, inner_parts, spot)
+
+    def rows_home(d, row_grad):
+        home = home_add(row_grad.reshape(holders, capacity, -1), experts, copies)
+        row_sum = nn(combines[d], home[:, :width])
+        gate_sum = nn(places[d], home[:, width:])
         lanes = gate_sum[:rows] + jnp.roll(gate_sum[rows:], 2, axis=1)
         row_back = jnp.concatenate([row_sum, lanes], axis=1)
-        if d:
-            row_back = shifted(row_back.astype(bf16), -d % size, size)
-        backs.append(row_back)
-        row_back = row_back.astype(f32)
-        row_total = row_back if row_total is None else row_total + row_back
+        return home, shifted(row_back.astype(bf16), -d % size, size) if d else row_back
+
+    got_rows = [send_rows(0, *grad_rows[:2])]
+    kept = [work(0, got_rows[0])]
+    row_home, row_total = rows_home(0, kept[0][0])
+    row_backs = [row_total]
+    for d in order[1:]:
+        earlier = grad_rows[2:] + [inner_parts[k] for k in distances] if d == 1 else [got_rows[-1]]
+        got_rows.append(send_rows(d, row_home, *earlier))
+    for d in order[1:]:
+        kept.append(work(d, after(got_rows[d], kept[-1][0])))
+        row_grad = kept[d][0]
+        if d > 2:
+            row_grad = after(row_grad, row_backs[d - 2])
+        row_home, row_back = rows_home(d, row_grad)
+        row_backs.append(row_back)
+        row_total = row_total + row_back.astype(f32)
     gate_sum = row_total[:, width : width + 4]
     row_total = row_total[:, :width]
     mlp_gate_grad = gate_sum.reshape(rows, 2, 2).sum(2)
@@ -789,7 +838,7 @@
         new = (
             tn(scaled(code), pre_grad),
             tn(scaled(outer_codes[d]), activated),
-            tn(scaled(back), got_rows[d].reshape(-1, width)),
+            tn(scaled(back), got_rows[d]),
             tn(scaled(outer_low), grad_rows[d]),
         )
         sums = new if sums is None else tuple(a + b for a, b in zip(sums, new))
@@ -840,16 +889,19 @@
     output_low_sum = (output_low.astype(f32) * gate_column).reshape(2, rows, rank).sum(0)
     output_upper_grad = tn(output_low_sum.astype(bf16), middle_low)
 
-    def over_sequences(arrays):
+    def own_part(arrays):
         joined = [a.reshape(rank, size, -1) for a in arrays]
         joined = jnp.concatenate(joined, axis=2).transpose(1, 0, 2)
         mine = picked(joined, spot)
         for d in range(1, size):
             theirs = picked(joined, (spot + d) % size).astype(bf16)
             mine = mine + shifted(theirs, -d % size, size).astype(f32)
-        every = lax.all_gather(mine.astype(bf16), ("seq", "dp"), axis=0, tiled=False)
+        return joined, mine.astype(bf16)
+
+    def over_sequences(mine, widths):
+        every = lax.all_gather(mine, ("seq", "dp"), axis=0, tiled=False)
         every = every.reshape(size, holders, rank, -1)
-        return gather_adapters(every, adapter_all, adapters, [a.shape[1] for a in arrays])
+        return gather_adapters(every, adapter_all, adapters, widths)
 
     key_grad, value_grad, query_slots, query_sum = attend_back(
         query_rot,
@@ -870,14 +922,6 @@
     half = key_grad.shape[1]
     pair_low_grad = nt(key_grad, pair_up[:, :half]) + nt(value_grad, pair_up[:, half:])
     pair_low_grad = pair_low_grad.astype(bf16)
-    normed_grad = None
-    for d in range(size - 1, -1, -1):
-        block = slice(d * rows, (d + 1) * rows)
-        back = nt(key_grad[block], pair_weight[:, :half]) + nt(value_grad[block], pair_weight[:, half:])
-        back = back + nn(pair_low_grad[block], pair_down)
-        if d:
-            back = shifted(back.astype(bf16), -d % size, size).astype(f32)
-        normed_grad = back if normed_grad is None else normed_grad + back
     pair_upper_grad = jnp.concatenate([tn(pair_low, key_grad), tn(pair_low, value_grad)], axis=1)
     pair_lower_grad = sum(
         tn(pair_low_grad[d * rows : (d + 1) * rows], normed_parts[d]) for d in range(size)
@@ -885,23 +929,31 @@
     query_low_grad = nt(query_sum, query_upper).astype(bf16)
     query_upper_grad = tn(query_low, query_sum)
     query_lower_grad = tn(query_low_grad, normed)
-    late = over_sequences(
-        [
-            after(pair_lower_grad, mlp_sums),
-            pair_upper_grad,
-            query_lower_grad,
-            query_upper_grad,
-            output_lower_grad,
-            output_upper_grad,
-        ]
+    sequence_grads = [
+        pair_lower_grad,
+        pair_upper_grad,
+        query_lower_grad,
+        query_upper_grad,
+        output_lower_grad,
+        output_upper_grad,
+    ]
+    joined, mine = own_part(sequence_grads)
+    normed_grads = pair_back(
+        after(key_grad, joined), value_grad, pair_weight, pair_low_grad, pair_down
     )
+    mine = after(mine, mlp_sums, normed_grads)
+    late = over_sequences(mine, [a.shape[1] for a in sequence_grads])
+    back_parts = [
+        shifted(normed_grads[d * rows : (d + 1) * rows], -d % size, size) for d in range(1, size)
+    ]
+    normed_grad = normed_grads[:rows].astype(f32) + sum(back.astype(f32) for back in back_parts)
     input_parts = nt(query_back.reshape(holders * capacity, -1), query_full).astype(bf16)
     input_home = home_add(input_parts.reshape(holders, capacity, width), experts, copies)
     normed_grad = normed_grad + nn(place_any, input_home) + nn(query_low_grad, query_lower)
     normed_grad = normed_grad + nt(logit_grad.astype(bf16), router_weight)
     input_grad = norm_back(inputs, input_scale, norm_gain, normed_grad) + middle_grad
 
-    down_near = sum(after(down, input_home).astype(f32) for down in down_near)
+    down_near = sum(after(down, input_home, *back_parts).astype(f32) for down in down_near)
     down_near = down_near.astype(bf16).reshape(holders, capacity, width)
     down_total = nn(combines[0], home_add(down_near, experts, copies))
     for d, down in down_parts:

time: 1860 us -> 2010 us (1.081)
  waiting for transfers between devices: 919 us -> 1020 us
  matrix products: 353 us -> 285 us
  starting transfers between devices: 167 us -> 217 us
  local copies, waits for them, and re-layouts: 76.5 us -> 117 us
    ppermute x24, waiting for transfers between devices: 570 us -> 735 us  [shifted(): lax.ppermute(array, 'seq', [(k, (k - shift) % size) for k in range(size)])]
    dot_general x105 -> x93, matrix products: 353 us -> 285 us  [product(): lax.dot_general(left, right, (((left_dim,), (right_dim,)), ((), ())), pre...]
    all_gather x2, waiting for transfers between devices: 76.1 us -> 18.3 us  [the longest x1 18.3 us: body(): pair_weight = lax.all_gather(pair_own, 'dp', axis=0, tiled=False)]
    ppermute x24, starting transfers between devices: 56 us -> 105 us  [shifted(): lax.ppermute(array, 'seq', [(k, (k - shift) % size) for k in range(size)])]
    all_gather x1, waiting for transfers between devices: 45.8 us -> 0.01 us  [body(): query_full = lax.all_gather(query_weight[0], 'seq', axis=0, tiled=True)]
    all_to_all x24, waiting for transfers between devices: 226 us -> 262 us  [exchange(): return lax.all_to_all(buffer, 'dp', split_axis=0, concat_axis=0, tiled=True)]
    pallas_call x1 -> x2, Pallas kernels: 32.6 us -> 55 us  [the longest x1 31.8 us: project_pairs(): pl.pallas_call(functools.partial(pair_kernel, count, blocks // 2), grid=(...]
    unnamed x354 -> x373, local copies, waits for them, and re-layouts: 31.6 us -> 45.3 us
  transfers between devices with their start and end apart: 54 -> 54, of which waited for: 31 -> 31; matrix products, arithmetic and copies ran while one was open for 23% -> 20% of each run, Pallas kernels for 14% -> 14%
where the time goes in v4:
time: 2010 us; the launch traced here: 2000 us
  waiting for transfers between devices  1020 us (51%)
  Pallas kernels  292 us (15%)
  matrix products  285 us (14%)
  starting transfers between devices  217 us (11%)
  local copies, waits for them, and re-layouts  117 us (6%)
  other arithmetic  42.9 us (2%)
    ppermute x24, waiting for transfers between devices, shifted(): lax.ppermute(array, 'seq', [(k, (k - shift) % size) for k in range(size)])  735 us
    dot_general x93, matrix products, product(): lax.dot_general(left, right, (((left_dim,), (right_dim,)), ((), ())), pre...  285 us
    all_to_all x24, waiting for transfers between devices, exchange(): return lax.all_to_all(buffer, 'dp', split_axis=0, concat_axis=0, tiled=True)  262 us
    pallas_call x4, Pallas kernels, expert_block(): pl.pallas_call(functools.partial(expert_kernel, size, share), grid_spec=p...  124 us
    all_to_all x24, starting transfers between devices, exchange(): return lax.all_to_all(buffer, 'dp', split_axis=0, concat_axis=0, tiled=True)  111 us
    ppermute x24, starting transfers between devices, shifted(): lax.ppermute(array, 'seq', [(k, (k - shift) % size) for k in range(size)])  105 us
    unnamed x373, local copies, waits for them, and re-layouts  45.3 us
    pallas_call x1, Pallas kernels, attend_back(): pl.pallas_call(functools.partial(attend_back_kernel, 1.0 / math.sqrt(HD))...  44 us
  transfers between devices with their start and end apart: 54, of which 31 were waited for; matrix products, arithmetic and copies ran while one was open for 20% of the time, Pallas kernels for 14%

profile of v4, /device:TPU:0, one launch (start us, length us, event | category | flops | bytes accessed | tf_op | source)
XLA Modules:
  0.0 1996.3 jit_solution(16929458689250201792)
XLA Ops:
  9.2 5.2 all-to-all-start.3
  38.3 27.3 %all-to-all-done = bf16[8,96,2048]{2,1,0:T(8,128)(2,1)} async-done(((bf16[8,96,2048]{2,1,0:T(8,128)(2,1)}), bf16[8,96,2048]{2,1,0:T(8,128)(2,1)}, u32[]{:S(2)}, u32[]{:S(2)}) %all-to-all-start) | async-done | bytes 3145760 | tf_op jit(solution)/shard_map/all_to_all | solution.py:332
  77.8 66.7 %collective-permute-done.2 = bf16[384,2048]{1,0:T(8,128)(2,1)} collective-permute-done((bf16[384,2048]{1,0:T(8,128)(2,1)}, bf16[384,2048]{1,0:T(8,128)(2,1)}, u32[]{:S(2)}, u32[]{:S(2)}) %collective-permute-start.2) | collective-permute-done | bytes 1572896 | tf_op jit(solution)/shard_map/ppermute | solution.py:345
  148.5 102.9 %collective-permute-done.1 = bf16[384,2048]{1,0:T(8,128)(2,1)} collective-permute-done((bf16[384,2048]{1,0:T(8,128)(2,1)}, bf16[384,2048]{1,0:T(8,128)(2,1)}, u32[]{:S(2)}, u32[]{:S(2)}) %collective-permute-start.1) | collective-permute-done | bytes 1572896 | tf_op jit(solution)/shard_map/ppermute | solution.py:345
  282.7 11.8 convolution_convert_fusion.3
  300.4 40.3 %collective-permute-start.5 = (bf16[256,2176]{1,0:T(8,128)(2,1)S(1)}, bf16[256,2176]{1,0:T(8,128)(2,1)}, u32[]{:S(2)}, u32[]{:S(2)}) collective-permute-start(bf16[256,2176]{1,0:T(8,128)(2,1)S(1)} %fusion.98), channel_id=1, source_target_pairs={{0,8},{8,16},{16,24},{24,0},{1,9},{9,17},{17,25},{25,1},{2,10},{10... | collective-permute-start | bytes 3342344 | tf_op jit(solution)/shard_map/ppermute | solution.py:345
  344.7 24.8 %collective-permute-done.5 = bf16[256,2176]{1,0:T(8,128)(2,1)} collective-permute-done((bf16[256,2176]{1,0:T(8,128)(2,1)S(1)}, bf16[256,2176]{1,0:T(8,128)(2,1)}, u32[]{:S(2)}, u32[]{:S(2)}) %collective-permute-start.5) | collective-permute-done | bytes 1114144 | tf_op jit(solution)/shard_map/ppermute | solution.py:345
  369.5 47.4 %collective-permute-done.4 = bf16[256,2176]{1,0:T(8,128)(2,1)} collective-permute-done((bf16[256,2176]{1,0:T(8,128)(2,1)S(1)}, bf16[256,2176]{1,0:T(8,128)(2,1)}, u32[]{:S(2)}, u32[]{:S(2)}) %collective-permute-start.4) | collective-permute-done | bytes 1114144 | tf_op jit(solution)/shard_map/ppermute | solution.py:345
  416.9 18.3 all-gather.15.cloned.1.call-done
  445.3 5.1 collective-permute-start.6
  450.4 31.8 %pairs.1 = (bf16[1024,4096]{1,0:T(8,128)(2,1)}, bf16[1024,16]{1,0:T(8,128)(2,1)S(1)}) custom-call(bf16[256,2048]{1,0:T(8,128)(2,1)S(1)} %fusion.62.refs_0_, bf16[256,2048]{1,0:T(8,128)(2,1)S(1)} %copy-done.26, bf16[256,2048]{1,0:T(8,128)(2,1)S(1)} %copy-done.25, bf16[256,2048]{1,0:T(8,128)(2,1)S(1)} %copy-done.24, bf16[8,2048,512]{2,1,0:T(8,128)(2,1)} %bitcast.499, ...), custom_call_target="tpu_custom_call" | custom-call | flops 17179869184 | bytes 16777216 | tf_op jit(solution)/shard_map/pairs/pallas_call | solution.py:75
  482.2 33.7 %attend.1 = (bf16[512,2048]{1,0:T(8,128)(2,1)S(1)}, bf16[768,2048]{1,0:T(8,128)(2,1)}, bf16[512,2048]{1,0:T(8,128)(2,1)}, f32[16,512,1]{2,1,0:T(8,128)}) custom-call(bf16[768,2048]{1,0:T(8,128)(2,1)} %bitcast.8.home_ref, bf16[512,768]{1,0:T(8,128)(2,1)S(1)} %fusion.88.place_ref, bf16[256,16]{1,0:T(8,128)(2,1)S(1)} %convolution_convert_fusion.23.low_ref, ...), custom_call_target="tpu_custom_call" | custom-call | flops 4294967296 | bytes 8388608 | tf_op jit(solution)/shard_map/attend/pallas_call | solution.py:194
  521.7 181.4 %collective-permute-done.6.refs_2_ = bf16[512,2816]{1,0:T(8,128)(2,1)} collective-permute-done((bf16[512,2816]{1,0:T(8,128)(2,1)}, bf16[512,2816]{1,0:T(8,128)(2,1)}, u32[]{:S(2)}, u32[]{:S(2)}) %collective-permute-start.6) | collective-permute-done | bytes 2883616 | tf_op jit(solution)/shard_map/ppermute | solution.py:345
  703.1 7.2 all-gather.9.cloned.1.call-done
  710.4 11.8 convolution_convert_fusion.2
  741.6 23.1 %all-to-all-done.5 = bf16[8,96,2048]{2,1,0:T(8,128)(2,1)} async-done(((bf16[8,96,2048]{2,1,0:T(8,128)(2,1)}), bf16[8,96,2048]{2,1,0:T(8,128)(2,1)}, u32[]{:S(2)}, u32[]{:S(2)}) %all-to-all-start.5) | async-done | bytes 3145760 | tf_op jit(solution)/shard_map/all_to_all | solution.py:332
  776.2 28.5 %collective-permute-done.7.refs_1_ = bf16[512,2816]{1,0:T(8,128)(2,1)} collective-permute-done((bf16[512,2816]{1,0:T(8,128)(2,1)}, bf16[512,2816]{1,0:T(8,128)(2,1)}, u32[]{:S(2)}, u32[]{:S(2)}) %collective-permute-start.7) | collective-permute-done | bytes 2883616 | tf_op jit(solution)/shard_map/ppermute | solution.py:345
  811.8 69.3 %collective-permute-done.11 = bf16[256,2176]{1,0:T(8,128)(2,1)} collective-permute-done((bf16[256,2176]{1,0:T(8,128)(2,1)}, bf16[256,2176]{1,0:T(8,128)(2,1)}, u32[]{:S(2)}, u32[]{:S(2)}) %collective-permute-start.11) | collective-permute-done | bytes 1114144 | tf_op jit(solution)/shard_map/ppermute | solution.py:345
  905.9 33.7 %all-to-all-done.6 = bf16[8,96,2048]{2,1,0:T(8,128)(2,1)} async-done(((bf16[8,96,2048]{2,1,0:T(8,128)(2,1)}), bf16[8,96,2048]{2,1,0:T(8,128)(2,1)}, u32[]{:S(2)}, u32[]{:S(2)}) %all-to-all-start.6) | async-done | bytes 3145760 | tf_op jit(solution)/shard_map/all_to_all | solution.py:332
  948.2 33.9 %all-to-all-done.9 = bf16[8,96,2048]{2,1,0:T(8,128)(2,1)} async-done(((bf16[8,96,2048]{2,1,0:T(8,128)(2,1)}), bf16[8,96,2048]{2,1,0:T(8,128)(2,1)}, u32[]{:S(2)}, u32[]{:S(2)}) %all-to-all-start.9) | async-done | bytes 3145760 | tf_op jit(solution)/shard_map/all_to_all | solution.py:332
  982.0 4.7 all-to-all-start.7
  1000.0 6.3 squeeze.95
  1006.3 20.7 %collective-permute-start.8 = (bf16[512,2816]{1,0:T(8,128)(2,1)}, bf16[512,2816]{1,0:T(8,128)(2,1)}, u32[]{:S(2)}, u32[]{:S(2)}) collective-permute-start(bf16[512,2816]{1,0:T(8,128)(2,1)} %copy-done.21), channel_id=1, source_target_pairs={{0,8},{8,16},{16,24},{24,0},{1,9},{9,17},{17,25},{25,1},{2,10},{10... | collective-permute-start | bytes 8650760 | tf_op jit(solution)/shard_map/ppermute | solution.py:345
  1027.1 6.8 dynamic-slice_reduce_fusion
  1043.0 8.6 fusion.14
  1055.2 34.5 %collective-permute-done.8.refs_3_ = bf16[512,2816]{1,0:T(8,128)(2,1)} collective-permute-done((bf16[512,2816]{1,0:T(8,128)(2,1)}, bf16[512,2816]{1,0:T(8,128)(2,1)}, u32[]{:S(2)}, u32[]{:S(2)}) %collective-permute-start.8) | collective-permute-done | bytes 2883616 | tf_op jit(solution)/shard_map/ppermute | solution.py:345
  1089.7 30.9 %experts.4 = (bf16[768,2176]{1,0:T(8,128)(2,1)}, bf16[768,1408]{1,0:T(8,128)(2,1)S(1)}, bf16[768,2816]{1,0:T(8,128)(2,1)}, bf16[768,128]{1,0:T(8,128)(2,1)S(1)}, bf16[768,128]{1,0:T(8,128)(2,1)S(1)}) custom-call(s32[1]{0:T(128)} %bitcast.37.spot_ref, bf16[768,2048]{1,0:T(8,128)(2,1)} %bitcast.43.x_ref, bf16[768,1408]{1,0:T(8,128)(2,1)S(1)} %add_convert_fusion.8.hidden_ref, ...), custom_call_target="tpu_custom_call" | custom-call | flops 17716740096 | bytes 27262976 | tf_op jit(solution)/shard_map/experts/pallas_call | solution.py:607
  1122.0 4.7 all-to-all-start.8
  1137.9 8.6 fusion.6
  1148.6 18.1 all-to-all-done.8
  1170.9 4.9 all-to-all-start.11
  1179.0 8.6 fusion.8
  1189.7 8.1 fusion.10
  1197.8 16.0 all-to-all-done.11
  1231.9 31.0 %experts.5 = (bf16[768,2176]{1,0:T(8,128)(2,1)}, bf16[768,1408]{1,0:T(8,128)(2,1)S(1)}, bf16[768,2816]{1,0:T(8,128)(2,1)}, bf16[768,128]{1,0:T(8,128)(2,1)S(1)}, bf16[768,128]{1,0:T(8,128)(2,1)S(1)}) custom-call(s32[1]{0:T(128)} %bitcast.37.spot_ref, bf16[768,2048]{1,0:T(8,128)(2,1)} %bitcast.62.x_ref, bf16[768,1408]{1,0:T(8,128)(2,1)S(1)} %add_convert_fusion.7.hidden_ref, ...), custom_call_target="tpu_custom_call" | custom-call | flops 17716740096 | bytes 27262976 | tf_op jit(solution)/shard_map/experts/pallas_call | solution.py:607
  1264.2 4.9 all-to-all-start.12
  1292.5 16.6 all-to-all-done.12
  1316.3 31.1 %experts.6 = (bf16[768,2176]{1,0:T(8,128)(2,1)}, bf16[768,1408]{1,0:T(8,128)(2,1)S(1)}, bf16[768,2816]{1,0:T(8,128)(2,1)}, bf16[768,128]{1,0:T(8,128)(2,1)S(1)}, bf16[768,128]{1,0:T(8,128)(2,1)S(1)}) custom-call(s32[1]{0:T(128)} %bitcast.37.spot_ref, bf16[768,2048]{1,0:T(8,128)(2,1)} %bitcast.68.x_ref, bf16[768,1408]{1,0:T(8,128)(2,1)S(1)} %copy-done.23, ...), custom_call_target="tpu_custom_call" | custom-call | flops 17716740096 | bytes 27262976 | tf_op jit(solution)/shard_map/experts/pallas_call | solution.py:607
  1371.5 31.0 %experts.7 = (bf16[768,2176]{1,0:T(8,128)(2,1)}, bf16[768,1408]{1,0:T(8,128)(2,1)S(1)}, bf16[768,2816]{1,0:T(8,128)(2,1)}, bf16[768,128]{1,0:T(8,128)(2,1)S(1)}, bf16[768,128]{1,0:T(8,128)(2,1)S(1)}) custom-call(s32[1]{0:T(128)} %bitcast.37.spot_ref, bf16[768,2048]{1,0:T(8,128)(2,1)} %bitcast.73.x_ref, bf16[768,1408]{1,0:T(8,128)(2,1)S(1)} %copy-done.22, ...), custom_call_target="tpu_custom_call" | custom-call | flops 17716740096 | bytes 27262976 | tf_op jit(solution)/shard_map/experts/pallas_call | solution.py:607
  1431.3 18.6 all-to-all-done.16
  1459.5 22.1 %collective-permute-done.12 = bf16[256,2176]{1,0:T(8,128)(2,1)} collective-permute-done((bf16[256,2176]{1,0:T(8,128)(2,1)}, bf16[256,2176]{1,0:T(8,128)(2,1)}, u32[]{:S(2)}, u32[]{:S(2)}) %collective-permute-start.12) | collective-permute-done | bytes 1114144 | tf_op jit(solution)/shard_map/ppermute | solution.py:345
  1481.6 20.6 %collective-permute-done.14 = bf16[256,2176]{1,0:T(8,128)(2,1)} collective-permute-done((bf16[256,2176]{1,0:T(8,128)(2,1)}, bf16[256,2176]{1,0:T(8,128)(2,1)}, u32[]{:S(2)}, u32[]{:S(2)}) %collective-permute-start.14) | collective-permute-done | bytes 1114144 | tf_op jit(solution)/shard_map/ppermute | solution.py:345
  1513.9 5.1 all-to-all-start.17
  1526.9 9.3 add_convert_fusion.3
  1539.9 19.1 all-to-all-done.17
  1559.0 11.9 convolution_convert_fusion.1
  1575.5 9.9 add_convert_fusion.2
  1587.1 10.6 add_convert_fusion.1
  1606.3 22.4 %all-to-all-done.18 = bf16[8,96,2048]{2,1,0:T(8,128)(2,1)} async-done(((bf16[8,96,2048]{2,1,0:T(8,128)(2,1)}), bf16[8,96,2048]{2,1,0:T(8,128)(2,1)}, u32[]{:S(2)}, u32[]{:S(2)}) %all-to-all-start.18) | async-done | bytes 3145760 | tf_op jit(solution)/shard_map/all_to_all | solution.py:332
  1631.7 44.0 %attend_back.1 = (bf16[1024,2048]{1,0:T(8,128)(2,1)}, bf16[1024,2048]{1,0:T(8,128)(2,1)}, bf16[768,2048]{1,0:T(8,128)(2,1)}, bf16[256,2048]{1,0:T(8,128)(2,1)S(1)}) custom-call(bf16[512,2048]{1,0:T(8,128)(2,1)} %get-tuple-element.95.query_ref, bf16[1024,4096]{1,0:T(8,128)(2,1)} %get-tuple-element.82.key_ref.value_ref, ...), custom_call_target="tpu_custom_call" | custom-call | flops 10737418240 | bytes 16777216 | tf_op jit(solution)/shard_map/attend_back/pallas_call | solution.py:289
  1675.8 4.8 all-to-all-start.20
  1699.2 19.2 all-to-all-done.20
  1718.5 11.9 convolution_convert_fusion
  1735.3 23.2 %pair_back.1 = bf16[1024,2048]{1,0:T(8,128)(2,1)S(1)} custom-call(bf16[1024,2048]{1,0:T(8,128)(2,1)} %get-tuple-element.127.key_ref, bf16[1024,2048]{1,0:T(8,128)(2,1)} %get-tuple-element.128.value_ref, bf16[8,2048,512]{2,1,0:T(8,128)(2,1)} %bitcast.500, bf16[1024,16]{1,0:T(8,128)(2,1)S(1)} %fusion.89.low_ref, bf16[16,2048]{1,0:T(8,128)(2,1)S(1)} %copy-done.45), custom_call_target="tpu_custom_call" | custom-call | flops 17179869184 | bytes 16777216 | tf_op jit(solution)/shard_map/pair_back/pallas_call | solution.py:129
  1761.7 11.2 all-to-all-done.21
  1786.5 9.7 add_convert_fusion.4
  1796.8 17.9 collective-permute-done.17
  1814.7 76.9 %collective-permute-done.16 = bf16[256,2048]{1,0:T(8,128)(2,1)S(1)} collective-permute-done((bf16[256,2048]{1,0:T(8,128)(2,1)}, bf16[256,2048]{1,0:T(8,128)(2,1)S(1)}, u32[]{:S(2)}, u32[]{:S(2)}) %collective-permute-start.16) | collective-permute-done | bytes 1048608 | tf_op jit(solution)/shard_map/ppermute | solution.py:345
  1891.6 8.2 add_convert_fusion
  1899.8 4.9 all-to-all-start.22
  1918.0 38.7 %collective-permute-done.20 = bf16[256,2048]{1,0:T(8,128)(2,1)} collective-permute-done((bf16[256,2048]{1,0:T(8,128)(2,1)S(1)}, bf16[256,2048]{1,0:T(8,128)(2,1)}, u32[]{:S(2)}, u32[]{:S(2)}) %collective-permute-start.20) | collective-permute-done | bytes 1048608 | tf_op jit(solution)/shard_map/ppermute | solution.py:345
  1956.8 4.8 fusion.105
  1961.5 19.3 unpack.1
  1982.9 6.0 gather_adapters.1
  (684 shorter events, 427.1 us)
Async XLA Ops:
  7.2 438.0 %copy-start = (bf16[8,16,4096]{2,1,0:T(8,128)(2,1)S(1)}, bf16[8,16,4096]{2,1,0:T(8,128)(2,1)}, u32[]{:S(2)}) copy-start(bf16[8,16,4096]{2,1,0:T(8,128)(2,1)} %param.37) | copy-start | bytes 3145732
  7.2 268.5 %all-gather.13.cloned.1.call-start = ((), (), s32[]{:S(2)}) async-start(), calls=%async_computation.28 | async-start | bytes 10485760 | tf_op jit(solution)/shard_map/all_gather | solution.py:685
  9.2 13.4 all-to-all-start.3
  17.4 426.4 %copy-start.151 = (f32[256]{0:T(256)}, f32[256]{0:T(256)S(1)}, u32[]{:S(2)}) copy-start(f32[256]{0:T(256)S(1)} %add_rsqrt_fusion.1) | copy-start | bytes 3076
  19.9 707.0 %copy-start.2 = (bf16[256,2048]{1,0:T(8,128)(2,1)}, bf16[256,2048]{1,0:T(8,128)(2,1)S(1)}, u32[]{:S(2)}) copy-start(bf16[256,2048]{1,0:T(8,128)(2,1)S(1)} %fusion.62.refs_0_) | copy-start | bytes 3145732
  23.2 42.4 %all-to-all-start = ((bf16[8,96,2048]{2,1,0:T(8,128)(2,1)}), bf16[8,96,2048]{2,1,0:T(8,128)(2,1)}, u32[]{:S(2)}, u32[]{:S(2)}) async-start(bf16[8,96,2048]{2,1,0:T(8,128)(2,1)} %bitcast.420), calls=%async_computation | async-start | bytes 6291456 | tf_op jit(solution)/shard_map/all_to_all | solution.py:332
  65.5 210.2 %all-to-all-start.2 = ((bf16[8,96,2048]{2,1,0:T(8,128)(2,1)}), bf16[8,96,2048]{2,1,0:T(8,128)(2,1)}, u32[]{:S(2)}, u32[]{:S(2)}) async-start(bf16[8,96,2048]{2,1,0:T(8,128)(2,1)} %bitcast.418), calls=%async_computation.2 | async-start | bytes 6291456 | tf_op jit(solution)/shard_map/all_to_all | solution.py:332
  70.1 365.0 %all-gather.15.cloned.1.call-start = ((), (), s32[]{:S(2)}) async-start(), calls=%async_computation.29 | async-start | bytes 18874368 | tf_op jit(solution)/shard_map/all_gather | solution.py:696
  71.4 73.0 %collective-permute-start.2 = (bf16[384,2048]{1,0:T(8,128)(2,1)}, bf16[384,2048]{1,0:T(8,128)(2,1)}, u32[]{:S(2)}, u32[]{:S(2)}) collective-permute-start(bf16[384,2048]{1,0:T(8,128)(2,1)} %pad_maximum_fusion.1), channel_id=1, source_target_pairs={{0,8},{8,16},{16,24},{24,0},{1,9},{9,17},{17,25},{25,1},{2,10},{10... | collective-permute-start | bytes 4718600 | tf_op jit(solution)/shard_map/ppermute | solution.py:345
  73.0 178.4 %collective-permute-start.1 = (bf16[384,2048]{1,0:T(8,128)(2,1)}, bf16[384,2048]{1,0:T(8,128)(2,1)}, u32[]{:S(2)}, u32[]{:S(2)}) collective-permute-start(bf16[384,2048]{1,0:T(8,128)(2,1)} %pad_maximum_fusion.1), channel_id=1, source_target_pairs={{0,16},{8,24},{16,0},{24,8},{1,17},{9,25},{17,1},{25,9},{2,18},{10... | collective-permute-start | bytes 4718600 | tf_op jit(solution)/shard_map/ppermute | solution.py:345
  75.6 183.0 %collective-permute-start = (bf16[384,2048]{1,0:T(8,128)(2,1)}, bf16[384,2048]{1,0:T(8,128)(2,1)}, u32[]{:S(2)}, u32[]{:S(2)}) collective-permute-start(bf16[384,2048]{1,0:T(8,128)(2,1)} %pad_maximum_fusion.1), channel_id=1, source_target_pairs={{0,24},{8,0},{16,8},{24,16},{1,25},{9,1},{17,9},{25,17},{2,26},{10... | collective-permute-start | bytes 4718600 | tf_op jit(solution)/shard_map/ppermute | solution.py:345
  77.8 956.2 %copy-start.46 = (s32[8]{0:T(128)}, s32[8]{0:T(128)S(1)}, u32[]{:S(2)}) copy-start(s32[8]{0:T(128)S(1)} %slice_reduce_fusion.4.ids_ref) | copy-start | bytes 100
  294.5 122.4 %all-to-all-start.1 = ((bf16[8,96,2048]{2,1,0:T(8,128)(2,1)}), bf16[8,96,2048]{2,1,0:T(8,128)(2,1)}, u32[]{:S(2)}, u32[]{:S(2)}) async-start(bf16[8,96,2048]{2,1,0:T(8,128)(2,1)} %bitcast.458), calls=%async_computation.1 | async-start | bytes 6291456 | tf_op jit(solution)/shard_map/all_to_all | solution.py:332
  299.0 411.3 %all-gather.9.cloned.1.call-start = ((), (), s32[]{:S(2)}) async-start(), calls=%async_computation.25 | async-start | bytes 10485760 | tf_op jit(solution)/shard_map/all_gather | solution.py:739
  300.4 69.1 %collective-permute-start.5 = (bf16[256,2176]{1,0:T(8,128)(2,1)S(1)}, bf16[256,2176]{1,0:T(8,128)(2,1)}, u32[]{:S(2)}, u32[]{:S(2)}) collective-permute-start(bf16[256,2176]{1,0:T(8,128)(2,1)S(1)} %fusion.98), channel_id=1, source_target_pairs={{0,8},{8,16},{16,24},{24,0},{1,9},{9,17},{17,25},{25,1},{2,10},{10... | collective-permute-start | bytes 3342344 | tf_op jit(solution)/shard_map/ppermute | solution.py:345
  340.7 76.2 %collective-permute-start.4 = (bf16[256,2176]{1,0:T(8,128)(2,1)S(1)}, bf16[256,2176]{1,0:T(8,128)(2,1)}, u32[]{:S(2)}, u32[]{:S(2)}) collective-permute-start(bf16[256,2176]{1,0:T(8,128)(2,1)S(1)} %fusion.98), channel_id=1, source_target_pairs={{0,16},{8,24},{16,0},{24,8},{1,17},{9,25},{17,1},{25,9},{2,18},{10... | collective-permute-start | bytes 3342344 | tf_op jit(solution)/shard_map/ppermute | solution.py:345
  344.5 72.4 %collective-permute-start.3 = (bf16[256,2176]{1,0:T(8,128)(2,1)S(1)}, bf16[256,2176]{1,0:T(8,128)(2,1)}, u32[]{:S(2)}, u32[]{:S(2)}) collective-permute-start(bf16[256,2176]{1,0:T(8,128)(2,1)S(1)} %fusion.98), channel_id=1, source_target_pairs={{0,24},{8,0},{16,8},{24,16},{1,25},{9,1},{17,9},{25,17},{2,26},{10... | collective-permute-start | bytes 3342344 | tf_op jit(solution)/shard_map/ppermute | solution.py:345
  445.3 257.8 %collective-permute-start.6 = (bf16[512,2816]{1,0:T(8,128)(2,1)}, bf16[512,2816]{1,0:T(8,128)(2,1)}, u32[]{:S(2)}, u32[]{:S(2)}) collective-permute-start(bf16[512,2816]{1,0:T(8,128)(2,1)} %cut.4), channel_id=1, source_target_pairs={{0,16},{8,24},{16,0},{24,8},{1,17},{9,25},{17,1},{25,9},{2,18},{10... | collective-permute-start | bytes 8650760 | tf_op jit(solution)/shard_map/ppermute | solution.py:345
  517.2 185.9 %all-to-all-start.4 = ((bf16[8,96,2048]{2,1,0:T(8,128)(2,1)}), bf16[8,96,2048]{2,1,0:T(8,128)(2,1)}, u32[]{:S(2)}, u32[]{:S(2)}) async-start(bf16[8,96,2048]{2,1,0:T(8,128)(2,1)} %bitcast.459), calls=%async_computation.4 | async-start | bytes 6291456 | tf_op jit(solution)/shard_map/all_to_all | solution.py:332
  722.2 42.5 %all-to-all-start.5 = ((bf16[8,96,2048]{2,1,0:T(8,128)(2,1)}), bf16[8,96,2048]{2,1,0:T(8,128)(2,1)}, u32[]{:S(2)}, u32[]{:S(2)}) async-start(bf16[8,96,2048]{2,1,0:T(8,128)(2,1)} %bitcast.455), calls=%async_computation.5 | async-start | bytes 6291456 | tf_op jit(solution)/shard_map/all_to_all | solution.py:332
  727.3 399.5 %copy-start.123 = (f32[256,2]{0,1:T(2,128)}, f32[256,2]{0,1:T(2,128)S(1)}, u32[]{:S(2)}) copy-start(f32[256,2]{0,1:T(2,128)S(1)} %select_reduce_fusion.3) | copy-start | bytes 6148
  727.4 399.4 %copy-start.135 = (f32[256]{0:T(256)}, f32[256]{0:T(256)S(1)}, u32[]{:S(2)}) copy-start(f32[256]{0:T(256)S(1)} %reduce_max.18) | copy-start | bytes 3076
  727.4 399.4 %copy-start.137 = (f32[256]{0:T(256)}, f32[256]{0:T(256)S(1)}, u32[]{:S(2)}) copy-start(f32[256]{0:T(256)S(1)} %fusion.207) | copy-start | bytes 3076
  736.4 298.9 %copy-start.140 = (s32[512]{0:T(512)}, s32[512]{0:T(512)S(1)}, u32[]{:S(2)}) copy-start(s32[512]{0:T(512)S(1)} %convert_add_fusion.1) | copy-start | bytes 6148
  739.2 65.5 %collective-permute-start.7 = (bf16[512,2816]{1,0:T(8,128)(2,1)}, bf16[512,2816]{1,0:T(8,128)(2,1)}, u32[]{:S(2)}, u32[]{:S(2)}) collective-permute-start(bf16[512,2816]{1,0:T(8,128)(2,1)} %cut.5), channel_id=1, source_target_pairs={{0,24},{8,0},{16,8},{24,16},{1,25},{9,1},{17,9},{25,17},{2,26},{10... | collective-permute-start | bytes 8650760 | tf_op jit(solution)/shard_map/ppermute | solution.py:345
  804.7 76.3 %collective-permute-start.11 = (bf16[256,2176]{1,0:T(8,128)(2,1)}, bf16[256,2176]{1,0:T(8,128)(2,1)}, u32[]{:S(2)}, u32[]{:S(2)}) collective-permute-start(bf16[256,2176]{1,0:T(8,128)(2,1)} %fusion.99), channel_id=1, source_target_pairs={{0,16},{8,24},{16,0},{24,8},{1,17},{9,25},{17,1},{25,9},{2,18},{10... | collective-permute-start | bytes 3342344 | tf_op jit(solution)/shard_map/ppermute | solution.py:345
  805.5 89.6 %copy-start.144 = (s32[512]{0:T(512)}, s32[512]{0:T(512)S(1)}, u32[]{:S(2)}) copy-start(s32[512]{0:T(512)S(1)} %convert_add_fusion.3) | copy-start | bytes 6148
  805.7 77.7 %collective-permute-start.9 = (bf16[256,2176]{1,0:T(8,128)(2,1)}, bf16[256,2176]{1,0:T(8,128)(2,1)}, u32[]{:S(2)}, u32[]{:S(2)}) collective-permute-start(bf16[256,2176]{1,0:T(8,128)(2,1)} %fusion.99), channel_id=1, source_target_pairs={{0,24},{8,0},{16,8},{24,16},{1,25},{9,1},{17,9},{25,17},{2,26},{10... | collective-permute-start | bytes 3342344 | tf_op jit(solution)/shard_map/ppermute | solution.py:345
  808.8 94.2 %copy-start.142 = (s32[512]{0:T(512)}, s32[512]{0:T(512)S(1)}, u32[]{:S(2)}) copy-start(s32[512]{0:T(512)S(1)} %convert_add_fusion.2) | copy-start | bytes 6148
  808.8 77.0 %collective-permute-start.13 = (bf16[256,2176]{1,0:T(8,128)(2,1)}, bf16[256,2176]{1,0:T(8,128)(2,1)}, u32[]{:S(2)}, u32[]{:S(2)}) collective-permute-start(bf16[256,2176]{1,0:T(8,128)(2,1)} %fusion.99), channel_id=1, source_target_pairs={{0,8},{8,16},{16,24},{24,0},{1,9},{9,17},{17,25},{25,1},{2,10},{10... | collective-permute-start | bytes 3342344 | tf_op jit(solution)/shard_map/ppermute | solution.py:345
  888.8 8.4 all-to-all-start.19
  897.2 42.3 %all-to-all-start.6 = ((bf16[8,96,2048]{2,1,0:T(8,128)(2,1)}), bf16[8,96,2048]{2,1,0:T(8,128)(2,1)}, u32[]{:S(2)}, u32[]{:S(2)}) async-start(bf16[8,96,2048]{2,1,0:T(8,128)(2,1)} %bitcast.424), calls=%async_computation.6 | async-start | bytes 6291456 | tf_op jit(solution)/shard_map/all_to_all | solution.py:332
  939.5 42.5 %all-to-all-start.9 = ((bf16[8,96,2048]{2,1,0:T(8,128)(2,1)}), bf16[8,96,2048]{2,1,0:T(8,128)(2,1)}, u32[]{:S(2)}, u32[]{:S(2)}) async-start(bf16[8,96,2048]{2,1,0:T(8,128)(2,1)} %bitcast.425), calls=%async_computation.9 | async-start | bytes 6291456 | tf_op jit(solution)/shard_map/all_to_all | solution.py:332
  982.0 56.3 %all-to-all-start.7 = ((bf16[8,96,2048]{2,1,0:T(8,128)(2,1)}), bf16[8,96,2048]{2,1,0:T(8,128)(2,1)}, u32[]{:S(2)}, u32[]{:S(2)}) async-start(bf16[8,96,2048]{2,1,0:T(8,128)(2,1)} %bitcast.419), calls=%async_computation.7 | async-start | bytes 6291456 | tf_op jit(solution)/shard_map/all_to_all | solution.py:332
  1006.3 83.4 %collective-permute-start.8 = (bf16[512,2816]{1,0:T(8,128)(2,1)}, bf16[512,2816]{1,0:T(8,128)(2,1)}, u32[]{:S(2)}, u32[]{:S(2)}) collective-permute-start(bf16[512,2816]{1,0:T(8,128)(2,1)} %copy-done.21), channel_id=1, source_target_pairs={{0,8},{8,16},{16,24},{24,0},{1,9},{9,17},{17,25},{25,1},{2,10},{10... | collective-permute-start | bytes 8650760 | tf_op jit(solution)/shard_map/ppermute | solution.py:345
  1038.3 83.7 %all-to-all-start.10 = ((bf16[8,96,2048]{2,1,0:T(8,128)(2,1)}), bf16[8,96,2048]{2,1,0:T(8,128)(2,1)}, u32[]{:S(2)}, u32[]{:S(2)}) async-start(bf16[8,96,2048]{2,1,0:T(8,128)(2,1)} %bitcast.422), calls=%async_computation.10 | async-start | bytes 6291456 | tf_op jit(solution)/shard_map/all_to_all | solution.py:332
  1122.0 44.7 %all-to-all-start.8 = ((bf16[8,96,2176]{2,1,0:T(8,128)(2,1)}), bf16[8,96,2176]{2,1,0:T(8,128)(2,1)}, u32[]{:S(2)}, u32[]{:S(2)}) async-start(bf16[8,96,2176]{2,1,0:T(8,128)(2,1)} %bitcast.449), calls=%async_computation.8 | async-start | bytes 6684672 | tf_op jit(solution)/shard_map/all_to_all | solution.py:332
  1170.9 42.8 %all-to-all-start.11 = ((bf16[8,96,2048]{2,1,0:T(8,128)(2,1)}), bf16[8,96,2048]{2,1,0:T(8,128)(2,1)}, u32[]{:S(2)}, u32[]{:S(2)}) async-start(bf16[8,96,2048]{2,1,0:T(8,128)(2,1)} %bitcast.426), calls=%async_computation.11 | async-start | bytes 6291456 | tf_op jit(solution)/shard_map/all_to_all | solution.py:332
  1217.9 46.3 %all-to-all-start.13 = ((bf16[8,96,2048]{2,1,0:T(8,128)(2,1)}), bf16[8,96,2048]{2,1,0:T(8,128)(2,1)}, u32[]{:S(2)}, u32[]{:S(2)}) async-start(bf16[8,96,2048]{2,1,0:T(8,128)(2,1)} %bitcast.423), calls=%async_computation.13 | async-start | bytes 6291456 | tf_op jit(solution)/shard_map/all_to_all | solution.py:332
  1264.2 44.9 %all-to-all-start.12 = ((bf16[8,96,2176]{2,1,0:T(8,128)(2,1)}), bf16[8,96,2176]{2,1,0:T(8,128)(2,1)}, u32[]{:S(2)}, u32[]{:S(2)}) async-start(bf16[8,96,2176]{2,1,0:T(8,128)(2,1)} %bitcast.452), calls=%async_computation.12 | async-start | bytes 6684672 | tf_op jit(solution)/shard_map/all_to_all | solution.py:332
  1309.1 51.8 %all-to-all-start.15 = ((bf16[8,96,2048]{2,1,0:T(8,128)(2,1)}), bf16[8,96,2048]{2,1,0:T(8,128)(2,1)}, u32[]{:S(2)}, u32[]{:S(2)}) async-start(bf16[8,96,2048]{2,1,0:T(8,128)(2,1)} %bitcast.421), calls=%async_computation.15 | async-start | bytes 6291456 | tf_op jit(solution)/shard_map/all_to_all | solution.py:332
  1360.9 44.5 %all-to-all-start.14 = ((bf16[8,96,2176]{2,1,0:T(8,128)(2,1)}), bf16[8,96,2176]{2,1,0:T(8,128)(2,1)}, u32[]{:S(2)}, u32[]{:S(2)}) async-start(bf16[8,96,2176]{2,1,0:T(8,128)(2,1)} %bitcast.451), calls=%async_computation.14 | async-start | bytes 6684672 | tf_op jit(solution)/shard_map/all_to_all | solution.py:332
  1368.9 33.6 %collective-permute-start.10 = (bf16[256,2176]{1,0:T(8,128)(2,1)S(1)}, bf16[256,2176]{1,0:T(8,128)(2,1)S(1)}, u32[]{:S(2)}, u32[]{:S(2)}) collective-permute-start(bf16[256,2176]{1,0:T(8,128)(2,1)S(1)} %pad_maximum_fusion.2), channel_id=1, source_target_pairs={{0,8},{8,16},{16,24},{24,0},{1,9},{9,17},{17,25},{25,1},{2,10},{10... | collective-permute-start | bytes 3342344 | tf_op jit(solution)/shard_map/ppermute | solution.py:345
  1405.4 44.5 %all-to-all-start.16 = ((bf16[8,96,2176]{2,1,0:T(8,128)(2,1)}), bf16[8,96,2176]{2,1,0:T(8,128)(2,1)}, u32[]{:S(2)}, u32[]{:S(2)}) async-start(bf16[8,96,2176]{2,1,0:T(8,128)(2,1)} %bitcast.450), calls=%async_computation.16 | async-start | bytes 6684672 | tf_op jit(solution)/shard_map/all_to_all | solution.py:332
  1409.9 126.3 %reduce-scatter.2.cloned.1.call-start = ((), (), s32[]{:S(2)}) async-start(), calls=%async_computation.26 | async-start | bytes 2396160 | tf_op jit(solution)/shard_map/reduce_scatter | solution.py:858
  1429.1 52.5 %collective-permute-start.12 = (bf16[256,2176]{1,0:T(8,128)(2,1)}, bf16[256,2176]{1,0:T(8,128)(2,1)}, u32[]{:S(2)}, u32[]{:S(2)}) collective-permute-start(bf16[256,2176]{1,0:T(8,128)(2,1)} %pad_maximum_fusion.3), channel_id=1, source_target_pairs={{0,16},{8,24},{16,0},{24,8},{1,17},{9,25},{17,1},{25,9},{2,18},{10... | collective-permute-start | bytes 3342344 | tf_op jit(solution)/shard_map/ppermute | solution.py:345
  1455.9 46.2 %collective-permute-start.14 = (bf16[256,2176]{1,0:T(8,128)(2,1)}, bf16[256,2176]{1,0:T(8,128)(2,1)}, u32[]{:S(2)}, u32[]{:S(2)}) collective-permute-start(bf16[256,2176]{1,0:T(8,128)(2,1)} %pad_maximum_fusion.4), channel_id=1, source_target_pairs={{0,24},{8,0},{16,8},{24,16},{1,25},{9,1},{17,9},{25,17},{2,26},{10... | collective-permute-start | bytes 3342344 | tf_op jit(solution)/shard_map/ppermute | solution.py:345
  1513.9 45.0 %all-to-all-start.17 = ((bf16[8,96,2048]{2,1,0:T(8,128)(2,1)}), bf16[8,96,2048]{2,1,0:T(8,128)(2,1)}, u32[]{:S(2)}, u32[]{:S(2)}) async-start(bf16[8,96,2048]{2,1,0:T(8,128)(2,1)} %bitcast.427), calls=%async_computation.17 | async-start | bytes 6291456 | tf_op jit(solution)/shard_map/all_to_all | solution.py:332
  1519.1 242.6 %all-gather.11.cloned.1.call-start = ((), (), s32[]{:S(2)}) async-start(), calls=%async_computation.27 | async-start | bytes 8785920 | tf_op jit(solution)/shard_map/all_gather | solution.py:859
  1570.9 57.8 %all-to-all-start.18 = ((bf16[8,96,2048]{2,1,0:T(8,128)(2,1)}), bf16[8,96,2048]{2,1,0:T(8,128)(2,1)}, u32[]{:S(2)}, u32[]{:S(2)}) async-start(bf16[8,96,2048]{2,1,0:T(8,128)(2,1)} %bitcast.457), calls=%async_computation.18 | async-start | bytes 6291456 | tf_op jit(solution)/shard_map/all_to_all | solution.py:332
  1597.7 294.0 %collective-permute-start.18 = (bf16[768,2048]{1,0:T(8,128)(2,1)}, bf16[768,2048]{1,0:T(8,128)(2,1)}, u32[]{:S(2)}, u32[]{:S(2)}) collective-permute-start(bf16[768,2048]{1,0:T(8,128)(2,1)} %add_convert_fusion.3), channel_id=1, source_target_pairs={{0,8},{8,16},{16,24},{24,0},{1,9},{9,17},{17,25},{25,1},{2,10},{10... | collective-permute-start | bytes 9437192 | tf_op jit(solution)/shard_map/ppermute | solution.py:345
  1599.9 196.9 %collective-permute-start.19 = (bf16[768,2048]{1,0:T(8,128)(2,1)}, bf16[768,2048]{1,0:T(8,128)(2,1)}, u32[]{:S(2)}, u32[]{:S(2)}) collective-permute-start(bf16[768,2048]{1,0:T(8,128)(2,1)} %add_convert_fusion.1), channel_id=1, source_target_pairs={{0,24},{8,0},{16,8},{24,16},{1,25},{9,1},{17,9},{25,17},{2,26},{10... | collective-permute-start | bytes 9437192 | tf_op jit(solution)/shard_map/ppermute | solution.py:345
  1675.8 42.7 %all-to-all-start.20 = ((bf16[8,96,2048]{2,1,0:T(8,128)(2,1)}), bf16[8,96,2048]{2,1,0:T(8,128)(2,1)}, u32[]{:S(2)}, u32[]{:S(2)}) async-start(bf16[8,96,2048]{2,1,0:T(8,128)(2,1)} %bitcast.454), calls=%async_computation.20 | async-start | bytes 6291456 | tf_op jit(solution)/shard_map/all_to_all | solution.py:332
  1694.3 66.2 %collective-permute-start.21 = (bf16[16,3584]{1,0:T(8,128)(2,1)S(1)}, bf16[16,3584]{1,0:T(8,128)(2,1)S(1)}, u32[]{:S(2)}, u32[]{:S(2)}) collective-permute-start(bf16[16,3584]{1,0:T(8,128)(2,1)S(1)} %get-tuple-element.166), channel_id=1, source_target_pairs={{0,8},{8,16},{16,24},{24,0},{1,9},{9,17},{17,25},{25,1},{2,10},{10... | collective-permute-start | bytes 344072 | tf_op jit(solution)/shard_map/ppermute | solution.py:345
  1697.0 63.6 %collective-permute-start.23 = (bf16[16,3584]{1,0:T(8,128)(2,1)S(1)}, bf16[16,3584]{1,0:T(8,128)(2,1)S(1)}, u32[]{:S(2)}, u32[]{:S(2)}) collective-permute-start(bf16[16,3584]{1,0:T(8,128)(2,1)S(1)} %get-tuple-element.167), channel_id=1, source_target_pairs={{0,24},{8,0},{16,8},{24,16},{1,25},{9,1},{17,9},{25,17},{2,26},{10... | collective-permute-start | bytes 344072 | tf_op jit(solution)/shard_map/ppermute | solution.py:345
  1698.7 62.3 %collective-permute-start.22 = (bf16[16,3584]{1,0:T(8,128)(2,1)S(1)}, bf16[16,3584]{1,0:T(8,128)(2,1)S(1)}, u32[]{:S(2)}, u32[]{:S(2)}) collective-permute-start(bf16[16,3584]{1,0:T(8,128)(2,1)S(1)} %get-tuple-element.168), channel_id=1, source_target_pairs={{0,16},{8,24},{16,0},{24,8},{1,17},{9,25},{17,1},{25,9},{2,18},{10... | collective-permute-start | bytes 344072 | tf_op jit(solution)/shard_map/ppermute | solution.py:345
  1730.4 42.5 %all-to-all-start.21 = ((bf16[8,96,2048]{2,1,0:T(8,128)(2,1)}), bf16[8,96,2048]{2,1,0:T(8,128)(2,1)}, u32[]{:S(2)}, u32[]{:S(2)}) async-start(bf16[8,96,2048]{2,1,0:T(8,128)(2,1)} %bitcast.456), calls=%async_computation.21 | async-start | bytes 6291456 | tf_op jit(solution)/shard_map/all_to_all | solution.py:332
  1735.0 245.9 %all-gather.17.cloned.1.call-start = ((), (), s32[]{:S(2)}) async-start(), calls=%async_computation.30 | async-start | bytes 3784704 | tf_op jit(solution)/shard_map/all_gather | solution.py:902
  1772.9 126.9 %all-to-all-start.23 = ((bf16[8,96,2048]{2,1,0:T(8,128)(2,1)}), bf16[8,96,2048]{2,1,0:T(8,128)(2,1)}, u32[]{:S(2)}, u32[]{:S(2)}) async-start(bf16[8,96,2048]{2,1,0:T(8,128)(2,1)} %bitcast.453), calls=%async_computation.23 | async-start | bytes 6291456 | tf_op jit(solution)/shard_map/all_to_all | solution.py:332
  1781.5 33.2 %collective-permute-start.17 = (bf16[256,2048]{1,0:T(8,128)(2,1)}, bf16[256,2048]{1,0:T(8,128)(2,1)S(1)}, u32[]{:S(2)}, u32[]{:S(2)}) collective-permute-start(bf16[256,2048]{1,0:T(8,128)(2,1)} %get-tuple-element.159), channel_id=1, source_target_pairs={{0,24},{8,0},{16,8},{24,16},{1,25},{9,1},{17,9},{25,17},{2,26},{10... | collective-permute-start | bytes 3145736 | tf_op jit(solution)/shard_map/ppermute | solution.py:345
  1785.9 105.7 %collective-permute-start.16 = (bf16[256,2048]{1,0:T(8,128)(2,1)}, bf16[256,2048]{1,0:T(8,128)(2,1)S(1)}, u32[]{:S(2)}, u32[]{:S(2)}) collective-permute-start(bf16[256,2048]{1,0:T(8,128)(2,1)} %get-tuple-element.160), channel_id=1, source_target_pairs={{0,16},{8,24},{16,0},{24,8},{1,17},{9,25},{17,1},{25,9},{2,18},{10... | collective-permute-start | bytes 3145736 | tf_op jit(solution)/shard_map/ppermute | solution.py:345
  1785.9 105.7 %collective-permute-start.15 = (bf16[256,2048]{1,0:T(8,128)(2,1)}, bf16[256,2048]{1,0:T(8,128)(2,1)}, u32[]{:S(2)}, u32[]{:S(2)}) collective-permute-start(bf16[256,2048]{1,0:T(8,128)(2,1)} %get-tuple-element.161), channel_id=1, source_target_pairs={{0,8},{8,16},{16,24},{24,0},{1,9},{9,17},{17,25},{25,1},{2,10},{10... | collective-permute-start | bytes 3145736 | tf_op jit(solution)/shard_map/ppermute | solution.py:345
  1899.8 56.9 %all-to-all-start.22 = ((bf16[8,96,2048]{2,1,0:T(8,128)(2,1)}), bf16[8,96,2048]{2,1,0:T(8,128)(2,1)}, u32[]{:S(2)}, u32[]{:S(2)}) async-start(bf16[8,96,2048]{2,1,0:T(8,128)(2,1)} %bitcast.428), calls=%async_computation.22 | async-start | bytes 6291456 | tf_op jit(solution)/shard_map/all_to_all | solution.py:332
  1908.2 48.6 %collective-permute-start.20 = (bf16[256,2048]{1,0:T(8,128)(2,1)S(1)}, bf16[256,2048]{1,0:T(8,128)(2,1)}, u32[]{:S(2)}, u32[]{:S(2)}) collective-permute-start(bf16[256,2048]{1,0:T(8,128)(2,1)S(1)} %convolution_convert_fusion.14), channel_id=1, source_target_pairs={{0,16},{8,24},{16,0},{24,8},{1,17},{9,25},{17,1},{25,9},{2,18},{10... | collective-permute-start | bytes 3145736 | tf_op jit(solution)/shard_map/ppermute | solution.py:345
  (164 other events, 1771.4 us)
Sparse Core Ops, SparseCore 0:
  9.6 264.2 all-gather.12
  276.4 158.7 all-gather.14
  436.8 273.5 all-gather.8
  1459.6 40.1 reduce-scatter.1
  1536.4 156.2 all-gather.10
  1761.9 114.7 all-gather.16

commit v5 on v4

--- a/solution.py
+++ b/solution.py
@@ -731,20 +731,24 @@
     pairs, pair_low = project_pairs(
         normed_parts, pair_weight, pair_down, pair_up, cosine_all, sine_all
     )
-    far = size // 2
-    inner_sent = [cut_share(mlp_in_weight[0], (spot - d) % size, size) for d in range(size)]
-    inner_parts = list(inner_sent)
-    inner_parts[far] = shifted(after(inner_sent[far], *early[1:]), far, size)
     output_own = after(output_weight[0], pair_weight, query_home, *early[1:])
     output_full = lax.all_gather(output_own, "seq", axis=0, tiled=True)
+    grad_rows = [grad_own.reshape(-1, width)]
+    for d in range(1, size):
+        sent = grad_parts[d] if d < 2 else after(grad_parts[d], pairs)
+        sent = tn(either(places[d]), sent).astype(bf16)
+        grad_rows.append(send_full(sent, experts, copies).reshape(-1, width))
     attended, output_slots, query_rot, totals = attend(
         query_home, place, query_low, query_upper, cosine, sine, pairs, bias
     )
 
     output_rows = send_cut(output_slots, experts, copies)
-    output_rows = after(output_rows, inner_parts[far])
+    output_rows = after(output_rows, *grad_rows[:3])
     output_parts = nn(output_rows.reshape(holders * capacity, -1), output_full).astype(bf16)
-    distances = [d for d in range(1, size) if d != far]
+    far = size // 2
+    distances = [d for d in range(1, size) if d != far] + ([far] if size > 1 else [])
+    inner_sent = [cut_share(mlp_in_weight[0], (spot - d) % size, size) for d in range(size)]
+    inner_parts = list(inner_sent)
     before = output_full
     for d in distances:
         before = inner_parts[d] = shifted(after(inner_sent[d], before), d, size)
@@ -760,17 +764,17 @@
     lanes = jnp.pad(jnp.concatenate(halves(mlp_gates), axis=1), ((0, 0), (0, 124)))
     packet = jnp.concatenate([normed_mlp, lanes], axis=1)
     packet = after(packet, *(inner_parts[d] for d in distances[:1]))
-    packets = [shifted(packet, d, size) for d in range(size)]
+    packet_all = lax.all_gather(packet, "seq", axis=0, tiled=True)
+    packets = [packet] + [
+        lax.dynamic_slice_in_dim(packet_all, (spot + d) % size * rows, rows, 0)
+        for d in range(1, size)
+    ]
     gates_there = [
         (p[:, width : width + 2].astype(f32) + p[:, width + 2 : width + 4].astype(f32)).T.reshape(-1, 1)
         for p in packets
     ]
     combines = [either((places[d].astype(f32) * gates_there[d]).astype(bf16)) for d in range(size)]
     order = list(range(size))
-    grad_rows = [grad_own.reshape(-1, width)]
-    for d in order[1:]:
-        sent = tn(either(places[d]), after(grad_parts[d], output_home)).astype(bf16)
-        grad_rows.append(send_full(sent, experts, copies).reshape(-1, width))
     outer_codes = [nt(got, outer_up).astype(bf16) * mask for got in grad_rows]
     hidden_grads = [
         (nt(got, outer_full) + nn(code, outer_down)).astype(bf16)
@@ -797,13 +801,13 @@
         row_back = jnp.concatenate([row_sum, lanes], axis=1)
         return home, shifted(row_back.astype(bf16), -d % size, size) if d else row_back
 
-    got_rows = [send_rows(0, *grad_rows[:2])]
+    got_rows = [send_rows(0)]
+    for d in order[1:]:
+        earlier = [inner_parts[k] for k in distances[:-1]] if d == 1 else []
+        got_rows.append(send_rows(d, got_rows[-1], *earlier))
     kept = [work(0, got_rows[0])]
     row_home, row_total = rows_home(0, kept[0][0])
     row_backs = [row_total]
-    for d in order[1:]:
-        earlier = grad_rows[2:] + [inner_parts[k] for k in distances] if d == 1 else [got_rows[-1]]
-        got_rows.append(send_rows(d, row_home, *earlier))
     for d in order[1:]:
         kept.append(work(d, after(got_rows[d], kept[-1][0])))
         row_grad = kept[d][0]
@@ -817,18 +821,17 @@
     mlp_gate_grad = gate_sum.reshape(rows, 2, 2).sum(2)
     mlp_logit_grad = gate_back(mlp_gates, mlp_hits, mlp_gate_grad)
 
-    down_near, down_parts, down_sent, sums = [], [], [], None
+    down_near, down_parts, down_made, sums = [], [], [], None
     for d in order:
         _, activated, pre_grad, code, back = kept[d]
         outer_low = nt(activated, outer_down).astype(bf16) * mask
         down = (nn(activated, outer_full) + nn(outer_low, outer_up)).astype(bf16)
+        down_made.append(down)
         if d in (0, 1, size - 1):
             if d:
-                down_sent.append(down)
                 down = shifted(after(down, row_home), -d % size, size)
             down_near.append(down)
         else:
-            down_sent.append(down)
             down_parts.append((d, down))
         scale = gate_slots[:, d, :].reshape(-1, 1)
 
@@ -874,11 +877,11 @@
     normed_mlp_grad = row_total + nt(mlp_logit_grad.astype(bf16), mlp_router_weight)
     middle_grad = norm_back(middle, middle_scale, mlp_gain, normed_mlp_grad)
     middle_grad = middle_grad + out_grad[0].astype(f32)
-    middle_low = middle_grad.astype(bf16)
+    middle_low = after(middle_grad.astype(bf16), *down_made)
     branch_rows = send_full(tn(place_any, middle_low).astype(bf16), experts, copies)
     head_parts = nt(branch_rows.reshape(-1, width), output_full).astype(bf16)
     head_home = home_join(head_parts.reshape(holders, capacity, -1), experts, copies)
-    head_home = after(head_home, mlp_own, *down_sent)
+    head_home = after(head_home, mlp_own)
     gate_grad = jnp.sum(middle_grad[None] * branch, axis=2).T
     logit_grad = gate_back(gates, hits, gate_grad)
     gate_column = gates.T.reshape(-1, 1)
@@ -946,18 +949,20 @@
     back_parts = [
         shifted(normed_grads[d * rows : (d + 1) * rows], -d % size, size) for d in range(1, size)
     ]
-    normed_grad = normed_grads[:rows].astype(f32) + sum(back.astype(f32) for back in back_parts)
+    down_near = sum(after(down, *back_parts).astype(f32) for down in down_near).astype(bf16)
+    down_near = after(down_near, query_back).reshape(holders, capacity, width)
+    down_home = home_add(down_near, experts, copies)
+    own_back = after(normed_grads[:rows], inner_up_grad)
+    normed_grad = own_back.astype(f32) + sum(back.astype(f32) for back in back_parts)
     input_parts = nt(query_back.reshape(holders * capacity, -1), query_full).astype(bf16)
     input_home = home_add(input_parts.reshape(holders, capacity, width), experts, copies)
     normed_grad = normed_grad + nn(place_any, input_home) + nn(query_low_grad, query_lower)
     normed_grad = normed_grad + nt(logit_grad.astype(bf16), router_weight)
     input_grad = norm_back(inputs, input_scale, norm_gain, normed_grad) + middle_grad
 
-    down_near = sum(after(down, input_home, *back_parts).astype(f32) for down in down_near)
-    down_near = down_near.astype(bf16).reshape(holders, capacity, width)
-    down_total = nn(combines[0], home_add(down_near, experts, copies))
+    down_total = nn(combines[0], down_home)
     for d, down in down_parts:
-        down = after(down, query_back).reshape(holders, capacity, width)
+        down = after(down, input_home).reshape(holders, capacity, width)
         home = home_add(down, experts, copies)
         down_total = down_total + shifted(nn(combines[d], home).astype(bf16), -d % size, size).astype(f32)
     result = (middle + down_total).astype(bf16)

time: 2010 us -> 1920 us (0.955)
  waiting for transfers between devices: 1020 us -> 958 us
  starting transfers between devices: 217 us -> 178 us
    ppermute x24 -> x21, waiting for transfers between devices: 735 us -> 641 us  [shifted(): lax.ppermute(array, 'seq', [(k, (k - shift) % size) for k in range(size)])]
    ppermute x24 -> x21, starting transfers between devices: 105 us -> 66.7 us  [shifted(): lax.ppermute(array, 'seq', [(k, (k - shift) % size) for k in range(size)])]
    all_to_all x24, waiting for transfers between devices: 262 us -> 287 us  [exchange(): return lax.all_to_all(buffer, 'dp', split_axis=0, concat_axis=0, tiled=True)]
    unnamed x373 -> x357, local copies, waits for them, and re-layouts: 45.3 us -> 49.3 us
  transfers between devices with their start and end apart: 54 -> 52, of which waited for: 31 -> 27; matrix products, arithmetic and copies ran while one was open for 20% -> 21% of each run, Pallas kernels for 14% -> 15%
where the time goes in v5:
time: 1920 us; the launch traced here: 1910 us
  waiting for transfers between devices  958 us (50%)
  matrix products  299 us (16%)
  Pallas kernels  293 us (15%)
  starting transfers between devices  178 us (9%)
  local copies, waits for them, and re-layouts  117 us (6%)
  other arithmetic  44.7 us (2%)
    ppermute x21, waiting for transfers between devices, shifted(): lax.ppermute(array, 'seq', [(k, (k - shift) % size) for k in range(size)])  641 us
    dot_general x93, matrix products, product(): lax.dot_general(left, right, (((left_dim,), (right_dim,)), ((), ())), pre...  299 us
    all_to_all x24, waiting for transfers between devices, exchange(): return lax.all_to_all(buffer, 'dp', split_axis=0, concat_axis=0, tiled=True)  287 us
    pallas_call x4, Pallas kernels, expert_block(): pl.pallas_call(functools.partial(expert_kernel, size, share), grid_spec=p...  124 us
    all_to_all x24, starting transfers between devices, exchange(): return lax.all_to_all(buffer, 'dp', split_axis=0, concat_axis=0, tiled=True)  111 us
    ppermute x21, starting transfers between devices, shifted(): lax.ppermute(array, 'seq', [(k, (k - shift) % size) for k in range(size)])  66.7 us
    unnamed x357, local copies, waits for them, and re-layouts  49.3 us
    pallas_call x1, Pallas kernels, attend_back(): pl.pallas_call(functools.partial(attend_back_kernel, 1.0 / math.sqrt(HD))...  44.2 us
  transfers between devices with their start and end apart: 52, of which 27 were waited for; matrix products, arithmetic and copies ran while one was open for 21% of the time, Pallas kernels for 15%

profile of v5, /device:TPU:0, one launch (start us, length us, event | category | flops | bytes accessed | tf_op | source)
XLA Modules:
  0.0 1908.5 jit_solution(12416008226543329163)
XLA Ops:
  9.2 5.2 all-to-all-start.3
  35.1 28.7 %all-to-all-done = bf16[8,96,2048]{2,1,0:T(8,128)(2,1)} async-done(((bf16[8,96,2048]{2,1,0:T(8,128)(2,1)}), bf16[8,96,2048]{2,1,0:T(8,128)(2,1)}, u32[]{:S(2)}, u32[]{:S(2)}) %all-to-all-start) | async-done | bytes 3145760 | tf_op jit(solution)/shard_map/all_to_all | solution.py:332
  63.8 4.6 all-to-all-start.2
  75.4 67.3 %collective-permute-done.2 = bf16[384,2048]{1,0:T(8,128)(2,1)} collective-permute-done((bf16[384,2048]{1,0:T(8,128)(2,1)}, bf16[384,2048]{1,0:T(8,128)(2,1)}, u32[]{:S(2)}, u32[]{:S(2)}) %collective-permute-start.2) | collective-permute-done | bytes 1572896 | tf_op jit(solution)/shard_map/ppermute | solution.py:345
  146.8 104.6 %collective-permute-done.1 = bf16[384,2048]{1,0:T(8,128)(2,1)} collective-permute-done((bf16[384,2048]{1,0:T(8,128)(2,1)}, bf16[384,2048]{1,0:T(8,128)(2,1)}, u32[]{:S(2)}, u32[]{:S(2)}) %collective-permute-start.1) | collective-permute-done | bytes 1572896 | tf_op jit(solution)/shard_map/ppermute | solution.py:345
  282.7 11.8 convolution_convert_fusion.3
  300.4 40.3 %collective-permute-start.5 = (bf16[256,2176]{1,0:T(8,128)(2,1)S(1)}, bf16[256,2176]{1,0:T(8,128)(2,1)}, u32[]{:S(2)}, u32[]{:S(2)}) collective-permute-start(bf16[256,2176]{1,0:T(8,128)(2,1)S(1)} %fusion.98), channel_id=1, source_target_pairs={{0,8},{8,16},{16,24},{24,0},{1,9},{9,17},{17,25},{25,1},{2,10},{10... | collective-permute-start | bytes 3342344 | tf_op jit(solution)/shard_map/ppermute | solution.py:345
  344.4 25.0 %collective-permute-done.5 = bf16[256,2176]{1,0:T(8,128)(2,1)} collective-permute-done((bf16[256,2176]{1,0:T(8,128)(2,1)S(1)}, bf16[256,2176]{1,0:T(8,128)(2,1)}, u32[]{:S(2)}, u32[]{:S(2)}) %collective-permute-start.5) | collective-permute-done | bytes 1114144 | tf_op jit(solution)/shard_map/ppermute | solution.py:345
  369.4 47.4 %collective-permute-done.4 = bf16[256,2176]{1,0:T(8,128)(2,1)} collective-permute-done((bf16[256,2176]{1,0:T(8,128)(2,1)S(1)}, bf16[256,2176]{1,0:T(8,128)(2,1)}, u32[]{:S(2)}, u32[]{:S(2)}) %collective-permute-start.4) | collective-permute-done | bytes 1114144 | tf_op jit(solution)/shard_map/ppermute | solution.py:345
  416.9 18.3 all-gather.18.cloned.1.call-done
  444.1 4.7 all-to-all-start.5
  456.8 31.6 %pairs.1 = (bf16[1024,4096]{1,0:T(8,128)(2,1)}, bf16[1024,16]{1,0:T(8,128)(2,1)S(1)}) custom-call(bf16[256,2048]{1,0:T(8,128)(2,1)S(1)} %fusion.62.refs_0_, bf16[256,2048]{1,0:T(8,128)(2,1)S(1)} %copy-done.22, bf16[256,2048]{1,0:T(8,128)(2,1)S(1)} %copy-done.21, bf16[256,2048]{1,0:T(8,128)(2,1)S(1)} %copy-done.20, bf16[8,2048,512]{2,1,0:T(8,128)(2,1)} %bitcast.504, ...), custom_call_target="tpu_custom_call" | custom-call | flops 17179869184 | bytes 16777216 | tf_op jit(solution)/shard_map/pairs/pallas_call | solution.py:75
  500.8 33.7 %attend.1 = (bf16[512,2048]{1,0:T(8,128)(2,1)S(1)}, bf16[768,2048]{1,0:T(8,128)(2,1)}, bf16[512,2048]{1,0:T(8,128)(2,1)}, f32[16,512,1]{2,1,0:T(8,128)}) custom-call(bf16[768,2048]{1,0:T(8,128)(2,1)} %bitcast.8.home_ref, bf16[512,768]{1,0:T(8,128)(2,1)S(1)} %fusion.88.place_ref, bf16[256,16]{1,0:T(8,128)(2,1)S(1)} %convolution_convert_fusion.23.low_ref, ...), custom_call_target="tpu_custom_call" | custom-call | flops 4294967296 | bytes 8388608 | tf_op jit(solution)/shard_map/attend/pallas_call | solution.py:194
  536.5 4.6 all-to-all-start.4
  541.6 37.4 %all-to-all-done.4 = bf16[8,96,2048]{2,1,0:T(8,128)(2,1)} async-done(((bf16[8,96,2048]{2,1,0:T(8,128)(2,1)}), bf16[8,96,2048]{2,1,0:T(8,128)(2,1)}, u32[]{:S(2)}, u32[]{:S(2)}) %all-to-all-start.4) | async-done | bytes 3145760 | tf_op jit(solution)/shard_map/all_to_all | solution.py:332
  579.0 9.9 all-gather.10.cloned.1.call-done
  588.9 11.8 convolution_convert_fusion.2
  626.1 6.3 squeeze.95
  632.5 6.8 dynamic-slice_reduce_fusion
  659.7 53.4 %collective-permute-done.6.refs_1_ = bf16[512,2816]{1,0:T(8,128)(2,1)} collective-permute-done((bf16[512,2816]{1,0:T(8,128)(2,1)}, bf16[512,2816]{1,0:T(8,128)(2,1)}, u32[]{:S(2)}, u32[]{:S(2)}) %collective-permute-start.6) | collective-permute-done | bytes 2883616 | tf_op jit(solution)/shard_map/ppermute | solution.py:345
  721.7 8.9 fusion.14
  739.0 7.1 fusion.10
  748.2 11.4 all-to-all-done.15
  765.5 4.7 all-to-all-start.8
  770.2 89.5 %collective-permute-done.7.refs_3_ = bf16[512,2816]{1,0:T(8,128)(2,1)} collective-permute-done((bf16[512,2816]{1,0:T(8,128)(2,1)}, bf16[512,2816]{1,0:T(8,128)(2,1)}, u32[]{:S(2)}, u32[]{:S(2)}) %collective-permute-start.7) | collective-permute-done | bytes 2883616 | tf_op jit(solution)/shard_map/ppermute | solution.py:345
  859.7 8.5 fusion.6
  882.8 102.2 %collective-permute-done.8.refs_2_ = bf16[512,2816]{1,0:T(8,128)(2,1)} collective-permute-done((bf16[512,2816]{1,0:T(8,128)(2,1)}, bf16[512,2816]{1,0:T(8,128)(2,1)}, u32[]{:S(2)}, u32[]{:S(2)}) %collective-permute-start.8) | collective-permute-done | bytes 2883616 | tf_op jit(solution)/shard_map/ppermute | solution.py:345
  986.6 30.9 %experts.4 = (bf16[768,2176]{1,0:T(8,128)(2,1)}, bf16[768,1408]{1,0:T(8,128)(2,1)S(1)}, bf16[768,2816]{1,0:T(8,128)(2,1)}, bf16[768,128]{1,0:T(8,128)(2,1)S(1)}, bf16[768,128]{1,0:T(8,128)(2,1)S(1)}) custom-call(s32[1]{0:T(128)} %bitcast.43.spot_ref, bf16[768,2048]{1,0:T(8,128)(2,1)} %bitcast.45.x_ref, bf16[768,1408]{1,0:T(8,128)(2,1)S(1)} %copy-done.19, ...), custom_call_target="tpu_custom_call" | custom-call | flops 17716740096 | bytes 27262976 | tf_op jit(solution)/shard_map/experts/pallas_call | solution.py:607
  1018.8 4.7 all-to-all-start.9
  1026.5 8.6 fusion.8
  1046.5 17.0 all-to-all-done.9
  1068.0 9.9 add_convert_fusion.4
  1091.9 13.9 all-to-all-done.10
  1110.0 4.7 all-to-all-start.12
  1116.3 31.0 %experts.5 = (bf16[768,2176]{1,0:T(8,128)(2,1)}, bf16[768,1408]{1,0:T(8,128)(2,1)S(1)}, bf16[768,2816]{1,0:T(8,128)(2,1)}, bf16[768,128]{1,0:T(8,128)(2,1)S(1)}, bf16[768,128]{1,0:T(8,128)(2,1)S(1)}) custom-call(s32[1]{0:T(128)} %bitcast.43.spot_ref, bf16[768,2048]{1,0:T(8,128)(2,1)} %bitcast.59.x_ref, bf16[768,1408]{1,0:T(8,128)(2,1)S(1)} %copy-done.17, ...), custom_call_target="tpu_custom_call" | custom-call | flops 17716740096 | bytes 27262976 | tf_op jit(solution)/shard_map/experts/pallas_call | solution.py:607
  1160.3 6.5 add_convert_fusion.3
  1166.8 4.9 all-to-all-start.11
  1173.4 31.1 %experts.6 = (bf16[768,2176]{1,0:T(8,128)(2,1)}, bf16[768,1408]{1,0:T(8,128)(2,1)S(1)}, bf16[768,2816]{1,0:T(8,128)(2,1)}, bf16[768,128]{1,0:T(8,128)(2,1)S(1)}, bf16[768,128]{1,0:T(8,128)(2,1)S(1)}) custom-call(s32[1]{0:T(128)} %bitcast.43.spot_ref, bf16[768,2048]{1,0:T(8,128)(2,1)} %bitcast.65.x_ref, bf16[768,1408]{1,0:T(8,128)(2,1)S(1)} %copy-done.18, ...), custom_call_target="tpu_custom_call" | custom-call | flops 17716740096 | bytes 27262976 | tf_op jit(solution)/shard_map/experts/pallas_call | solution.py:607
  1229.9 9.9 add_convert_fusion.2
  1245.4 19.3 %all-to-all-done.14 = bf16[8,96,2048]{2,1,0:T(8,128)(2,1)} async-done(((bf16[8,96,2048]{2,1,0:T(8,128)(2,1)}), bf16[8,96,2048]{2,1,0:T(8,128)(2,1)}, u32[]{:S(2)}, u32[]{:S(2)}) %all-to-all-start.14) | async-done | bytes 3145760 | tf_op jit(solution)/shard_map/all_to_all | solution.py:332
  1264.7 4.7 all-to-all-start.13
  1271.0 31.2 %experts.7 = (bf16[768,2176]{1,0:T(8,128)(2,1)}, bf16[768,1408]{1,0:T(8,128)(2,1)S(1)}, bf16[768,2816]{1,0:T(8,128)(2,1)}, bf16[768,128]{1,0:T(8,128)(2,1)S(1)}, bf16[768,128]{1,0:T(8,128)(2,1)S(1)}) custom-call(s32[1]{0:T(128)} %bitcast.43.spot_ref, bf16[768,2048]{1,0:T(8,128)(2,1)} %bitcast.71.x_ref, bf16[768,1408]{1,0:T(8,128)(2,1)S(1)} %copy-done.16, ...), custom_call_target="tpu_custom_call" | custom-call | flops 17716740096 | bytes 27262976 | tf_op jit(solution)/shard_map/experts/pallas_call | solution.py:607
  1315.4 4.6 all-to-all-start.16
  1333.6 32.2 %all-to-all-done.16 = bf16[8,96,2176]{2,1,0:T(8,128)(2,1)} async-done(((bf16[8,96,2176]{2,1,0:T(8,128)(2,1)}), bf16[8,96,2176]{2,1,0:T(8,128)(2,1)}, u32[]{:S(2)}, u32[]{:S(2)}) %all-to-all-start.16) | async-done | bytes 3342368 | tf_op jit(solution)/shard_map/all_to_all | solution.py:332
  1373.2 10.7 add_convert_fusion.1
  1385.4 23.7 %collective-permute-done.11 = bf16[256,2176]{1,0:T(8,128)(2,1)S(1)} collective-permute-done((bf16[256,2176]{1,0:T(8,128)(2,1)S(1)}, bf16[256,2176]{1,0:T(8,128)(2,1)S(1)}, u32[]{:S(2)}, u32[]{:S(2)}) %collective-permute-start.11) | collective-permute-done | bytes 1114144 | tf_op jit(solution)/shard_map/ppermute | solution.py:345
  1426.4 41.2 %all-to-all-done.17 = bf16[8,96,2048]{2,1,0:T(8,128)(2,1)} async-done(((bf16[8,96,2048]{2,1,0:T(8,128)(2,1)}), bf16[8,96,2048]{2,1,0:T(8,128)(2,1)}, u32[]{:S(2)}, u32[]{:S(2)}) %all-to-all-start.17) | async-done | bytes 3145760 | tf_op jit(solution)/shard_map/all_to_all | solution.py:332
  1467.6 11.9 convolution_convert_fusion.1
  1479.6 4.6 all-to-all-start.18
  1502.1 32.7 %all-to-all-done.18 = bf16[8,96,2048]{2,1,0:T(8,128)(2,1)} async-done(((bf16[8,96,2048]{2,1,0:T(8,128)(2,1)}), bf16[8,96,2048]{2,1,0:T(8,128)(2,1)}, u32[]{:S(2)}, u32[]{:S(2)}) %all-to-all-start.18) | async-done | bytes 3145760 | tf_op jit(solution)/shard_map/all_to_all | solution.py:332
  1537.9 44.2 %attend_back.1 = (bf16[1024,2048]{1,0:T(8,128)(2,1)}, bf16[1024,2048]{1,0:T(8,128)(2,1)}, bf16[768,2048]{1,0:T(8,128)(2,1)}, bf16[256,2048]{1,0:T(8,128)(2,1)S(1)}) custom-call(bf16[512,2048]{1,0:T(8,128)(2,1)} %get-tuple-element.95.query_ref, bf16[1024,4096]{1,0:T(8,128)(2,1)} %get-tuple-element.83.key_ref.value_ref, ...), custom_call_target="tpu_custom_call" | custom-call | flops 10737418240 | bytes 16777216 | tf_op jit(solution)/shard_map/attend_back/pallas_call | solution.py:289
  1599.1 25.5 %all-to-all-done.20 = bf16[8,96,2048]{2,1,0:T(8,128)(2,1)} async-done(((bf16[8,96,2048]{2,1,0:T(8,128)(2,1)}), bf16[8,96,2048]{2,1,0:T(8,128)(2,1)}, u32[]{:S(2)}, u32[]{:S(2)}) %all-to-all-start.20) | async-done | bytes 3145760 | tf_op jit(solution)/shard_map/all_to_all | solution.py:332
  1624.6 12.0 convolution_convert_fusion
  1647.4 23.4 %pair_back.1 = bf16[1024,2048]{1,0:T(8,128)(2,1)S(1)} custom-call(bf16[1024,2048]{1,0:T(8,128)(2,1)} %get-tuple-element.126.key_ref, bf16[1024,2048]{1,0:T(8,128)(2,1)} %get-tuple-element.127.value_ref, bf16[8,2048,512]{2,1,0:T(8,128)(2,1)} %bitcast.505, bf16[1024,16]{1,0:T(8,128)(2,1)S(1)} %fusion.89.low_ref, bf16[16,2048]{1,0:T(8,128)(2,1)S(1)} %copy-done.41), custom_call_target="tpu_custom_call" | custom-call | flops 17179869184 | bytes 16777216 | tf_op jit(solution)/shard_map/pair_back/pallas_call | solution.py:129
  1672.9 6.1 all-to-all-done.22
  1690.2 25.3 %collective-permute-done.14 = bf16[256,2048]{1,0:T(8,128)(2,1)} collective-permute-done((bf16[256,2048]{1,0:T(8,128)(2,1)S(1)}, bf16[256,2048]{1,0:T(8,128)(2,1)}, u32[]{:S(2)}, u32[]{:S(2)}) %collective-permute-start.14) | collective-permute-done | bytes 1048608 | tf_op jit(solution)/shard_map/ppermute | solution.py:345
  1715.5 79.3 %collective-permute-done.13 = bf16[256,2048]{1,0:T(8,128)(2,1)} collective-permute-done((bf16[256,2048]{1,0:T(8,128)(2,1)S(1)}, bf16[256,2048]{1,0:T(8,128)(2,1)}, u32[]{:S(2)}, u32[]{:S(2)}) %collective-permute-start.13) | collective-permute-done | bytes 1048608 | tf_op jit(solution)/shard_map/ppermute | solution.py:345
  1794.8 6.6 add_convert_fusion
  1801.5 5.1 all-to-all-start.21
  1823.0 21.6 %all-to-all-done.21 = bf16[8,96,2048]{2,1,0:T(8,128)(2,1)} async-done(((bf16[8,96,2048]{2,1,0:T(8,128)(2,1)}), bf16[8,96,2048]{2,1,0:T(8,128)(2,1)}, u32[]{:S(2)}, u32[]{:S(2)}) %all-to-all-start.21) | async-done | bytes 3145760 | tf_op jit(solution)/shard_map/all_to_all | solution.py:332
  1844.5 18.8 collective-permute-done.17
  1863.3 4.8 fusion.105
  1868.1 19.9 %unpack.1 = (f32[8,16,11264]{2,1,0:T(8,128)}, f32[8,16,5632]{2,1,0:T(8,128)}, f32[8,16,2048]{2,1,0:T(8,128)}, f32[8,16,2048]{2,1,0:T(8,128)}) custom-call(bf16[4,8,16,8320]{3,2,1,0:T(8,128)(2,1)} %bitcast.433), custom_call_target="tpu_custom_call" | custom-call | bytes 32243712 | tf_op jit(solution)/shard_map/unpack/pallas_call | solution.py:485
  1895.2 6.0 gather_adapters.1
  (662 shorter events, 415.8 us)
Async XLA Ops:
  7.2 431.2 %copy-start = (bf16[8,16,4096]{2,1,0:T(8,128)(2,1)S(1)}, bf16[8,16,4096]{2,1,0:T(8,128)(2,1)}, u32[]{:S(2)}) copy-start(bf16[8,16,4096]{2,1,0:T(8,128)(2,1)} %param.37) | copy-start | bytes 3145732
  7.2 268.5 %all-gather.16.cloned.1.call-start = ((), (), s32[]{:S(2)}) async-start(), calls=%async_computation.29 | async-start | bytes 10485760 | tf_op jit(solution)/shard_map/all_gather | solution.py:685
  9.2 12.2 all-to-all-start.3
  18.6 522.5 %copy-start.2 = (bf16[256,2048]{1,0:T(8,128)(2,1)}, bf16[256,2048]{1,0:T(8,128)(2,1)S(1)}, u32[]{:S(2)}) copy-start(bf16[256,2048]{1,0:T(8,128)(2,1)S(1)} %fusion.62.refs_0_) | copy-start | bytes 3145732
  21.4 42.4 %all-to-all-start = ((bf16[8,96,2048]{2,1,0:T(8,128)(2,1)}), bf16[8,96,2048]{2,1,0:T(8,128)(2,1)}, u32[]{:S(2)}, u32[]{:S(2)}) async-start(bf16[8,96,2048]{2,1,0:T(8,128)(2,1)} %bitcast.425), calls=%async_computation | async-start | bytes 6291456 | tf_op jit(solution)/shard_map/all_to_all | solution.py:332
  63.8 212.0 %all-to-all-start.2 = ((bf16[8,96,2048]{2,1,0:T(8,128)(2,1)}), bf16[8,96,2048]{2,1,0:T(8,128)(2,1)}, u32[]{:S(2)}, u32[]{:S(2)}) async-start(bf16[8,96,2048]{2,1,0:T(8,128)(2,1)} %bitcast.421), calls=%async_computation.2 | async-start | bytes 6291456 | tf_op jit(solution)/shard_map/all_to_all | solution.py:332
  68.4 366.8 %all-gather.18.cloned.1.call-start = ((), (), s32[]{:S(2)}) async-start(), calls=%async_computation.30 | async-start | bytes 18874368 | tf_op jit(solution)/shard_map/all_gather | solution.py:696
  69.7 73.0 %collective-permute-start.2 = (bf16[384,2048]{1,0:T(8,128)(2,1)}, bf16[384,2048]{1,0:T(8,128)(2,1)}, u32[]{:S(2)}, u32[]{:S(2)}) collective-permute-start(bf16[384,2048]{1,0:T(8,128)(2,1)} %pad_maximum_fusion.1), channel_id=1, source_target_pairs={{0,8},{8,16},{16,24},{24,0},{1,9},{9,17},{17,25},{25,1},{2,10},{10... | collective-permute-start | bytes 4718600 | tf_op jit(solution)/shard_map/ppermute | solution.py:345
  71.4 180.0 %collective-permute-start.1 = (bf16[384,2048]{1,0:T(8,128)(2,1)}, bf16[384,2048]{1,0:T(8,128)(2,1)}, u32[]{:S(2)}, u32[]{:S(2)}) collective-permute-start(bf16[384,2048]{1,0:T(8,128)(2,1)} %pad_maximum_fusion.1), channel_id=1, source_target_pairs={{0,16},{8,24},{16,0},{24,8},{1,17},{9,25},{17,1},{25,9},{2,18},{10... | collective-permute-start | bytes 4718600 | tf_op jit(solution)/shard_map/ppermute | solution.py:345
  74.0 184.6 %collective-permute-start = (bf16[384,2048]{1,0:T(8,128)(2,1)}, bf16[384,2048]{1,0:T(8,128)(2,1)}, u32[]{:S(2)}, u32[]{:S(2)}) collective-permute-start(bf16[384,2048]{1,0:T(8,128)(2,1)} %pad_maximum_fusion.1), channel_id=1, source_target_pairs={{0,24},{8,0},{16,8},{24,16},{1,25},{9,1},{17,9},{25,17},{2,26},{10... | collective-permute-start | bytes 4718600 | tf_op jit(solution)/shard_map/ppermute | solution.py:345
  75.4 564.9 %copy-start.42 = (s32[8]{0:T(128)}, s32[8]{0:T(128)S(1)}, u32[]{:S(2)}) copy-start(s32[8]{0:T(128)S(1)} %slice_reduce_fusion.4.ids_ref) | copy-start | bytes 100
  294.5 122.4 %all-to-all-start.1 = ((bf16[8,96,2048]{2,1,0:T(8,128)(2,1)}), bf16[8,96,2048]{2,1,0:T(8,128)(2,1)}, u32[]{:S(2)}, u32[]{:S(2)}) async-start(bf16[8,96,2048]{2,1,0:T(8,128)(2,1)} %bitcast.461), calls=%async_computation.1 | async-start | bytes 6291456 | tf_op jit(solution)/shard_map/all_to_all | solution.py:332
  299.0 289.9 %all-gather.10.cloned.1.call-start = ((), (), s32[]{:S(2)}) async-start(), calls=%async_computation.25 | async-start | bytes 10485760 | tf_op jit(solution)/shard_map/all_gather | solution.py:735
  300.4 69.1 %collective-permute-start.5 = (bf16[256,2176]{1,0:T(8,128)(2,1)S(1)}, bf16[256,2176]{1,0:T(8,128)(2,1)}, u32[]{:S(2)}, u32[]{:S(2)}) collective-permute-start(bf16[256,2176]{1,0:T(8,128)(2,1)S(1)} %fusion.98), channel_id=1, source_target_pairs={{0,8},{8,16},{16,24},{24,0},{1,9},{9,17},{17,25},{25,1},{2,10},{10... | collective-permute-start | bytes 3342344 | tf_op jit(solution)/shard_map/ppermute | solution.py:345
  340.6 76.2 %collective-permute-start.4 = (bf16[256,2176]{1,0:T(8,128)(2,1)S(1)}, bf16[256,2176]{1,0:T(8,128)(2,1)}, u32[]{:S(2)}, u32[]{:S(2)}) collective-permute-start(bf16[256,2176]{1,0:T(8,128)(2,1)S(1)} %fusion.98), channel_id=1, source_target_pairs={{0,16},{8,24},{16,0},{24,8},{1,17},{9,25},{17,1},{25,9},{2,18},{10... | collective-permute-start | bytes 3342344 | tf_op jit(solution)/shard_map/ppermute | solution.py:345
  344.4 72.4 %collective-permute-start.3 = (bf16[256,2176]{1,0:T(8,128)(2,1)S(1)}, bf16[256,2176]{1,0:T(8,128)(2,1)}, u32[]{:S(2)}, u32[]{:S(2)}) collective-permute-start(bf16[256,2176]{1,0:T(8,128)(2,1)S(1)} %fusion.98), channel_id=1, source_target_pairs={{0,24},{8,0},{16,8},{24,16},{1,25},{9,1},{17,9},{25,17},{2,26},{10... | collective-permute-start | bytes 3342344 | tf_op jit(solution)/shard_map/ppermute | solution.py:345
  444.1 47.0 %all-to-all-start.5 = ((bf16[8,96,2048]{2,1,0:T(8,128)(2,1)}), bf16[8,96,2048]{2,1,0:T(8,128)(2,1)}, u32[]{:S(2)}, u32[]{:S(2)}) async-start(bf16[8,96,2048]{2,1,0:T(8,128)(2,1)} %bitcast.428), calls=%async_computation.5 | async-start | bytes 6291456 | tf_op jit(solution)/shard_map/all_to_all | solution.py:332
  451.6 425.1 %copy-start.130 = (s32[512]{0:T(512)}, s32[512]{0:T(512)S(1)}, u32[]{:S(2)}) copy-start(s32[512]{0:T(512)S(1)} %convert_add_fusion.2) | copy-start | bytes 6148
  491.2 45.3 %all-to-all-start.6 = ((bf16[8,96,2048]{2,1,0:T(8,128)(2,1)}), bf16[8,96,2048]{2,1,0:T(8,128)(2,1)}, u32[]{:S(2)}, u32[]{:S(2)}) async-start(bf16[8,96,2048]{2,1,0:T(8,128)(2,1)} %bitcast.426), calls=%async_computation.6 | async-start | bytes 6291456 | tf_op jit(solution)/shard_map/all_to_all | solution.py:332
  536.5 42.5 %all-to-all-start.4 = ((bf16[8,96,2048]{2,1,0:T(8,128)(2,1)}), bf16[8,96,2048]{2,1,0:T(8,128)(2,1)}, u32[]{:S(2)}, u32[]{:S(2)}) async-start(bf16[8,96,2048]{2,1,0:T(8,128)(2,1)} %bitcast.462), calls=%async_computation.4 | async-start | bytes 6291456 | tf_op jit(solution)/shard_map/all_to_all | solution.py:332
  541.5 97.9 %copy-start.111 = (f32[256,2]{0,1:T(2,128)}, f32[256,2]{0,1:T(2,128)S(1)}, u32[]{:S(2)}) copy-start(f32[256,2]{0,1:T(2,128)S(1)} %select_reduce_fusion.3) | copy-start | bytes 6148
  541.6 97.8 %copy-start.123 = (f32[256]{0:T(256)}, f32[256]{0:T(256)S(1)}, u32[]{:S(2)}) copy-start(f32[256]{0:T(256)S(1)} %reduce_max.18) | copy-start | bytes 3076
  600.7 47.6 %all-to-all-start.7 = ((bf16[8,96,2048]{2,1,0:T(8,128)(2,1)}), bf16[8,96,2048]{2,1,0:T(8,128)(2,1)}, u32[]{:S(2)}, u32[]{:S(2)}) async-start(bf16[8,96,2048]{2,1,0:T(8,128)(2,1)} %bitcast.457), calls=%async_computation.7 | async-start | bytes 6291456 | tf_op jit(solution)/shard_map/all_to_all | solution.py:332
  605.2 267.4 %all-gather.12.cloned.1.call-start = ((), (), s32[]{:S(2)}) async-start(), calls=%async_computation.26 | async-start | bytes 5570560 | tf_op jit(solution)/shard_map/all_gather | solution.py:767
  605.9 51.8 %copy-start.134 = (s32[256,2]{0,1:T(2,128)}, s32[256,2]{0,1:T(2,128)S(1)}, u32[]{:S(2)}) copy-start(s32[256,2]{0,1:T(2,128)S(1)} %copy.263) | copy-start | bytes 6148
  643.9 231.5 %copy-start.132 = (s32[512]{0:T(512)}, s32[512]{0:T(512)S(1)}, u32[]{:S(2)}) copy-start(s32[512]{0:T(512)S(1)} %convert_add_fusion.1) | copy-start | bytes 6148
  647.8 65.2 %collective-permute-start.6 = (bf16[512,2816]{1,0:T(8,128)(2,1)}, bf16[512,2816]{1,0:T(8,128)(2,1)}, u32[]{:S(2)}, u32[]{:S(2)}) collective-permute-start(bf16[512,2816]{1,0:T(8,128)(2,1)} %cut.4), channel_id=1, source_target_pairs={{0,24},{8,0},{16,8},{24,16},{1,25},{9,1},{17,9},{25,17},{2,26},{10... | collective-permute-start | bytes 8650760 | tf_op jit(solution)/shard_map/ppermute | solution.py:345
  717.2 42.4 %all-to-all-start.15 = ((bf16[8,96,2048]{2,1,0:T(8,128)(2,1)}), bf16[8,96,2048]{2,1,0:T(8,128)(2,1)}, u32[]{:S(2)}, u32[]{:S(2)}) async-start(bf16[8,96,2048]{2,1,0:T(8,128)(2,1)} %bitcast.429), calls=%async_computation.15 | async-start | bytes 6291456 | tf_op jit(solution)/shard_map/all_to_all | solution.py:332
  733.8 125.9 %collective-permute-start.7 = (bf16[512,2816]{1,0:T(8,128)(2,1)}, bf16[512,2816]{1,0:T(8,128)(2,1)}, u32[]{:S(2)}, u32[]{:S(2)}) collective-permute-start(bf16[512,2816]{1,0:T(8,128)(2,1)} %cut.7), channel_id=1, source_target_pairs={{0,8},{8,16},{16,24},{24,0},{1,9},{9,17},{17,25},{25,1},{2,10},{10... | collective-permute-start | bytes 8650760 | tf_op jit(solution)/shard_map/ppermute | solution.py:345
  762.6 105.6 %copy-start.99 = (bf16[768,128]{1,0:T(8,128)(2,1)}, bf16[768,128]{1,0:T(8,128)(2,1)S(1)}, u32[]{:S(2)}) copy-start(bf16[768,128]{1,0:T(8,128)(2,1)S(1)} %fusion.94) | copy-start | bytes 589828
  765.5 113.1 %all-to-all-start.8 = ((bf16[8,96,2048]{2,1,0:T(8,128)(2,1)}), bf16[8,96,2048]{2,1,0:T(8,128)(2,1)}, u32[]{:S(2)}, u32[]{:S(2)}) async-start(bf16[8,96,2048]{2,1,0:T(8,128)(2,1)} %bitcast.422), calls=%async_computation.8 | async-start | bytes 6291456 | tf_op jit(solution)/shard_map/all_to_all | solution.py:332
  859.7 125.3 %collective-permute-start.8 = (bf16[512,2816]{1,0:T(8,128)(2,1)}, bf16[512,2816]{1,0:T(8,128)(2,1)}, u32[]{:S(2)}, u32[]{:S(2)}) collective-permute-start(bf16[512,2816]{1,0:T(8,128)(2,1)} %copy-done.15), channel_id=1, source_target_pairs={{0,16},{8,24},{16,0},{24,8},{1,17},{9,25},{17,1},{25,9},{2,18},{10... | collective-permute-start | bytes 8650760 | tf_op jit(solution)/shard_map/ppermute | solution.py:345
  870.3 114.7 %copy-start.44 = (bf16[8,2048,16]{1,2,0:T(8,128)(2,1)S(1)}, bf16[8,2048,16]{1,2,0:T(8,128)(2,1)}, u32[]{:S(2)}) copy-start(bf16[8,2048,16]{1,2,0:T(8,128)(2,1)} %param.42) | copy-start | bytes 1572868
  878.6 140.2 %all-to-all-start.19 = ((f32[8,4,96]{2,1,0:T(4,128)}), f32[8,4,96]{2,1,0:T(4,128)S(1)}, u32[]{:S(2)}, u32[]{:S(2)}) async-start(f32[8,4,96]{2,1,0:T(4,128)} %maximum_bitcast_fusion), calls=%async_computation.19 | async-start | bytes 32768 | tf_op jit(solution)/shard_map/all_to_all | solution.py:332
  1018.8 44.7 %all-to-all-start.9 = ((bf16[8,96,2176]{2,1,0:T(8,128)(2,1)}), bf16[8,96,2176]{2,1,0:T(8,128)(2,1)}, u32[]{:S(2)}, u32[]{:S(2)}) async-start(bf16[8,96,2176]{2,1,0:T(8,128)(2,1)} %bitcast.455), calls=%async_computation.9 | async-start | bytes 6684672 | tf_op jit(solution)/shard_map/all_to_all | solution.py:332
  1063.5 42.3 %all-to-all-start.10 = ((bf16[8,96,2048]{2,1,0:T(8,128)(2,1)}), bf16[8,96,2048]{2,1,0:T(8,128)(2,1)}, u32[]{:S(2)}, u32[]{:S(2)}) async-start(bf16[8,96,2048]{2,1,0:T(8,128)(2,1)} %bitcast.424), calls=%async_computation.10 | async-start | bytes 6291456 | tf_op jit(solution)/shard_map/all_to_all | solution.py:332
  1110.0 56.8 %all-to-all-start.12 = ((bf16[8,96,2048]{2,1,0:T(8,128)(2,1)}), bf16[8,96,2048]{2,1,0:T(8,128)(2,1)}, u32[]{:S(2)}, u32[]{:S(2)}) async-start(bf16[8,96,2048]{2,1,0:T(8,128)(2,1)} %bitcast.427), calls=%async_computation.12 | async-start | bytes 6291456 | tf_op jit(solution)/shard_map/all_to_all | solution.py:332
  1166.8 55.4 %all-to-all-start.11 = ((bf16[8,96,2176]{2,1,0:T(8,128)(2,1)}), bf16[8,96,2176]{2,1,0:T(8,128)(2,1)}, u32[]{:S(2)}, u32[]{:S(2)}) async-start(bf16[8,96,2176]{2,1,0:T(8,128)(2,1)} %bitcast.454), calls=%async_computation.11 | async-start | bytes 6684672 | tf_op jit(solution)/shard_map/all_to_all | solution.py:332
  1222.2 42.5 %all-to-all-start.14 = ((bf16[8,96,2048]{2,1,0:T(8,128)(2,1)}), bf16[8,96,2048]{2,1,0:T(8,128)(2,1)}, u32[]{:S(2)}, u32[]{:S(2)}) async-start(bf16[8,96,2048]{2,1,0:T(8,128)(2,1)} %bitcast.423), calls=%async_computation.14 | async-start | bytes 6291456 | tf_op jit(solution)/shard_map/all_to_all | solution.py:332
  1245.4 56.9 %collective-permute-start.9 = (bf16[256,2176]{1,0:T(8,128)(2,1)}, bf16[256,2176]{1,0:T(8,128)(2,1)}, u32[]{:S(2)}, u32[]{:S(2)}) collective-permute-start(bf16[256,2176]{1,0:T(8,128)(2,1)} %pad_maximum_fusion.2), channel_id=1, source_target_pairs={{0,8},{8,16},{16,24},{24,0},{1,9},{9,17},{17,25},{25,1},{2,10},{10... | collective-permute-start | bytes 3342344 | tf_op jit(solution)/shard_map/ppermute | solution.py:345
  1264.7 50.7 %all-to-all-start.13 = ((bf16[8,96,2176]{2,1,0:T(8,128)(2,1)}), bf16[8,96,2176]{2,1,0:T(8,128)(2,1)}, u32[]{:S(2)}, u32[]{:S(2)}) async-start(bf16[8,96,2176]{2,1,0:T(8,128)(2,1)} %bitcast.452), calls=%async_computation.13 | async-start | bytes 6684672 | tf_op jit(solution)/shard_map/all_to_all | solution.py:332
  1315.4 50.3 %all-to-all-start.16 = ((bf16[8,96,2176]{2,1,0:T(8,128)(2,1)}), bf16[8,96,2176]{2,1,0:T(8,128)(2,1)}, u32[]{:S(2)}, u32[]{:S(2)}) async-start(bf16[8,96,2176]{2,1,0:T(8,128)(2,1)} %bitcast.453), calls=%async_computation.16 | async-start | bytes 6684672 | tf_op jit(solution)/shard_map/all_to_all | solution.py:332
  1320.1 105.9 %reduce-scatter.2.cloned.1.call-start = ((), (), s32[]{:S(2)}) async-start(), calls=%async_computation.27 | async-start | bytes 2396160 | tf_op jit(solution)/shard_map/reduce_scatter | solution.py:861
  1333.6 51.8 %collective-permute-start.10 = (bf16[256,2176]{1,0:T(8,128)(2,1)}, bf16[256,2176]{1,0:T(8,128)(2,1)}, u32[]{:S(2)}, u32[]{:S(2)}) collective-permute-start(bf16[256,2176]{1,0:T(8,128)(2,1)} %pad_maximum_fusion.3), channel_id=1, source_target_pairs={{0,16},{8,24},{16,0},{24,8},{1,17},{9,25},{17,1},{25,9},{2,18},{10... | collective-permute-start | bytes 3342344 | tf_op jit(solution)/shard_map/ppermute | solution.py:345
  1370.5 38.6 %collective-permute-start.11 = (bf16[256,2176]{1,0:T(8,128)(2,1)S(1)}, bf16[256,2176]{1,0:T(8,128)(2,1)S(1)}, u32[]{:S(2)}, u32[]{:S(2)}) collective-permute-start(bf16[256,2176]{1,0:T(8,128)(2,1)S(1)} %pad_maximum_fusion.4), channel_id=1, source_target_pairs={{0,24},{8,0},{16,8},{24,16},{1,25},{9,1},{17,9},{25,17},{2,26},{10... | collective-permute-start | bytes 3342344 | tf_op jit(solution)/shard_map/ppermute | solution.py:345
  1421.4 46.2 %all-to-all-start.17 = ((bf16[8,96,2048]{2,1,0:T(8,128)(2,1)}), bf16[8,96,2048]{2,1,0:T(8,128)(2,1)}, u32[]{:S(2)}, u32[]{:S(2)}) async-start(bf16[8,96,2048]{2,1,0:T(8,128)(2,1)} %bitcast.430), calls=%async_computation.17 | async-start | bytes 6291456 | tf_op jit(solution)/shard_map/all_to_all | solution.py:332
  1425.9 258.4 %all-gather.14.cloned.1.call-start = ((), (), s32[]{:S(2)}) async-start(), calls=%async_computation.28 | async-start | bytes 8785920 | tf_op jit(solution)/shard_map/all_gather | solution.py:862
  1479.6 55.2 %all-to-all-start.18 = ((bf16[8,96,2048]{2,1,0:T(8,128)(2,1)}), bf16[8,96,2048]{2,1,0:T(8,128)(2,1)}, u32[]{:S(2)}, u32[]{:S(2)}) async-start(bf16[8,96,2048]{2,1,0:T(8,128)(2,1)} %bitcast.458), calls=%async_computation.18 | async-start | bytes 6291456 | tf_op jit(solution)/shard_map/all_to_all | solution.py:332
  1489.4 45.5 %copy-start.36 = (bf16[16,2048]{1,0:T(8,128)(2,1)S(1)}, bf16[16,2048]{1,0:T(8,128)(2,1)}, u32[]{:S(2)}) copy-start(bf16[16,2048]{1,0:T(8,128)(2,1)} %copy-done.35) | copy-start | bytes 196612
  1493.4 301.4 %collective-permute-start.15 = (bf16[768,2048]{1,0:T(8,128)(2,1)}, bf16[768,2048]{1,0:T(8,128)(2,1)}, u32[]{:S(2)}, u32[]{:S(2)}) collective-permute-start(bf16[768,2048]{1,0:T(8,128)(2,1)} %add_convert_fusion.3), channel_id=1, source_target_pairs={{0,8},{8,16},{16,24},{24,0},{1,9},{9,17},{17,25},{25,1},{2,10},{10... | collective-permute-start | bytes 9437192 | tf_op jit(solution)/shard_map/ppermute | solution.py:345
  1493.4 196.8 %collective-permute-start.16 = (bf16[768,2048]{1,0:T(8,128)(2,1)}, bf16[768,2048]{1,0:T(8,128)(2,1)}, u32[]{:S(2)}, u32[]{:S(2)}) collective-permute-start(bf16[768,2048]{1,0:T(8,128)(2,1)} %add_convert_fusion.1), channel_id=1, source_target_pairs={{0,24},{8,0},{16,8},{24,16},{1,25},{9,1},{17,9},{25,17},{2,26},{10... | collective-permute-start | bytes 9437192 | tf_op jit(solution)/shard_map/ppermute | solution.py:345
  1582.1 42.5 %all-to-all-start.20 = ((bf16[8,96,2048]{2,1,0:T(8,128)(2,1)}), bf16[8,96,2048]{2,1,0:T(8,128)(2,1)}, u32[]{:S(2)}, u32[]{:S(2)}) async-start(bf16[8,96,2048]{2,1,0:T(8,128)(2,1)} %bitcast.459), calls=%async_computation.20 | async-start | bytes 6291456 | tf_op jit(solution)/shard_map/all_to_all | solution.py:332
  1636.6 42.5 %all-to-all-start.22 = ((bf16[8,96,2048]{2,1,0:T(8,128)(2,1)}), bf16[8,96,2048]{2,1,0:T(8,128)(2,1)}, u32[]{:S(2)}, u32[]{:S(2)}) async-start(bf16[8,96,2048]{2,1,0:T(8,128)(2,1)} %bitcast.460), calls=%async_computation.22 | async-start | bytes 6291456 | tf_op jit(solution)/shard_map/all_to_all | solution.py:332
  1643.5 40.0 %collective-permute-start.18 = (bf16[16,3584]{1,0:T(8,128)(2,1)S(1)}, bf16[16,3584]{1,0:T(8,128)(2,1)S(1)}, u32[]{:S(2)}, u32[]{:S(2)}) collective-permute-start(bf16[16,3584]{1,0:T(8,128)(2,1)S(1)} %get-tuple-element.177), channel_id=1, source_target_pairs={{0,8},{8,16},{16,24},{24,0},{1,9},{9,17},{17,25},{25,1},{2,10},{10... | collective-permute-start | bytes 344072 | tf_op jit(solution)/shard_map/ppermute | solution.py:345
  1645.1 38.5 %collective-permute-start.20 = (bf16[16,3584]{1,0:T(8,128)(2,1)S(1)}, bf16[16,3584]{1,0:T(8,128)(2,1)S(1)}, u32[]{:S(2)}, u32[]{:S(2)}) collective-permute-start(bf16[16,3584]{1,0:T(8,128)(2,1)S(1)} %get-tuple-element.178), channel_id=1, source_target_pairs={{0,24},{8,0},{16,8},{24,16},{1,25},{9,1},{17,9},{25,17},{2,26},{10... | collective-permute-start | bytes 344072 | tf_op jit(solution)/shard_map/ppermute | solution.py:345
  1647.4 36.2 %collective-permute-start.19 = (bf16[16,3584]{1,0:T(8,128)(2,1)S(1)}, bf16[16,3584]{1,0:T(8,128)(2,1)S(1)}, u32[]{:S(2)}, u32[]{:S(2)}) collective-permute-start(bf16[16,3584]{1,0:T(8,128)(2,1)S(1)} %get-tuple-element.179), channel_id=1, source_target_pairs={{0,16},{8,24},{16,0},{24,8},{1,17},{9,25},{17,1},{25,9},{2,18},{10... | collective-permute-start | bytes 344072 | tf_op jit(solution)/shard_map/ppermute | solution.py:345
  1679.0 122.4 %all-to-all-start.23 = ((bf16[8,96,2048]{2,1,0:T(8,128)(2,1)}), bf16[8,96,2048]{2,1,0:T(8,128)(2,1)}, u32[]{:S(2)}, u32[]{:S(2)}) async-start(bf16[8,96,2048]{2,1,0:T(8,128)(2,1)} %bitcast.456), calls=%async_computation.23 | async-start | bytes 6291456 | tf_op jit(solution)/shard_map/all_to_all | solution.py:332
  1683.5 209.6 %all-gather.20.cloned.1.call-start = ((), (), s32[]{:S(2)}) async-start(), calls=%async_computation.31 | async-start | bytes 3784704 | tf_op jit(solution)/shard_map/all_gather | solution.py:905
  1684.3 110.5 %copy-start.86 = (bf16[768,2048]{1,0:T(8,128)(2,1)S(1)}, bf16[768,2048]{1,0:T(8,128)(2,1)}, u32[]{:S(2)}) copy-start(bf16[768,2048]{1,0:T(8,128)(2,1)} %add_convert_fusion.4) | copy-start | bytes 9437188
  1687.2 28.3 %collective-permute-start.14 = (bf16[256,2048]{1,0:T(8,128)(2,1)S(1)}, bf16[256,2048]{1,0:T(8,128)(2,1)}, u32[]{:S(2)}, u32[]{:S(2)}) collective-permute-start(bf16[256,2048]{1,0:T(8,128)(2,1)S(1)} %get-tuple-element.170), channel_id=1, source_target_pairs={{0,24},{8,0},{16,8},{24,16},{1,25},{9,1},{17,9},{25,17},{2,26},{10... | collective-permute-start | bytes 3145736 | tf_op jit(solution)/shard_map/ppermute | solution.py:345
  1689.5 105.3 %collective-permute-start.13 = (bf16[256,2048]{1,0:T(8,128)(2,1)S(1)}, bf16[256,2048]{1,0:T(8,128)(2,1)}, u32[]{:S(2)}, u32[]{:S(2)}) collective-permute-start(bf16[256,2048]{1,0:T(8,128)(2,1)S(1)} %get-tuple-element.171), channel_id=1, source_target_pairs={{0,16},{8,24},{16,0},{24,8},{1,17},{9,25},{17,1},{25,9},{2,18},{10... | collective-permute-start | bytes 3145736 | tf_op jit(solution)/shard_map/ppermute | solution.py:345
  1690.2 104.6 %collective-permute-start.12 = (bf16[256,2048]{1,0:T(8,128)(2,1)S(1)}, bf16[256,2048]{1,0:T(8,128)(2,1)}, u32[]{:S(2)}, u32[]{:S(2)}) collective-permute-start(bf16[256,2048]{1,0:T(8,128)(2,1)S(1)} %get-tuple-element.172), channel_id=1, source_target_pairs={{0,8},{8,16},{16,24},{24,0},{1,9},{9,17},{17,25},{25,1},{2,10},{10... | collective-permute-start | bytes 3145736 | tf_op jit(solution)/shard_map/ppermute | solution.py:345
  1801.5 43.1 %all-to-all-start.21 = ((bf16[8,96,2048]{2,1,0:T(8,128)(2,1)}), bf16[8,96,2048]{2,1,0:T(8,128)(2,1)}, u32[]{:S(2)}, u32[]{:S(2)}) async-start(bf16[8,96,2048]{2,1,0:T(8,128)(2,1)} %bitcast.431), calls=%async_computation.21 | async-start | bytes 6291456 | tf_op jit(solution)/shard_map/all_to_all | solution.py:332
  1814.0 49.4 %collective-permute-start.17 = (bf16[256,2048]{1,0:T(8,128)(2,1)}, bf16[256,2048]{1,0:T(8,128)(2,1)}, u32[]{:S(2)}, u32[]{:S(2)}) collective-permute-start(bf16[256,2048]{1,0:T(8,128)(2,1)} %convolution_convert_fusion.14), channel_id=1, source_target_pairs={{0,16},{8,24},{16,0},{24,8},{1,17},{9,25},{17,1},{25,9},{2,18},{10... | collective-permute-start | bytes 3145736 | tf_op jit(solution)/shard_map/ppermute | solution.py:345
  (154 other events, 1228.8 us)
Sparse Core Ops, SparseCore 0:
  9.6 264.2 all-gather.15
  276.4 158.7 all-gather.17
  436.8 152.0 all-gather.9
  713.2 142.8 all-gather.11
  1324.3 49.4 reduce-scatter.1
  1429.6 156.4 all-gather.13
  1688.2 123.0 all-gather.19

commit v6 on v5

--- a/solution.py
+++ b/solution.py
@@ -743,11 +743,11 @@
     )
 
     output_rows = send_cut(output_slots, experts, copies)
-    output_rows = after(output_rows, *grad_rows[:3])
+    inner_sent = [cut_share(mlp_in_weight[0], (spot - d) % size, size) for d in range(size)]
+    output_rows = after(output_rows, *grad_rows[:3], *inner_sent)
     output_parts = nn(output_rows.reshape(holders * capacity, -1), output_full).astype(bf16)
     far = size // 2
     distances = [d for d in range(1, size) if d != far] + ([far] if size > 1 else [])
-    inner_sent = [cut_share(mlp_in_weight[0], (spot - d) % size, size) for d in range(size)]
     inner_parts = list(inner_sent)
     before = output_full
     for d in distances:
@@ -805,9 +805,9 @@
     for d in order[1:]:
         earlier = [inner_parts[k] for k in distances[:-1]] if d == 1 else []
         got_rows.append(send_rows(d, got_rows[-1], *earlier))
-    kept = [work(0, got_rows[0])]
+    kept = [work(0, after(got_rows[0], got_rows[-1]))]
     row_home, row_total = rows_home(0, kept[0][0])
-    row_backs = [row_total]
+    row_backs, row_homes = [row_total], [row_home]
     for d in order[1:]:
         kept.append(work(d, after(got_rows[d], kept[-1][0])))
         row_grad = kept[d][0]
@@ -815,24 +815,20 @@
             row_grad = after(row_grad, row_backs[d - 2])
         row_home, row_back = rows_home(d, row_grad)
         row_backs.append(row_back)
+        row_homes.append(row_home)
         row_total = row_total + row_back.astype(f32)
     gate_sum = row_total[:, width : width + 4]
     row_total = row_total[:, :width]
     mlp_gate_grad = gate_sum.reshape(rows, 2, 2).sum(2)
     mlp_logit_grad = gate_back(mlp_gates, mlp_hits, mlp_gate_grad)
 
-    down_near, down_parts, down_made, sums = [], [], [], None
+    outer_lows, sums = [], None
     for d in order:
         _, activated, pre_grad, code, back = kept[d]
+        there = row_homes[min(d, size - 2)] if size > 1 else row_homes[0]
+        activated, pre_grad = after(activated, there), after(pre_grad, there)
         outer_low = nt(activated, outer_down).astype(bf16) * mask
-        down = (nn(activated, outer_full) + nn(outer_low, outer_up)).astype(bf16)
-        down_made.append(down)
-        if d in (0, 1, size - 1):
-            if d:
-                down = shifted(after(down, row_home), -d % size, size)
-            down_near.append(down)
-        else:
-            down_parts.append((d, down))
+        outer_lows.append(outer_low)
         scale = gate_slots[:, d, :].reshape(-1, 1)
 
         def scaled(array):
@@ -846,6 +842,7 @@
         )
         sums = new if sums is None else tuple(a + b for a, b in zip(sums, new))
 
+
     inner_up_sum, outer_down_sum, inner_down_sum, outer_up_sum = sums
 
     def widened(array):
@@ -857,9 +854,27 @@
 
     wide = [widened(inner_up_sum), widened(outer_down_sum), inner_down_sum, outer_up_sum]
     ends = [sum(a.shape[1] for a in wide[: k + 1]) for k in range(3)]
-    mlp_own = jnp.concatenate(wide, axis=1).astype(bf16)
+    mlp_own = after(jnp.concatenate(wide, axis=1).astype(bf16), row_home)
     mlp_sums = lax.psum_scatter(mlp_own, "dp", scatter_dimension=0, tiled=True)
-    mlp_sums = lax.all_gather(mlp_sums, ("seq", "dp"), axis=0, tiled=True)
+
+    def down_back(d, before_matmul, before_sending):
+        activated = after(kept[d][1], before_matmul)
+        down = (nn(activated, outer_full) + nn(outer_lows[d], outer_up)).astype(bf16)
+        down = after(down, before_sending).reshape(holders, capacity, width)
+        home = home_add(down, experts, copies)
+        made = nn(combines[d], home)
+        return home, shifted(made.astype(bf16), -d % size, size).astype(f32) if d else made
+
+    down_turns = order[1:] + [0]
+    down_home, down_total = down_back(down_turns[0], row_homes[-2], row_home)
+
+    normed_mlp_grad = row_total + nt(mlp_logit_grad.astype(bf16), mlp_router_weight)
+    middle_grad = norm_back(middle, middle_scale, mlp_gain, normed_mlp_grad)
+    middle_grad = middle_grad + out_grad[0].astype(f32)
+    middle_low = middle_grad.astype(bf16)
+    branch_sent = tn(place_any, after(middle_low, down_home)).astype(bf16)
+    branch_rows = send_full(branch_sent, experts, copies)
+    mlp_sums = lax.all_gather(after(mlp_sums, branch_rows), ("seq", "dp"), axis=0, tiled=True)
     if copies == 1 and share % 128 == 0:
         inner_up_grad, outer_down_grad, inner_down_grad, outer_up_grad = unpack_sums(
             mlp_sums.reshape(size, adapters, rank, -1), share, width
@@ -873,14 +888,10 @@
         outer_down_grad = outer_down_grad.reshape(adapters, rank, -1)
         inner_down_grad = jnp.sum(inner_down_grad, 0).reshape(adapters, rank, width)
         outer_up_grad = jnp.sum(outer_up_grad, 0).reshape(adapters, rank, width)
-
-    normed_mlp_grad = row_total + nt(mlp_logit_grad.astype(bf16), mlp_router_weight)
-    middle_grad = norm_back(middle, middle_scale, mlp_gain, normed_mlp_grad)
-    middle_grad = middle_grad + out_grad[0].astype(f32)
-    middle_low = after(middle_grad.astype(bf16), *down_made)
-    branch_rows = send_full(tn(place_any, middle_low).astype(bf16), experts, copies)
     head_parts = nt(branch_rows.reshape(-1, width), output_full).astype(bf16)
     head_home = home_join(head_parts.reshape(holders, capacity, -1), experts, copies)
+    down_home, made = down_back(down_turns[1], head_parts, head_home)
+    down_total = down_total + made
     head_home = after(head_home, mlp_own)
     gate_grad = jnp.sum(middle_grad[None] * branch, axis=2).T
     logit_grad = gate_back(gates, hits, gate_grad)
@@ -921,7 +932,7 @@
         cosine_all,
         sine_all,
     )
-    query_back = send_cut(query_slots, experts, copies)
+    query_back = send_cut(after(query_slots, down_home), experts, copies)
     half = key_grad.shape[1]
     pair_low_grad = nt(key_grad, pair_up[:, :half]) + nt(value_grad, pair_up[:, half:])
     pair_low_grad = pair_low_grad.astype(bf16)
@@ -949,22 +960,17 @@
     back_parts = [
         shifted(normed_grads[d * rows : (d + 1) * rows], -d % size, size) for d in range(1, size)
     ]
-    down_near = sum(after(down, *back_parts).astype(f32) for down in down_near).astype(bf16)
-    down_near = after(down_near, query_back).reshape(holders, capacity, width)
-    down_home = home_add(down_near, experts, copies)
-    own_back = after(normed_grads[:rows], inner_up_grad)
-    normed_grad = own_back.astype(f32) + sum(back.astype(f32) for back in back_parts)
+    normed_grad = normed_grads[:rows].astype(f32) + sum(back.astype(f32) for back in back_parts)
     input_parts = nt(query_back.reshape(holders * capacity, -1), query_full).astype(bf16)
     input_home = home_add(input_parts.reshape(holders, capacity, width), experts, copies)
+    input_home = after(input_home, inner_up_grad)
     normed_grad = normed_grad + nn(place_any, input_home) + nn(query_low_grad, query_lower)
     normed_grad = normed_grad + nt(logit_grad.astype(bf16), router_weight)
     input_grad = norm_back(inputs, input_scale, norm_gain, normed_grad) + middle_grad
 
-    down_total = nn(combines[0], down_home)
-    for d, down in down_parts:
-        down = after(down, input_home).reshape(holders, capacity, width)
-        home = home_add(down, experts, copies)
-        down_total = down_total + shifted(nn(combines[d], home).astype(bf16), -d % size, size).astype(f32)
+    for d in down_turns[2:]:
+        down_home, made = down_back(d, query_slots, input_home)
+        down_total = down_total + made
     result = (middle + down_total).astype(bf16)
 
     return (

time: 1920 us -> 1920 us (level); the launches traced: 1910 us -> 1880 us
  waiting for transfers between devices: 958 us -> 928 us
    ppermute x21, waiting for transfers between devices: 641 us -> 456 us  [shifted(): lax.ppermute(array, 'seq', [(k, (k - shift) % size) for k in range(size)])]
    all_gather x1, waiting for transfers between devices: 0.01 us -> 131 us  [body(): packet_all = lax.all_gather(packet, 'seq', axis=0, tiled=True)]
    all_to_all x24 -> x26, waiting for transfers between devices: 287 us -> 312 us  [exchange(): return lax.all_to_all(buffer, 'dp', split_axis=0, concat_axis=0, tiled=True)]
    all_to_all x24 -> x26, starting transfers between devices: 111 us -> 120 us  [exchange(): return lax.all_to_all(buffer, 'dp', split_axis=0, concat_axis=0, tiled=True)]
    dot_general x93 -> x95, matrix products: 299 us -> 291 us  [product(): lax.dot_general(left, right, (((left_dim,), (right_dim,)), ((), ())), pre...]
    unnamed x357 -> x387, local copies, waits for them, and re-layouts: 49.3 us -> 53.5 us
  transfers between devices with their start and end apart: 52 -> 54, of which waited for: 27 -> 27; matrix products, arithmetic and copies ran while one was open for 21% -> 21% of each run, Pallas kernels for 15% -> 15%
where the time goes in v6:
time: 1920 us; the launch traced here: 1880 us
  waiting for transfers between devices  928 us (48%)
  Pallas kernels  292 us (15%)
  matrix products  291 us (15%)
  starting transfers between devices  186 us (10%)
  local copies, waits for them, and re-layouts  127 us (7%)
  other arithmetic  39.4 us (2%)
    ppermute x21, waiting for transfers between devices, shifted(): lax.ppermute(array, 'seq', [(k, (k - shift) % size) for k in range(size)])  456 us
    all_to_all x26, waiting for transfers between devices, exchange(): return lax.all_to_all(buffer, 'dp', split_axis=0, concat_axis=0, tiled=True)  312 us
    dot_general x95, matrix products, product(): lax.dot_general(left, right, (((left_dim,), (right_dim,)), ((), ())), pre...  291 us
    all_gather x1, waiting for transfers between devices, body(): packet_all = lax.all_gather(packet, 'seq', axis=0, tiled=True)  131 us
    pallas_call x4, Pallas kernels, expert_block(): pl.pallas_call(functools.partial(expert_kernel, size, share), grid_spec=p...  124 us
    all_to_all x26, starting transfers between devices, exchange(): return lax.all_to_all(buffer, 'dp', split_axis=0, concat_axis=0, tiled=True)  120 us
    ppermute x21, starting transfers between devices, shifted(): lax.ppermute(array, 'seq', [(k, (k - shift) % size) for k in range(size)])  65.7 us
    unnamed x387, local copies, waits for them, and re-layouts  53.5 us
  transfers between devices with their start and end apart: 54, of which 27 were waited for; matrix products, arithmetic and copies ran while one was open for 21% of the time, Pallas kernels for 15%

profile of v6, /device:TPU:0, one launch (start us, length us, event | category | flops | bytes accessed | tf_op | source)
XLA Modules:
  0.0 1882.0 jit_solution(9369998938805207540)
XLA Ops:
  9.2 5.2 all-to-all-start.3
  22.5 4.6 all-to-all-start
  38.3 26.7 %all-to-all-done = bf16[8,96,2048]{2,1,0:T(8,128)(2,1)} async-done(((bf16[8,96,2048]{2,1,0:T(8,128)(2,1)}), bf16[8,96,2048]{2,1,0:T(8,128)(2,1)}, u32[]{:S(2)}, u32[]{:S(2)}) %all-to-all-start) | async-done | bytes 3145760 | tf_op jit(solution)/shard_map/all_to_all | solution.py:332
  76.6 67.4 %collective-permute-done.2 = bf16[384,2048]{1,0:T(8,128)(2,1)} collective-permute-done((bf16[384,2048]{1,0:T(8,128)(2,1)}, bf16[384,2048]{1,0:T(8,128)(2,1)}, u32[]{:S(2)}, u32[]{:S(2)}) %collective-permute-start.2) | collective-permute-done | bytes 1572896 | tf_op jit(solution)/shard_map/ppermute | solution.py:345
  148.1 103.3 %collective-permute-done.1 = bf16[384,2048]{1,0:T(8,128)(2,1)} collective-permute-done((bf16[384,2048]{1,0:T(8,128)(2,1)}, bf16[384,2048]{1,0:T(8,128)(2,1)}, u32[]{:S(2)}, u32[]{:S(2)}) %collective-permute-start.1) | collective-permute-done | bytes 1572896 | tf_op jit(solution)/shard_map/ppermute | solution.py:345
  282.7 11.8 convolution_convert_fusion.3
  300.4 40.3 %collective-permute-start.5 = (bf16[256,2176]{1,0:T(8,128)(2,1)S(1)}, bf16[256,2176]{1,0:T(8,128)(2,1)}, u32[]{:S(2)}, u32[]{:S(2)}) collective-permute-start(bf16[256,2176]{1,0:T(8,128)(2,1)S(1)} %fusion.86), channel_id=1, source_target_pairs={{0,8},{8,16},{16,24},{24,0},{1,9},{9,17},{17,25},{25,1},{2,10},{10... | collective-permute-start | bytes 3342344 | tf_op jit(solution)/shard_map/ppermute | solution.py:345
  344.4 25.0 %collective-permute-done.5 = bf16[256,2176]{1,0:T(8,128)(2,1)} collective-permute-done((bf16[256,2176]{1,0:T(8,128)(2,1)S(1)}, bf16[256,2176]{1,0:T(8,128)(2,1)}, u32[]{:S(2)}, u32[]{:S(2)}) %collective-permute-start.5) | collective-permute-done | bytes 1114144 | tf_op jit(solution)/shard_map/ppermute | solution.py:345
  369.4 47.4 %collective-permute-done.4 = bf16[256,2176]{1,0:T(8,128)(2,1)} collective-permute-done((bf16[256,2176]{1,0:T(8,128)(2,1)S(1)}, bf16[256,2176]{1,0:T(8,128)(2,1)}, u32[]{:S(2)}, u32[]{:S(2)}) %collective-permute-start.4) | collective-permute-done | bytes 1114144 | tf_op jit(solution)/shard_map/ppermute | solution.py:345
  416.9 18.4 all-gather.18.cloned.1.call-done
  444.1 4.7 all-to-all-start.5
  456.7 31.7 %pairs.1 = (bf16[1024,4096]{1,0:T(8,128)(2,1)}, bf16[1024,16]{1,0:T(8,128)(2,1)S(1)}) custom-call(bf16[256,2048]{1,0:T(8,128)(2,1)S(1)} %fusion.50.refs_0_, bf16[256,2048]{1,0:T(8,128)(2,1)S(1)} %copy-done.28, bf16[256,2048]{1,0:T(8,128)(2,1)S(1)} %copy-done.27, bf16[256,2048]{1,0:T(8,128)(2,1)S(1)} %copy-done.26, bf16[8,2048,512]{2,1,0:T(8,128)(2,1)} %bitcast.500, ...), custom_call_target="tpu_custom_call" | custom-call | flops 17179869184 | bytes 16777216 | tf_op jit(solution)/shard_map/pairs/pallas_call | solution.py:75
  500.6 33.7 %attend.1 = (bf16[512,2048]{1,0:T(8,128)(2,1)S(1)}, bf16[768,2048]{1,0:T(8,128)(2,1)}, bf16[512,2048]{1,0:T(8,128)(2,1)}, f32[16,512,1]{2,1,0:T(8,128)}) custom-call(bf16[768,2048]{1,0:T(8,128)(2,1)} %bitcast.8.home_ref, bf16[512,768]{1,0:T(8,128)(2,1)S(1)} %fusion.76.place_ref, bf16[256,16]{1,0:T(8,128)(2,1)S(1)} %convolution_convert_fusion.25.low_ref, ...), custom_call_target="tpu_custom_call" | custom-call | flops 4294967296 | bytes 8388608 | tf_op jit(solution)/shard_map/attend/pallas_call | solution.py:194
  554.8 23.8 %all-to-all-done.4 = bf16[8,96,2048]{2,1,0:T(8,128)(2,1)} async-done(((bf16[8,96,2048]{2,1,0:T(8,128)(2,1)}), bf16[8,96,2048]{2,1,0:T(8,128)(2,1)}, u32[]{:S(2)}, u32[]{:S(2)}) %all-to-all-start.4) | async-done | bytes 3145760 | tf_op jit(solution)/shard_map/all_to_all | solution.py:332
  578.7 10.2 all-gather.10.cloned.1.call-done
  588.9 11.8 convolution_convert_fusion.2
  610.4 32.8 %all-to-all-done.7 = bf16[8,96,2048]{2,1,0:T(8,128)(2,1)} async-done(((bf16[8,96,2048]{2,1,0:T(8,128)(2,1)}), bf16[8,96,2048]{2,1,0:T(8,128)(2,1)}, u32[]{:S(2)}, u32[]{:S(2)}) %all-to-all-start.7) | async-done | bytes 3145760 | tf_op jit(solution)/shard_map/all_to_all | solution.py:332
  654.5 20.7 %collective-permute-done.6.refs_1_ = bf16[512,2816]{1,0:T(8,128)(2,1)} collective-permute-done((bf16[512,2816]{1,0:T(8,128)(2,1)}, bf16[512,2816]{1,0:T(8,128)(2,1)}, u32[]{:S(2)}, u32[]{:S(2)}) %collective-permute-start.6) | collective-permute-done | bytes 2883616 | tf_op jit(solution)/shard_map/ppermute | solution.py:345
  683.8 130.7 %all-gather.12.cloned.1.call-done = bf16[1024,2176]{1,0:T(8,128)(2,1)} async-done(((bf16[256,2176]{1,0:T(8,128)(2,1)}), bf16[1024,2176]{1,0:T(8,128)(2,1)}) %all-gather.12.cloned.1.call-update) | async-done | bytes 4456464 | tf_op jit(solution)/shard_map/all_gather | solution.py:767
  830.7 32.5 %all-to-all-done.9 = bf16[8,96,2048]{2,1,0:T(8,128)(2,1)} async-done(((bf16[8,96,2048]{2,1,0:T(8,128)(2,1)}), bf16[8,96,2048]{2,1,0:T(8,128)(2,1)}, u32[]{:S(2)}, u32[]{:S(2)}) %all-to-all-start.9) | async-done | bytes 3145760 | tf_op jit(solution)/shard_map/all_to_all | solution.py:332
  863.2 4.6 all-to-all-start.14
  873.8 6.5 squeeze.95
  880.3 6.8 dynamic-slice_reduce_fusion
  887.3 9.9 fusion.14
  899.8 5.9 all-to-all-done.14
  905.7 4.7 all-to-all-start.10
  921.7 7.0 fusion.12
  934.3 14.0 all-to-all-done.10
  952.4 4.8 all-to-all-start.11
  957.3 8.5 fusion.6
  976.2 19.0 %all-to-all-done.11 = bf16[8,96,2048]{2,1,0:T(8,128)(2,1)} async-done(((bf16[8,96,2048]{2,1,0:T(8,128)(2,1)}), bf16[8,96,2048]{2,1,0:T(8,128)(2,1)}, u32[]{:S(2)}, u32[]{:S(2)}) %all-to-all-start.11) | async-done | bytes 3145760 | tf_op jit(solution)/shard_map/all_to_all | solution.py:332
  998.5 60.9 %collective-permute-done.8.refs_2_ = bf16[512,2816]{1,0:T(8,128)(2,1)} collective-permute-done((bf16[512,2816]{1,0:T(8,128)(2,1)}, bf16[512,2816]{1,0:T(8,128)(2,1)}, u32[]{:S(2)}, u32[]{:S(2)}) %collective-permute-start.8) | collective-permute-done | bytes 2883616 | tf_op jit(solution)/shard_map/ppermute | solution.py:345
  1061.0 31.0 %experts.4 = (bf16[768,2176]{1,0:T(8,128)(2,1)}, bf16[768,1408]{1,0:T(8,128)(2,1)S(1)}, bf16[768,2816]{1,0:T(8,128)(2,1)}, bf16[768,128]{1,0:T(8,128)(2,1)S(1)}, bf16[768,128]{1,0:T(8,128)(2,1)S(1)}) custom-call(s32[1]{0:T(128)} %bitcast.46.spot_ref, bf16[768,2048]{1,0:T(8,128)(2,1)} %bitcast.48.x_ref, bf16[768,1408]{1,0:T(8,128)(2,1)S(1)} %copy-done.24, ...), custom_call_target="tpu_custom_call" | custom-call | flops 17716740096 | bytes 27262976 | tf_op jit(solution)/shard_map/experts/pallas_call | solution.py:607
  1093.3 4.8 all-to-all-start.17
  1101.0 9.9 fusion.10
  1110.9 31.0 %experts.5 = (bf16[768,2176]{1,0:T(8,128)(2,1)}, bf16[768,1408]{1,0:T(8,128)(2,1)S(1)}, bf16[768,2816]{1,0:T(8,128)(2,1)}, bf16[768,128]{1,0:T(8,128)(2,1)S(1)}, bf16[768,128]{1,0:T(8,128)(2,1)S(1)}) custom-call(s32[1]{0:T(128)} %bitcast.46.spot_ref, bf16[768,2048]{1,0:T(8,128)(2,1)} %bitcast.50.x_ref, bf16[768,1408]{1,0:T(8,128)(2,1)S(1)} %copy-done.23, ...), custom_call_target="tpu_custom_call" | custom-call | flops 17716740096 | bytes 27262976 | tf_op jit(solution)/shard_map/experts/pallas_call | solution.py:607
  1143.2 4.8 all-to-all-start.13
  1155.3 31.0 %experts.6 = (bf16[768,2176]{1,0:T(8,128)(2,1)}, bf16[768,1408]{1,0:T(8,128)(2,1)S(1)}, bf16[768,2816]{1,0:T(8,128)(2,1)}, bf16[768,128]{1,0:T(8,128)(2,1)S(1)}, bf16[768,128]{1,0:T(8,128)(2,1)S(1)}) custom-call(s32[1]{0:T(128)} %bitcast.46.spot_ref, bf16[768,2048]{1,0:T(8,128)(2,1)} %bitcast.53.x_ref, bf16[768,1408]{1,0:T(8,128)(2,1)S(1)} %copy-done.25, ...), custom_call_target="tpu_custom_call" | custom-call | flops 17716740096 | bytes 27262976 | tf_op jit(solution)/shard_map/experts/pallas_call | solution.py:607
  1195.8 4.9 all-to-all-start.12
  1203.4 31.2 %experts.7 = (bf16[768,2176]{1,0:T(8,128)(2,1)}, bf16[768,1408]{1,0:T(8,128)(2,1)S(1)}, bf16[768,2816]{1,0:T(8,128)(2,1)}, bf16[768,128]{1,0:T(8,128)(2,1)S(1)}, bf16[768,128]{1,0:T(8,128)(2,1)S(1)}) custom-call(s32[1]{0:T(128)} %bitcast.46.spot_ref, bf16[768,2048]{1,0:T(8,128)(2,1)} %bitcast.55.x_ref, bf16[768,1408]{1,0:T(8,128)(2,1)S(1)} %copy-done.22, ...), custom_call_target="tpu_custom_call" | custom-call | flops 17716740096 | bytes 27262976 | tf_op jit(solution)/shard_map/experts/pallas_call | solution.py:607
  1278.3 5.7 collective-permute-done.9
  1285.1 4.8 all-to-all-start.15
  1299.3 5.0 fusion.8
  1307.0 22.9 %all-to-all-done.15 = bf16[8,96,2176]{2,1,0:T(8,128)(2,1)} async-done(((bf16[8,96,2176]{2,1,0:T(8,128)(2,1)}), bf16[8,96,2176]{2,1,0:T(8,128)(2,1)}, u32[]{:S(2)}, u32[]{:S(2)}) %all-to-all-start.15) | async-done | bytes 3342368 | tf_op jit(solution)/shard_map/all_to_all | solution.py:332
  1343.3 16.1 collective-permute-done.12
  1370.3 16.0 all-to-all-done.16
  1393.5 37.8 %all-to-all-done.18 = bf16[8,96,2048]{2,1,0:T(8,128)(2,1)} async-done(((bf16[8,96,2048]{2,1,0:T(8,128)(2,1)}), bf16[8,96,2048]{2,1,0:T(8,128)(2,1)}, u32[]{:S(2)}, u32[]{:S(2)}) %all-to-all-start.18) | async-done | bytes 3145760 | tf_op jit(solution)/shard_map/all_to_all | solution.py:332
  1431.4 12.3 convolution_convert_fusion.1
  1463.8 7.8 fusion.4
  1474.2 25.5 %all-to-all-done.19 = bf16[8,96,2048]{2,1,0:T(8,128)(2,1)} async-done(((bf16[8,96,2048]{2,1,0:T(8,128)(2,1)}), bf16[8,96,2048]{2,1,0:T(8,128)(2,1)}, u32[]{:S(2)}, u32[]{:S(2)}) %all-to-all-start.19) | async-done | bytes 3145760 | tf_op jit(solution)/shard_map/all_to_all | solution.py:332
  1499.7 4.8 all-to-all-start.20
  1507.6 44.1 %attend_back.1 = (bf16[1024,2048]{1,0:T(8,128)(2,1)}, bf16[1024,2048]{1,0:T(8,128)(2,1)}, bf16[768,2048]{1,0:T(8,128)(2,1)}, bf16[256,2048]{1,0:T(8,128)(2,1)S(1)}) custom-call(bf16[512,2048]{1,0:T(8,128)(2,1)} %get-tuple-element.130.query_ref, bf16[1024,4096]{1,0:T(8,128)(2,1)} %get-tuple-element.96.key_ref.value_ref, ...), custom_call_target="tpu_custom_call" | custom-call | flops 10737418240 | bytes 16777216 | tf_op jit(solution)/shard_map/attend_back/pallas_call | solution.py:289
  1575.9 30.1 %all-to-all-done.22 = bf16[8,96,2048]{2,1,0:T(8,128)(2,1)} async-done(((bf16[8,96,2048]{2,1,0:T(8,128)(2,1)}), bf16[8,96,2048]{2,1,0:T(8,128)(2,1)}, u32[]{:S(2)}, u32[]{:S(2)}) %all-to-all-start.22) | async-done | bytes 3145760 | tf_op jit(solution)/shard_map/all_to_all | solution.py:332
  1606.1 11.9 convolution_convert_fusion
  1622.6 23.4 %pair_back.1 = bf16[1024,2048]{1,0:T(8,128)(2,1)S(1)} custom-call(bf16[1024,2048]{1,0:T(8,128)(2,1)} %get-tuple-element.162.key_ref, bf16[1024,2048]{1,0:T(8,128)(2,1)} %get-tuple-element.163.value_ref, bf16[8,2048,512]{2,1,0:T(8,128)(2,1)} %bitcast.501, bf16[1024,16]{1,0:T(8,128)(2,1)S(1)} %fusion.77.low_ref, bf16[16,2048]{1,0:T(8,128)(2,1)S(1)} %copy-done.47), custom_call_target="tpu_custom_call" | custom-call | flops 17179869184 | bytes 16777216 | tf_op jit(solution)/shard_map/pair_back/pallas_call | solution.py:129
  1649.8 7.8 fusion.2
  1660.3 19.3 %unpack.1 = (f32[8,16,11264]{2,1,0:T(8,128)}, f32[8,16,5632]{2,1,0:T(8,128)}, f32[8,16,2048]{2,1,0:T(8,128)}, f32[8,16,2048]{2,1,0:T(8,128)}) custom-call(bf16[4,8,16,8320]{3,2,1,0:T(8,128)(2,1)} %bitcast.434), custom_call_target="tpu_custom_call" | custom-call | bytes 32243712 | tf_op jit(solution)/shard_map/unpack/pallas_call | solution.py:485
  1693.6 7.1 fusion
  1703.4 25.0 %all-to-all-done.24 = bf16[8,96,2048]{2,1,0:T(8,128)(2,1)} async-done(((bf16[8,96,2048]{2,1,0:T(8,128)(2,1)}), bf16[8,96,2048]{2,1,0:T(8,128)(2,1)}, u32[]{:S(2)}, u32[]{:S(2)}) %all-to-all-start.24) | async-done | bytes 3145760 | tf_op jit(solution)/shard_map/all_to_all | solution.py:332
  1728.4 4.7 all-to-all-start.25
  1750.2 88.4 %collective-permute-done.16 = bf16[256,2048]{1,0:T(8,128)(2,1)} collective-permute-done((bf16[256,2048]{1,0:T(8,128)(2,1)}, bf16[256,2048]{1,0:T(8,128)(2,1)}, u32[]{:S(2)}, u32[]{:S(2)}) %collective-permute-start.16) | collective-permute-done | bytes 1048608 | tf_op jit(solution)/shard_map/ppermute | solution.py:345
  1843.6 17.5 collective-permute-done.13
  1861.1 5.5 fusion.93
  1868.6 6.0 gather_adapters.1
  (695 shorter events, 429.7 us)
Async XLA Ops:
  7.2 431.2 %copy-start = (bf16[8,16,4096]{2,1,0:T(8,128)(2,1)S(1)}, bf16[8,16,4096]{2,1,0:T(8,128)(2,1)}, u32[]{:S(2)}) copy-start(bf16[8,16,4096]{2,1,0:T(8,128)(2,1)} %param.37) | copy-start | bytes 3145732
  7.2 268.5 %all-gather.16.cloned.1.call-start = ((), (), s32[]{:S(2)}) async-start(), calls=%async_computation.31 | async-start | bytes 10485760 | tf_op jit(solution)/shard_map/all_gather | solution.py:685
  9.2 13.3 all-to-all-start.3
  17.4 481.1 %copy-start.159 = (f32[256]{0:T(256)}, f32[256]{0:T(256)S(1)}, u32[]{:S(2)}) copy-start(f32[256]{0:T(256)S(1)} %add_rsqrt_fusion.1) | copy-start | bytes 3076
  19.8 585.6 %copy-start.2 = (bf16[256,2048]{1,0:T(8,128)(2,1)}, bf16[256,2048]{1,0:T(8,128)(2,1)S(1)}, u32[]{:S(2)}) copy-start(bf16[256,2048]{1,0:T(8,128)(2,1)S(1)} %fusion.50.refs_0_) | copy-start | bytes 3145732
  22.5 42.5 %all-to-all-start = ((bf16[8,96,2048]{2,1,0:T(8,128)(2,1)}), bf16[8,96,2048]{2,1,0:T(8,128)(2,1)}, u32[]{:S(2)}, u32[]{:S(2)}) async-start(bf16[8,96,2048]{2,1,0:T(8,128)(2,1)} %bitcast.422), calls=%async_computation | async-start | bytes 6291456 | tf_op jit(solution)/shard_map/all_to_all | solution.py:332
  65.1 210.7 %all-to-all-start.2 = ((bf16[8,96,2048]{2,1,0:T(8,128)(2,1)}), bf16[8,96,2048]{2,1,0:T(8,128)(2,1)}, u32[]{:S(2)}, u32[]{:S(2)}) async-start(bf16[8,96,2048]{2,1,0:T(8,128)(2,1)} %bitcast.419), calls=%async_computation.2 | async-start | bytes 6291456 | tf_op jit(solution)/shard_map/all_to_all | solution.py:332
  69.7 365.6 %all-gather.18.cloned.1.call-start = ((), (), s32[]{:S(2)}) async-start(), calls=%async_computation.32 | async-start | bytes 18874368 | tf_op jit(solution)/shard_map/all_gather | solution.py:696
  71.0 73.1 %collective-permute-start.2 = (bf16[384,2048]{1,0:T(8,128)(2,1)}, bf16[384,2048]{1,0:T(8,128)(2,1)}, u32[]{:S(2)}, u32[]{:S(2)}) collective-permute-start(bf16[384,2048]{1,0:T(8,128)(2,1)} %pad_maximum_fusion.1), channel_id=1, source_target_pairs={{0,8},{8,16},{16,24},{24,0},{1,9},{9,17},{17,25},{25,1},{2,10},{10... | collective-permute-start | bytes 4718600 | tf_op jit(solution)/shard_map/ppermute | solution.py:345
  72.6 178.8 %collective-permute-start.1 = (bf16[384,2048]{1,0:T(8,128)(2,1)}, bf16[384,2048]{1,0:T(8,128)(2,1)}, u32[]{:S(2)}, u32[]{:S(2)}) collective-permute-start(bf16[384,2048]{1,0:T(8,128)(2,1)} %pad_maximum_fusion.1), channel_id=1, source_target_pairs={{0,16},{8,24},{16,0},{24,8},{1,17},{9,25},{17,1},{25,9},{2,18},{10... | collective-permute-start | bytes 4718600 | tf_op jit(solution)/shard_map/ppermute | solution.py:345
  75.1 183.4 %collective-permute-start = (bf16[384,2048]{1,0:T(8,128)(2,1)}, bf16[384,2048]{1,0:T(8,128)(2,1)}, u32[]{:S(2)}, u32[]{:S(2)}) collective-permute-start(bf16[384,2048]{1,0:T(8,128)(2,1)} %pad_maximum_fusion.1), channel_id=1, source_target_pairs={{0,24},{8,0},{16,8},{24,16},{1,25},{9,1},{17,9},{25,17},{2,26},{10... | collective-permute-start | bytes 4718600 | tf_op jit(solution)/shard_map/ppermute | solution.py:345
  76.6 810.6 %copy-start.48 = (s32[8]{0:T(128)}, s32[8]{0:T(128)S(1)}, u32[]{:S(2)}) copy-start(s32[8]{0:T(128)S(1)} %slice_reduce_fusion.4.ids_ref) | copy-start | bytes 100
  294.5 122.3 %all-to-all-start.1 = ((bf16[8,96,2048]{2,1,0:T(8,128)(2,1)}), bf16[8,96,2048]{2,1,0:T(8,128)(2,1)}, u32[]{:S(2)}, u32[]{:S(2)}) async-start(bf16[8,96,2048]{2,1,0:T(8,128)(2,1)} %bitcast.459), calls=%async_computation.1 | async-start | bytes 6291456 | tf_op jit(solution)/shard_map/all_to_all | solution.py:332
  299.0 289.9 %all-gather.10.cloned.1.call-start = ((), (), s32[]{:S(2)}) async-start(), calls=%async_computation.27 | async-start | bytes 10485760 | tf_op jit(solution)/shard_map/all_gather | solution.py:735
  300.4 69.1 %collective-permute-start.5 = (bf16[256,2176]{1,0:T(8,128)(2,1)S(1)}, bf16[256,2176]{1,0:T(8,128)(2,1)}, u32[]{:S(2)}, u32[]{:S(2)}) collective-permute-start(bf16[256,2176]{1,0:T(8,128)(2,1)S(1)} %fusion.86), channel_id=1, source_target_pairs={{0,8},{8,16},{16,24},{24,0},{1,9},{9,17},{17,25},{25,1},{2,10},{10... | collective-permute-start | bytes 3342344 | tf_op jit(solution)/shard_map/ppermute | solution.py:345
  340.6 76.2 %collective-permute-start.4 = (bf16[256,2176]{1,0:T(8,128)(2,1)S(1)}, bf16[256,2176]{1,0:T(8,128)(2,1)}, u32[]{:S(2)}, u32[]{:S(2)}) collective-permute-start(bf16[256,2176]{1,0:T(8,128)(2,1)S(1)} %fusion.86), channel_id=1, source_target_pairs={{0,16},{8,24},{16,0},{24,8},{1,17},{9,25},{17,1},{25,9},{2,18},{10... | collective-permute-start | bytes 3342344 | tf_op jit(solution)/shard_map/ppermute | solution.py:345
  344.4 72.4 %collective-permute-start.3 = (bf16[256,2176]{1,0:T(8,128)(2,1)S(1)}, bf16[256,2176]{1,0:T(8,128)(2,1)}, u32[]{:S(2)}, u32[]{:S(2)}) collective-permute-start(bf16[256,2176]{1,0:T(8,128)(2,1)S(1)} %fusion.86), channel_id=1, source_target_pairs={{0,24},{8,0},{16,8},{24,16},{1,25},{9,1},{17,9},{25,17},{2,26},{10... | collective-permute-start | bytes 3342344 | tf_op jit(solution)/shard_map/ppermute | solution.py:345
  439.7 533.3 %copy-start.147 = (s32[512]{0:T(512)}, s32[512]{0:T(512)S(1)}, u32[]{:S(2)}) copy-start(s32[512]{0:T(512)S(1)} %convert_add_fusion.3) | copy-start | bytes 6148
  444.1 47.0 %all-to-all-start.5 = ((bf16[8,96,2048]{2,1,0:T(8,128)(2,1)}), bf16[8,96,2048]{2,1,0:T(8,128)(2,1)}, u32[]{:S(2)}, u32[]{:S(2)}) async-start(bf16[8,96,2048]{2,1,0:T(8,128)(2,1)} %bitcast.425), calls=%async_computation.5 | async-start | bytes 6291456 | tf_op jit(solution)/shard_map/all_to_all | solution.py:332
  451.6 522.7 %copy-start.149 = (s32[512]{0:T(512)}, s32[512]{0:T(512)S(1)}, u32[]{:S(2)}) copy-start(s32[512]{0:T(512)S(1)} %convert_add_fusion.2) | copy-start | bytes 6148
  491.1 45.2 %all-to-all-start.6 = ((bf16[8,96,2048]{2,1,0:T(8,128)(2,1)}), bf16[8,96,2048]{2,1,0:T(8,128)(2,1)}, u32[]{:S(2)}, u32[]{:S(2)}) async-start(bf16[8,96,2048]{2,1,0:T(8,128)(2,1)} %bitcast.423), calls=%async_computation.6 | async-start | bytes 6291456 | tf_op jit(solution)/shard_map/all_to_all | solution.py:332
  536.3 42.3 %all-to-all-start.4 = ((bf16[8,96,2048]{2,1,0:T(8,128)(2,1)}), bf16[8,96,2048]{2,1,0:T(8,128)(2,1)}, u32[]{:S(2)}, u32[]{:S(2)}) async-start(bf16[8,96,2048]{2,1,0:T(8,128)(2,1)} %bitcast.455), calls=%async_computation.4 | async-start | bytes 6291456 | tf_op jit(solution)/shard_map/all_to_all | solution.py:332
  600.7 42.5 %all-to-all-start.7 = ((bf16[8,96,2048]{2,1,0:T(8,128)(2,1)}), bf16[8,96,2048]{2,1,0:T(8,128)(2,1)}, u32[]{:S(2)}, u32[]{:S(2)}) async-start(bf16[8,96,2048]{2,1,0:T(8,128)(2,1)} %bitcast.460), calls=%async_computation.7 | async-start | bytes 6291456 | tf_op jit(solution)/shard_map/all_to_all | solution.py:332
  605.3 209.2 %all-gather.12.cloned.1.call-start = ((), (), s32[]{:S(2)}) async-start(), calls=%async_computation.28 | async-start | bytes 5570560 | tf_op jit(solution)/shard_map/all_gather | solution.py:767
  609.7 65.4 %collective-permute-start.6 = (bf16[512,2816]{1,0:T(8,128)(2,1)}, bf16[512,2816]{1,0:T(8,128)(2,1)}, u32[]{:S(2)}, u32[]{:S(2)}) collective-permute-start(bf16[512,2816]{1,0:T(8,128)(2,1)} %copy-done.21), channel_id=1, source_target_pairs={{0,24},{8,0},{16,8},{24,16},{1,25},{9,1},{17,9},{25,17},{2,26},{10... | collective-permute-start | bytes 8650760 | tf_op jit(solution)/shard_map/ppermute | solution.py:345
  676.5 141.6 %collective-permute-start.7 = (bf16[512,2816]{1,0:T(8,128)(2,1)}, bf16[512,2816]{1,0:T(8,128)(2,1)}, u32[]{:S(2)}, u32[]{:S(2)}) collective-permute-start(bf16[512,2816]{1,0:T(8,128)(2,1)} %copy-done.20), channel_id=1, source_target_pairs={{0,8},{8,16},{16,24},{24,0},{1,9},{9,17},{17,25},{25,1},{2,10},{10... | collective-permute-start | bytes 8650760 | tf_op jit(solution)/shard_map/ppermute | solution.py:345
  679.3 138.8 %all-to-all-start.8 = ((bf16[8,96,2048]{2,1,0:T(8,128)(2,1)}), bf16[8,96,2048]{2,1,0:T(8,128)(2,1)}, u32[]{:S(2)}, u32[]{:S(2)}) async-start(bf16[8,96,2048]{2,1,0:T(8,128)(2,1)} %bitcast.420), calls=%async_computation.8 | async-start | bytes 6291456 | tf_op jit(solution)/shard_map/all_to_all | solution.py:332
  683.8 134.3 %copy-start.80 = (bf16[512,768]{1,0:T(8,128)(2,1)S(1)}, bf16[512,768]{1,0:T(8,128)(2,1)}, u32[]{:S(2)}) copy-start(bf16[512,768]{1,0:T(8,128)(2,1)} %copy-done.79) | copy-start | bytes 2359300
  820.8 42.4 %all-to-all-start.9 = ((bf16[8,96,2048]{2,1,0:T(8,128)(2,1)}), bf16[8,96,2048]{2,1,0:T(8,128)(2,1)}, u32[]{:S(2)}, u32[]{:S(2)}) async-start(bf16[8,96,2048]{2,1,0:T(8,128)(2,1)} %bitcast.427), calls=%async_computation.9 | async-start | bytes 6291456 | tf_op jit(solution)/shard_map/all_to_all | solution.py:332
  827.8 143.9 %copy-start.151 = (s32[512]{0:T(512)}, s32[512]{0:T(512)S(1)}, u32[]{:S(2)}) copy-start(s32[512]{0:T(512)S(1)} %convert_add_fusion.1) | copy-start | bytes 6148
  863.2 42.5 %all-to-all-start.14 = ((bf16[8,96,2048]{2,1,0:T(8,128)(2,1)}), bf16[8,96,2048]{2,1,0:T(8,128)(2,1)}, u32[]{:S(2)}, u32[]{:S(2)}) async-start(bf16[8,96,2048]{2,1,0:T(8,128)(2,1)} %bitcast.424), calls=%async_computation.14 | async-start | bytes 6291456 | tf_op jit(solution)/shard_map/all_to_all | solution.py:332
  905.7 42.6 %all-to-all-start.10 = ((bf16[8,96,2048]{2,1,0:T(8,128)(2,1)}), bf16[8,96,2048]{2,1,0:T(8,128)(2,1)}, u32[]{:S(2)}, u32[]{:S(2)}) async-start(bf16[8,96,2048]{2,1,0:T(8,128)(2,1)} %bitcast.426), calls=%async_computation.10 | async-start | bytes 6291456 | tf_op jit(solution)/shard_map/all_to_all | solution.py:332
  933.6 125.8 %collective-permute-start.8 = (bf16[512,2816]{1,0:T(8,128)(2,1)}, bf16[512,2816]{1,0:T(8,128)(2,1)}, u32[]{:S(2)}, u32[]{:S(2)}) collective-permute-start(bf16[512,2816]{1,0:T(8,128)(2,1)} %cut.6), channel_id=1, source_target_pairs={{0,16},{8,24},{16,0},{24,8},{1,17},{9,25},{17,1},{25,9},{2,18},{10... | collective-permute-start | bytes 8650760 | tf_op jit(solution)/shard_map/ppermute | solution.py:345
  952.4 42.7 %all-to-all-start.11 = ((bf16[8,96,2048]{2,1,0:T(8,128)(2,1)}), bf16[8,96,2048]{2,1,0:T(8,128)(2,1)}, u32[]{:S(2)}, u32[]{:S(2)}) async-start(bf16[8,96,2048]{2,1,0:T(8,128)(2,1)} %bitcast.421), calls=%async_computation.11 | async-start | bytes 6291456 | tf_op jit(solution)/shard_map/all_to_all | solution.py:332
  995.2 98.1 %all-to-all-start.21 = ((f32[8,4,96]{2,1,0:T(4,128)}), f32[8,4,96]{2,1,0:T(4,128)S(1)}, u32[]{:S(2)}, u32[]{:S(2)}) async-start(f32[8,4,96]{2,1,0:T(4,128)} %maximum_bitcast_fusion), calls=%async_computation.21 | async-start | bytes 32768 | tf_op jit(solution)/shard_map/all_to_all | solution.py:332
  1093.3 49.9 %all-to-all-start.17 = ((bf16[8,96,2176]{2,1,0:T(8,128)(2,1)}), bf16[8,96,2176]{2,1,0:T(8,128)(2,1)}, u32[]{:S(2)}, u32[]{:S(2)}) async-start(bf16[8,96,2176]{2,1,0:T(8,128)(2,1)} %bitcast.454), calls=%async_computation.17 | async-start | bytes 6684672 | tf_op jit(solution)/shard_map/all_to_all | solution.py:332
  1143.2 52.6 %all-to-all-start.13 = ((bf16[8,96,2176]{2,1,0:T(8,128)(2,1)}), bf16[8,96,2176]{2,1,0:T(8,128)(2,1)}, u32[]{:S(2)}, u32[]{:S(2)}) async-start(bf16[8,96,2176]{2,1,0:T(8,128)(2,1)} %bitcast.453), calls=%async_computation.13 | async-start | bytes 6684672 | tf_op jit(solution)/shard_map/all_to_all | solution.py:332
  1195.8 49.9 %all-to-all-start.12 = ((bf16[8,96,2176]{2,1,0:T(8,128)(2,1)}), bf16[8,96,2176]{2,1,0:T(8,128)(2,1)}, u32[]{:S(2)}, u32[]{:S(2)}) async-start(bf16[8,96,2176]{2,1,0:T(8,128)(2,1)} %bitcast.452), calls=%async_computation.12 | async-start | bytes 6684672 | tf_op jit(solution)/shard_map/all_to_all | solution.py:332
  1254.8 29.3 %collective-permute-start.9 = (bf16[256,2176]{1,0:T(8,128)(2,1)S(1)}, bf16[256,2176]{1,0:T(8,128)(2,1)S(1)}, u32[]{:S(2)}, u32[]{:S(2)}) collective-permute-start(bf16[256,2176]{1,0:T(8,128)(2,1)S(1)} %pad_maximum_fusion.2), channel_id=1, source_target_pairs={{0,8},{8,16},{16,24},{24,0},{1,9},{9,17},{17,25},{25,1},{2,10},{10... | collective-permute-start | bytes 3342344 | tf_op jit(solution)/shard_map/ppermute | solution.py:345
  1261.2 82.1 %collective-permute-start.11 = (bf16[256,2176]{1,0:T(8,128)(2,1)}, bf16[256,2176]{1,0:T(8,128)(2,1)}, u32[]{:S(2)}, u32[]{:S(2)}) collective-permute-start(bf16[256,2176]{1,0:T(8,128)(2,1)} %pad_maximum_fusion.3), channel_id=1, source_target_pairs={{0,16},{8,24},{16,0},{24,8},{1,17},{9,25},{17,1},{25,9},{2,18},{10... | collective-permute-start | bytes 3342344 | tf_op jit(solution)/shard_map/ppermute | solution.py:345
  1285.1 44.8 %all-to-all-start.15 = ((bf16[8,96,2176]{2,1,0:T(8,128)(2,1)}), bf16[8,96,2176]{2,1,0:T(8,128)(2,1)}, u32[]{:S(2)}, u32[]{:S(2)}) async-start(bf16[8,96,2176]{2,1,0:T(8,128)(2,1)} %bitcast.451), calls=%async_computation.15 | async-start | bytes 6684672 | tf_op jit(solution)/shard_map/all_to_all | solution.py:332
  1335.8 23.7 %collective-permute-start.12 = (bf16[256,2176]{1,0:T(8,128)(2,1)}, bf16[256,2176]{1,0:T(8,128)(2,1)}, u32[]{:S(2)}, u32[]{:S(2)}) collective-permute-start(bf16[256,2176]{1,0:T(8,128)(2,1)} %pad_maximum_fusion.4), channel_id=1, source_target_pairs={{0,24},{8,0},{16,8},{24,16},{1,25},{9,1},{17,9},{25,17},{2,26},{10... | collective-permute-start | bytes 3342344 | tf_op jit(solution)/shard_map/ppermute | solution.py:345
  1338.1 48.2 %all-to-all-start.16 = ((bf16[8,96,2048]{2,1,0:T(8,128)(2,1)}), bf16[8,96,2048]{2,1,0:T(8,128)(2,1)}, u32[]{:S(2)}, u32[]{:S(2)}) async-start(bf16[8,96,2048]{2,1,0:T(8,128)(2,1)} %bitcast.429), calls=%async_computation.16 | async-start | bytes 6291456 | tf_op jit(solution)/shard_map/all_to_all | solution.py:332
  1342.7 50.8 %reduce-scatter.2.cloned.1.call-start = ((), (), s32[]{:S(2)}) async-start(), calls=%async_computation.29 | async-start | bytes 2396160 | tf_op jit(solution)/shard_map/reduce_scatter | solution.py:858
  1389.0 42.4 %all-to-all-start.18 = ((bf16[8,96,2048]{2,1,0:T(8,128)(2,1)}), bf16[8,96,2048]{2,1,0:T(8,128)(2,1)}, u32[]{:S(2)}, u32[]{:S(2)}) async-start(bf16[8,96,2048]{2,1,0:T(8,128)(2,1)} %bitcast.428), calls=%async_computation.18 | async-start | bytes 6291456 | tf_op jit(solution)/shard_map/all_to_all | solution.py:332
  1393.4 256.3 %all-gather.14.cloned.1.call-start = ((), (), s32[]{:S(2)}) async-start(), calls=%async_computation.30 | async-start | bytes 8785920 | tf_op jit(solution)/shard_map/all_gather | solution.py:877
  1443.7 56.0 %all-to-all-start.19 = ((bf16[8,96,2048]{2,1,0:T(8,128)(2,1)}), bf16[8,96,2048]{2,1,0:T(8,128)(2,1)}, u32[]{:S(2)}, u32[]{:S(2)}) async-start(bf16[8,96,2048]{2,1,0:T(8,128)(2,1)} %bitcast.457), calls=%async_computation.19 | async-start | bytes 6291456 | tf_op jit(solution)/shard_map/all_to_all | solution.py:332
  1499.7 63.8 %all-to-all-start.20 = ((bf16[8,96,2048]{2,1,0:T(8,128)(2,1)}), bf16[8,96,2048]{2,1,0:T(8,128)(2,1)}, u32[]{:S(2)}, u32[]{:S(2)}) async-start(bf16[8,96,2048]{2,1,0:T(8,128)(2,1)} %bitcast.432), calls=%async_computation.20 | async-start | bytes 6291456 | tf_op jit(solution)/shard_map/all_to_all | solution.py:332
  1563.5 42.6 %all-to-all-start.22 = ((bf16[8,96,2048]{2,1,0:T(8,128)(2,1)}), bf16[8,96,2048]{2,1,0:T(8,128)(2,1)}, u32[]{:S(2)}, u32[]{:S(2)}) async-start(bf16[8,96,2048]{2,1,0:T(8,128)(2,1)} %bitcast.456), calls=%async_computation.22 | async-start | bytes 6291456 | tf_op jit(solution)/shard_map/all_to_all | solution.py:332
  1572.0 76.0 %collective-permute-start.18 = (bf16[16,3584]{1,0:T(8,128)(2,1)S(1)}, bf16[16,3584]{1,0:T(8,128)(2,1)S(1)}, u32[]{:S(2)}, u32[]{:S(2)}) collective-permute-start(bf16[16,3584]{1,0:T(8,128)(2,1)S(1)} %get-tuple-element.202), channel_id=1, source_target_pairs={{0,8},{8,16},{16,24},{24,0},{1,9},{9,17},{17,25},{25,1},{2,10},{10... | collective-permute-start | bytes 344072 | tf_op jit(solution)/shard_map/ppermute | solution.py:345
  1572.9 75.2 %collective-permute-start.20 = (bf16[16,3584]{1,0:T(8,128)(2,1)S(1)}, bf16[16,3584]{1,0:T(8,128)(2,1)S(1)}, u32[]{:S(2)}, u32[]{:S(2)}) collective-permute-start(bf16[16,3584]{1,0:T(8,128)(2,1)S(1)} %get-tuple-element.203), channel_id=1, source_target_pairs={{0,24},{8,0},{16,8},{24,16},{1,25},{9,1},{17,9},{25,17},{2,26},{10... | collective-permute-start | bytes 344072 | tf_op jit(solution)/shard_map/ppermute | solution.py:345
  1575.9 72.2 %collective-permute-start.19 = (bf16[16,3584]{1,0:T(8,128)(2,1)S(1)}, bf16[16,3584]{1,0:T(8,128)(2,1)S(1)}, u32[]{:S(2)}, u32[]{:S(2)}) collective-permute-start(bf16[16,3584]{1,0:T(8,128)(2,1)S(1)} %get-tuple-element.204), channel_id=1, source_target_pairs={{0,16},{8,24},{16,0},{24,8},{1,17},{9,25},{17,1},{25,9},{2,18},{10... | collective-permute-start | bytes 344072 | tf_op jit(solution)/shard_map/ppermute | solution.py:345
  1618.0 61.6 %all-to-all-start.23 = ((bf16[8,96,2048]{2,1,0:T(8,128)(2,1)}), bf16[8,96,2048]{2,1,0:T(8,128)(2,1)}, u32[]{:S(2)}, u32[]{:S(2)}) async-start(bf16[8,96,2048]{2,1,0:T(8,128)(2,1)} %bitcast.458), calls=%async_computation.23 | async-start | bytes 6291456 | tf_op jit(solution)/shard_map/all_to_all | solution.py:332
  1622.6 244.0 %all-gather.20.cloned.1.call-start = ((), (), s32[]{:S(2)}) async-start(), calls=%async_computation.33 | async-start | bytes 3784704 | tf_op jit(solution)/shard_map/all_gather | solution.py:916
  1679.6 48.8 %all-to-all-start.24 = ((bf16[8,96,2048]{2,1,0:T(8,128)(2,1)}), bf16[8,96,2048]{2,1,0:T(8,128)(2,1)}, u32[]{:S(2)}, u32[]{:S(2)}) async-start(bf16[8,96,2048]{2,1,0:T(8,128)(2,1)} %bitcast.431), calls=%async_computation.25 | async-start | bytes 6291456 | tf_op jit(solution)/shard_map/all_to_all | solution.py:332
  1689.7 57.4 %collective-permute-start.15 = (bf16[256,2048]{1,0:T(8,128)(2,1)}, bf16[256,2048]{1,0:T(8,128)(2,1)S(1)}, u32[]{:S(2)}, u32[]{:S(2)}) collective-permute-start(bf16[256,2048]{1,0:T(8,128)(2,1)} %get-tuple-element.195), channel_id=1, source_target_pairs={{0,8},{8,16},{16,24},{24,0},{1,9},{9,17},{17,25},{25,1},{2,10},{10... | collective-permute-start | bytes 3145736 | tf_op jit(solution)/shard_map/ppermute | solution.py:345
  1690.5 59.7 %collective-permute-start.17 = (bf16[256,2048]{1,0:T(8,128)(2,1)}, bf16[256,2048]{1,0:T(8,128)(2,1)}, u32[]{:S(2)}, u32[]{:S(2)}) collective-permute-start(bf16[256,2048]{1,0:T(8,128)(2,1)} %get-tuple-element.196), channel_id=1, source_target_pairs={{0,24},{8,0},{16,8},{24,16},{1,25},{9,1},{17,9},{25,17},{2,26},{10... | collective-permute-start | bytes 3145736 | tf_op jit(solution)/shard_map/ppermute | solution.py:345
  1693.6 145.0 %collective-permute-start.16 = (bf16[256,2048]{1,0:T(8,128)(2,1)}, bf16[256,2048]{1,0:T(8,128)(2,1)}, u32[]{:S(2)}, u32[]{:S(2)}) collective-permute-start(bf16[256,2048]{1,0:T(8,128)(2,1)} %get-tuple-element.197), channel_id=1, source_target_pairs={{0,16},{8,24},{16,0},{24,8},{1,17},{9,25},{17,1},{25,9},{2,18},{10... | collective-permute-start | bytes 3145736 | tf_op jit(solution)/shard_map/ppermute | solution.py:345
  1728.4 132.7 %all-to-all-start.25 = ((bf16[8,96,2048]{2,1,0:T(8,128)(2,1)}), bf16[8,96,2048]{2,1,0:T(8,128)(2,1)}, u32[]{:S(2)}, u32[]{:S(2)}) async-start(bf16[8,96,2048]{2,1,0:T(8,128)(2,1)} %bitcast.430), calls=%async_computation.26 | async-start | bytes 6291456 | tf_op jit(solution)/shard_map/all_to_all | solution.py:332
  1736.3 107.3 %collective-permute-start.10 = (bf16[256,2048]{1,0:T(8,128)(2,1)S(1)}, bf16[256,2048]{1,0:T(8,128)(2,1)}, u32[]{:S(2)}, u32[]{:S(2)}) collective-permute-start(bf16[256,2048]{1,0:T(8,128)(2,1)S(1)} %convolution_convert_fusion.16), channel_id=1, source_target_pairs={{0,8},{8,16},{16,24},{24,0},{1,9},{9,17},{17,25},{25,1},{2,10},{10... | collective-permute-start | bytes 3145736 | tf_op jit(solution)/shard_map/ppermute | solution.py:345
  1740.1 121.0 %collective-permute-start.13 = (bf16[256,2048]{1,0:T(8,128)(2,1)S(1)}, bf16[256,2048]{1,0:T(8,128)(2,1)}, u32[]{:S(2)}, u32[]{:S(2)}) collective-permute-start(bf16[256,2048]{1,0:T(8,128)(2,1)S(1)} %convolution_convert_fusion.15), channel_id=1, source_target_pairs={{0,16},{8,24},{16,0},{24,8},{1,17},{9,25},{17,1},{25,9},{2,18},{10... | collective-permute-start | bytes 3145736 | tf_op jit(solution)/shard_map/ppermute | solution.py:345
  1743.1 95.6 %copy-start.59 = (bf16[1,256,2048]{2,1,0:T(8,128)(2,1)S(1)}, bf16[1,256,2048]{2,1,0:T(8,128)(2,1)}, u32[]{:S(2)}) copy-start(bf16[1,256,2048]{2,1,0:T(8,128)(2,1)} %param.26) | copy-start | bytes 3145732
  1743.1 95.5 %copy-start.73 = (f32[256,2048]{1,0:T(8,128)S(1)}, f32[256,2048]{1,0:T(8,128)}, u32[]{:S(2)}) copy-start(f32[256,2048]{1,0:T(8,128)} %fusion.216) | copy-start | bytes 6291460
  1747.1 114.0 %collective-permute-start.14 = (bf16[256,2048]{1,0:T(8,128)(2,1)}, bf16[256,2048]{1,0:T(8,128)(2,1)}, u32[]{:S(2)}, u32[]{:S(2)}) collective-permute-start(bf16[256,2048]{1,0:T(8,128)(2,1)} %convolution_convert_fusion.14), channel_id=1, source_target_pairs={{0,24},{8,0},{16,8},{24,16},{1,25},{9,1},{17,9},{25,17},{2,26},{10... | collective-permute-start | bytes 3145736 | tf_op jit(solution)/shard_map/ppermute | solution.py:345
  (171 other events, 1673.7 us)
Sparse Core Ops, SparseCore 0:
  9.6 264.2 all-gather.15
  276.4 158.7 all-gather.17
  436.8 152.0 all-gather.9
  675.3 139.2 all-gather.11
  1346.6 46.8 reduce-scatter.1
  1431.5 91.3 all-gather.13
  1649.9 83.7 all-gather.19

commit v7 on v6

--- a/solution.py
+++ b/solution.py
@@ -749,9 +749,8 @@
     far = size // 2
     distances = [d for d in range(1, size) if d != far] + ([far] if size > 1 else [])
     inner_parts = list(inner_sent)
-    before = output_full
-    for d in distances:
-        before = inner_parts[d] = shifted(after(inner_sent[d], before), d, size)
+    for d in distances[:1]:
+        inner_parts[d] = shifted(after(inner_sent[d], output_full), d, size)
     output_home = home_add(output_parts.reshape(holders, capacity, width), experts, copies)
     output_low = nt(attended, output_lower).astype(bf16)
     branch = nn(place, output_home) + nn(output_low, output_upper)
@@ -765,6 +764,9 @@
     packet = jnp.concatenate([normed_mlp, lanes], axis=1)
     packet = after(packet, *(inner_parts[d] for d in distances[:1]))
     packet_all = lax.all_gather(packet, "seq", axis=0, tiled=True)
+    before = packet_all
+    for d in distances[1:]:
+        before = inner_parts[d] = shifted(after(inner_sent[d], before), d, size)
     packets = [packet] + [
         lax.dynamic_slice_in_dim(packet_all, (spot + d) % size * rows, rows, 0)
         for d in range(1, size)
@@ -803,16 +805,14 @@
 
     got_rows = [send_rows(0)]
     for d in order[1:]:
-        earlier = [inner_parts[k] for k in distances[:-1]] if d == 1 else []
+        earlier = [inner_parts[distances[min(d - 1, size - 2)]]]
         got_rows.append(send_rows(d, got_rows[-1], *earlier))
-    kept = [work(0, after(got_rows[0], got_rows[-1]))]
+    kept = [work(0, after(got_rows[0], got_rows[-2]) if size > 1 else got_rows[0])]
     row_home, row_total = rows_home(0, kept[0][0])
     row_backs, row_homes = [row_total], [row_home]
     for d in order[1:]:
         kept.append(work(d, after(got_rows[d], kept[-1][0])))
         row_grad = kept[d][0]
-        if d > 2:
-            row_grad = after(row_grad, row_backs[d - 2])
         row_home, row_back = rows_home(d, row_grad)
         row_backs.append(row_back)
         row_homes.append(row_home)
@@ -875,19 +875,6 @@
     branch_sent = tn(place_any, after(middle_low, down_home)).astype(bf16)
     branch_rows = send_full(branch_sent, experts, copies)
     mlp_sums = lax.all_gather(after(mlp_sums, branch_rows), ("seq", "dp"), axis=0, tiled=True)
-    if copies == 1 and share % 128 == 0:
-        inner_up_grad, outer_down_grad, inner_down_grad, outer_up_grad = unpack_sums(
-            mlp_sums.reshape(size, adapters, rank, -1), share, width
-        )
-    else:
-        mlp_sums = mlp_sums.astype(f32).reshape(size, codes, -1)
-        inner_up_grad, outer_down_grad, inner_down_grad, outer_up_grad = jnp.split(mlp_sums, ends, axis=2)
-        inner_up_grad = inner_up_grad.reshape(size, codes, copies, 2, share).transpose(1, 3, 2, 0, 4)
-        inner_up_grad = inner_up_grad.reshape(adapters, rank, -1)
-        outer_down_grad = outer_down_grad.reshape(size, codes, copies, share).transpose(1, 2, 0, 3)
-        outer_down_grad = outer_down_grad.reshape(adapters, rank, -1)
-        inner_down_grad = jnp.sum(inner_down_grad, 0).reshape(adapters, rank, width)
-        outer_up_grad = jnp.sum(outer_up_grad, 0).reshape(adapters, rank, width)
     head_parts = nt(branch_rows.reshape(-1, width), output_full).astype(bf16)
     head_home = home_join(head_parts.reshape(holders, capacity, -1), experts, copies)
     down_home, made = down_back(down_turns[1], head_parts, head_home)
@@ -902,15 +889,6 @@
     output_lower_grad = tn(output_low_scaled, attended)
     output_low_sum = (output_low.astype(f32) * gate_column).reshape(2, rows, rank).sum(0)
     output_upper_grad = tn(output_low_sum.astype(bf16), middle_low)
-
-    def own_part(arrays):
-        joined = [a.reshape(rank, size, -1) for a in arrays]
-        joined = jnp.concatenate(joined, axis=2).transpose(1, 0, 2)
-        mine = picked(joined, spot)
-        for d in range(1, size):
-            theirs = picked(joined, (spot + d) % size).astype(bf16)
-            mine = mine + shifted(theirs, -d % size, size).astype(f32)
-        return joined, mine.astype(bf16)
 
     def over_sequences(mine, widths):
         every = lax.all_gather(mine, ("seq", "dp"), axis=0, tiled=False)
@@ -933,6 +911,22 @@
         sine_all,
     )
     query_back = send_cut(after(query_slots, down_home), experts, copies)
+    input_parts = nt(query_back.reshape(holders * capacity, -1), query_full).astype(bf16)
+    input_home = home_add(input_parts.reshape(holders, capacity, width), experts, copies)
+    mlp_sums = after(mlp_sums, input_parts)
+    if copies == 1 and share % 128 == 0:
+        inner_up_grad, outer_down_grad, inner_down_grad, outer_up_grad = unpack_sums(
+            mlp_sums.reshape(size, adapters, rank, -1), share, width
+        )
+    else:
+        mlp_sums = mlp_sums.astype(f32).reshape(size, codes, -1)
+        inner_up_grad, outer_down_grad, inner_down_grad, outer_up_grad = jnp.split(mlp_sums, ends, axis=2)
+        inner_up_grad = inner_up_grad.reshape(size, codes, copies, 2, share).transpose(1, 3, 2, 0, 4)
+        inner_up_grad = inner_up_grad.reshape(adapters, rank, -1)
+        outer_down_grad = outer_down_grad.reshape(size, codes, copies, share).transpose(1, 2, 0, 3)
+        outer_down_grad = outer_down_grad.reshape(adapters, rank, -1)
+        inner_down_grad = jnp.sum(inner_down_grad, 0).reshape(adapters, rank, width)
+        outer_up_grad = jnp.sum(outer_up_grad, 0).reshape(adapters, rank, width)
     half = key_grad.shape[1]
     pair_low_grad = nt(key_grad, pair_up[:, :half]) + nt(value_grad, pair_up[:, half:])
     pair_low_grad = pair_low_grad.astype(bf16)
@@ -951,19 +945,22 @@
         output_lower_grad,
         output_upper_grad,
     ]
-    joined, mine = own_part(sequence_grads)
-    normed_grads = pair_back(
-        after(key_grad, joined), value_grad, pair_weight, pair_low_grad, pair_down
-    )
-    mine = after(mine, mlp_sums, normed_grads)
+    joined = jnp.concatenate([a.reshape(rank, size, -1) for a in sequence_grads], axis=2)
+    joined = joined.transpose(1, 0, 2)
+    normed_grads = pair_back(key_grad, value_grad, pair_weight, pair_low_grad, pair_down)
+    mine = picked(joined, spot)
+    back_parts = []
+    for d in range(1, size):
+        theirs = picked(joined, (spot + d) % size).astype(bf16).reshape(-1, width)
+        theirs = jnp.pad(theirs, ((0, -theirs.shape[0] % 16), (0, 0)))
+        packet = jnp.concatenate([normed_grads[d * rows : (d + 1) * rows], theirs], axis=0)
+        packet = after(shifted(packet, -d % size, size), inner_up_grad)
+        back_parts.append(packet[:rows])
+        adapter_rows = mine.size // width
+        mine = mine + packet[rows : rows + adapter_rows].astype(f32).reshape(mine.shape)
+    mine = after(mine.astype(bf16), mlp_sums)
     late = over_sequences(mine, [a.shape[1] for a in sequence_grads])
-    back_parts = [
-        shifted(normed_grads[d * rows : (d + 1) * rows], -d % size, size) for d in range(1, size)
-    ]
     normed_grad = normed_grads[:rows].astype(f32) + sum(back.astype(f32) for back in back_parts)
-    input_parts = nt(query_back.reshape(holders * capacity, -1), query_full).astype(bf16)
-    input_home = home_add(input_parts.reshape(holders, capacity, width), experts, copies)
-    input_home = after(input_home, inner_up_grad)
     normed_grad = normed_grad + nn(place_any, input_home) + nn(query_low_grad, query_lower)
     normed_grad = normed_grad + nt(logit_grad.astype(bf16), router_weight)
     input_grad = norm_back(inputs, input_scale, norm_gain, normed_grad) + middle_grad

time: 1920 us -> 1840 us (0.958)
  waiting for transfers between devices: 928 us -> 826 us
  starting transfers between devices: 186 us -> 227 us
    all_to_all x26, waiting for transfers between devices: 312 us -> 189 us  [exchange(): return lax.all_to_all(buffer, 'dp', split_axis=0, concat_axis=0, tiled=True)]
    ppermute x21 -> x18, waiting for transfers between devices: 456 us -> 520 us  [shifted(): lax.ppermute(array, 'seq', [(k, (k - shift) % size) for k in range(size)])]
    all_gather x1, waiting for transfers between devices: 131 us -> 76.6 us  [body(): packet_all = lax.all_gather(packet, 'seq', axis=0, tiled=True)]
    ppermute x21 -> x18, starting transfers between devices: 65.7 us -> 107 us  [shifted(): lax.ppermute(array, 'seq', [(k, (k - shift) % size) for k in range(size)])]
    unnamed x387 -> x373, local copies, waits for them, and re-layouts: 53.5 us -> 48.7 us
  transfers between devices with their start and end apart: 54 -> 51, of which waited for: 27 -> 30; matrix products, arithmetic and copies ran while one was open for 21% -> 22% of each run, Pallas kernels for 15% -> 16%
where the time goes in v7:
time: 1840 us; the launch traced here: 1810 us
  waiting for transfers between devices  826 us (45%)
  Pallas kernels  291 us (16%)
  matrix products  287 us (16%)
  starting transfers between devices  227 us (12%)
  local copies, waits for them, and re-layouts  122 us (7%)
  other arithmetic  39.9 us (2%)
  between operations  18.5 us (1%)
    ppermute x18, waiting for transfers between devices, shifted(): lax.ppermute(array, 'seq', [(k, (k - shift) % size) for k in range(size)])  520 us
    dot_general x95, matrix products, product(): lax.dot_general(left, right, (((left_dim,), (right_dim,)), ((), ())), pre...  287 us
    all_to_all x26, waiting for transfers between devices, exchange(): return lax.all_to_all(buffer, 'dp', split_axis=0, concat_axis=0, tiled=True)  189 us
    pallas_call x4, Pallas kernels, expert_block(): pl.pallas_call(functools.partial(expert_kernel, size, share), grid_spec=p...  124 us
    all_to_all x26, starting transfers between devices, exchange(): return lax.all_to_all(buffer, 'dp', split_axis=0, concat_axis=0, tiled=True)  120 us
    ppermute x18, starting transfers between devices, shifted(): lax.ppermute(array, 'seq', [(k, (k - shift) % size) for k in range(size)])  107 us
    all_gather x1, waiting for transfers between devices, body(): packet_all = lax.all_gather(packet, 'seq', axis=0, tiled=True)  76.6 us
    unnamed x373, local copies, waits for them, and re-layouts  48.7 us
  transfers between devices with their start and end apart: 51, of which 30 were waited for; matrix products, arithmetic and copies ran while one was open for 22% of the time, Pallas kernels for 16%

profile of v7, /device:TPU:0, one launch (start us, length us, event | category | flops | bytes accessed | tf_op | source)
XLA Modules:
  0.0 1811.4 jit_solution(3120748630174437950)
XLA Ops:
  9.2 5.2 all-to-all-start.3
  34.0 28.7 %all-to-all-done = bf16[8,96,2048]{2,1,0:T(8,128)(2,1)} async-done(((bf16[8,96,2048]{2,1,0:T(8,128)(2,1)}), bf16[8,96,2048]{2,1,0:T(8,128)(2,1)}, u32[]{:S(2)}, u32[]{:S(2)}) %all-to-all-start) | async-done | bytes 3145760 | tf_op jit(solution)/shard_map/all_to_all | solution.py:332
  74.2 67.4 %collective-permute-done.2 = bf16[384,2048]{1,0:T(8,128)(2,1)} collective-permute-done((bf16[384,2048]{1,0:T(8,128)(2,1)}, bf16[384,2048]{1,0:T(8,128)(2,1)}, u32[]{:S(2)}, u32[]{:S(2)}) %collective-permute-start.2) | collective-permute-done | bytes 1572896 | tf_op jit(solution)/shard_map/ppermute | solution.py:345
  145.6 105.7 %collective-permute-done.1 = bf16[384,2048]{1,0:T(8,128)(2,1)} collective-permute-done((bf16[384,2048]{1,0:T(8,128)(2,1)}, bf16[384,2048]{1,0:T(8,128)(2,1)}, u32[]{:S(2)}, u32[]{:S(2)}) %collective-permute-start.1) | collective-permute-done | bytes 1572896 | tf_op jit(solution)/shard_map/ppermute | solution.py:345
  282.7 11.8 convolution_convert_fusion.3
  300.4 40.3 %collective-permute-start.5 = (bf16[256,2176]{1,0:T(8,128)(2,1)S(1)}, bf16[256,2176]{1,0:T(8,128)(2,1)}, u32[]{:S(2)}, u32[]{:S(2)}) collective-permute-start(bf16[256,2176]{1,0:T(8,128)(2,1)S(1)} %fusion.93), channel_id=1, source_target_pairs={{0,8},{8,16},{16,24},{24,0},{1,9},{9,17},{17,25},{25,1},{2,10},{10... | collective-permute-start | bytes 3342344 | tf_op jit(solution)/shard_map/ppermute | solution.py:345
  344.5 25.0 %collective-permute-done.5 = bf16[256,2176]{1,0:T(8,128)(2,1)} collective-permute-done((bf16[256,2176]{1,0:T(8,128)(2,1)S(1)}, bf16[256,2176]{1,0:T(8,128)(2,1)}, u32[]{:S(2)}, u32[]{:S(2)}) %collective-permute-start.5) | collective-permute-done | bytes 1114144 | tf_op jit(solution)/shard_map/ppermute | solution.py:345
  369.5 47.4 %collective-permute-done.4 = bf16[256,2176]{1,0:T(8,128)(2,1)} collective-permute-done((bf16[256,2176]{1,0:T(8,128)(2,1)S(1)}, bf16[256,2176]{1,0:T(8,128)(2,1)}, u32[]{:S(2)}, u32[]{:S(2)}) %collective-permute-start.4) | collective-permute-done | bytes 1114144 | tf_op jit(solution)/shard_map/ppermute | solution.py:345
  416.9 18.4 %all-gather.18.cloned.1.call-done = bf16[16384,512]{1,0:T(8,128)(2,1)} async-done(((bf16[2048,512]{1,0:T(8,128)(2,1)}), bf16[16384,512]{1,0:T(8,128)(2,1)}) %all-gather.18.cloned.1.call-update) | async-done | bytes 16777232 | tf_op jit(solution)/shard_map/all_gather | solution.py:696
  444.2 4.7 all-to-all-start.5
  456.8 31.5 %pairs.1 = (bf16[1024,4096]{1,0:T(8,128)(2,1)}, bf16[1024,16]{1,0:T(8,128)(2,1)S(1)}) custom-call(bf16[256,2048]{1,0:T(8,128)(2,1)S(1)} %fusion.54.refs_0_, bf16[256,2048]{1,0:T(8,128)(2,1)S(1)} %copy-done.27, bf16[256,2048]{1,0:T(8,128)(2,1)S(1)} %copy-done.26, bf16[256,2048]{1,0:T(8,128)(2,1)S(1)} %copy-done.25, bf16[8,2048,512]{2,1,0:T(8,128)(2,1)} %bitcast.498, ...), custom_call_target="tpu_custom_call" | custom-call | flops 17179869184 | bytes 16777216 | tf_op jit(solution)/shard_map/pairs/pallas_call | solution.py:75
  500.8 33.7 %attend.1 = (bf16[512,2048]{1,0:T(8,128)(2,1)S(1)}, bf16[768,2048]{1,0:T(8,128)(2,1)}, bf16[512,2048]{1,0:T(8,128)(2,1)}, f32[16,512,1]{2,1,0:T(8,128)}) custom-call(bf16[768,2048]{1,0:T(8,128)(2,1)} %bitcast.8.home_ref, bf16[512,768]{1,0:T(8,128)(2,1)S(1)} %fusion.80.place_ref, bf16[256,16]{1,0:T(8,128)(2,1)S(1)} %convolution_convert_fusion.25.low_ref, ...), custom_call_target="tpu_custom_call" | custom-call | flops 4294967296 | bytes 8388608 | tf_op jit(solution)/shard_map/attend/pallas_call | solution.py:194
  554.9 23.9 %all-to-all-done.4 = bf16[8,96,2048]{2,1,0:T(8,128)(2,1)} async-done(((bf16[8,96,2048]{2,1,0:T(8,128)(2,1)}), bf16[8,96,2048]{2,1,0:T(8,128)(2,1)}, u32[]{:S(2)}, u32[]{:S(2)}) %all-to-all-start.4) | async-done | bytes 3145760 | tf_op jit(solution)/shard_map/all_to_all | solution.py:332
  578.8 10.1 all-gather.10.cloned.1.call-done
  588.9 11.8 convolution_convert_fusion.2
  609.8 11.3 collective-permute-start.6
  621.1 22.1 %all-to-all-done.7 = bf16[8,96,2048]{2,1,0:T(8,128)(2,1)} async-done(((bf16[8,96,2048]{2,1,0:T(8,128)(2,1)}), bf16[8,96,2048]{2,1,0:T(8,128)(2,1)}, u32[]{:S(2)}, u32[]{:S(2)}) %all-to-all-start.7) | async-done | bytes 3145760 | tf_op jit(solution)/shard_map/all_to_all | solution.py:332
  654.6 31.3 %collective-permute-done.6.refs_1_ = bf16[512,2816]{1,0:T(8,128)(2,1)} collective-permute-done((bf16[512,2816]{1,0:T(8,128)(2,1)}, bf16[512,2816]{1,0:T(8,128)(2,1)}, u32[]{:S(2)}, u32[]{:S(2)}) %collective-permute-start.6) | collective-permute-done | bytes 2883616 | tf_op jit(solution)/shard_map/ppermute | solution.py:345
  694.5 76.6 %all-gather.12.cloned.1.call-done = bf16[1024,2176]{1,0:T(8,128)(2,1)} async-done(((bf16[256,2176]{1,0:T(8,128)(2,1)}), bf16[1024,2176]{1,0:T(8,128)(2,1)}) %all-gather.12.cloned.1.call-update) | async-done | bytes 4456464 | tf_op jit(solution)/shard_map/all_gather | solution.py:766
  787.7 6.5 squeeze.95
  794.2 6.8 dynamic-slice_reduce_fusion
  804.1 15.5 all-to-all-done.9
  819.6 21.3 %collective-permute-done.7.refs_3_ = bf16[512,2816]{1,0:T(8,128)(2,1)} collective-permute-done((bf16[512,2816]{1,0:T(8,128)(2,1)}, bf16[512,2816]{1,0:T(8,128)(2,1)}, u32[]{:S(2)}, u32[]{:S(2)}) %collective-permute-start.7) | collective-permute-done | bytes 2883616 | tf_op jit(solution)/shard_map/ppermute | solution.py:345
  845.1 4.9 all-to-all-start.10
  850.0 8.5 fusion.14
  869.3 18.6 %all-to-all-done.10 = bf16[8,96,2048]{2,1,0:T(8,128)(2,1)} async-done(((bf16[8,96,2048]{2,1,0:T(8,128)(2,1)}), bf16[8,96,2048]{2,1,0:T(8,128)(2,1)}, u32[]{:S(2)}, u32[]{:S(2)}) %all-to-all-start.10) | async-done | bytes 3145760 | tf_op jit(solution)/shard_map/all_to_all | solution.py:332
  892.3 8.5 fusion.12
  911.2 83.8 %collective-permute-done.8.refs_2_ = bf16[512,2816]{1,0:T(8,128)(2,1)} collective-permute-done((bf16[512,2816]{1,0:T(8,128)(2,1)}, bf16[512,2816]{1,0:T(8,128)(2,1)}, u32[]{:S(2)}, u32[]{:S(2)}) %collective-permute-start.8) | collective-permute-done | bytes 2883616 | tf_op jit(solution)/shard_map/ppermute | solution.py:345
  1003.7 4.6 all-to-all-start.13
  1008.3 8.6 fusion.6
  1022.0 31.0 %experts.4 = (bf16[768,2176]{1,0:T(8,128)(2,1)}, bf16[768,1408]{1,0:T(8,128)(2,1)S(1)}, bf16[768,2816]{1,0:T(8,128)(2,1)}, bf16[768,128]{1,0:T(8,128)(2,1)S(1)}, bf16[768,128]{1,0:T(8,128)(2,1)S(1)}) custom-call(s32[1]{0:T(128)} %bitcast.46.spot_ref, bf16[768,2048]{1,0:T(8,128)(2,1)} %bitcast.48.x_ref, bf16[768,1408]{1,0:T(8,128)(2,1)S(1)} %copy-done.21, ...), custom_call_target="tpu_custom_call" | custom-call | flops 17716740096 | bytes 27262976 | tf_op jit(solution)/shard_map/experts/pallas_call | solution.py:607
  1054.3 5.0 all-to-all-start.17
  1062.9 9.9 fusion.10
  1072.8 31.1 %experts.5 = (bf16[768,2176]{1,0:T(8,128)(2,1)}, bf16[768,1408]{1,0:T(8,128)(2,1)S(1)}, bf16[768,2816]{1,0:T(8,128)(2,1)}, bf16[768,128]{1,0:T(8,128)(2,1)S(1)}, bf16[768,128]{1,0:T(8,128)(2,1)S(1)}) custom-call(s32[1]{0:T(128)} %bitcast.46.spot_ref, bf16[768,2048]{1,0:T(8,128)(2,1)} %bitcast.50.x_ref, bf16[768,1408]{1,0:T(8,128)(2,1)S(1)} %copy-done.22, ...), custom_call_target="tpu_custom_call" | custom-call | flops 17716740096 | bytes 27262976 | tf_op jit(solution)/shard_map/experts/pallas_call | solution.py:607
  1105.2 4.8 all-to-all-start.12
  1120.0 31.0 %experts.6 = (bf16[768,2176]{1,0:T(8,128)(2,1)}, bf16[768,1408]{1,0:T(8,128)(2,1)S(1)}, bf16[768,2816]{1,0:T(8,128)(2,1)}, bf16[768,128]{1,0:T(8,128)(2,1)S(1)}, bf16[768,128]{1,0:T(8,128)(2,1)S(1)}) custom-call(s32[1]{0:T(128)} %bitcast.46.spot_ref, bf16[768,2048]{1,0:T(8,128)(2,1)} %bitcast.52.x_ref, bf16[768,1408]{1,0:T(8,128)(2,1)S(1)} %copy-done.24, ...), custom_call_target="tpu_custom_call" | custom-call | flops 17716740096 | bytes 27262976 | tf_op jit(solution)/shard_map/experts/pallas_call | solution.py:607
  1155.8 4.9 all-to-all-start.11
  1163.4 31.0 %experts.7 = (bf16[768,2176]{1,0:T(8,128)(2,1)}, bf16[768,1408]{1,0:T(8,128)(2,1)S(1)}, bf16[768,2816]{1,0:T(8,128)(2,1)}, bf16[768,128]{1,0:T(8,128)(2,1)S(1)}, bf16[768,128]{1,0:T(8,128)(2,1)S(1)}) custom-call(s32[1]{0:T(128)} %bitcast.46.spot_ref, bf16[768,2048]{1,0:T(8,128)(2,1)} %bitcast.66.x_ref, bf16[768,1408]{1,0:T(8,128)(2,1)S(1)} %copy-done.23, ...), custom_call_target="tpu_custom_call" | custom-call | flops 17716740096 | bytes 27262976 | tf_op jit(solution)/shard_map/experts/pallas_call | solution.py:607
  1247.9 5.0 fusion.8
  1270.1 31.9 %collective-permute-done.11 = bf16[256,2176]{1,0:T(8,128)(2,1)} collective-permute-done((bf16[256,2176]{1,0:T(8,128)(2,1)}, bf16[256,2176]{1,0:T(8,128)(2,1)}, u32[]{:S(2)}, u32[]{:S(2)}) %collective-permute-start.11) | collective-permute-done | bytes 1114144 | tf_op jit(solution)/shard_map/ppermute | solution.py:345
  1301.9 10.6 collective-permute-done.12
  1330.4 37.8 %all-to-all-done.18 = bf16[8,96,2048]{2,1,0:T(8,128)(2,1)} async-done(((bf16[8,96,2048]{2,1,0:T(8,128)(2,1)}), bf16[8,96,2048]{2,1,0:T(8,128)(2,1)}, u32[]{:S(2)}, u32[]{:S(2)}) %all-to-all-start.18) | async-done | bytes 3145760 | tf_op jit(solution)/shard_map/all_to_all | solution.py:332
  1368.2 11.9 convolution_convert_fusion.1
  1380.2 5.0 all-to-all-start.19
  1396.6 7.8 fusion.4
  1407.1 25.5 %all-to-all-done.19 = bf16[8,96,2048]{2,1,0:T(8,128)(2,1)} async-done(((bf16[8,96,2048]{2,1,0:T(8,128)(2,1)}), bf16[8,96,2048]{2,1,0:T(8,128)(2,1)}, u32[]{:S(2)}, u32[]{:S(2)}) %all-to-all-start.19) | async-done | bytes 3145760 | tf_op jit(solution)/shard_map/all_to_all | solution.py:332
  1440.3 44.1 %attend_back.1 = (bf16[1024,2048]{1,0:T(8,128)(2,1)}, bf16[1024,2048]{1,0:T(8,128)(2,1)}, bf16[768,2048]{1,0:T(8,128)(2,1)}, bf16[256,2048]{1,0:T(8,128)(2,1)S(1)}) custom-call(bf16[512,2048]{1,0:T(8,128)(2,1)} %get-tuple-element.131.query_ref, bf16[1024,4096]{1,0:T(8,128)(2,1)} %get-tuple-element.98.key_ref.value_ref, ...), custom_call_target="tpu_custom_call" | custom-call | flops 10737418240 | bytes 16777216 | tf_op jit(solution)/shard_map/attend_back/pallas_call | solution.py:289
  1498.0 4.8 all-to-all-start.22
  1508.7 23.2 %pair_back.1 = bf16[1024,2048]{1,0:T(8,128)(2,1)S(1)} custom-call(bf16[1024,2048]{1,0:T(8,128)(2,1)} %get-tuple-element.160.key_ref, bf16[1024,2048]{1,0:T(8,128)(2,1)} %get-tuple-element.161.value_ref, bf16[8,2048,512]{2,1,0:T(8,128)(2,1)} %bitcast.499, bf16[1024,16]{1,0:T(8,128)(2,1)S(1)} %fusion.81.low_ref, bf16[16,2048]{1,0:T(8,128)(2,1)S(1)} %copy-done.46), custom_call_target="tpu_custom_call" | custom-call | flops 17179869184 | bytes 16777216 | tf_op jit(solution)/shard_map/pair_back/pallas_call | solution.py:129
  1534.0 6.7 all-to-all-done.22
  1540.7 11.9 convolution_convert_fusion
  1559.5 10.7 collective-permute-start.16
  1576.0 7.1 fusion.2
  1585.8 9.2 all-to-all-done.23
  1599.5 19.3 %unpack.1 = (f32[8,16,11264]{2,1,0:T(8,128)}, f32[8,16,5632]{2,1,0:T(8,128)}, f32[8,16,2048]{2,1,0:T(8,128)}, f32[8,16,2048]{2,1,0:T(8,128)}) custom-call(bf16[4,8,16,8320]{3,2,1,0:T(8,128)(2,1)} %bitcast.430), custom_call_target="tpu_custom_call" | custom-call | bytes 32243712 | tf_op jit(solution)/shard_map/unpack/pallas_call | solution.py:485
  1622.3 28.2 %collective-permute-done.15 = bf16[288,2048]{1,0:T(8,128)(2,1)} collective-permute-done((bf16[288,2048]{1,0:T(8,128)(2,1)}, bf16[288,2048]{1,0:T(8,128)(2,1)}, u32[]{:S(2)}, u32[]{:S(2)}) %collective-permute-start.15) | collective-permute-done | bytes 1179680 | tf_op jit(solution)/shard_map/ppermute | solution.py:345
  1655.3 7.8 fusion
  1674.2 22.7 %collective-permute-start.9 = (bf16[256,2048]{1,0:T(8,128)(2,1)}, bf16[256,2048]{1,0:T(8,128)(2,1)S(1)}, u32[]{:S(2)}, u32[]{:S(2)}) collective-permute-start(bf16[256,2048]{1,0:T(8,128)(2,1)} %convolution_convert_fusion.16), channel_id=1, source_target_pairs={{0,8},{8,16},{16,24},{24,0},{1,9},{9,17},{17,25},{25,1},{2,10},{10... | collective-permute-start | bytes 3145736 | tf_op jit(solution)/shard_map/ppermute | solution.py:345
  1710.5 14.3 collective-permute-done.9
  1724.8 30.6 %collective-permute-done.13 = bf16[256,2048]{1,0:T(8,128)(2,1)} collective-permute-done((bf16[256,2048]{1,0:T(8,128)(2,1)}, bf16[256,2048]{1,0:T(8,128)(2,1)}, u32[]{:S(2)}, u32[]{:S(2)}) %collective-permute-start.13) | collective-permute-done | bytes 1048608 | tf_op jit(solution)/shard_map/ppermute | solution.py:345
  1755.5 15.2 collective-permute-done.14
  1770.7 5.1 fusion.100
  1784.9 11.4 all-gather.20.cloned.1.call-done
  1798.3 6.0 gather_adapters.1
  (687 shorter events, 435.6 us)
Async XLA Ops:
  7.2 431.3 %copy-start = (bf16[8,16,4096]{2,1,0:T(8,128)(2,1)S(1)}, bf16[8,16,4096]{2,1,0:T(8,128)(2,1)}, u32[]{:S(2)}) copy-start(bf16[8,16,4096]{2,1,0:T(8,128)(2,1)} %param.37) | copy-start | bytes 3145732
  7.2 268.6 %all-gather.16.cloned.1.call-start = ((), (), s32[]{:S(2)}) async-start(), calls=%async_computation.31 | async-start | bytes 10485760 | tf_op jit(solution)/shard_map/all_gather | solution.py:685
  9.2 10.9 all-to-all-start.3
  17.4 588.1 %copy-start.2 = (bf16[256,2048]{1,0:T(8,128)(2,1)}, bf16[256,2048]{1,0:T(8,128)(2,1)S(1)}, u32[]{:S(2)}) copy-start(bf16[256,2048]{1,0:T(8,128)(2,1)S(1)} %fusion.54.refs_0_) | copy-start | bytes 3145732
  20.1 42.5 %all-to-all-start = ((bf16[8,96,2048]{2,1,0:T(8,128)(2,1)}), bf16[8,96,2048]{2,1,0:T(8,128)(2,1)}, u32[]{:S(2)}, u32[]{:S(2)}) async-start(bf16[8,96,2048]{2,1,0:T(8,128)(2,1)} %bitcast.418), calls=%async_computation | async-start | bytes 6291456 | tf_op jit(solution)/shard_map/all_to_all | solution.py:332
  62.7 213.1 %all-to-all-start.2 = ((bf16[8,96,2048]{2,1,0:T(8,128)(2,1)}), bf16[8,96,2048]{2,1,0:T(8,128)(2,1)}, u32[]{:S(2)}, u32[]{:S(2)}) async-start(bf16[8,96,2048]{2,1,0:T(8,128)(2,1)} %bitcast.415), calls=%async_computation.2 | async-start | bytes 6291456 | tf_op jit(solution)/shard_map/all_to_all | solution.py:332
  67.3 368.0 %all-gather.18.cloned.1.call-start = ((), (), s32[]{:S(2)}) async-start(), calls=%async_computation.32 | async-start | bytes 18874368 | tf_op jit(solution)/shard_map/all_gather | solution.py:696
  68.6 73.1 %collective-permute-start.2 = (bf16[384,2048]{1,0:T(8,128)(2,1)}, bf16[384,2048]{1,0:T(8,128)(2,1)}, u32[]{:S(2)}, u32[]{:S(2)}) collective-permute-start(bf16[384,2048]{1,0:T(8,128)(2,1)} %pad_maximum_fusion.1), channel_id=1, source_target_pairs={{0,8},{8,16},{16,24},{24,0},{1,9},{9,17},{17,25},{25,1},{2,10},{10... | collective-permute-start | bytes 4718600 | tf_op jit(solution)/shard_map/ppermute | solution.py:345
  70.1 181.3 %collective-permute-start.1 = (bf16[384,2048]{1,0:T(8,128)(2,1)}, bf16[384,2048]{1,0:T(8,128)(2,1)}, u32[]{:S(2)}, u32[]{:S(2)}) collective-permute-start(bf16[384,2048]{1,0:T(8,128)(2,1)} %pad_maximum_fusion.1), channel_id=1, source_target_pairs={{0,16},{8,24},{16,0},{24,8},{1,17},{9,25},{17,1},{25,9},{2,18},{10... | collective-permute-start | bytes 4718600 | tf_op jit(solution)/shard_map/ppermute | solution.py:345
  72.7 185.9 %collective-permute-start = (bf16[384,2048]{1,0:T(8,128)(2,1)}, bf16[384,2048]{1,0:T(8,128)(2,1)}, u32[]{:S(2)}, u32[]{:S(2)}) collective-permute-start(bf16[384,2048]{1,0:T(8,128)(2,1)} %pad_maximum_fusion.1), channel_id=1, source_target_pairs={{0,24},{8,0},{16,8},{24,16},{1,25},{9,1},{17,9},{25,17},{2,26},{10... | collective-permute-start | bytes 4718600 | tf_op jit(solution)/shard_map/ppermute | solution.py:345
  74.2 726.9 %copy-start.47 = (s32[8]{0:T(128)}, s32[8]{0:T(128)S(1)}, u32[]{:S(2)}) copy-start(s32[8]{0:T(128)S(1)} %slice_reduce_fusion.4.ids_ref) | copy-start | bytes 100
  294.6 122.3 %all-to-all-start.1 = ((bf16[8,96,2048]{2,1,0:T(8,128)(2,1)}), bf16[8,96,2048]{2,1,0:T(8,128)(2,1)}, u32[]{:S(2)}, u32[]{:S(2)}) async-start(bf16[8,96,2048]{2,1,0:T(8,128)(2,1)} %bitcast.457), calls=%async_computation.1 | async-start | bytes 6291456 | tf_op jit(solution)/shard_map/all_to_all | solution.py:332
  299.0 289.9 %all-gather.10.cloned.1.call-start = ((), (), s32[]{:S(2)}) async-start(), calls=%async_computation.27 | async-start | bytes 10485760 | tf_op jit(solution)/shard_map/all_gather | solution.py:735
  300.4 69.1 %collective-permute-start.5 = (bf16[256,2176]{1,0:T(8,128)(2,1)S(1)}, bf16[256,2176]{1,0:T(8,128)(2,1)}, u32[]{:S(2)}, u32[]{:S(2)}) collective-permute-start(bf16[256,2176]{1,0:T(8,128)(2,1)S(1)} %fusion.93), channel_id=1, source_target_pairs={{0,8},{8,16},{16,24},{24,0},{1,9},{9,17},{17,25},{25,1},{2,10},{10... | collective-permute-start | bytes 3342344 | tf_op jit(solution)/shard_map/ppermute | solution.py:345
  340.7 76.2 %collective-permute-start.4 = (bf16[256,2176]{1,0:T(8,128)(2,1)S(1)}, bf16[256,2176]{1,0:T(8,128)(2,1)}, u32[]{:S(2)}, u32[]{:S(2)}) collective-permute-start(bf16[256,2176]{1,0:T(8,128)(2,1)S(1)} %fusion.93), channel_id=1, source_target_pairs={{0,16},{8,24},{16,0},{24,8},{1,17},{9,25},{17,1},{25,9},{2,18},{10... | collective-permute-start | bytes 3342344 | tf_op jit(solution)/shard_map/ppermute | solution.py:345
  344.5 72.4 %collective-permute-start.3 = (bf16[256,2176]{1,0:T(8,128)(2,1)S(1)}, bf16[256,2176]{1,0:T(8,128)(2,1)}, u32[]{:S(2)}, u32[]{:S(2)}) collective-permute-start(bf16[256,2176]{1,0:T(8,128)(2,1)S(1)} %fusion.93), channel_id=1, source_target_pairs={{0,24},{8,0},{16,8},{24,16},{1,25},{9,1},{17,9},{25,17},{2,26},{10... | collective-permute-start | bytes 3342344 | tf_op jit(solution)/shard_map/ppermute | solution.py:345
  444.2 46.9 %all-to-all-start.5 = ((bf16[8,96,2048]{2,1,0:T(8,128)(2,1)}), bf16[8,96,2048]{2,1,0:T(8,128)(2,1)}, u32[]{:S(2)}, u32[]{:S(2)}) async-start(bf16[8,96,2048]{2,1,0:T(8,128)(2,1)} %bitcast.422), calls=%async_computation.5 | async-start | bytes 6291456 | tf_op jit(solution)/shard_map/all_to_all | solution.py:332
  491.1 45.3 %all-to-all-start.6 = ((bf16[8,96,2048]{2,1,0:T(8,128)(2,1)}), bf16[8,96,2048]{2,1,0:T(8,128)(2,1)}, u32[]{:S(2)}, u32[]{:S(2)}) async-start(bf16[8,96,2048]{2,1,0:T(8,128)(2,1)} %bitcast.419), calls=%async_computation.6 | async-start | bytes 6291456 | tf_op jit(solution)/shard_map/all_to_all | solution.py:332
  536.4 42.3 %all-to-all-start.4 = ((bf16[8,96,2048]{2,1,0:T(8,128)(2,1)}), bf16[8,96,2048]{2,1,0:T(8,128)(2,1)}, u32[]{:S(2)}, u32[]{:S(2)}) async-start(bf16[8,96,2048]{2,1,0:T(8,128)(2,1)} %bitcast.453), calls=%async_computation.4 | async-start | bytes 6291456 | tf_op jit(solution)/shard_map/all_to_all | solution.py:332
  600.8 42.5 %all-to-all-start.7 = ((bf16[8,96,2048]{2,1,0:T(8,128)(2,1)}), bf16[8,96,2048]{2,1,0:T(8,128)(2,1)}, u32[]{:S(2)}, u32[]{:S(2)}) async-start(bf16[8,96,2048]{2,1,0:T(8,128)(2,1)} %bitcast.458), calls=%async_computation.7 | async-start | bytes 6291456 | tf_op jit(solution)/shard_map/all_to_all | solution.py:332
  605.4 165.6 %all-gather.12.cloned.1.call-start = ((), (), s32[]{:S(2)}) async-start(), calls=%async_computation.28 | async-start | bytes 5570560 | tf_op jit(solution)/shard_map/all_gather | solution.py:766
  605.5 47.1 %copy-start.146 = (s32[256,2]{0,1:T(2,128)}, s32[256,2]{0,1:T(2,128)S(1)}, u32[]{:S(2)}) copy-start(s32[256,2]{0,1:T(2,128)S(1)} %copy.263) | copy-start | bytes 6148
  609.8 76.0 %collective-permute-start.6 = (bf16[512,2816]{1,0:T(8,128)(2,1)}, bf16[512,2816]{1,0:T(8,128)(2,1)}, u32[]{:S(2)}, u32[]{:S(2)}) collective-permute-start(bf16[512,2816]{1,0:T(8,128)(2,1)} %copy-done.19), channel_id=1, source_target_pairs={{0,24},{8,0},{16,8},{24,16},{1,25},{9,1},{17,9},{25,17},{2,26},{10... | collective-permute-start | bytes 8650760 | tf_op jit(solution)/shard_map/ppermute | solution.py:345
  689.9 84.6 %all-to-all-start.8 = ((bf16[8,96,2048]{2,1,0:T(8,128)(2,1)}), bf16[8,96,2048]{2,1,0:T(8,128)(2,1)}, u32[]{:S(2)}, u32[]{:S(2)}) async-start(bf16[8,96,2048]{2,1,0:T(8,128)(2,1)} %bitcast.416), calls=%async_computation.8 | async-start | bytes 6291456 | tf_op jit(solution)/shard_map/all_to_all | solution.py:332
  694.4 80.1 %copy-start.79 = (bf16[512,768]{1,0:T(8,128)(2,1)S(1)}, bf16[512,768]{1,0:T(8,128)(2,1)}, u32[]{:S(2)}) copy-start(bf16[512,768]{1,0:T(8,128)(2,1)} %copy-done.78) | copy-start | bytes 2359300
  774.5 66.4 %collective-permute-start.7 = (bf16[512,2816]{1,0:T(8,128)(2,1)}, bf16[512,2816]{1,0:T(8,128)(2,1)}, u32[]{:S(2)}, u32[]{:S(2)}) collective-permute-start(bf16[512,2816]{1,0:T(8,128)(2,1)} %copy-done.18), channel_id=1, source_target_pairs={{0,8},{8,16},{16,24},{24,0},{1,9},{9,17},{17,25},{25,1},{2,10},{10... | collective-permute-start | bytes 8650760 | tf_op jit(solution)/shard_map/ppermute | solution.py:345
  777.2 42.4 %all-to-all-start.9 = ((bf16[8,96,2048]{2,1,0:T(8,128)(2,1)}), bf16[8,96,2048]{2,1,0:T(8,128)(2,1)}, u32[]{:S(2)}, u32[]{:S(2)}) async-start(bf16[8,96,2048]{2,1,0:T(8,128)(2,1)} %bitcast.420), calls=%async_computation.9 | async-start | bytes 6291456 | tf_op jit(solution)/shard_map/all_to_all | solution.py:332
  787.7 113.2 %copy-start.61 = (bf16[128,1,1408]{2,0,1:T(8,128)(2,1)}, bf16[128,1,1408]{2,0,1:T(8,128)(2,1)S(1)}, u32[]{:S(2)}) copy-start(bf16[128,1,1408]{2,0,1:T(8,128)(2,1)S(1)} %copy.303) | copy-start | bytes 1081348
  804.1 54.4 %copy-start.107 = (bf16[768,128]{1,0:T(8,128)(2,1)}, bf16[768,128]{1,0:T(8,128)(2,1)S(1)}, u32[]{:S(2)}) copy-start(bf16[768,128]{1,0:T(8,128)(2,1)S(1)} %fusion.85) | copy-start | bytes 589828
  845.1 42.8 %all-to-all-start.10 = ((bf16[8,96,2048]{2,1,0:T(8,128)(2,1)}), bf16[8,96,2048]{2,1,0:T(8,128)(2,1)}, u32[]{:S(2)}, u32[]{:S(2)}) async-start(bf16[8,96,2048]{2,1,0:T(8,128)(2,1)} %bitcast.421), calls=%async_computation.10 | async-start | bytes 6291456 | tf_op jit(solution)/shard_map/all_to_all | solution.py:332
  869.3 125.8 %collective-permute-start.8 = (bf16[512,2816]{1,0:T(8,128)(2,1)}, bf16[512,2816]{1,0:T(8,128)(2,1)}, u32[]{:S(2)}, u32[]{:S(2)}) collective-permute-start(bf16[512,2816]{1,0:T(8,128)(2,1)} %cut.6), channel_id=1, source_target_pairs={{0,16},{8,24},{16,0},{24,8},{1,17},{9,25},{17,1},{25,9},{2,18},{10... | collective-permute-start | bytes 8650760 | tf_op jit(solution)/shard_map/ppermute | solution.py:345
  887.9 107.2 %all-to-all-start.14 = ((bf16[8,96,2048]{2,1,0:T(8,128)(2,1)}), bf16[8,96,2048]{2,1,0:T(8,128)(2,1)}, u32[]{:S(2)}, u32[]{:S(2)}) async-start(bf16[8,96,2048]{2,1,0:T(8,128)(2,1)} %bitcast.417), calls=%async_computation.14 | async-start | bytes 6291456 | tf_op jit(solution)/shard_map/all_to_all | solution.py:332
  903.0 96.0 %copy-start.81 = (bf16[512,768]{1,0:T(8,128)(2,1)S(1)}, bf16[512,768]{1,0:T(8,128)(2,1)}, u32[]{:S(2)}) copy-start(bf16[512,768]{1,0:T(8,128)(2,1)} %copy-done.80) | copy-start | bytes 2359300
  995.0 8.6 all-to-all-start.21
  1003.7 50.6 %all-to-all-start.13 = ((bf16[8,96,2048]{2,1,0:T(8,128)(2,1)}), bf16[8,96,2048]{2,1,0:T(8,128)(2,1)}, u32[]{:S(2)}, u32[]{:S(2)}) async-start(bf16[8,96,2048]{2,1,0:T(8,128)(2,1)} %bitcast.423), calls=%async_computation.13 | async-start | bytes 6291456 | tf_op jit(solution)/shard_map/all_to_all | solution.py:332
  1054.3 50.9 %all-to-all-start.17 = ((bf16[8,96,2176]{2,1,0:T(8,128)(2,1)}), bf16[8,96,2176]{2,1,0:T(8,128)(2,1)}, u32[]{:S(2)}, u32[]{:S(2)}) async-start(bf16[8,96,2176]{2,1,0:T(8,128)(2,1)} %bitcast.452), calls=%async_computation.17 | async-start | bytes 6684672 | tf_op jit(solution)/shard_map/all_to_all | solution.py:332
  1105.2 50.7 %all-to-all-start.12 = ((bf16[8,96,2176]{2,1,0:T(8,128)(2,1)}), bf16[8,96,2176]{2,1,0:T(8,128)(2,1)}, u32[]{:S(2)}, u32[]{:S(2)}) async-start(bf16[8,96,2176]{2,1,0:T(8,128)(2,1)} %bitcast.450), calls=%async_computation.12 | async-start | bytes 6684672 | tf_op jit(solution)/shard_map/all_to_all | solution.py:332
  1155.8 50.0 %all-to-all-start.11 = ((bf16[8,96,2176]{2,1,0:T(8,128)(2,1)}), bf16[8,96,2176]{2,1,0:T(8,128)(2,1)}, u32[]{:S(2)}, u32[]{:S(2)}) async-start(bf16[8,96,2176]{2,1,0:T(8,128)(2,1)} %bitcast.451), calls=%async_computation.11 | async-start | bytes 6684672 | tf_op jit(solution)/shard_map/all_to_all | solution.py:332
  1205.8 50.0 %all-to-all-start.15 = ((bf16[8,96,2176]{2,1,0:T(8,128)(2,1)}), bf16[8,96,2176]{2,1,0:T(8,128)(2,1)}, u32[]{:S(2)}, u32[]{:S(2)}) async-start(bf16[8,96,2176]{2,1,0:T(8,128)(2,1)} %bitcast.449), calls=%async_computation.15 | async-start | bytes 6684672 | tf_op jit(solution)/shard_map/all_to_all | solution.py:332
  1224.9 45.1 %collective-permute-start.10 = (bf16[256,2176]{1,0:T(8,128)(2,1)}, bf16[256,2176]{1,0:T(8,128)(2,1)}, u32[]{:S(2)}, u32[]{:S(2)}) collective-permute-start(bf16[256,2176]{1,0:T(8,128)(2,1)} %pad_maximum_fusion.2), channel_id=1, source_target_pairs={{0,8},{8,16},{16,24},{24,0},{1,9},{9,17},{17,25},{25,1},{2,10},{10... | collective-permute-start | bytes 3342344 | tf_op jit(solution)/shard_map/ppermute | solution.py:345
  1231.6 70.3 %collective-permute-start.11 = (bf16[256,2176]{1,0:T(8,128)(2,1)}, bf16[256,2176]{1,0:T(8,128)(2,1)}, u32[]{:S(2)}, u32[]{:S(2)}) collective-permute-start(bf16[256,2176]{1,0:T(8,128)(2,1)} %pad_maximum_fusion.3), channel_id=1, source_target_pairs={{0,16},{8,24},{16,0},{24,8},{1,17},{9,25},{17,1},{25,9},{2,18},{10... | collective-permute-start | bytes 3342344 | tf_op jit(solution)/shard_map/ppermute | solution.py:345
  1261.7 50.8 %collective-permute-start.12 = (bf16[256,2176]{1,0:T(8,128)(2,1)}, bf16[256,2176]{1,0:T(8,128)(2,1)}, u32[]{:S(2)}, u32[]{:S(2)}) collective-permute-start(bf16[256,2176]{1,0:T(8,128)(2,1)} %pad_maximum_fusion.4), channel_id=1, source_target_pairs={{0,24},{8,0},{16,8},{24,16},{1,25},{9,1},{17,9},{25,17},{2,26},{10... | collective-permute-start | bytes 3342344 | tf_op jit(solution)/shard_map/ppermute | solution.py:345
  1264.8 58.3 %all-to-all-start.16 = ((bf16[8,96,2048]{2,1,0:T(8,128)(2,1)}), bf16[8,96,2048]{2,1,0:T(8,128)(2,1)}, u32[]{:S(2)}, u32[]{:S(2)}) async-start(bf16[8,96,2048]{2,1,0:T(8,128)(2,1)} %bitcast.425), calls=%async_computation.16 | async-start | bytes 6291456 | tf_op jit(solution)/shard_map/all_to_all | solution.py:332
  1269.4 61.0 %reduce-scatter.2.cloned.1.call-start = ((), (), s32[]{:S(2)}) async-start(), calls=%async_computation.29 | async-start | bytes 2396160 | tf_op jit(solution)/shard_map/reduce_scatter | solution.py:858
  1270.0 47.1 %copy-start.148 = (f32[256,2]{0,1:T(2,128)S(1)}, f32[256,2]{0,1:T(2,128)}, u32[]{:S(2)}) copy-start(f32[256,2]{0,1:T(2,128)} %get-tuple-element.188) | copy-start | bytes 6148
  1270.0 47.2 %copy-start.147 = (s32[256,2]{0,1:T(2,128)S(1)}, s32[256,2]{0,1:T(2,128)}, u32[]{:S(2)}) copy-start(s32[256,2]{0,1:T(2,128)} %copy-done.146) | copy-start | bytes 6148
  1270.0 47.2 %copy-start.128 = (bf16[2048,8]{0,1:T(8,128)(2,1)S(1)}, bf16[2048,8]{0,1:T(8,128)(2,1)}, u32[]{:S(2)}) copy-start(bf16[2048,8]{0,1:T(8,128)(2,1)} %param.33) | copy-start | bytes 98308
  1270.0 47.2 %copy-start.133 = (f32[2048]{0:T(1024)S(1)}, f32[2048]{0:T(1024)}, u32[]{:S(2)}) copy-start(f32[2048]{0:T(1024)} %param.32) | copy-start | bytes 24580
  1325.8 42.4 %all-to-all-start.18 = ((bf16[8,96,2048]{2,1,0:T(8,128)(2,1)}), bf16[8,96,2048]{2,1,0:T(8,128)(2,1)}, u32[]{:S(2)}, u32[]{:S(2)}) async-start(bf16[8,96,2048]{2,1,0:T(8,128)(2,1)} %bitcast.424), calls=%async_computation.18 | async-start | bytes 6291456 | tf_op jit(solution)/shard_map/all_to_all | solution.py:332
  1330.3 269.2 %all-gather.14.cloned.1.call-start = ((), (), s32[]{:S(2)}) async-start(), calls=%async_computation.30 | async-start | bytes 8785920 | tf_op jit(solution)/shard_map/all_gather | solution.py:877
  1380.2 52.4 %all-to-all-start.19 = ((bf16[8,96,2048]{2,1,0:T(8,128)(2,1)}), bf16[8,96,2048]{2,1,0:T(8,128)(2,1)}, u32[]{:S(2)}, u32[]{:S(2)}) async-start(bf16[8,96,2048]{2,1,0:T(8,128)(2,1)} %bitcast.455), calls=%async_computation.19 | async-start | bytes 6291456 | tf_op jit(solution)/shard_map/all_to_all | solution.py:332
  1432.6 65.4 %all-to-all-start.20 = ((bf16[8,96,2048]{2,1,0:T(8,128)(2,1)}), bf16[8,96,2048]{2,1,0:T(8,128)(2,1)}, u32[]{:S(2)}, u32[]{:S(2)}) async-start(bf16[8,96,2048]{2,1,0:T(8,128)(2,1)} %bitcast.426), calls=%async_computation.20 | async-start | bytes 6291456 | tf_op jit(solution)/shard_map/all_to_all | solution.py:332
  1498.0 42.7 %all-to-all-start.22 = ((bf16[8,96,2048]{2,1,0:T(8,128)(2,1)}), bf16[8,96,2048]{2,1,0:T(8,128)(2,1)}, u32[]{:S(2)}, u32[]{:S(2)}) async-start(bf16[8,96,2048]{2,1,0:T(8,128)(2,1)} %bitcast.454), calls=%async_computation.22 | async-start | bytes 6291456 | tf_op jit(solution)/shard_map/all_to_all | solution.py:332
  1552.6 42.4 %all-to-all-start.23 = ((bf16[8,96,2048]{2,1,0:T(8,128)(2,1)}), bf16[8,96,2048]{2,1,0:T(8,128)(2,1)}, u32[]{:S(2)}, u32[]{:S(2)}) async-start(bf16[8,96,2048]{2,1,0:T(8,128)(2,1)} %bitcast.456), calls=%async_computation.23 | async-start | bytes 6291456 | tf_op jit(solution)/shard_map/all_to_all | solution.py:332
  1559.5 62.9 %collective-permute-start.16 = (bf16[288,2048]{1,0:T(8,128)(2,1)S(1)}, bf16[288,2048]{1,0:T(8,128)(2,1)}, u32[]{:S(2)}, u32[]{:S(2)}) collective-permute-start(bf16[288,2048]{1,0:T(8,128)(2,1)S(1)} %fusion.83), channel_id=1, source_target_pairs={{0,16},{8,24},{16,0},{24,8},{1,17},{9,25},{17,1},{25,9},{2,18},{10... | collective-permute-start | bytes 3538952 | tf_op jit(solution)/shard_map/ppermute | solution.py:345
  1571.3 50.6 %collective-permute-start.17 = (bf16[288,2048]{1,0:T(8,128)(2,1)}, bf16[288,2048]{1,0:T(8,128)(2,1)}, u32[]{:S(2)}, u32[]{:S(2)}) collective-permute-start(bf16[288,2048]{1,0:T(8,128)(2,1)} %fusion.84), channel_id=1, source_target_pairs={{0,24},{8,0},{16,8},{24,16},{1,25},{9,1},{17,9},{25,17},{2,26},{10... | collective-permute-start | bytes 3538952 | tf_op jit(solution)/shard_map/ppermute | solution.py:345
  1575.8 74.7 %collective-permute-start.15 = (bf16[288,2048]{1,0:T(8,128)(2,1)}, bf16[288,2048]{1,0:T(8,128)(2,1)}, u32[]{:S(2)}, u32[]{:S(2)}) collective-permute-start(bf16[288,2048]{1,0:T(8,128)(2,1)} %fusion.82), channel_id=1, source_target_pairs={{0,8},{8,16},{16,24},{24,0},{1,9},{9,17},{17,25},{25,1},{2,10},{10... | collective-permute-start | bytes 3538952 | tf_op jit(solution)/shard_map/ppermute | solution.py:345
  1595.0 70.6 %all-to-all-start.24 = ((bf16[8,96,2048]{2,1,0:T(8,128)(2,1)}), bf16[8,96,2048]{2,1,0:T(8,128)(2,1)}, u32[]{:S(2)}, u32[]{:S(2)}) async-start(bf16[8,96,2048]{2,1,0:T(8,128)(2,1)} %bitcast.427), calls=%async_computation.24 | async-start | bytes 6291456 | tf_op jit(solution)/shard_map/all_to_all | solution.py:332
  1599.5 196.8 %all-gather.20.cloned.1.call-start = ((), (), s32[]{:S(2)}) async-start(), calls=%async_computation.33 | async-start | bytes 3784704 | tf_op jit(solution)/shard_map/all_gather | solution.py:894
  1665.7 89.8 %all-to-all-start.25 = ((bf16[8,96,2048]{2,1,0:T(8,128)(2,1)}), bf16[8,96,2048]{2,1,0:T(8,128)(2,1)}, u32[]{:S(2)}, u32[]{:S(2)}) async-start(bf16[8,96,2048]{2,1,0:T(8,128)(2,1)} %bitcast.428), calls=%async_computation.25 | async-start | bytes 6291456 | tf_op jit(solution)/shard_map/all_to_all | solution.py:332
  1674.2 50.7 %collective-permute-start.9 = (bf16[256,2048]{1,0:T(8,128)(2,1)}, bf16[256,2048]{1,0:T(8,128)(2,1)S(1)}, u32[]{:S(2)}, u32[]{:S(2)}) collective-permute-start(bf16[256,2048]{1,0:T(8,128)(2,1)} %convolution_convert_fusion.16), channel_id=1, source_target_pairs={{0,8},{8,16},{16,24},{24,0},{1,9},{9,17},{17,25},{25,1},{2,10},{10... | collective-permute-start | bytes 3145736 | tf_op jit(solution)/shard_map/ppermute | solution.py:345
  1700.9 54.6 %collective-permute-start.13 = (bf16[256,2048]{1,0:T(8,128)(2,1)}, bf16[256,2048]{1,0:T(8,128)(2,1)}, u32[]{:S(2)}, u32[]{:S(2)}) collective-permute-start(bf16[256,2048]{1,0:T(8,128)(2,1)} %convolution_convert_fusion.15), channel_id=1, source_target_pairs={{0,16},{8,24},{16,0},{24,8},{1,17},{9,25},{17,1},{25,9},{2,18},{10... | collective-permute-start | bytes 3145736 | tf_op jit(solution)/shard_map/ppermute | solution.py:345
  1706.6 64.0 %collective-permute-start.14 = (bf16[256,2048]{1,0:T(8,128)(2,1)}, bf16[256,2048]{1,0:T(8,128)(2,1)}, u32[]{:S(2)}, u32[]{:S(2)}) collective-permute-start(bf16[256,2048]{1,0:T(8,128)(2,1)} %convolution_convert_fusion.14), channel_id=1, source_target_pairs={{0,24},{8,0},{16,8},{24,16},{1,25},{9,1},{17,9},{25,17},{2,26},{10... | collective-permute-start | bytes 3145736 | tf_op jit(solution)/shard_map/ppermute | solution.py:345
  1709.8 60.9 %copy-start.95 = (bf16[512,768]{1,0:T(8,128)(2,1)S(1)}, bf16[512,768]{1,0:T(8,128)(2,1)}, u32[]{:S(2)}) copy-start(bf16[512,768]{1,0:T(8,128)(2,1)} %get-tuple-element.210) | copy-start | bytes 2359300
  (161 other events, 1088.2 us)
Sparse Core Ops, SparseCore 0:
  9.6 264.2 all-gather.15
  276.4 158.8 all-gather.17
  436.8 152.0 all-gather.9
  686.0 84.9 all-gather.11
  1273.4 47.6 reduce-scatter.1
  1368.3 121.7 all-gather.13
  1655.4 140.8 all-gather.19

commit v8 on v7

--- a/solution.py
+++ b/solution.py
@@ -795,8 +795,9 @@
     def work(d, got):
         return expert_block(got, hidden_grads[d], mask, inner_up, inner_down, inner_parts, spot)
 
-    def rows_home(d, row_grad):
+    def rows_home(d, row_grad, *earlier):
         home = home_add(row_grad.reshape(holders, capacity, -1), experts, copies)
+        home = after(home, *earlier)
         row_sum = nn(combines[d], home[:, :width])
         gate_sum = nn(places[d], home[:, width:])
         lanes = gate_sum[:rows] + jnp.roll(gate_sum[rows:], 2, axis=1)
@@ -807,16 +808,17 @@
     for d in order[1:]:
         earlier = [inner_parts[distances[min(d - 1, size - 2)]]]
         got_rows.append(send_rows(d, got_rows[-1], *earlier))
-    kept = [work(0, after(got_rows[0], got_rows[-2]) if size > 1 else got_rows[0])]
-    row_home, row_total = rows_home(0, kept[0][0])
-    row_backs, row_homes = [row_total], [row_home]
-    for d in order[1:]:
-        kept.append(work(d, after(got_rows[d], kept[-1][0])))
-        row_grad = kept[d][0]
-        row_home, row_back = rows_home(d, row_grad)
+    turns = order[1:] + [0]
+    kept, row_homes, row_backs, row_total = {}, [], [], None
+    ready = got_rows[1:-1] + hidden_grads
+    for d in turns:
+        kept[d] = work(d, after(got_rows[d], *ready))
+        ready = [kept[d][0]]
+        row_home, row_back = rows_home(d, kept[d][0], *(row_backs if d == 0 else []))
+        row_homes.append(row_home)
         row_backs.append(row_back)
-        row_homes.append(row_home)
-        row_total = row_total + row_back.astype(f32)
+        row_back = row_back.astype(f32)
+        row_total = row_back if row_total is None else row_total + row_back
     gate_sum = row_total[:, width : width + 4]
     row_total = row_total[:, :width]
     mlp_gate_grad = gate_sum.reshape(rows, 2, 2).sum(2)

time: 1840 us -> 1840 us (level)
  starting transfers between devices: 227 us -> 205 us
    all_to_all x26, waiting for transfers between devices: 189 us -> 262 us  [exchange(): return lax.all_to_all(buffer, 'dp', split_axis=0, concat_axis=0, tiled=True)]
    ppermute x18, waiting for transfers between devices: 520 us -> 488 us  [shifted(): lax.ppermute(array, 'seq', [(k, (k - shift) % size) for k in range(size)])]
    all_gather x1, waiting for transfers between devices: 76.6 us -> 54 us  [body(): packet_all = lax.all_gather(packet, 'seq', axis=0, tiled=True)]
    ppermute x18, starting transfers between devices: 107 us -> 85.9 us  [shifted(): lax.ppermute(array, 'seq', [(k, (k - shift) % size) for k in range(size)])]
    unnamed x373 -> x347, local copies, waits for them, and re-layouts: 48.7 us -> 53.9 us
  transfers between devices with their start and end apart: 51 -> 51, of which waited for: 30 -> 29; matrix products, arithmetic and copies ran while one was open for 22% -> 22% of each run, Pallas kernels for 16% -> 16%
where the time goes in v8:
time: 1840 us; the launch traced here: 1810 us
  waiting for transfers between devices  833 us (45%)
  matrix products  293 us (16%)
  Pallas kernels  293 us (16%)
  starting transfers between devices  205 us (11%)
  local copies, waits for them, and re-layouts  125 us (7%)
  other arithmetic  40.7 us (2%)
    ppermute x18, waiting for transfers between devices, shifted(): lax.ppermute(array, 'seq', [(k, (k - shift) % size) for k in range(size)])  488 us
    dot_general x95, matrix products, product(): lax.dot_general(left, right, (((left_dim,), (right_dim,)), ((), ())), pre...  293 us
    all_to_all x26, waiting for transfers between devices, exchange(): return lax.all_to_all(buffer, 'dp', split_axis=0, concat_axis=0, tiled=True)  262 us
    pallas_call x4, Pallas kernels, expert_block(): pl.pallas_call(functools.partial(expert_kernel, size, share), grid_spec=p...  125 us
    all_to_all x26, starting transfers between devices, exchange(): return lax.all_to_all(buffer, 'dp', split_axis=0, concat_axis=0, tiled=True)  119 us
    ppermute x18, starting transfers between devices, shifted(): lax.ppermute(array, 'seq', [(k, (k - shift) % size) for k in range(size)])  85.9 us
    all_gather x1, waiting for transfers between devices, body(): packet_all = lax.all_gather(packet, 'seq', axis=0, tiled=True)  54 us
    unnamed x347, local copies, waits for them, and re-layouts  53.9 us
  transfers between devices with their start and end apart: 51, of which 29 were waited for; matrix products, arithmetic and copies ran while one was open for 22% of the time, Pallas kernels for 16%

profile of v8, /device:TPU:0, one launch (start us, length us, event | category | flops | bytes accessed | tf_op | source)
XLA Modules:
  0.0 1807.9 jit_solution(10141702326550736898)
XLA Ops:
  9.2 5.2 all-to-all-start.3
  20.2 4.6 all-to-all-start
  36.0 26.7 %all-to-all-done = bf16[8,96,2048]{2,1,0:T(8,128)(2,1)} async-done(((bf16[8,96,2048]{2,1,0:T(8,128)(2,1)}), bf16[8,96,2048]{2,1,0:T(8,128)(2,1)}, u32[]{:S(2)}, u32[]{:S(2)}) %all-to-all-start) | async-done | bytes 3145760 | tf_op jit(solution)/shard_map/all_to_all | solution.py:332
  74.2 67.4 %collective-permute-done.2 = bf16[384,2048]{1,0:T(8,128)(2,1)} collective-permute-done((bf16[384,2048]{1,0:T(8,128)(2,1)}, bf16[384,2048]{1,0:T(8,128)(2,1)}, u32[]{:S(2)}, u32[]{:S(2)}) %collective-permute-start.2) | collective-permute-done | bytes 1572896 | tf_op jit(solution)/shard_map/ppermute | solution.py:345
  145.7 105.7 %collective-permute-done.1 = bf16[384,2048]{1,0:T(8,128)(2,1)} collective-permute-done((bf16[384,2048]{1,0:T(8,128)(2,1)}, bf16[384,2048]{1,0:T(8,128)(2,1)}, u32[]{:S(2)}, u32[]{:S(2)}) %collective-permute-start.1) | collective-permute-done | bytes 1572896 | tf_op jit(solution)/shard_map/ppermute | solution.py:345
  282.7 11.8 convolution_convert_fusion.3
  300.4 40.3 %collective-permute-start.5 = (bf16[256,2176]{1,0:T(8,128)(2,1)S(1)}, bf16[256,2176]{1,0:T(8,128)(2,1)}, u32[]{:S(2)}, u32[]{:S(2)}) collective-permute-start(bf16[256,2176]{1,0:T(8,128)(2,1)S(1)} %fusion.91), channel_id=1, source_target_pairs={{0,8},{8,16},{16,24},{24,0},{1,9},{9,17},{17,25},{25,1},{2,10},{10... | collective-permute-start | bytes 3342344 | tf_op jit(solution)/shard_map/ppermute | solution.py:345
  344.5 25.0 %collective-permute-done.5 = bf16[256,2176]{1,0:T(8,128)(2,1)} collective-permute-done((bf16[256,2176]{1,0:T(8,128)(2,1)S(1)}, bf16[256,2176]{1,0:T(8,128)(2,1)}, u32[]{:S(2)}, u32[]{:S(2)}) %collective-permute-start.5) | collective-permute-done | bytes 1114144 | tf_op jit(solution)/shard_map/ppermute | solution.py:345
  369.5 47.4 %collective-permute-done.4 = bf16[256,2176]{1,0:T(8,128)(2,1)} collective-permute-done((bf16[256,2176]{1,0:T(8,128)(2,1)S(1)}, bf16[256,2176]{1,0:T(8,128)(2,1)}, u32[]{:S(2)}, u32[]{:S(2)}) %collective-permute-start.4) | collective-permute-done | bytes 1114144 | tf_op jit(solution)/shard_map/ppermute | solution.py:345
  416.9 18.4 %all-gather.18.cloned.1.call-done = bf16[16384,512]{1,0:T(8,128)(2,1)} async-done(((bf16[2048,512]{1,0:T(8,128)(2,1)}), bf16[16384,512]{1,0:T(8,128)(2,1)}) %all-gather.18.cloned.1.call-update) | async-done | bytes 16777232 | tf_op jit(solution)/shard_map/all_gather | solution.py:696
  444.2 5.0 all-to-all-start.5
  457.0 31.6 %pairs.1 = (bf16[1024,4096]{1,0:T(8,128)(2,1)}, bf16[1024,16]{1,0:T(8,128)(2,1)S(1)}) custom-call(bf16[256,2048]{1,0:T(8,128)(2,1)S(1)} %fusion.52.refs_0_, bf16[256,2048]{1,0:T(8,128)(2,1)S(1)} %copy-done.27, bf16[256,2048]{1,0:T(8,128)(2,1)S(1)} %copy-done.26, bf16[256,2048]{1,0:T(8,128)(2,1)S(1)} %copy-done.25, bf16[8,2048,512]{2,1,0:T(8,128)(2,1)} %bitcast.498, ...), custom_call_target="tpu_custom_call" | custom-call | flops 17179869184 | bytes 16777216 | tf_op jit(solution)/shard_map/pairs/pallas_call | solution.py:75
  500.8 33.7 %attend.1 = (bf16[512,2048]{1,0:T(8,128)(2,1)S(1)}, bf16[768,2048]{1,0:T(8,128)(2,1)}, bf16[512,2048]{1,0:T(8,128)(2,1)}, f32[16,512,1]{2,1,0:T(8,128)}) custom-call(bf16[768,2048]{1,0:T(8,128)(2,1)} %bitcast.8.home_ref, bf16[512,768]{1,0:T(8,128)(2,1)S(1)} %fusion.78.place_ref, bf16[256,16]{1,0:T(8,128)(2,1)S(1)} %convolution_convert_fusion.25.low_ref, ...), custom_call_target="tpu_custom_call" | custom-call | flops 4294967296 | bytes 8388608 | tf_op jit(solution)/shard_map/attend/pallas_call | solution.py:194
  554.6 24.3 %all-to-all-done.4 = bf16[8,96,2048]{2,1,0:T(8,128)(2,1)} async-done(((bf16[8,96,2048]{2,1,0:T(8,128)(2,1)}), bf16[8,96,2048]{2,1,0:T(8,128)(2,1)}, u32[]{:S(2)}, u32[]{:S(2)}) %all-to-all-start.4) | async-done | bytes 3145760 | tf_op jit(solution)/shard_map/all_to_all | solution.py:332
  578.9 10.1 all-gather.10.cloned.1.call-done
  588.9 11.8 convolution_convert_fusion.2
  610.2 33.0 %all-to-all-done.7 = bf16[8,96,2048]{2,1,0:T(8,128)(2,1)} async-done(((bf16[8,96,2048]{2,1,0:T(8,128)(2,1)}), bf16[8,96,2048]{2,1,0:T(8,128)(2,1)}, u32[]{:S(2)}, u32[]{:S(2)}) %all-to-all-start.7) | async-done | bytes 3145760 | tf_op jit(solution)/shard_map/all_to_all | solution.py:332
  654.6 20.4 %collective-permute-done.6.refs_1_ = bf16[512,2816]{1,0:T(8,128)(2,1)} collective-permute-done((bf16[512,2816]{1,0:T(8,128)(2,1)}, bf16[512,2816]{1,0:T(8,128)(2,1)}, u32[]{:S(2)}, u32[]{:S(2)}) %collective-permute-start.6) | collective-permute-done | bytes 2883616 | tf_op jit(solution)/shard_map/ppermute | solution.py:345
  689.7 6.5 squeeze.95
  696.1 6.8 dynamic-slice_reduce_fusion
  706.2 54.0 %all-gather.12.cloned.1.call-done = bf16[1024,2176]{1,0:T(8,128)(2,1)} async-done(((bf16[256,2176]{1,0:T(8,128)(2,1)}), bf16[1024,2176]{1,0:T(8,128)(2,1)}) %all-gather.12.cloned.1.call-update) | async-done | bytes 4456464 | tf_op jit(solution)/shard_map/all_gather | solution.py:766
  767.9 4.8 all-to-all-start.9
  772.8 8.5 fusion.14
  792.2 18.5 %all-to-all-done.9 = bf16[8,96,2048]{2,1,0:T(8,128)(2,1)} async-done(((bf16[8,96,2048]{2,1,0:T(8,128)(2,1)}), bf16[8,96,2048]{2,1,0:T(8,128)(2,1)}, u32[]{:S(2)}, u32[]{:S(2)}) %all-to-all-start.9) | async-done | bytes 3145760 | tf_op jit(solution)/shard_map/all_to_all | solution.py:332
  815.1 8.5 fusion.12
  825.7 9.9 fusion.10
  835.6 20.8 %collective-permute-done.7.refs_3_ = bf16[512,2816]{1,0:T(8,128)(2,1)} collective-permute-done((bf16[512,2816]{1,0:T(8,128)(2,1)}, bf16[512,2816]{1,0:T(8,128)(2,1)}, u32[]{:S(2)}, u32[]{:S(2)}) %collective-permute-start.7) | collective-permute-done | bytes 2883616 | tf_op jit(solution)/shard_map/ppermute | solution.py:345
  866.7 9.8 fusion.8
  884.6 16.9 all-to-all-done.10
  905.1 76.5 %collective-permute-done.8.refs_2_ = bf16[512,2816]{1,0:T(8,128)(2,1)} collective-permute-done((bf16[512,2816]{1,0:T(8,128)(2,1)}, bf16[512,2816]{1,0:T(8,128)(2,1)}, u32[]{:S(2)}, u32[]{:S(2)}) %collective-permute-start.8) | collective-permute-done | bytes 2883616 | tf_op jit(solution)/shard_map/ppermute | solution.py:345
  1004.9 31.0 %experts.4 = (bf16[768,2176]{1,0:T(8,128)(2,1)}, bf16[768,1408]{1,0:T(8,128)(2,1)S(1)}, bf16[768,2816]{1,0:T(8,128)(2,1)}, bf16[768,128]{1,0:T(8,128)(2,1)S(1)}, bf16[768,128]{1,0:T(8,128)(2,1)S(1)}) custom-call(s32[1]{0:T(128)} %bitcast.46.spot_ref, bf16[768,2048]{1,0:T(8,128)(2,1)} %bitcast.50.x_ref, bf16[768,1408]{1,0:T(8,128)(2,1)S(1)} %copy-done.22, ...), custom_call_target="tpu_custom_call" | custom-call | flops 17716740096 | bytes 27262976 | tf_op jit(solution)/shard_map/experts/pallas_call | solution.py:607
  1037.9 4.7 all-to-all-start.16
  1045.2 31.2 %experts.5 = (bf16[768,2176]{1,0:T(8,128)(2,1)}, bf16[768,1408]{1,0:T(8,128)(2,1)S(1)}, bf16[768,2816]{1,0:T(8,128)(2,1)}, bf16[768,128]{1,0:T(8,128)(2,1)S(1)}, bf16[768,128]{1,0:T(8,128)(2,1)S(1)}) custom-call(s32[1]{0:T(128)} %bitcast.46.spot_ref, bf16[768,2048]{1,0:T(8,128)(2,1)} %bitcast.52.x_ref, bf16[768,1408]{1,0:T(8,128)(2,1)S(1)} %copy-done.24, ...), custom_call_target="tpu_custom_call" | custom-call | flops 17716740096 | bytes 27262976 | tf_op jit(solution)/shard_map/experts/pallas_call | solution.py:607
  1077.8 31.4 %experts.6 = (bf16[768,2176]{1,0:T(8,128)(2,1)}, bf16[768,1408]{1,0:T(8,128)(2,1)S(1)}, bf16[768,2816]{1,0:T(8,128)(2,1)}, bf16[768,128]{1,0:T(8,128)(2,1)S(1)}, bf16[768,128]{1,0:T(8,128)(2,1)S(1)}) custom-call(s32[1]{0:T(128)} %bitcast.46.spot_ref, bf16[768,2048]{1,0:T(8,128)(2,1)} %bitcast.63.x_ref, bf16[768,1408]{1,0:T(8,128)(2,1)S(1)} %copy-done.23, ...), custom_call_target="tpu_custom_call" | custom-call | flops 17716740096 | bytes 27262976 | tf_op jit(solution)/shard_map/experts/pallas_call | solution.py:607
  1110.5 4.6 all-to-all-start.14
  1117.8 31.0 %experts.7 = (bf16[768,2176]{1,0:T(8,128)(2,1)}, bf16[768,1408]{1,0:T(8,128)(2,1)S(1)}, bf16[768,2816]{1,0:T(8,128)(2,1)}, bf16[768,128]{1,0:T(8,128)(2,1)S(1)}, bf16[768,128]{1,0:T(8,128)(2,1)S(1)}) custom-call(s32[1]{0:T(128)} %bitcast.46.spot_ref, bf16[768,2048]{1,0:T(8,128)(2,1)} %bitcast.48.x_ref, bf16[768,1408]{1,0:T(8,128)(2,1)S(1)} %copy-done.21, ...), custom_call_target="tpu_custom_call" | custom-call | flops 17716740096 | bytes 27262976 | tf_op jit(solution)/shard_map/experts/pallas_call | solution.py:607
  1162.2 4.7 all-to-all-start.13
  1191.1 15.8 all-to-all-done.13
  1231.0 7.1 fusion.6
  1243.3 6.3 collective-permute-done.10
  1251.4 21.1 %collective-permute-done.11 = bf16[256,2176]{1,0:T(8,128)(2,1)} collective-permute-done((bf16[256,2176]{1,0:T(8,128)(2,1)}, bf16[256,2176]{1,0:T(8,128)(2,1)}, u32[]{:S(2)}, u32[]{:S(2)}) %collective-permute-start.11) | collective-permute-done | bytes 1114144 | tf_op jit(solution)/shard_map/ppermute | solution.py:345
  1293.6 32.8 %all-to-all-done.17 = bf16[8,96,2048]{2,1,0:T(8,128)(2,1)} async-done(((bf16[8,96,2048]{2,1,0:T(8,128)(2,1)}), bf16[8,96,2048]{2,1,0:T(8,128)(2,1)}, u32[]{:S(2)}, u32[]{:S(2)}) %all-to-all-start.17) | async-done | bytes 3145760 | tf_op jit(solution)/shard_map/all_to_all | solution.py:332
  1333.8 37.6 %all-to-all-done.18 = bf16[8,96,2048]{2,1,0:T(8,128)(2,1)} async-done(((bf16[8,96,2048]{2,1,0:T(8,128)(2,1)}), bf16[8,96,2048]{2,1,0:T(8,128)(2,1)}, u32[]{:S(2)}, u32[]{:S(2)}) %all-to-all-start.18) | async-done | bytes 3145760 | tf_op jit(solution)/shard_map/all_to_all | solution.py:332
  1371.5 11.9 convolution_convert_fusion.1
  1383.4 4.6 all-to-all-start.19
  1399.4 7.8 fusion.4
  1409.9 29.1 %all-to-all-done.19 = bf16[8,96,2048]{2,1,0:T(8,128)(2,1)} async-done(((bf16[8,96,2048]{2,1,0:T(8,128)(2,1)}), bf16[8,96,2048]{2,1,0:T(8,128)(2,1)}, u32[]{:S(2)}, u32[]{:S(2)}) %all-to-all-start.19) | async-done | bytes 3145760 | tf_op jit(solution)/shard_map/all_to_all | solution.py:332
  1439.0 4.8 all-to-all-start.20
  1446.9 44.1 %attend_back.1 = (bf16[1024,2048]{1,0:T(8,128)(2,1)}, bf16[1024,2048]{1,0:T(8,128)(2,1)}, bf16[768,2048]{1,0:T(8,128)(2,1)}, bf16[256,2048]{1,0:T(8,128)(2,1)S(1)}) custom-call(bf16[512,2048]{1,0:T(8,128)(2,1)} %get-tuple-element.133.query_ref, bf16[1024,4096]{1,0:T(8,128)(2,1)} %get-tuple-element.99.key_ref.value_ref, ...), custom_call_target="tpu_custom_call" | custom-call | flops 10737418240 | bytes 16777216 | tf_op jit(solution)/shard_map/attend_back/pallas_call | solution.py:289
  1504.3 4.9 all-to-all-start.22
  1515.1 23.2 %pair_back.1 = bf16[1024,2048]{1,0:T(8,128)(2,1)S(1)} custom-call(bf16[1024,2048]{1,0:T(8,128)(2,1)} %get-tuple-element.162.key_ref, bf16[1024,2048]{1,0:T(8,128)(2,1)} %get-tuple-element.163.value_ref, bf16[8,2048,512]{2,1,0:T(8,128)(2,1)} %bitcast.499, bf16[1024,16]{1,0:T(8,128)(2,1)S(1)} %fusion.79.low_ref, bf16[16,2048]{1,0:T(8,128)(2,1)S(1)} %copy-done.48), custom_call_target="tpu_custom_call" | custom-call | flops 17179869184 | bytes 16777216 | tf_op jit(solution)/shard_map/pair_back/pallas_call | solution.py:129
  1540.4 6.7 all-to-all-done.22
  1547.1 11.9 convolution_convert_fusion
  1572.6 7.1 fusion.2
  1582.3 19.1 %all-to-all-done.23 = bf16[8,96,2048]{2,1,0:T(8,128)(2,1)} async-done(((bf16[8,96,2048]{2,1,0:T(8,128)(2,1)}), bf16[8,96,2048]{2,1,0:T(8,128)(2,1)}, u32[]{:S(2)}, u32[]{:S(2)}) %all-to-all-start.23) | async-done | bytes 3145760 | tf_op jit(solution)/shard_map/all_to_all | solution.py:332
  1605.9 19.3 %unpack.1 = (f32[8,16,11264]{2,1,0:T(8,128)}, f32[8,16,5632]{2,1,0:T(8,128)}, f32[8,16,2048]{2,1,0:T(8,128)}, f32[8,16,2048]{2,1,0:T(8,128)}) custom-call(bf16[4,8,16,8320]{3,2,1,0:T(8,128)(2,1)} %bitcast.430), custom_call_target="tpu_custom_call" | custom-call | bytes 32243712 | tf_op jit(solution)/shard_map/unpack/pallas_call | solution.py:485
  1625.2 21.6 %collective-permute-done.15 = bf16[288,2048]{1,0:T(8,128)(2,1)} collective-permute-done((bf16[288,2048]{1,0:T(8,128)(2,1)}, bf16[288,2048]{1,0:T(8,128)(2,1)}, u32[]{:S(2)}, u32[]{:S(2)}) %collective-permute-start.15) | collective-permute-done | bytes 1179680 | tf_op jit(solution)/shard_map/ppermute | solution.py:345
  1651.5 7.8 fusion
  1670.4 24.8 %collective-permute-start.12 = (bf16[256,2048]{1,0:T(8,128)(2,1)}, bf16[256,2048]{1,0:T(8,128)(2,1)S(1)}, u32[]{:S(2)}, u32[]{:S(2)}) collective-permute-start(bf16[256,2048]{1,0:T(8,128)(2,1)} %convolution_convert_fusion.16), channel_id=1, source_target_pairs={{0,8},{8,16},{16,24},{24,0},{1,9},{9,17},{17,25},{25,1},{2,10},{10... | collective-permute-start | bytes 3145736 | tf_op jit(solution)/shard_map/ppermute | solution.py:345
  1706.6 16.6 collective-permute-done.12
  1723.2 36.6 %collective-permute-done.13 = bf16[256,2048]{1,0:T(8,128)(2,1)} collective-permute-done((bf16[256,2048]{1,0:T(8,128)(2,1)}, bf16[256,2048]{1,0:T(8,128)(2,1)}, u32[]{:S(2)}, u32[]{:S(2)}) %collective-permute-start.13) | collective-permute-done | bytes 1048608 | tf_op jit(solution)/shard_map/ppermute | solution.py:345
  1759.9 18.9 %collective-permute-done.14 = bf16[256,2048]{1,0:T(8,128)(2,1)} collective-permute-done((bf16[256,2048]{1,0:T(8,128)(2,1)}, bf16[256,2048]{1,0:T(8,128)(2,1)}, u32[]{:S(2)}, u32[]{:S(2)}) %collective-permute-start.14) | collective-permute-done | bytes 1048608 | tf_op jit(solution)/shard_map/ppermute | solution.py:345
  1778.8 5.1 fusion.98
  1794.9 6.0 gather_adapters.1
  (660 shorter events, 434.4 us)
Async XLA Ops:
  7.2 431.2 %copy-start = (bf16[8,16,4096]{2,1,0:T(8,128)(2,1)S(1)}, bf16[8,16,4096]{2,1,0:T(8,128)(2,1)}, u32[]{:S(2)}) copy-start(bf16[8,16,4096]{2,1,0:T(8,128)(2,1)} %param.37) | copy-start | bytes 3145732
  7.2 268.6 %all-gather.16.cloned.1.call-start = ((), (), s32[]{:S(2)}) async-start(), calls=%async_computation.31 | async-start | bytes 10485760 | tf_op jit(solution)/shard_map/all_gather | solution.py:685
  9.2 11.0 all-to-all-start.3
  15.6 483.0 %copy-start.141 = (f32[256]{0:T(256)}, f32[256]{0:T(256)S(1)}, u32[]{:S(2)}) copy-start(f32[256]{0:T(256)S(1)} %add_rsqrt_fusion.1) | copy-start | bytes 3076
  17.4 588.1 %copy-start.2 = (bf16[256,2048]{1,0:T(8,128)(2,1)}, bf16[256,2048]{1,0:T(8,128)(2,1)S(1)}, u32[]{:S(2)}) copy-start(bf16[256,2048]{1,0:T(8,128)(2,1)S(1)} %fusion.52.refs_0_) | copy-start | bytes 3145732
  20.2 42.5 %all-to-all-start = ((bf16[8,96,2048]{2,1,0:T(8,128)(2,1)}), bf16[8,96,2048]{2,1,0:T(8,128)(2,1)}, u32[]{:S(2)}, u32[]{:S(2)}) async-start(bf16[8,96,2048]{2,1,0:T(8,128)(2,1)} %bitcast.419), calls=%async_computation | async-start | bytes 6291456 | tf_op jit(solution)/shard_map/all_to_all | solution.py:332
  62.7 213.1 %all-to-all-start.2 = ((bf16[8,96,2048]{2,1,0:T(8,128)(2,1)}), bf16[8,96,2048]{2,1,0:T(8,128)(2,1)}, u32[]{:S(2)}, u32[]{:S(2)}) async-start(bf16[8,96,2048]{2,1,0:T(8,128)(2,1)} %bitcast.416), calls=%async_computation.2 | async-start | bytes 6291456 | tf_op jit(solution)/shard_map/all_to_all | solution.py:332
  67.3 368.0 %all-gather.18.cloned.1.call-start = ((), (), s32[]{:S(2)}) async-start(), calls=%async_computation.32 | async-start | bytes 18874368 | tf_op jit(solution)/shard_map/all_gather | solution.py:696
  68.6 73.0 %collective-permute-start.2 = (bf16[384,2048]{1,0:T(8,128)(2,1)}, bf16[384,2048]{1,0:T(8,128)(2,1)}, u32[]{:S(2)}, u32[]{:S(2)}) collective-permute-start(bf16[384,2048]{1,0:T(8,128)(2,1)} %pad_maximum_fusion.1), channel_id=1, source_target_pairs={{0,8},{8,16},{16,24},{24,0},{1,9},{9,17},{17,25},{25,1},{2,10},{10... | collective-permute-start | bytes 4718600 | tf_op jit(solution)/shard_map/ppermute | solution.py:345
  70.2 181.2 %collective-permute-start.1 = (bf16[384,2048]{1,0:T(8,128)(2,1)}, bf16[384,2048]{1,0:T(8,128)(2,1)}, u32[]{:S(2)}, u32[]{:S(2)}) collective-permute-start(bf16[384,2048]{1,0:T(8,128)(2,1)} %pad_maximum_fusion.1), channel_id=1, source_target_pairs={{0,16},{8,24},{16,0},{24,8},{1,17},{9,25},{17,1},{25,9},{2,18},{10... | collective-permute-start | bytes 4718600 | tf_op jit(solution)/shard_map/ppermute | solution.py:345
  72.8 185.8 %collective-permute-start = (bf16[384,2048]{1,0:T(8,128)(2,1)}, bf16[384,2048]{1,0:T(8,128)(2,1)}, u32[]{:S(2)}, u32[]{:S(2)}) collective-permute-start(bf16[384,2048]{1,0:T(8,128)(2,1)} %pad_maximum_fusion.1), channel_id=1, source_target_pairs={{0,24},{8,0},{16,8},{24,16},{1,25},{9,1},{17,9},{25,17},{2,26},{10... | collective-permute-start | bytes 4718600 | tf_op jit(solution)/shard_map/ppermute | solution.py:345
  74.2 628.8 %copy-start.49 = (s32[8]{0:T(128)}, s32[8]{0:T(128)S(1)}, u32[]{:S(2)}) copy-start(s32[8]{0:T(128)S(1)} %slice_reduce_fusion.4.ids_ref) | copy-start | bytes 100
  294.6 122.3 %all-to-all-start.1 = ((bf16[8,96,2048]{2,1,0:T(8,128)(2,1)}), bf16[8,96,2048]{2,1,0:T(8,128)(2,1)}, u32[]{:S(2)}, u32[]{:S(2)}) async-start(bf16[8,96,2048]{2,1,0:T(8,128)(2,1)} %bitcast.457), calls=%async_computation.1 | async-start | bytes 6291456 | tf_op jit(solution)/shard_map/all_to_all | solution.py:332
  299.0 289.9 %all-gather.10.cloned.1.call-start = ((), (), s32[]{:S(2)}) async-start(), calls=%async_computation.27 | async-start | bytes 10485760 | tf_op jit(solution)/shard_map/all_gather | solution.py:735
  300.4 69.1 %collective-permute-start.5 = (bf16[256,2176]{1,0:T(8,128)(2,1)S(1)}, bf16[256,2176]{1,0:T(8,128)(2,1)}, u32[]{:S(2)}, u32[]{:S(2)}) collective-permute-start(bf16[256,2176]{1,0:T(8,128)(2,1)S(1)} %fusion.91), channel_id=1, source_target_pairs={{0,8},{8,16},{16,24},{24,0},{1,9},{9,17},{17,25},{25,1},{2,10},{10... | collective-permute-start | bytes 3342344 | tf_op jit(solution)/shard_map/ppermute | solution.py:345
  340.7 76.2 %collective-permute-start.4 = (bf16[256,2176]{1,0:T(8,128)(2,1)S(1)}, bf16[256,2176]{1,0:T(8,128)(2,1)}, u32[]{:S(2)}, u32[]{:S(2)}) collective-permute-start(bf16[256,2176]{1,0:T(8,128)(2,1)S(1)} %fusion.91), channel_id=1, source_target_pairs={{0,16},{8,24},{16,0},{24,8},{1,17},{9,25},{17,1},{25,9},{2,18},{10... | collective-permute-start | bytes 3342344 | tf_op jit(solution)/shard_map/ppermute | solution.py:345
  344.5 72.4 %collective-permute-start.3 = (bf16[256,2176]{1,0:T(8,128)(2,1)S(1)}, bf16[256,2176]{1,0:T(8,128)(2,1)}, u32[]{:S(2)}, u32[]{:S(2)}) collective-permute-start(bf16[256,2176]{1,0:T(8,128)(2,1)S(1)} %fusion.91), channel_id=1, source_target_pairs={{0,24},{8,0},{16,8},{24,16},{1,25},{9,1},{17,9},{25,17},{2,26},{10... | collective-permute-start | bytes 3342344 | tf_op jit(solution)/shard_map/ppermute | solution.py:345
  444.2 47.2 %all-to-all-start.5 = ((bf16[8,96,2048]{2,1,0:T(8,128)(2,1)}), bf16[8,96,2048]{2,1,0:T(8,128)(2,1)}, u32[]{:S(2)}, u32[]{:S(2)}) async-start(bf16[8,96,2048]{2,1,0:T(8,128)(2,1)} %bitcast.422), calls=%async_computation.5 | async-start | bytes 6291456 | tf_op jit(solution)/shard_map/all_to_all | solution.py:332
  451.9 428.3 %copy-start.134 = (s32[512]{0:T(512)}, s32[512]{0:T(512)S(1)}, u32[]{:S(2)}) copy-start(s32[512]{0:T(512)S(1)} %convert_add_fusion.2) | copy-start | bytes 6148
  491.3 45.2 %all-to-all-start.6 = ((bf16[8,96,2048]{2,1,0:T(8,128)(2,1)}), bf16[8,96,2048]{2,1,0:T(8,128)(2,1)}, u32[]{:S(2)}, u32[]{:S(2)}) async-start(bf16[8,96,2048]{2,1,0:T(8,128)(2,1)} %bitcast.420), calls=%async_computation.6 | async-start | bytes 6291456 | tf_op jit(solution)/shard_map/all_to_all | solution.py:332
  536.5 42.3 %all-to-all-start.4 = ((bf16[8,96,2048]{2,1,0:T(8,128)(2,1)}), bf16[8,96,2048]{2,1,0:T(8,128)(2,1)}, u32[]{:S(2)}, u32[]{:S(2)}) async-start(bf16[8,96,2048]{2,1,0:T(8,128)(2,1)} %bitcast.453), calls=%async_computation.4 | async-start | bytes 6291456 | tf_op jit(solution)/shard_map/all_to_all | solution.py:332
  600.8 42.5 %all-to-all-start.7 = ((bf16[8,96,2048]{2,1,0:T(8,128)(2,1)}), bf16[8,96,2048]{2,1,0:T(8,128)(2,1)}, u32[]{:S(2)}, u32[]{:S(2)}) async-start(bf16[8,96,2048]{2,1,0:T(8,128)(2,1)} %bitcast.458), calls=%async_computation.7 | async-start | bytes 6291456 | tf_op jit(solution)/shard_map/all_to_all | solution.py:332
  605.4 154.8 %all-gather.12.cloned.1.call-start = ((), (), s32[]{:S(2)}) async-start(), calls=%async_computation.28 | async-start | bytes 5570560 | tf_op jit(solution)/shard_map/all_gather | solution.py:766
  605.5 47.1 %copy-start.136 = (s32[256,2]{0,1:T(2,128)}, s32[256,2]{0,1:T(2,128)S(1)}, u32[]{:S(2)}) copy-start(s32[256,2]{0,1:T(2,128)S(1)} %copy.263) | copy-start | bytes 6148
  605.9 41.1 %copy-start.115 = (f32[256,2]{0,1:T(2,128)}, f32[256,2]{0,1:T(2,128)S(1)}, u32[]{:S(2)}) copy-start(f32[256,2]{0,1:T(2,128)S(1)} %select_reduce_fusion.3) | copy-start | bytes 6148
  606.9 40.1 %copy-start.40 = (bf16[16,2048]{1,0:T(8,128)(2,1)}, bf16[16,2048]{1,0:T(8,128)(2,1)S(1)}, u32[]{:S(2)}) copy-start(bf16[16,2048]{1,0:T(8,128)(2,1)S(1)} %dynamic-slice_bitcast_fusion.1.down_ref) | copy-start | bytes 196612
  609.8 65.2 %collective-permute-start.6 = (bf16[512,2816]{1,0:T(8,128)(2,1)}, bf16[512,2816]{1,0:T(8,128)(2,1)}, u32[]{:S(2)}, u32[]{:S(2)}) collective-permute-start(bf16[512,2816]{1,0:T(8,128)(2,1)} %copy-done.19), channel_id=1, source_target_pairs={{0,24},{8,0},{16,8},{24,16},{1,25},{9,1},{17,9},{25,17},{2,26},{10... | collective-permute-start | bytes 8650760 | tf_op jit(solution)/shard_map/ppermute | solution.py:345
  679.0 84.7 %all-to-all-start.8 = ((bf16[8,96,2048]{2,1,0:T(8,128)(2,1)}), bf16[8,96,2048]{2,1,0:T(8,128)(2,1)}, u32[]{:S(2)}, u32[]{:S(2)}) async-start(bf16[8,96,2048]{2,1,0:T(8,128)(2,1)} %bitcast.415), calls=%async_computation.8 | async-start | bytes 6291456 | tf_op jit(solution)/shard_map/all_to_all | solution.py:332
  689.6 308.0 %copy-start.62 = (bf16[128,1,1408]{2,0,1:T(8,128)(2,1)}, bf16[128,1,1408]{2,0,1:T(8,128)(2,1)S(1)}, u32[]{:S(2)}) copy-start(bf16[128,1,1408]{2,0,1:T(8,128)(2,1)S(1)} %copy.303) | copy-start | bytes 1081348
  706.1 75.2 %copy-start.104 = (bf16[768,128]{1,0:T(8,128)(2,1)}, bf16[768,128]{1,0:T(8,128)(2,1)S(1)}, u32[]{:S(2)}) copy-start(bf16[768,128]{1,0:T(8,128)(2,1)S(1)} %fusion.83) | copy-start | bytes 589828
  767.9 42.8 %all-to-all-start.9 = ((bf16[8,96,2048]{2,1,0:T(8,128)(2,1)}), bf16[8,96,2048]{2,1,0:T(8,128)(2,1)}, u32[]{:S(2)}, u32[]{:S(2)}) async-start(bf16[8,96,2048]{2,1,0:T(8,128)(2,1)} %bitcast.421), calls=%async_computation.9 | async-start | bytes 6291456 | tf_op jit(solution)/shard_map/all_to_all | solution.py:332
  789.4 67.0 %collective-permute-start.7 = (bf16[512,2816]{1,0:T(8,128)(2,1)}, bf16[512,2816]{1,0:T(8,128)(2,1)}, u32[]{:S(2)}, u32[]{:S(2)}) collective-permute-start(bf16[512,2816]{1,0:T(8,128)(2,1)} %cut.7), channel_id=1, source_target_pairs={{0,8},{8,16},{16,24},{24,0},{1,9},{9,17},{17,25},{25,1},{2,10},{10... | collective-permute-start | bytes 8650760 | tf_op jit(solution)/shard_map/ppermute | solution.py:345
  810.7 48.5 %all-to-all-start.11 = ((bf16[8,96,2048]{2,1,0:T(8,128)(2,1)}), bf16[8,96,2048]{2,1,0:T(8,128)(2,1)}, u32[]{:S(2)}, u32[]{:S(2)}) async-start(bf16[8,96,2048]{2,1,0:T(8,128)(2,1)} %bitcast.423), calls=%async_computation.11 | async-start | bytes 6291456 | tf_op jit(solution)/shard_map/all_to_all | solution.py:332
  856.4 125.2 %collective-permute-start.8 = (bf16[512,2816]{1,0:T(8,128)(2,1)}, bf16[512,2816]{1,0:T(8,128)(2,1)}, u32[]{:S(2)}, u32[]{:S(2)}) collective-permute-start(bf16[512,2816]{1,0:T(8,128)(2,1)} %cut.6), channel_id=1, source_target_pairs={{0,16},{8,24},{16,0},{24,8},{1,17},{9,25},{17,1},{25,9},{2,18},{10... | collective-permute-start | bytes 8650760 | tf_op jit(solution)/shard_map/ppermute | solution.py:345
  859.2 42.4 %all-to-all-start.10 = ((bf16[8,96,2048]{2,1,0:T(8,128)(2,1)}), bf16[8,96,2048]{2,1,0:T(8,128)(2,1)}, u32[]{:S(2)}, u32[]{:S(2)}) async-start(bf16[8,96,2048]{2,1,0:T(8,128)(2,1)} %bitcast.417), calls=%async_computation.10 | async-start | bytes 6291456 | tf_op jit(solution)/shard_map/all_to_all | solution.py:332
  866.6 131.0 %copy-start.102 = (bf16[768,128]{1,0:T(8,128)(2,1)}, bf16[768,128]{1,0:T(8,128)(2,1)S(1)}, u32[]{:S(2)}) copy-start(bf16[768,128]{1,0:T(8,128)(2,1)S(1)} %fusion.85) | copy-start | bytes 589828
  901.5 84.3 %all-to-all-start.21 = ((f32[8,4,96]{2,1,0:T(4,128)}), f32[8,4,96]{2,1,0:T(4,128)S(1)}, u32[]{:S(2)}, u32[]{:S(2)}) async-start(f32[8,4,96]{2,1,0:T(4,128)} %maximum_bitcast_fusion), calls=%async_computation.21 | async-start | bytes 32768 | tf_op jit(solution)/shard_map/all_to_all | solution.py:332
  985.8 51.4 %all-to-all-start.12 = ((bf16[8,96,2048]{2,1,0:T(8,128)(2,1)}), bf16[8,96,2048]{2,1,0:T(8,128)(2,1)}, u32[]{:S(2)}, u32[]{:S(2)}) async-start(bf16[8,96,2048]{2,1,0:T(8,128)(2,1)} %bitcast.418), calls=%async_computation.12 | async-start | bytes 6291456 | tf_op jit(solution)/shard_map/all_to_all | solution.py:332
  1037.9 72.6 %all-to-all-start.16 = ((bf16[8,96,2176]{2,1,0:T(8,128)(2,1)}), bf16[8,96,2176]{2,1,0:T(8,128)(2,1)}, u32[]{:S(2)}, u32[]{:S(2)}) async-start(bf16[8,96,2176]{2,1,0:T(8,128)(2,1)} %bitcast.452), calls=%async_computation.16 | async-start | bytes 6684672 | tf_op jit(solution)/shard_map/all_to_all | solution.py:332
  1110.5 51.7 %all-to-all-start.14 = ((bf16[8,96,2176]{2,1,0:T(8,128)(2,1)}), bf16[8,96,2176]{2,1,0:T(8,128)(2,1)}, u32[]{:S(2)}, u32[]{:S(2)}) async-start(bf16[8,96,2176]{2,1,0:T(8,128)(2,1)} %bitcast.451), calls=%async_computation.14 | async-start | bytes 6684672 | tf_op jit(solution)/shard_map/all_to_all | solution.py:332
  1162.2 44.7 %all-to-all-start.13 = ((bf16[8,96,2176]{2,1,0:T(8,128)(2,1)}), bf16[8,96,2176]{2,1,0:T(8,128)(2,1)}, u32[]{:S(2)}, u32[]{:S(2)}) async-start(bf16[8,96,2176]{2,1,0:T(8,128)(2,1)} %bitcast.450), calls=%async_computation.13 | async-start | bytes 6684672 | tf_op jit(solution)/shard_map/all_to_all | solution.py:332
  1172.7 70.6 %collective-permute-start.9 = (bf16[256,2176]{1,0:T(8,128)(2,1)}, bf16[256,2176]{1,0:T(8,128)(2,1)}, u32[]{:S(2)}, u32[]{:S(2)}) collective-permute-start(bf16[256,2176]{1,0:T(8,128)(2,1)} %pad_maximum_fusion.2), channel_id=1, source_target_pairs={{0,8},{8,16},{16,24},{24,0},{1,9},{9,17},{17,25},{25,1},{2,10},{10... | collective-permute-start | bytes 3342344 | tf_op jit(solution)/shard_map/ppermute | solution.py:345
  1177.0 72.6 %collective-permute-start.10 = (bf16[256,2176]{1,0:T(8,128)(2,1)}, bf16[256,2176]{1,0:T(8,128)(2,1)}, u32[]{:S(2)}, u32[]{:S(2)}) collective-permute-start(bf16[256,2176]{1,0:T(8,128)(2,1)} %pad_maximum_fusion.3), channel_id=1, source_target_pairs={{0,16},{8,24},{16,0},{24,8},{1,17},{9,25},{17,1},{25,9},{2,18},{10... | collective-permute-start | bytes 3342344 | tf_op jit(solution)/shard_map/ppermute | solution.py:345
  1206.9 44.5 %all-to-all-start.15 = ((bf16[8,96,2176]{2,1,0:T(8,128)(2,1)}), bf16[8,96,2176]{2,1,0:T(8,128)(2,1)}, u32[]{:S(2)}, u32[]{:S(2)}) async-start(bf16[8,96,2176]{2,1,0:T(8,128)(2,1)} %bitcast.449), calls=%async_computation.15 | async-start | bytes 6684672 | tf_op jit(solution)/shard_map/all_to_all | solution.py:332
  1211.4 122.4 %reduce-scatter.2.cloned.1.call-start = ((), (), s32[]{:S(2)}) async-start(), calls=%async_computation.29 | async-start | bytes 2396160 | tf_op jit(solution)/shard_map/reduce_scatter | solution.py:860
  1221.2 51.3 %collective-permute-start.11 = (bf16[256,2176]{1,0:T(8,128)(2,1)}, bf16[256,2176]{1,0:T(8,128)(2,1)}, u32[]{:S(2)}, u32[]{:S(2)}) collective-permute-start(bf16[256,2176]{1,0:T(8,128)(2,1)} %pad_maximum_fusion.4), channel_id=1, source_target_pairs={{0,24},{8,0},{16,8},{24,16},{1,25},{9,1},{17,9},{25,17},{2,26},{10... | collective-permute-start | bytes 3342344 | tf_op jit(solution)/shard_map/ppermute | solution.py:345
  1278.2 48.2 %all-to-all-start.17 = ((bf16[8,96,2048]{2,1,0:T(8,128)(2,1)}), bf16[8,96,2048]{2,1,0:T(8,128)(2,1)}, u32[]{:S(2)}, u32[]{:S(2)}) async-start(bf16[8,96,2048]{2,1,0:T(8,128)(2,1)} %bitcast.425), calls=%async_computation.17 | async-start | bytes 6291456 | tf_op jit(solution)/shard_map/all_to_all | solution.py:332
  1329.1 42.4 %all-to-all-start.18 = ((bf16[8,96,2048]{2,1,0:T(8,128)(2,1)}), bf16[8,96,2048]{2,1,0:T(8,128)(2,1)}, u32[]{:S(2)}, u32[]{:S(2)}) async-start(bf16[8,96,2048]{2,1,0:T(8,128)(2,1)} %bitcast.424), calls=%async_computation.18 | async-start | bytes 6291456 | tf_op jit(solution)/shard_map/all_to_all | solution.py:332
  1333.5 272.4 %all-gather.14.cloned.1.call-start = ((), (), s32[]{:S(2)}) async-start(), calls=%async_computation.30 | async-start | bytes 8785920 | tf_op jit(solution)/shard_map/all_gather | solution.py:879
  1383.4 55.5 %all-to-all-start.19 = ((bf16[8,96,2048]{2,1,0:T(8,128)(2,1)}), bf16[8,96,2048]{2,1,0:T(8,128)(2,1)}, u32[]{:S(2)}, u32[]{:S(2)}) async-start(bf16[8,96,2048]{2,1,0:T(8,128)(2,1)} %bitcast.455), calls=%async_computation.19 | async-start | bytes 6291456 | tf_op jit(solution)/shard_map/all_to_all | solution.py:332
  1439.0 65.3 %all-to-all-start.20 = ((bf16[8,96,2048]{2,1,0:T(8,128)(2,1)}), bf16[8,96,2048]{2,1,0:T(8,128)(2,1)}, u32[]{:S(2)}, u32[]{:S(2)}) async-start(bf16[8,96,2048]{2,1,0:T(8,128)(2,1)} %bitcast.426), calls=%async_computation.20 | async-start | bytes 6291456 | tf_op jit(solution)/shard_map/all_to_all | solution.py:332
  1446.9 44.1 %copy-start.46 = (bf16[16,4096]{1,0:T(8,128)(2,1)S(1)}, bf16[16,4096]{1,0:T(8,128)(2,1)}, u32[]{:S(2)}) copy-start(bf16[16,4096]{1,0:T(8,128)(2,1)} %copy-done.45) | copy-start | bytes 393220
  1504.3 42.8 %all-to-all-start.22 = ((bf16[8,96,2048]{2,1,0:T(8,128)(2,1)}), bf16[8,96,2048]{2,1,0:T(8,128)(2,1)}, u32[]{:S(2)}, u32[]{:S(2)}) async-start(bf16[8,96,2048]{2,1,0:T(8,128)(2,1)} %bitcast.454), calls=%async_computation.22 | async-start | bytes 6291456 | tf_op jit(solution)/shard_map/all_to_all | solution.py:332
  1559.0 42.4 %all-to-all-start.23 = ((bf16[8,96,2048]{2,1,0:T(8,128)(2,1)}), bf16[8,96,2048]{2,1,0:T(8,128)(2,1)}, u32[]{:S(2)}, u32[]{:S(2)}) async-start(bf16[8,96,2048]{2,1,0:T(8,128)(2,1)} %bitcast.456), calls=%async_computation.23 | async-start | bytes 6291456 | tf_op jit(solution)/shard_map/all_to_all | solution.py:332
  1565.8 59.4 %collective-permute-start.16 = (bf16[288,2048]{1,0:T(8,128)(2,1)S(1)}, bf16[288,2048]{1,0:T(8,128)(2,1)}, u32[]{:S(2)}, u32[]{:S(2)}) collective-permute-start(bf16[288,2048]{1,0:T(8,128)(2,1)S(1)} %fusion.81), channel_id=1, source_target_pairs={{0,16},{8,24},{16,0},{24,8},{1,17},{9,25},{17,1},{25,9},{2,18},{10... | collective-permute-start | bytes 3538952 | tf_op jit(solution)/shard_map/ppermute | solution.py:345
  1567.0 58.1 %collective-permute-start.17 = (bf16[288,2048]{1,0:T(8,128)(2,1)}, bf16[288,2048]{1,0:T(8,128)(2,1)}, u32[]{:S(2)}, u32[]{:S(2)}) collective-permute-start(bf16[288,2048]{1,0:T(8,128)(2,1)} %fusion.82), channel_id=1, source_target_pairs={{0,24},{8,0},{16,8},{24,16},{1,25},{9,1},{17,9},{25,17},{2,26},{10... | collective-permute-start | bytes 3538952 | tf_op jit(solution)/shard_map/ppermute | solution.py:345
  1572.1 74.7 %collective-permute-start.15 = (bf16[288,2048]{1,0:T(8,128)(2,1)}, bf16[288,2048]{1,0:T(8,128)(2,1)}, u32[]{:S(2)}, u32[]{:S(2)}) collective-permute-start(bf16[288,2048]{1,0:T(8,128)(2,1)} %fusion.80), channel_id=1, source_target_pairs={{0,8},{8,16},{16,24},{24,0},{1,9},{9,17},{17,25},{25,1},{2,10},{10... | collective-permute-start | bytes 3538952 | tf_op jit(solution)/shard_map/ppermute | solution.py:345
  1601.4 60.5 %all-to-all-start.24 = ((bf16[8,96,2048]{2,1,0:T(8,128)(2,1)}), bf16[8,96,2048]{2,1,0:T(8,128)(2,1)}, u32[]{:S(2)}, u32[]{:S(2)}) async-start(bf16[8,96,2048]{2,1,0:T(8,128)(2,1)} %bitcast.427), calls=%async_computation.24 | async-start | bytes 6291456 | tf_op jit(solution)/shard_map/all_to_all | solution.py:332
  1605.8 187.0 %all-gather.20.cloned.1.call-start = ((), (), s32[]{:S(2)}) async-start(), calls=%async_computation.33 | async-start | bytes 3784704 | tf_op jit(solution)/shard_map/all_gather | solution.py:896
  1661.9 98.0 %all-to-all-start.25 = ((bf16[8,96,2048]{2,1,0:T(8,128)(2,1)}), bf16[8,96,2048]{2,1,0:T(8,128)(2,1)}, u32[]{:S(2)}, u32[]{:S(2)}) async-start(bf16[8,96,2048]{2,1,0:T(8,128)(2,1)} %bitcast.428), calls=%async_computation.25 | async-start | bytes 6291456 | tf_op jit(solution)/shard_map/all_to_all | solution.py:332
  1670.4 52.8 %collective-permute-start.12 = (bf16[256,2048]{1,0:T(8,128)(2,1)}, bf16[256,2048]{1,0:T(8,128)(2,1)S(1)}, u32[]{:S(2)}, u32[]{:S(2)}) collective-permute-start(bf16[256,2048]{1,0:T(8,128)(2,1)} %convolution_convert_fusion.16), channel_id=1, source_target_pairs={{0,8},{8,16},{16,24},{24,0},{1,9},{9,17},{17,25},{25,1},{2,10},{10... | collective-permute-start | bytes 3145736 | tf_op jit(solution)/shard_map/ppermute | solution.py:345
  1699.2 60.7 %collective-permute-start.13 = (bf16[256,2048]{1,0:T(8,128)(2,1)}, bf16[256,2048]{1,0:T(8,128)(2,1)}, u32[]{:S(2)}, u32[]{:S(2)}) collective-permute-start(bf16[256,2048]{1,0:T(8,128)(2,1)} %convolution_convert_fusion.15), channel_id=1, source_target_pairs={{0,16},{8,24},{16,0},{24,8},{1,17},{9,25},{17,1},{25,9},{2,18},{10... | collective-permute-start | bytes 3145736 | tf_op jit(solution)/shard_map/ppermute | solution.py:345
  1703.2 75.6 %collective-permute-start.14 = (bf16[256,2048]{1,0:T(8,128)(2,1)}, bf16[256,2048]{1,0:T(8,128)(2,1)}, u32[]{:S(2)}, u32[]{:S(2)}) collective-permute-start(bf16[256,2048]{1,0:T(8,128)(2,1)} %convolution_convert_fusion.14), channel_id=1, source_target_pairs={{0,24},{8,0},{16,8},{24,16},{1,25},{9,1},{17,9},{25,17},{2,26},{10... | collective-permute-start | bytes 3145736 | tf_op jit(solution)/shard_map/ppermute | solution.py:345
  1705.9 72.9 %copy-start.91 = (bf16[512,768]{1,0:T(8,128)(2,1)S(1)}, bf16[512,768]{1,0:T(8,128)(2,1)}, u32[]{:S(2)}) copy-start(bf16[512,768]{1,0:T(8,128)(2,1)} %get-tuple-element.212) | copy-start | bytes 2359300
  (148 other events, 912.8 us)
Sparse Core Ops, SparseCore 0:
  9.6 264.2 all-gather.15
  276.4 158.8 all-gather.17
  436.9 152.0 all-gather.9
  675.1 84.9 all-gather.11
  1274.1 56.0 reduce-scatter.1
  1371.6 91.3 all-gather.13
  1651.6 123.7 all-gather.19

commit v9 on v7

--- a/solution.py
+++ b/solution.py
@@ -807,7 +807,7 @@
     for d in order[1:]:
         earlier = [inner_parts[distances[min(d - 1, size - 2)]]]
         got_rows.append(send_rows(d, got_rows[-1], *earlier))
-    kept = [work(0, after(got_rows[0], got_rows[-2]) if size > 1 else got_rows[0])]
+    kept = [work(0, after(got_rows[0], *got_rows[1:-1], *hidden_grads))]
     row_home, row_total = rows_home(0, kept[0][0])
     row_backs, row_homes = [row_total], [row_home]
     for d in order[1:]:

time: 1840 us -> 1830 us (level)
  waiting for transfers between devices: 826 us -> 802 us
    all_gather x1, waiting for transfers between devices: 76.6 us -> 54 us  [body(): packet_all = lax.all_gather(packet, 'seq', axis=0, tiled=True)]
    unnamed x373 -> x369, local copies, waits for them, and re-layouts: 48.7 us -> 49.9 us
where the time goes in v9:
time: 1830 us; the launch traced here: 1790 us
  waiting for transfers between devices  802 us (44%)
  Pallas kernels  292 us (16%)
  matrix products  290 us (16%)
  starting transfers between devices  225 us (12%)
  local copies, waits for them, and re-layouts  124 us (7%)
  other arithmetic  39.8 us (2%)
  between operations  18.7 us (1%)
    ppermute x18, waiting for transfers between devices, shifted(): lax.ppermute(array, 'seq', [(k, (k - shift) % size) for k in range(size)])  511 us
    dot_general x95, matrix products, product(): lax.dot_general(left, right, (((left_dim,), (right_dim,)), ((), ())), pre...  290 us
    all_to_all x26, waiting for transfers between devices, exchange(): return lax.all_to_all(buffer, 'dp', split_axis=0, concat_axis=0, tiled=True)  196 us
    pallas_call x4, Pallas kernels, expert_block(): pl.pallas_call(functools.partial(expert_kernel, size, share), grid_spec=p...  124 us
    all_to_all x26, starting transfers between devices, exchange(): return lax.all_to_all(buffer, 'dp', split_axis=0, concat_axis=0, tiled=True)  119 us
    ppermute x18, starting transfers between devices, shifted(): lax.ppermute(array, 'seq', [(k, (k - shift) % size) for k in range(size)])  106 us
    all_gather x1, waiting for transfers between devices, body(): packet_all = lax.all_gather(packet, 'seq', axis=0, tiled=True)  54 us
    unnamed x369, local copies, waits for them, and re-layouts  49.9 us
  transfers between devices with their start and end apart: 51, of which 30 were waited for; matrix products, arithmetic and copies ran while one was open for 22% of the time, Pallas kernels for 16%

profile of v9, /device:TPU:0, one launch (start us, length us, event | category | flops | bytes accessed | tf_op | source)
XLA Modules:
  0.0 1791.8 jit_solution(9885930199235609314)
XLA Ops:
  9.2 5.2 all-to-all-start.3
  34.0 28.7 %all-to-all-done = bf16[8,96,2048]{2,1,0:T(8,128)(2,1)} async-done(((bf16[8,96,2048]{2,1,0:T(8,128)(2,1)}), bf16[8,96,2048]{2,1,0:T(8,128)(2,1)}, u32[]{:S(2)}, u32[]{:S(2)}) %all-to-all-start) | async-done | bytes 3145760 | tf_op jit(solution)/shard_map/all_to_all | solution.py:332
  74.2 67.4 %collective-permute-done.2 = bf16[384,2048]{1,0:T(8,128)(2,1)} collective-permute-done((bf16[384,2048]{1,0:T(8,128)(2,1)}, bf16[384,2048]{1,0:T(8,128)(2,1)}, u32[]{:S(2)}, u32[]{:S(2)}) %collective-permute-start.2) | collective-permute-done | bytes 1572896 | tf_op jit(solution)/shard_map/ppermute | solution.py:345
  145.7 105.7 %collective-permute-done.1 = bf16[384,2048]{1,0:T(8,128)(2,1)} collective-permute-done((bf16[384,2048]{1,0:T(8,128)(2,1)}, bf16[384,2048]{1,0:T(8,128)(2,1)}, u32[]{:S(2)}, u32[]{:S(2)}) %collective-permute-start.1) | collective-permute-done | bytes 1572896 | tf_op jit(solution)/shard_map/ppermute | solution.py:345
  282.7 11.8 convolution_convert_fusion.3
  300.4 40.3 %collective-permute-start.5 = (bf16[256,2176]{1,0:T(8,128)(2,1)S(1)}, bf16[256,2176]{1,0:T(8,128)(2,1)}, u32[]{:S(2)}, u32[]{:S(2)}) collective-permute-start(bf16[256,2176]{1,0:T(8,128)(2,1)S(1)} %fusion.93), channel_id=1, source_target_pairs={{0,8},{8,16},{16,24},{24,0},{1,9},{9,17},{17,25},{25,1},{2,10},{10... | collective-permute-start | bytes 3342344 | tf_op jit(solution)/shard_map/ppermute | solution.py:345
  344.5 25.0 %collective-permute-done.5 = bf16[256,2176]{1,0:T(8,128)(2,1)} collective-permute-done((bf16[256,2176]{1,0:T(8,128)(2,1)S(1)}, bf16[256,2176]{1,0:T(8,128)(2,1)}, u32[]{:S(2)}, u32[]{:S(2)}) %collective-permute-start.5) | collective-permute-done | bytes 1114144 | tf_op jit(solution)/shard_map/ppermute | solution.py:345
  369.5 47.4 %collective-permute-done.4 = bf16[256,2176]{1,0:T(8,128)(2,1)} collective-permute-done((bf16[256,2176]{1,0:T(8,128)(2,1)S(1)}, bf16[256,2176]{1,0:T(8,128)(2,1)}, u32[]{:S(2)}, u32[]{:S(2)}) %collective-permute-start.4) | collective-permute-done | bytes 1114144 | tf_op jit(solution)/shard_map/ppermute | solution.py:345
  416.9 18.3 %all-gather.18.cloned.1.call-done = bf16[16384,512]{1,0:T(8,128)(2,1)} async-done(((bf16[2048,512]{1,0:T(8,128)(2,1)}), bf16[16384,512]{1,0:T(8,128)(2,1)}) %all-gather.18.cloned.1.call-update) | async-done | bytes 16777232 | tf_op jit(solution)/shard_map/all_gather | solution.py:696
  444.2 4.8 all-to-all-start.5
  456.8 31.6 %pairs.1 = (bf16[1024,4096]{1,0:T(8,128)(2,1)}, bf16[1024,16]{1,0:T(8,128)(2,1)S(1)}) custom-call(bf16[256,2048]{1,0:T(8,128)(2,1)S(1)} %fusion.54.refs_0_, bf16[256,2048]{1,0:T(8,128)(2,1)S(1)} %copy-done.26, bf16[256,2048]{1,0:T(8,128)(2,1)S(1)} %copy-done.25, bf16[256,2048]{1,0:T(8,128)(2,1)S(1)} %copy-done.24, bf16[8,2048,512]{2,1,0:T(8,128)(2,1)} %bitcast.498, ...), custom_call_target="tpu_custom_call" | custom-call | flops 17179869184 | bytes 16777216 | tf_op jit(solution)/shard_map/pairs/pallas_call | solution.py:75
  500.9 33.7 %attend.1 = (bf16[512,2048]{1,0:T(8,128)(2,1)S(1)}, bf16[768,2048]{1,0:T(8,128)(2,1)}, bf16[512,2048]{1,0:T(8,128)(2,1)}, f32[16,512,1]{2,1,0:T(8,128)}) custom-call(bf16[768,2048]{1,0:T(8,128)(2,1)} %bitcast.8.home_ref, bf16[512,768]{1,0:T(8,128)(2,1)S(1)} %fusion.80.place_ref, bf16[256,16]{1,0:T(8,128)(2,1)S(1)} %convolution_convert_fusion.25.low_ref, ...), custom_call_target="tpu_custom_call" | custom-call | flops 4294967296 | bytes 8388608 | tf_op jit(solution)/shard_map/attend/pallas_call | solution.py:194
  554.5 24.4 %all-to-all-done.4 = bf16[8,96,2048]{2,1,0:T(8,128)(2,1)} async-done(((bf16[8,96,2048]{2,1,0:T(8,128)(2,1)}), bf16[8,96,2048]{2,1,0:T(8,128)(2,1)}, u32[]{:S(2)}, u32[]{:S(2)}) %all-to-all-start.4) | async-done | bytes 3145760 | tf_op jit(solution)/shard_map/all_to_all | solution.py:332
  578.9 10.0 all-gather.10.cloned.1.call-done
  588.9 11.8 convolution_convert_fusion.2
  609.8 10.5 collective-permute-start.6
  620.3 22.9 %all-to-all-done.7 = bf16[8,96,2048]{2,1,0:T(8,128)(2,1)} async-done(((bf16[8,96,2048]{2,1,0:T(8,128)(2,1)}), bf16[8,96,2048]{2,1,0:T(8,128)(2,1)}, u32[]{:S(2)}, u32[]{:S(2)}) %all-to-all-start.7) | async-done | bytes 3145760 | tf_op jit(solution)/shard_map/all_to_all | solution.py:332
  654.6 30.5 %collective-permute-done.6.refs_1_ = bf16[512,2816]{1,0:T(8,128)(2,1)} collective-permute-done((bf16[512,2816]{1,0:T(8,128)(2,1)}, bf16[512,2816]{1,0:T(8,128)(2,1)}, u32[]{:S(2)}, u32[]{:S(2)}) %collective-permute-start.6) | collective-permute-done | bytes 2883616 | tf_op jit(solution)/shard_map/ppermute | solution.py:345
  699.7 6.5 squeeze.95
  706.2 6.8 dynamic-slice_reduce_fusion
  716.2 54.0 %all-gather.12.cloned.1.call-done = bf16[1024,2176]{1,0:T(8,128)(2,1)} async-done(((bf16[256,2176]{1,0:T(8,128)(2,1)}), bf16[1024,2176]{1,0:T(8,128)(2,1)}) %all-gather.12.cloned.1.call-update) | async-done | bytes 4456464 | tf_op jit(solution)/shard_map/all_gather | solution.py:766
  778.0 4.9 all-to-all-start.9
  782.9 8.5 fusion.14
  802.3 18.5 %all-to-all-done.9 = bf16[8,96,2048]{2,1,0:T(8,128)(2,1)} async-done(((bf16[8,96,2048]{2,1,0:T(8,128)(2,1)}), bf16[8,96,2048]{2,1,0:T(8,128)(2,1)}, u32[]{:S(2)}, u32[]{:S(2)}) %all-to-all-start.9) | async-done | bytes 3145760 | tf_op jit(solution)/shard_map/all_to_all | solution.py:332
  825.3 8.5 fusion.12
  835.8 9.8 fusion.10
  845.7 20.9 %collective-permute-done.7.refs_3_ = bf16[512,2816]{1,0:T(8,128)(2,1)} collective-permute-done((bf16[512,2816]{1,0:T(8,128)(2,1)}, bf16[512,2816]{1,0:T(8,128)(2,1)}, u32[]{:S(2)}, u32[]{:S(2)}) %collective-permute-start.7) | collective-permute-done | bytes 2883616 | tf_op jit(solution)/shard_map/ppermute | solution.py:345
  876.8 9.8 fusion.8
  894.8 16.9 all-to-all-done.10
  915.2 76.6 %collective-permute-done.8.refs_2_ = bf16[512,2816]{1,0:T(8,128)(2,1)} collective-permute-done((bf16[512,2816]{1,0:T(8,128)(2,1)}, bf16[512,2816]{1,0:T(8,128)(2,1)}, u32[]{:S(2)}, u32[]{:S(2)}) %collective-permute-start.8) | collective-permute-done | bytes 2883616 | tf_op jit(solution)/shard_map/ppermute | solution.py:345
  1012.3 31.0 %experts.4 = (bf16[768,2176]{1,0:T(8,128)(2,1)}, bf16[768,1408]{1,0:T(8,128)(2,1)S(1)}, bf16[768,2816]{1,0:T(8,128)(2,1)}, bf16[768,128]{1,0:T(8,128)(2,1)S(1)}, bf16[768,128]{1,0:T(8,128)(2,1)S(1)}) custom-call(s32[1]{0:T(128)} %bitcast.46.spot_ref, bf16[768,2048]{1,0:T(8,128)(2,1)} %bitcast.48.x_ref, bf16[768,1408]{1,0:T(8,128)(2,1)S(1)} %copy-done.20, ...), custom_call_target="tpu_custom_call" | custom-call | flops 17716740096 | bytes 27262976 | tf_op jit(solution)/shard_map/experts/pallas_call | solution.py:607
  1044.6 4.7 all-to-all-start.17
  1052.0 30.9 %experts.5 = (bf16[768,2176]{1,0:T(8,128)(2,1)}, bf16[768,1408]{1,0:T(8,128)(2,1)S(1)}, bf16[768,2816]{1,0:T(8,128)(2,1)}, bf16[768,128]{1,0:T(8,128)(2,1)S(1)}, bf16[768,128]{1,0:T(8,128)(2,1)S(1)}) custom-call(s32[1]{0:T(128)} %bitcast.46.spot_ref, bf16[768,2048]{1,0:T(8,128)(2,1)} %bitcast.50.x_ref, bf16[768,1408]{1,0:T(8,128)(2,1)S(1)} %copy-done.21, ...), custom_call_target="tpu_custom_call" | custom-call | flops 17716740096 | bytes 27262976 | tf_op jit(solution)/shard_map/experts/pallas_call | solution.py:607
  1084.3 5.1 all-to-all-done.17
  1089.3 4.9 all-to-all-start.13
  1100.0 31.0 %experts.6 = (bf16[768,2176]{1,0:T(8,128)(2,1)}, bf16[768,1408]{1,0:T(8,128)(2,1)S(1)}, bf16[768,2816]{1,0:T(8,128)(2,1)}, bf16[768,128]{1,0:T(8,128)(2,1)S(1)}, bf16[768,128]{1,0:T(8,128)(2,1)S(1)}) custom-call(s32[1]{0:T(128)} %bitcast.46.spot_ref, bf16[768,2048]{1,0:T(8,128)(2,1)} %bitcast.52.x_ref, bf16[768,1408]{1,0:T(8,128)(2,1)S(1)} %copy-done.23, ...), custom_call_target="tpu_custom_call" | custom-call | flops 17716740096 | bytes 27262976 | tf_op jit(solution)/shard_map/experts/pallas_call | solution.py:607
  1135.9 4.6 all-to-all-start.12
  1143.2 31.0 %experts.7 = (bf16[768,2176]{1,0:T(8,128)(2,1)}, bf16[768,1408]{1,0:T(8,128)(2,1)S(1)}, bf16[768,2816]{1,0:T(8,128)(2,1)}, bf16[768,128]{1,0:T(8,128)(2,1)S(1)}, bf16[768,128]{1,0:T(8,128)(2,1)S(1)}) custom-call(s32[1]{0:T(128)} %bitcast.46.spot_ref, bf16[768,2048]{1,0:T(8,128)(2,1)} %bitcast.68.x_ref, bf16[768,1408]{1,0:T(8,128)(2,1)S(1)} %copy-done.22, ...), custom_call_target="tpu_custom_call" | custom-call | flops 17716740096 | bytes 27262976 | tf_op jit(solution)/shard_map/experts/pallas_call | solution.py:607
  1228.2 5.0 fusion.6
  1250.8 31.6 %collective-permute-done.11 = bf16[256,2176]{1,0:T(8,128)(2,1)} collective-permute-done((bf16[256,2176]{1,0:T(8,128)(2,1)}, bf16[256,2176]{1,0:T(8,128)(2,1)}, u32[]{:S(2)}, u32[]{:S(2)}) %collective-permute-start.11) | collective-permute-done | bytes 1114144 | tf_op jit(solution)/shard_map/ppermute | solution.py:345
  1282.4 10.8 collective-permute-done.12
  1311.0 37.8 %all-to-all-done.18 = bf16[8,96,2048]{2,1,0:T(8,128)(2,1)} async-done(((bf16[8,96,2048]{2,1,0:T(8,128)(2,1)}), bf16[8,96,2048]{2,1,0:T(8,128)(2,1)}, u32[]{:S(2)}, u32[]{:S(2)}) %all-to-all-start.18) | async-done | bytes 3145760 | tf_op jit(solution)/shard_map/all_to_all | solution.py:332
  1348.8 11.9 convolution_convert_fusion.1
  1360.8 4.8 all-to-all-start.19
  1377.0 7.8 fusion.4
  1387.4 25.5 %all-to-all-done.19 = bf16[8,96,2048]{2,1,0:T(8,128)(2,1)} async-done(((bf16[8,96,2048]{2,1,0:T(8,128)(2,1)}), bf16[8,96,2048]{2,1,0:T(8,128)(2,1)}, u32[]{:S(2)}, u32[]{:S(2)}) %all-to-all-start.19) | async-done | bytes 3145760 | tf_op jit(solution)/shard_map/all_to_all | solution.py:332
  1420.6 44.1 %attend_back.1 = (bf16[1024,2048]{1,0:T(8,128)(2,1)}, bf16[1024,2048]{1,0:T(8,128)(2,1)}, bf16[768,2048]{1,0:T(8,128)(2,1)}, bf16[256,2048]{1,0:T(8,128)(2,1)S(1)}) custom-call(bf16[512,2048]{1,0:T(8,128)(2,1)} %get-tuple-element.131.query_ref, bf16[1024,4096]{1,0:T(8,128)(2,1)} %get-tuple-element.98.key_ref.value_ref, ...), custom_call_target="tpu_custom_call" | custom-call | flops 10737418240 | bytes 16777216 | tf_op jit(solution)/shard_map/attend_back/pallas_call | solution.py:289
  1478.5 4.8 all-to-all-start.22
  1489.2 23.2 %pair_back.1 = bf16[1024,2048]{1,0:T(8,128)(2,1)S(1)} custom-call(bf16[1024,2048]{1,0:T(8,128)(2,1)} %get-tuple-element.160.key_ref, bf16[1024,2048]{1,0:T(8,128)(2,1)} %get-tuple-element.161.value_ref, bf16[8,2048,512]{2,1,0:T(8,128)(2,1)} %bitcast.499, bf16[1024,16]{1,0:T(8,128)(2,1)S(1)} %fusion.81.low_ref, bf16[16,2048]{1,0:T(8,128)(2,1)S(1)} %copy-done.45), custom_call_target="tpu_custom_call" | custom-call | flops 17179869184 | bytes 16777216 | tf_op jit(solution)/shard_map/pair_back/pallas_call | solution.py:129
  1514.4 6.7 all-to-all-done.22
  1521.2 11.9 convolution_convert_fusion
  1539.9 10.4 collective-permute-start.16
  1556.2 7.1 fusion.2
  1565.9 9.5 all-to-all-done.23
  1580.0 19.3 %unpack.1 = (f32[8,16,11264]{2,1,0:T(8,128)}, f32[8,16,5632]{2,1,0:T(8,128)}, f32[8,16,2048]{2,1,0:T(8,128)}, f32[8,16,2048]{2,1,0:T(8,128)}) custom-call(bf16[4,8,16,8320]{3,2,1,0:T(8,128)(2,1)} %bitcast.430), custom_call_target="tpu_custom_call" | custom-call | bytes 32243712 | tf_op jit(solution)/shard_map/unpack/pallas_call | solution.py:485
  1602.5 28.2 %collective-permute-done.15 = bf16[288,2048]{1,0:T(8,128)(2,1)} collective-permute-done((bf16[288,2048]{1,0:T(8,128)(2,1)}, bf16[288,2048]{1,0:T(8,128)(2,1)}, u32[]{:S(2)}, u32[]{:S(2)}) %collective-permute-start.15) | collective-permute-done | bytes 1179680 | tf_op jit(solution)/shard_map/ppermute | solution.py:345
  1635.4 7.8 fusion
  1654.3 22.7 %collective-permute-start.9 = (bf16[256,2048]{1,0:T(8,128)(2,1)}, bf16[256,2048]{1,0:T(8,128)(2,1)S(1)}, u32[]{:S(2)}, u32[]{:S(2)}) collective-permute-start(bf16[256,2048]{1,0:T(8,128)(2,1)} %convolution_convert_fusion.16), channel_id=1, source_target_pairs={{0,8},{8,16},{16,24},{24,0},{1,9},{9,17},{17,25},{25,1},{2,10},{10... | collective-permute-start | bytes 3145736 | tf_op jit(solution)/shard_map/ppermute | solution.py:345
  1690.7 14.3 collective-permute-done.9
  1705.0 30.6 %collective-permute-done.13 = bf16[256,2048]{1,0:T(8,128)(2,1)} collective-permute-done((bf16[256,2048]{1,0:T(8,128)(2,1)}, bf16[256,2048]{1,0:T(8,128)(2,1)}, u32[]{:S(2)}, u32[]{:S(2)}) %collective-permute-start.13) | collective-permute-done | bytes 1048608 | tf_op jit(solution)/shard_map/ppermute | solution.py:345
  1735.6 15.2 collective-permute-done.14
  1750.8 5.1 fusion.100
  1765.0 11.4 all-gather.20.cloned.1.call-done
  1778.4 6.0 gather_adapters.1
  (683 shorter events, 444.4 us)
Async XLA Ops:
  7.2 431.3 %copy-start = (bf16[8,16,4096]{2,1,0:T(8,128)(2,1)S(1)}, bf16[8,16,4096]{2,1,0:T(8,128)(2,1)}, u32[]{:S(2)}) copy-start(bf16[8,16,4096]{2,1,0:T(8,128)(2,1)} %param.37) | copy-start | bytes 3145732
  7.2 268.6 %all-gather.16.cloned.1.call-start = ((), (), s32[]{:S(2)}) async-start(), calls=%async_computation.31 | async-start | bytes 10485760 | tf_op jit(solution)/shard_map/all_gather | solution.py:685
  9.2 10.9 all-to-all-start.3
  17.4 588.1 %copy-start.2 = (bf16[256,2048]{1,0:T(8,128)(2,1)}, bf16[256,2048]{1,0:T(8,128)(2,1)S(1)}, u32[]{:S(2)}) copy-start(bf16[256,2048]{1,0:T(8,128)(2,1)S(1)} %fusion.54.refs_0_) | copy-start | bytes 3145732
  20.2 42.5 %all-to-all-start = ((bf16[8,96,2048]{2,1,0:T(8,128)(2,1)}), bf16[8,96,2048]{2,1,0:T(8,128)(2,1)}, u32[]{:S(2)}, u32[]{:S(2)}) async-start(bf16[8,96,2048]{2,1,0:T(8,128)(2,1)} %bitcast.418), calls=%async_computation | async-start | bytes 6291456 | tf_op jit(solution)/shard_map/all_to_all | solution.py:332
  62.7 213.1 %all-to-all-start.2 = ((bf16[8,96,2048]{2,1,0:T(8,128)(2,1)}), bf16[8,96,2048]{2,1,0:T(8,128)(2,1)}, u32[]{:S(2)}, u32[]{:S(2)}) async-start(bf16[8,96,2048]{2,1,0:T(8,128)(2,1)} %bitcast.416), calls=%async_computation.2 | async-start | bytes 6291456 | tf_op jit(solution)/shard_map/all_to_all | solution.py:332
  67.3 368.0 %all-gather.18.cloned.1.call-start = ((), (), s32[]{:S(2)}) async-start(), calls=%async_computation.32 | async-start | bytes 18874368 | tf_op jit(solution)/shard_map/all_gather | solution.py:696
  68.6 73.0 %collective-permute-start.2 = (bf16[384,2048]{1,0:T(8,128)(2,1)}, bf16[384,2048]{1,0:T(8,128)(2,1)}, u32[]{:S(2)}, u32[]{:S(2)}) collective-permute-start(bf16[384,2048]{1,0:T(8,128)(2,1)} %pad_maximum_fusion.1), channel_id=1, source_target_pairs={{0,8},{8,16},{16,24},{24,0},{1,9},{9,17},{17,25},{25,1},{2,10},{10... | collective-permute-start | bytes 4718600 | tf_op jit(solution)/shard_map/ppermute | solution.py:345
  70.2 181.2 %collective-permute-start.1 = (bf16[384,2048]{1,0:T(8,128)(2,1)}, bf16[384,2048]{1,0:T(8,128)(2,1)}, u32[]{:S(2)}, u32[]{:S(2)}) collective-permute-start(bf16[384,2048]{1,0:T(8,128)(2,1)} %pad_maximum_fusion.1), channel_id=1, source_target_pairs={{0,16},{8,24},{16,0},{24,8},{1,17},{9,25},{17,1},{25,9},{2,18},{10... | collective-permute-start | bytes 4718600 | tf_op jit(solution)/shard_map/ppermute | solution.py:345
  72.7 185.8 %collective-permute-start = (bf16[384,2048]{1,0:T(8,128)(2,1)}, bf16[384,2048]{1,0:T(8,128)(2,1)}, u32[]{:S(2)}, u32[]{:S(2)}) collective-permute-start(bf16[384,2048]{1,0:T(8,128)(2,1)} %pad_maximum_fusion.1), channel_id=1, source_target_pairs={{0,24},{8,0},{16,8},{24,16},{1,25},{9,1},{17,9},{25,17},{2,26},{10... | collective-permute-start | bytes 4718600 | tf_op jit(solution)/shard_map/ppermute | solution.py:345
  74.2 638.9 %copy-start.46 = (s32[8]{0:T(128)}, s32[8]{0:T(128)S(1)}, u32[]{:S(2)}) copy-start(s32[8]{0:T(128)S(1)} %slice_reduce_fusion.4.ids_ref) | copy-start | bytes 100
  294.6 122.4 %all-to-all-start.1 = ((bf16[8,96,2048]{2,1,0:T(8,128)(2,1)}), bf16[8,96,2048]{2,1,0:T(8,128)(2,1)}, u32[]{:S(2)}, u32[]{:S(2)}) async-start(bf16[8,96,2048]{2,1,0:T(8,128)(2,1)} %bitcast.457), calls=%async_computation.1 | async-start | bytes 6291456 | tf_op jit(solution)/shard_map/all_to_all | solution.py:332
  299.0 289.9 %all-gather.10.cloned.1.call-start = ((), (), s32[]{:S(2)}) async-start(), calls=%async_computation.27 | async-start | bytes 10485760 | tf_op jit(solution)/shard_map/all_gather | solution.py:735
  300.4 69.1 %collective-permute-start.5 = (bf16[256,2176]{1,0:T(8,128)(2,1)S(1)}, bf16[256,2176]{1,0:T(8,128)(2,1)}, u32[]{:S(2)}, u32[]{:S(2)}) collective-permute-start(bf16[256,2176]{1,0:T(8,128)(2,1)S(1)} %fusion.93), channel_id=1, source_target_pairs={{0,8},{8,16},{16,24},{24,0},{1,9},{9,17},{17,25},{25,1},{2,10},{10... | collective-permute-start | bytes 3342344 | tf_op jit(solution)/shard_map/ppermute | solution.py:345
  340.7 76.2 %collective-permute-start.4 = (bf16[256,2176]{1,0:T(8,128)(2,1)S(1)}, bf16[256,2176]{1,0:T(8,128)(2,1)}, u32[]{:S(2)}, u32[]{:S(2)}) collective-permute-start(bf16[256,2176]{1,0:T(8,128)(2,1)S(1)} %fusion.93), channel_id=1, source_target_pairs={{0,16},{8,24},{16,0},{24,8},{1,17},{9,25},{17,1},{25,9},{2,18},{10... | collective-permute-start | bytes 3342344 | tf_op jit(solution)/shard_map/ppermute | solution.py:345
  344.5 72.4 %collective-permute-start.3 = (bf16[256,2176]{1,0:T(8,128)(2,1)S(1)}, bf16[256,2176]{1,0:T(8,128)(2,1)}, u32[]{:S(2)}, u32[]{:S(2)}) collective-permute-start(bf16[256,2176]{1,0:T(8,128)(2,1)S(1)} %fusion.93), channel_id=1, source_target_pairs={{0,24},{8,0},{16,8},{24,16},{1,25},{9,1},{17,9},{25,17},{2,26},{10... | collective-permute-start | bytes 3342344 | tf_op jit(solution)/shard_map/ppermute | solution.py:345
  439.8 453.1 %copy-start.138 = (s32[512]{0:T(512)}, s32[512]{0:T(512)S(1)}, u32[]{:S(2)}) copy-start(s32[512]{0:T(512)S(1)} %convert_add_fusion.3) | copy-start | bytes 6148
  444.2 47.0 %all-to-all-start.5 = ((bf16[8,96,2048]{2,1,0:T(8,128)(2,1)}), bf16[8,96,2048]{2,1,0:T(8,128)(2,1)}, u32[]{:S(2)}, u32[]{:S(2)}) async-start(bf16[8,96,2048]{2,1,0:T(8,128)(2,1)} %bitcast.421), calls=%async_computation.5 | async-start | bytes 6291456 | tf_op jit(solution)/shard_map/all_to_all | solution.py:332
  451.7 438.6 %copy-start.140 = (s32[512]{0:T(512)}, s32[512]{0:T(512)S(1)}, u32[]{:S(2)}) copy-start(s32[512]{0:T(512)S(1)} %convert_add_fusion.2) | copy-start | bytes 6148
  491.2 45.3 %all-to-all-start.6 = ((bf16[8,96,2048]{2,1,0:T(8,128)(2,1)}), bf16[8,96,2048]{2,1,0:T(8,128)(2,1)}, u32[]{:S(2)}, u32[]{:S(2)}) async-start(bf16[8,96,2048]{2,1,0:T(8,128)(2,1)} %bitcast.419), calls=%async_computation.6 | async-start | bytes 6291456 | tf_op jit(solution)/shard_map/all_to_all | solution.py:332
  536.5 42.4 %all-to-all-start.4 = ((bf16[8,96,2048]{2,1,0:T(8,128)(2,1)}), bf16[8,96,2048]{2,1,0:T(8,128)(2,1)}, u32[]{:S(2)}, u32[]{:S(2)}) async-start(bf16[8,96,2048]{2,1,0:T(8,128)(2,1)} %bitcast.453), calls=%async_computation.4 | async-start | bytes 6291456 | tf_op jit(solution)/shard_map/all_to_all | solution.py:332
  600.8 42.5 %all-to-all-start.7 = ((bf16[8,96,2048]{2,1,0:T(8,128)(2,1)}), bf16[8,96,2048]{2,1,0:T(8,128)(2,1)}, u32[]{:S(2)}, u32[]{:S(2)}) async-start(bf16[8,96,2048]{2,1,0:T(8,128)(2,1)} %bitcast.458), calls=%async_computation.7 | async-start | bytes 6291456 | tf_op jit(solution)/shard_map/all_to_all | solution.py:332
  605.4 164.9 %all-gather.12.cloned.1.call-start = ((), (), s32[]{:S(2)}) async-start(), calls=%async_computation.28 | async-start | bytes 5570560 | tf_op jit(solution)/shard_map/all_gather | solution.py:766
  605.5 47.1 %copy-start.144 = (s32[256,2]{0,1:T(2,128)}, s32[256,2]{0,1:T(2,128)S(1)}, u32[]{:S(2)}) copy-start(s32[256,2]{0,1:T(2,128)S(1)} %copy.263) | copy-start | bytes 6148
  609.8 75.3 %collective-permute-start.6 = (bf16[512,2816]{1,0:T(8,128)(2,1)}, bf16[512,2816]{1,0:T(8,128)(2,1)}, u32[]{:S(2)}, u32[]{:S(2)}) collective-permute-start(bf16[512,2816]{1,0:T(8,128)(2,1)} %copy-done.18), channel_id=1, source_target_pairs={{0,24},{8,0},{16,8},{24,16},{1,25},{9,1},{17,9},{25,17},{2,26},{10... | collective-permute-start | bytes 8650760 | tf_op jit(solution)/shard_map/ppermute | solution.py:345
  689.1 84.7 %all-to-all-start.8 = ((bf16[8,96,2048]{2,1,0:T(8,128)(2,1)}), bf16[8,96,2048]{2,1,0:T(8,128)(2,1)}, u32[]{:S(2)}, u32[]{:S(2)}) async-start(bf16[8,96,2048]{2,1,0:T(8,128)(2,1)} %bitcast.415), calls=%async_computation.8 | async-start | bytes 6291456 | tf_op jit(solution)/shard_map/all_to_all | solution.py:332
  699.7 303.7 %copy-start.60 = (bf16[128,1,1408]{2,0,1:T(8,128)(2,1)}, bf16[128,1,1408]{2,0,1:T(8,128)(2,1)S(1)}, u32[]{:S(2)}) copy-start(bf16[128,1,1408]{2,0,1:T(8,128)(2,1)S(1)} %copy.303) | copy-start | bytes 1081348
  716.2 75.2 %copy-start.100 = (bf16[768,128]{1,0:T(8,128)(2,1)}, bf16[768,128]{1,0:T(8,128)(2,1)S(1)}, u32[]{:S(2)}) copy-start(bf16[768,128]{1,0:T(8,128)(2,1)S(1)} %fusion.85) | copy-start | bytes 589828
  778.0 42.8 %all-to-all-start.9 = ((bf16[8,96,2048]{2,1,0:T(8,128)(2,1)}), bf16[8,96,2048]{2,1,0:T(8,128)(2,1)}, u32[]{:S(2)}, u32[]{:S(2)}) async-start(bf16[8,96,2048]{2,1,0:T(8,128)(2,1)} %bitcast.420), calls=%async_computation.9 | async-start | bytes 6291456 | tf_op jit(solution)/shard_map/all_to_all | solution.py:332
  796.1 95.5 %copy-start.142 = (s32[512]{0:T(512)}, s32[512]{0:T(512)S(1)}, u32[]{:S(2)}) copy-start(s32[512]{0:T(512)S(1)} %convert_add_fusion.1) | copy-start | bytes 6148
  799.6 67.0 %collective-permute-start.7 = (bf16[512,2816]{1,0:T(8,128)(2,1)}, bf16[512,2816]{1,0:T(8,128)(2,1)}, u32[]{:S(2)}, u32[]{:S(2)}) collective-permute-start(bf16[512,2816]{1,0:T(8,128)(2,1)} %cut.7), channel_id=1, source_target_pairs={{0,8},{8,16},{16,24},{24,0},{1,9},{9,17},{17,25},{25,1},{2,10},{10... | collective-permute-start | bytes 8650760 | tf_op jit(solution)/shard_map/ppermute | solution.py:345
  820.8 48.5 %all-to-all-start.11 = ((bf16[8,96,2048]{2,1,0:T(8,128)(2,1)}), bf16[8,96,2048]{2,1,0:T(8,128)(2,1)}, u32[]{:S(2)}, u32[]{:S(2)}) async-start(bf16[8,96,2048]{2,1,0:T(8,128)(2,1)} %bitcast.422), calls=%async_computation.11 | async-start | bytes 6291456 | tf_op jit(solution)/shard_map/all_to_all | solution.py:332
  866.6 125.2 %collective-permute-start.8 = (bf16[512,2816]{1,0:T(8,128)(2,1)}, bf16[512,2816]{1,0:T(8,128)(2,1)}, u32[]{:S(2)}, u32[]{:S(2)}) collective-permute-start(bf16[512,2816]{1,0:T(8,128)(2,1)} %cut.6), channel_id=1, source_target_pairs={{0,16},{8,24},{16,0},{24,8},{1,17},{9,25},{17,1},{25,9},{2,18},{10... | collective-permute-start | bytes 8650760 | tf_op jit(solution)/shard_map/ppermute | solution.py:345
  869.3 42.4 %all-to-all-start.10 = ((bf16[8,96,2048]{2,1,0:T(8,128)(2,1)}), bf16[8,96,2048]{2,1,0:T(8,128)(2,1)}, u32[]{:S(2)}, u32[]{:S(2)}) async-start(bf16[8,96,2048]{2,1,0:T(8,128)(2,1)} %bitcast.417), calls=%async_computation.10 | async-start | bytes 6291456 | tf_op jit(solution)/shard_map/all_to_all | solution.py:332
  876.7 131.0 %copy-start.98 = (bf16[768,128]{1,0:T(8,128)(2,1)}, bf16[768,128]{1,0:T(8,128)(2,1)S(1)}, u32[]{:S(2)}) copy-start(bf16[768,128]{1,0:T(8,128)(2,1)S(1)} %fusion.87) | copy-start | bytes 589828
  911.6 84.3 %all-to-all-start.21 = ((f32[8,4,96]{2,1,0:T(4,128)}), f32[8,4,96]{2,1,0:T(4,128)S(1)}, u32[]{:S(2)}, u32[]{:S(2)}) async-start(f32[8,4,96]{2,1,0:T(4,128)} %maximum_bitcast_fusion), calls=%async_computation.21 | async-start | bytes 32768 | tf_op jit(solution)/shard_map/all_to_all | solution.py:332
  995.9 48.7 %all-to-all-start.14 = ((bf16[8,96,2048]{2,1,0:T(8,128)(2,1)}), bf16[8,96,2048]{2,1,0:T(8,128)(2,1)}, u32[]{:S(2)}, u32[]{:S(2)}) async-start(bf16[8,96,2048]{2,1,0:T(8,128)(2,1)} %bitcast.423), calls=%async_computation.14 | async-start | bytes 6291456 | tf_op jit(solution)/shard_map/all_to_all | solution.py:332
  1044.6 44.7 %all-to-all-start.17 = ((bf16[8,96,2176]{2,1,0:T(8,128)(2,1)}), bf16[8,96,2176]{2,1,0:T(8,128)(2,1)}, u32[]{:S(2)}, u32[]{:S(2)}) async-start(bf16[8,96,2176]{2,1,0:T(8,128)(2,1)} %bitcast.452), calls=%async_computation.17 | async-start | bytes 6684672 | tf_op jit(solution)/shard_map/all_to_all | solution.py:332
  1089.3 46.5 %all-to-all-start.13 = ((bf16[8,96,2176]{2,1,0:T(8,128)(2,1)}), bf16[8,96,2176]{2,1,0:T(8,128)(2,1)}, u32[]{:S(2)}, u32[]{:S(2)}) async-start(bf16[8,96,2176]{2,1,0:T(8,128)(2,1)} %bitcast.450), calls=%async_computation.13 | async-start | bytes 6684672 | tf_op jit(solution)/shard_map/all_to_all | solution.py:332
  1135.9 50.4 %all-to-all-start.12 = ((bf16[8,96,2176]{2,1,0:T(8,128)(2,1)}), bf16[8,96,2176]{2,1,0:T(8,128)(2,1)}, u32[]{:S(2)}, u32[]{:S(2)}) async-start(bf16[8,96,2176]{2,1,0:T(8,128)(2,1)} %bitcast.451), calls=%async_computation.12 | async-start | bytes 6684672 | tf_op jit(solution)/shard_map/all_to_all | solution.py:332
  1186.3 50.0 %all-to-all-start.15 = ((bf16[8,96,2176]{2,1,0:T(8,128)(2,1)}), bf16[8,96,2176]{2,1,0:T(8,128)(2,1)}, u32[]{:S(2)}, u32[]{:S(2)}) async-start(bf16[8,96,2176]{2,1,0:T(8,128)(2,1)} %bitcast.449), calls=%async_computation.15 | async-start | bytes 6684672 | tf_op jit(solution)/shard_map/all_to_all | solution.py:332
  1205.4 45.4 %collective-permute-start.10 = (bf16[256,2176]{1,0:T(8,128)(2,1)}, bf16[256,2176]{1,0:T(8,128)(2,1)}, u32[]{:S(2)}, u32[]{:S(2)}) collective-permute-start(bf16[256,2176]{1,0:T(8,128)(2,1)} %pad_maximum_fusion.2), channel_id=1, source_target_pairs={{0,8},{8,16},{16,24},{24,0},{1,9},{9,17},{17,25},{25,1},{2,10},{10... | collective-permute-start | bytes 3342344 | tf_op jit(solution)/shard_map/ppermute | solution.py:345
  1212.1 70.3 %collective-permute-start.11 = (bf16[256,2176]{1,0:T(8,128)(2,1)}, bf16[256,2176]{1,0:T(8,128)(2,1)}, u32[]{:S(2)}, u32[]{:S(2)}) collective-permute-start(bf16[256,2176]{1,0:T(8,128)(2,1)} %pad_maximum_fusion.3), channel_id=1, source_target_pairs={{0,16},{8,24},{16,0},{24,8},{1,17},{9,25},{17,1},{25,9},{2,18},{10... | collective-permute-start | bytes 3342344 | tf_op jit(solution)/shard_map/ppermute | solution.py:345
  1242.2 51.0 %collective-permute-start.12 = (bf16[256,2176]{1,0:T(8,128)(2,1)}, bf16[256,2176]{1,0:T(8,128)(2,1)}, u32[]{:S(2)}, u32[]{:S(2)}) collective-permute-start(bf16[256,2176]{1,0:T(8,128)(2,1)} %pad_maximum_fusion.4), channel_id=1, source_target_pairs={{0,24},{8,0},{16,8},{24,16},{1,25},{9,1},{17,9},{25,17},{2,26},{10... | collective-permute-start | bytes 3342344 | tf_op jit(solution)/shard_map/ppermute | solution.py:345
  1245.5 58.2 %all-to-all-start.16 = ((bf16[8,96,2048]{2,1,0:T(8,128)(2,1)}), bf16[8,96,2048]{2,1,0:T(8,128)(2,1)}, u32[]{:S(2)}, u32[]{:S(2)}) async-start(bf16[8,96,2048]{2,1,0:T(8,128)(2,1)} %bitcast.425), calls=%async_computation.16 | async-start | bytes 6291456 | tf_op jit(solution)/shard_map/all_to_all | solution.py:332
  1250.1 60.8 %reduce-scatter.2.cloned.1.call-start = ((), (), s32[]{:S(2)}) async-start(), calls=%async_computation.29 | async-start | bytes 2396160 | tf_op jit(solution)/shard_map/reduce_scatter | solution.py:858
  1250.7 47.0 %copy-start.122 = (bf16[2048,8]{0,1:T(8,128)(2,1)S(1)}, bf16[2048,8]{0,1:T(8,128)(2,1)}, u32[]{:S(2)}) copy-start(bf16[2048,8]{0,1:T(8,128)(2,1)} %param.33) | copy-start | bytes 98308
  1250.8 47.0 %copy-start.127 = (f32[2048]{0:T(1024)S(1)}, f32[2048]{0:T(1024)}, u32[]{:S(2)}) copy-start(f32[2048]{0:T(1024)} %param.32) | copy-start | bytes 24580
  1306.4 42.4 %all-to-all-start.18 = ((bf16[8,96,2048]{2,1,0:T(8,128)(2,1)}), bf16[8,96,2048]{2,1,0:T(8,128)(2,1)}, u32[]{:S(2)}, u32[]{:S(2)}) async-start(bf16[8,96,2048]{2,1,0:T(8,128)(2,1)} %bitcast.424), calls=%async_computation.18 | async-start | bytes 6291456 | tf_op jit(solution)/shard_map/all_to_all | solution.py:332
  1310.9 269.1 %all-gather.14.cloned.1.call-start = ((), (), s32[]{:S(2)}) async-start(), calls=%async_computation.30 | async-start | bytes 8785920 | tf_op jit(solution)/shard_map/all_gather | solution.py:877
  1360.8 52.1 %all-to-all-start.19 = ((bf16[8,96,2048]{2,1,0:T(8,128)(2,1)}), bf16[8,96,2048]{2,1,0:T(8,128)(2,1)}, u32[]{:S(2)}, u32[]{:S(2)}) async-start(bf16[8,96,2048]{2,1,0:T(8,128)(2,1)} %bitcast.455), calls=%async_computation.19 | async-start | bytes 6291456 | tf_op jit(solution)/shard_map/all_to_all | solution.py:332
  1412.9 65.5 %all-to-all-start.20 = ((bf16[8,96,2048]{2,1,0:T(8,128)(2,1)}), bf16[8,96,2048]{2,1,0:T(8,128)(2,1)}, u32[]{:S(2)}, u32[]{:S(2)}) async-start(bf16[8,96,2048]{2,1,0:T(8,128)(2,1)} %bitcast.426), calls=%async_computation.20 | async-start | bytes 6291456 | tf_op jit(solution)/shard_map/all_to_all | solution.py:332
  1478.5 42.7 %all-to-all-start.22 = ((bf16[8,96,2048]{2,1,0:T(8,128)(2,1)}), bf16[8,96,2048]{2,1,0:T(8,128)(2,1)}, u32[]{:S(2)}, u32[]{:S(2)}) async-start(bf16[8,96,2048]{2,1,0:T(8,128)(2,1)} %bitcast.454), calls=%async_computation.22 | async-start | bytes 6291456 | tf_op jit(solution)/shard_map/all_to_all | solution.py:332
  1533.1 42.4 %all-to-all-start.23 = ((bf16[8,96,2048]{2,1,0:T(8,128)(2,1)}), bf16[8,96,2048]{2,1,0:T(8,128)(2,1)}, u32[]{:S(2)}, u32[]{:S(2)}) async-start(bf16[8,96,2048]{2,1,0:T(8,128)(2,1)} %bitcast.456), calls=%async_computation.23 | async-start | bytes 6291456 | tf_op jit(solution)/shard_map/all_to_all | solution.py:332
  1539.9 62.6 %collective-permute-start.16 = (bf16[288,2048]{1,0:T(8,128)(2,1)S(1)}, bf16[288,2048]{1,0:T(8,128)(2,1)}, u32[]{:S(2)}, u32[]{:S(2)}) collective-permute-start(bf16[288,2048]{1,0:T(8,128)(2,1)S(1)} %fusion.83), channel_id=1, source_target_pairs={{0,16},{8,24},{16,0},{24,8},{1,17},{9,25},{17,1},{25,9},{2,18},{10... | collective-permute-start | bytes 3538952 | tf_op jit(solution)/shard_map/ppermute | solution.py:345
  1551.4 50.6 %collective-permute-start.17 = (bf16[288,2048]{1,0:T(8,128)(2,1)}, bf16[288,2048]{1,0:T(8,128)(2,1)}, u32[]{:S(2)}, u32[]{:S(2)}) collective-permute-start(bf16[288,2048]{1,0:T(8,128)(2,1)} %fusion.84), channel_id=1, source_target_pairs={{0,24},{8,0},{16,8},{24,16},{1,25},{9,1},{17,9},{25,17},{2,26},{10... | collective-permute-start | bytes 3538952 | tf_op jit(solution)/shard_map/ppermute | solution.py:345
  1556.0 74.7 %collective-permute-start.15 = (bf16[288,2048]{1,0:T(8,128)(2,1)}, bf16[288,2048]{1,0:T(8,128)(2,1)}, u32[]{:S(2)}, u32[]{:S(2)}) collective-permute-start(bf16[288,2048]{1,0:T(8,128)(2,1)} %fusion.82), channel_id=1, source_target_pairs={{0,8},{8,16},{16,24},{24,0},{1,9},{9,17},{17,25},{25,1},{2,10},{10... | collective-permute-start | bytes 3538952 | tf_op jit(solution)/shard_map/ppermute | solution.py:345
  1575.5 70.3 %all-to-all-start.24 = ((bf16[8,96,2048]{2,1,0:T(8,128)(2,1)}), bf16[8,96,2048]{2,1,0:T(8,128)(2,1)}, u32[]{:S(2)}, u32[]{:S(2)}) async-start(bf16[8,96,2048]{2,1,0:T(8,128)(2,1)} %bitcast.427), calls=%async_computation.24 | async-start | bytes 6291456 | tf_op jit(solution)/shard_map/all_to_all | solution.py:332
  1579.9 196.5 %all-gather.20.cloned.1.call-start = ((), (), s32[]{:S(2)}) async-start(), calls=%async_computation.33 | async-start | bytes 3784704 | tf_op jit(solution)/shard_map/all_gather | solution.py:894
  1645.8 89.8 %all-to-all-start.25 = ((bf16[8,96,2048]{2,1,0:T(8,128)(2,1)}), bf16[8,96,2048]{2,1,0:T(8,128)(2,1)}, u32[]{:S(2)}, u32[]{:S(2)}) async-start(bf16[8,96,2048]{2,1,0:T(8,128)(2,1)} %bitcast.428), calls=%async_computation.25 | async-start | bytes 6291456 | tf_op jit(solution)/shard_map/all_to_all | solution.py:332
  1654.3 50.7 %collective-permute-start.9 = (bf16[256,2048]{1,0:T(8,128)(2,1)}, bf16[256,2048]{1,0:T(8,128)(2,1)S(1)}, u32[]{:S(2)}, u32[]{:S(2)}) collective-permute-start(bf16[256,2048]{1,0:T(8,128)(2,1)} %convolution_convert_fusion.16), channel_id=1, source_target_pairs={{0,8},{8,16},{16,24},{24,0},{1,9},{9,17},{17,25},{25,1},{2,10},{10... | collective-permute-start | bytes 3145736 | tf_op jit(solution)/shard_map/ppermute | solution.py:345
  1681.0 54.6 %collective-permute-start.13 = (bf16[256,2048]{1,0:T(8,128)(2,1)}, bf16[256,2048]{1,0:T(8,128)(2,1)}, u32[]{:S(2)}, u32[]{:S(2)}) collective-permute-start(bf16[256,2048]{1,0:T(8,128)(2,1)} %convolution_convert_fusion.15), channel_id=1, source_target_pairs={{0,16},{8,24},{16,0},{24,8},{1,17},{9,25},{17,1},{25,9},{2,18},{10... | collective-permute-start | bytes 3145736 | tf_op jit(solution)/shard_map/ppermute | solution.py:345
  1686.8 64.0 %collective-permute-start.14 = (bf16[256,2048]{1,0:T(8,128)(2,1)}, bf16[256,2048]{1,0:T(8,128)(2,1)}, u32[]{:S(2)}, u32[]{:S(2)}) collective-permute-start(bf16[256,2048]{1,0:T(8,128)(2,1)} %convolution_convert_fusion.14), channel_id=1, source_target_pairs={{0,24},{8,0},{16,8},{24,16},{1,25},{9,1},{17,9},{25,17},{2,26},{10... | collective-permute-start | bytes 3145736 | tf_op jit(solution)/shard_map/ppermute | solution.py:345
  1690.0 60.8 %copy-start.90 = (bf16[512,768]{1,0:T(8,128)(2,1)S(1)}, bf16[512,768]{1,0:T(8,128)(2,1)}, u32[]{:S(2)}) copy-start(bf16[512,768]{1,0:T(8,128)(2,1)} %get-tuple-element.210) | copy-start | bytes 2359300
  (159 other events, 1143.9 us)
Sparse Core Ops, SparseCore 0:
  9.6 264.2 all-gather.15
  276.4 158.8 all-gather.17
  436.8 152.0 all-gather.9
  685.2 84.9 all-gather.11
  1254.1 47.6 reduce-scatter.1
  1348.9 121.3 all-gather.13
  1635.5 140.8 all-gather.19
